TPU v7x, 32 devices: a whole 2x2x4 slice. The times are simulated.
32 devices in a mesh: frame: 4 (over z), space: 4 (over y, core), tensor: 2 (over x).
Axes of the slice: x: 2, y: 2, z: 4, core: 2. Of those that a mesh axis runs over, the one named last changes fastest.
Arguments:
- inputs: bfloat16 [2, 8, 576, 2048], P(None, 'frame', 'space'), may hold values from -6 to 6
- upstream: bfloat16 [2, 8, 576, 2048], P(None, 'frame', 'space'), may hold values from -6 to 6
- action_ids: int32 [2, 8], P(None, 'frame'), may hold values from 0 to 7
- frame_time: int32 [2, 8], replicated, may hold values from 0 to 7, each once within a row
- action_table: float32 [8, 2048], replicated, may hold values from -3 to 3
- gain: float32 [2048], replicated, may hold values from 0.5 to 1.5
- w_qkv: bfloat16 [2048, 3, 2048], P(('frame', 'space'), None, 'tensor'), may hold values from -1 to 1
- w_out: bfloat16 [2048, 2048], P(('frame', 'space'), 'tensor'), may hold values from -0.125 to 0.125
Outputs:
- grad_inputs: bfloat16 [2, 8, 576, 2048], P(None, 'frame', 'space')
- grad_qkv: float32 [2048, 3, 2048], P(('frame', 'space'), None, 'tensor')
- grad_out_proj: float32 [2048, 2048], P(('frame', 'space'), 'tensor')
- grad_gain: float32 [2048], replicated
- grad_actions: float32 [8, 2048], replicated
All inputs are finite; a program needn't handle non-finite values.
Results may differ from a plain program's by a relative error of at most 0.018.
The roundings to bfloat16 on the way count: a program that leaves them out, or rounds other values in their place, can miss the bound.
Values may be sent and summed in bfloat16 or wider, within the bound.
No kernel may reach another device: no remote copies, remote signals or barrier semaphores. Data moves between devices by JAX's collectives and lax.ppermute only.
A program may use at most 128 MiB of HBM per device.

v0:
```python
import functools
import math

import jax
import jax.numpy as jnp
from jax import lax
from jax.experimental import pallas as pl
from jax.experimental.pallas import tpu as pltpu
from jax.sharding import PartitionSpec as P

HEAD = 128
NORM_EPSILON = 1e-06
UPSTREAM_TOP = 6.0
WIRE = jnp.float16
WIRE_TOP = 32768.0


def after(value, *earlier):
    return lax.optimization_barrier((value, *earlier))[0]


def dot_nt(a, b):
    return lax.dot_general(a, b, (((1,), (1,)), ((), ())), preferred_element_type=jnp.float32)


def dot_nn(a, b):
    return lax.dot_general(a, b, (((1,), (0,)), ((), ())), preferred_element_type=jnp.float32)


def dot_tn(a, b):
    return lax.dot_general(a, b, (((0,), (0,)), ((), ())), preferred_element_type=jnp.float32)


def attention_kernel(
    late_ref, early_ref, qkv_ref, grad_ref, mixed_ref, merged_ref, peak_qkv_ref, peak_out_ref
):
    frames, group, width = grad_ref.shape
    rows = frames * group
    scale = 1.0 / math.sqrt(HEAD)

    def load(ref, start):
        block = ref[:, :, start : start + HEAD]
        if group % 16:
            return block.astype(jnp.float32).reshape(rows, HEAD).astype(jnp.bfloat16)
        return block.reshape(rows, HEAD)

    def store(ref, start, value):
        if group % 16:
            ref[:, :, start : start + HEAD] = value.reshape(frames, group, HEAD).astype(
                jnp.bfloat16
            )
        else:
            ref[:, :, start : start + HEAD] = value.astype(jnp.bfloat16).reshape(
                frames, group, HEAD
            )

    def peak(value):
        return jnp.max(jnp.abs(value).reshape(rows // 8, 8, HEAD), axis=0)

    @pl.when(pl.program_id(0) == 0)
    def _():
        peak_qkv_ref[...] = jnp.zeros_like(peak_qkv_ref)
        peak_out_ref[...] = jnp.zeros_like(peak_out_ref)

    row_id = lax.broadcasted_iota(jnp.int32, (rows, rows), 0)
    col_id = lax.broadcasted_iota(jnp.int32, (rows, rows), 1)
    allowed = (row_id % group == col_id % group) & (early_ref[...] <= late_ref[...])
    starts = range(0, width, HEAD)
    query = [load(qkv_ref, i) for i in starts]
    key = [load(qkv_ref, width + i) for i in starts]
    value = [load(qkv_ref, 2 * width + i) for i in starts]
    grad = [load(grad_ref, i) for i in starts]
    heads = range(len(query))
    scores = [jnp.where(allowed, dot_nt(query[h], key[h]) * scale, -1e30) for h in heads]
    grad_probs = [dot_nt(grad[h], value[h]) for h in heads]
    exponent = [jnp.exp(scores[h] - jnp.max(scores[h], -1, keepdims=True)) for h in heads]
    probabilities = [exponent[h] / jnp.sum(exponent[h], -1, keepdims=True) for h in heads]
    rounded = [probabilities[h].astype(jnp.bfloat16) for h in heads]
    mean_grad = [jnp.sum(grad_probs[h] * probabilities[h], -1, keepdims=True) for h in heads]
    mixed = [dot_nn(rounded[h], value[h]) for h in heads]
    grad_value = [dot_tn(rounded[h], grad[h]) for h in heads]
    grad_scores = [probabilities[h] * (grad_probs[h] - mean_grad[h]) for h in heads]
    high = [grad_scores[h].astype(jnp.bfloat16) for h in heads]
    low = [(grad_scores[h] - high[h].astype(jnp.float32)).astype(jnp.bfloat16) for h in heads]
    grad_query = [(dot_nn(high[h], key[h]) + dot_nn(low[h], key[h])) * scale for h in heads]
    grad_key = [(dot_tn(high[h], query[h]) + dot_tn(low[h], query[h])) * scale for h in heads]
    top_out, top_qkv = peak_out_ref[...], peak_qkv_ref[...]
    for h, start in enumerate(starts):
        store(mixed_ref, start, mixed[h])
        store(merged_ref, start, grad_query[h])
        store(merged_ref, width + start, grad_key[h])
        store(merged_ref, 2 * width + start, grad_value[h])
        top_out = jnp.maximum(top_out, peak(mixed[h]))
        for term in (grad_query[h], grad_key[h], grad_value[h]):
            top_qkv = jnp.maximum(top_qkv, peak(term))
    peak_out_ref[...] = top_out
    peak_qkv_ref[...] = top_qkv


def temporal_attention(qkv, grad_heads, times):
    frames, pairs, width = grad_heads.shape
    group = 16 if pairs % 16 == 0 else 8
    rows = frames * group
    per_row = jnp.repeat(times.astype(jnp.float32), group)
    work = pairs // group * rows * rows * (width // HEAD)
    fixed = lambda i: (0, 0)
    moving = lambda i: (0, i, 0)
    return pl.pallas_call(
        attention_kernel,
        grid=(pairs // group,),
        in_specs=[
            pl.BlockSpec((rows, 1), fixed),
            pl.BlockSpec((1, rows), fixed),
            pl.BlockSpec((frames, group, 3 * width), moving),
            pl.BlockSpec((frames, group, width), moving),
        ],
        out_specs=[
            pl.BlockSpec((frames, group, width), moving),
            pl.BlockSpec((frames, group, 3 * width), moving),
            pl.BlockSpec((8, HEAD), fixed),
            pl.BlockSpec((8, HEAD), fixed),
        ],
        out_shape=[
            jax.ShapeDtypeStruct((frames, pairs, width), jnp.bfloat16),
            jax.ShapeDtypeStruct((frames, pairs, 3 * width), jnp.bfloat16),
            jax.ShapeDtypeStruct((8, HEAD), jnp.float32),
            jax.ShapeDtypeStruct((8, HEAD), jnp.float32),
        ],
        compiler_params=pltpu.CompilerParams(vmem_limit_bytes=40 * 1024 * 1024),
        cost_estimate=pl.CostEstimate(
            flops=16 * work * HEAD,
            bytes_accessed=16 * frames * pairs * width,
            transcendentals=work,
        ),
        name="temporal_attention",
    )(per_row[:, None], per_row[None, :], qkv, grad_heads)


def on_device(
    depth, spaces, tensors, inputs, upstream, action_ids, frame_time, action_table, gain, w_qkv, w_out
):
    batch, local_frames, local_space, features = inputs.shape
    actions = action_table.shape[0]
    shard_rows, _, channels = w_qkv.shape
    z = lax.axis_index("frame")
    s = lax.axis_index("space")
    x = lax.axis_index("tensor")
    y, core = s // 2, s % 2
    frames = depth * local_frames
    pairs = batch * local_space // depth
    slots = depth // batch
    slice_width = features // tensors
    head_width = channels // 2
    width = 4 * head_width
    tokens = frames * 2 * pairs

    def ring(value, shift):
        return lax.ppermute(value, "frame", [(i, (i + shift) % depth) for i in range(depth)])

    def swap_z(value, bit):
        return lax.ppermute(value, "frame", [(i, i ^ bit) for i in range(depth)])

    def swap_core(value):
        return lax.ppermute(value, "space", [(i, i ^ 1) for i in range(spaces)])

    def swap_y(value):
        return lax.ppermute(value, "space", [(i, i ^ 2) for i in range(spaces)])

    def swap_x(value):
        return lax.ppermute(value, "tensor", [(0, 1), (1, 0)])

    def join_x(own):
        if tensors == 2:
            other = swap_x(own)
            first = jnp.where(x == 0, own, other)
            second = jnp.where(x == 0, other, own)
            return jnp.concatenate([first, second], -1)
        return lax.all_gather(own, "tensor", axis=own.ndim - 1, tiled=True)

    def cut_x(value, which=None):
        which = x if which is None else which
        return lax.dynamic_slice_in_dim(value, which * slice_width, slice_width, value.ndim - 1)

    def place(j):
        return j // slots, (j % slots) * pairs

    shards = [w_qkv[:, 0], w_qkv[:, 1], w_qkv[:, 2], w_out]

    def core_half(which):
        return jnp.concatenate(
            [jnp.where(which == 0, t[:, :head_width], t[:, head_width:]) for t in shards], 1
        )

    mine, sent = core_half(core), core_half(1 - core)
    other = swap_core(sent)
    block = jnp.concatenate(
        [jnp.where(core == 0, mine, other), jnp.where(core == 0, other, mine)], 0
    )

    def pieces(rows, k, start, size):
        rollout, first = place((z + k) % depth)
        return lax.dynamic_slice(
            rows, (rollout, 0, first, start), (1, local_frames, pairs, size)
        )[0]

    collected = []
    for k in range(depth):
        if k == 0:
            collected.append([pieces(rows, k, 0, features) for rows in (inputs, upstream)])
            continue
        start = x * slice_width
        if k > 1:
            start = after(start, sent)
        piece = jnp.stack([pieces(rows, k, start, slice_width) for rows in (inputs, upstream)])
        piece = join_x(ring(piece, k))
        collected.append([piece[0], piece[1]])
    own_inputs = jnp.concatenate([both_rows[0] for both_rows in collected], 0)
    own_upstream = jnp.concatenate([both_rows[1] for both_rows in collected], 0)

    block_rows = 2 * shard_rows
    weights = jnp.zeros((features, width), jnp.bfloat16)
    for k in range(depth):
        if k:
            block = ring(block, 1)
        start = (z - k) % depth * (2 * block_rows)
        weights = lax.dynamic_update_slice(weights, block, (start + y * block_rows, 0))
        weights = lax.dynamic_update_slice(
            weights, swap_y(block), (start + (1 - y) * block_rows, 0)
        )
    weight_qkv, weight_out = weights[:, : 3 * head_width], weights[:, 3 * head_width :]
    rollout, _ = place(z)
    ids = jnp.concatenate(
        [
            lax.dynamic_index_in_dim(
                ring(action_ids, k) if k else action_ids, rollout, 0, keepdims=False
            )
            for k in range(depth)
        ]
    )
    order = (
        (z - jnp.arange(depth, dtype=jnp.int32)[:, None]) % depth * local_frames
        + jnp.arange(local_frames, dtype=jnp.int32)[None, :]
    ).reshape(frames)
    own_time = lax.dynamic_index_in_dim(frame_time, rollout, 0, keepdims=False)
    times = jnp.sum(
        jnp.where(
            order[:, None] == jnp.arange(frames, dtype=jnp.int32)[None, :], own_time[None, :], 0
        ),
        1,
    )
    onehot = (ids[:, None] == jnp.arange(actions, dtype=jnp.int32)[None, :]).astype(jnp.float32)
    embedded = jnp.dot(onehot, action_table, precision=lax.Precision.HIGHEST)
    hidden = own_inputs.astype(jnp.float32) + embedded[:, None, :]
    inverse = lax.rsqrt(jnp.mean(hidden * hidden, -1, keepdims=True) + NORM_EPSILON)
    normed = (hidden * inverse * gain).astype(jnp.bfloat16)

    def both(own):
        return jnp.concatenate([own, swap_core(own)], 1).reshape(tokens, features)

    all_upstream = both(own_upstream)
    all_normed = both(normed)
    qkv = dot_nn(all_normed, weight_qkv).astype(jnp.bfloat16)
    grad_heads = dot_nn(all_upstream, weight_out).astype(jnp.bfloat16)
    mixed, merged, peak_qkv, peak_out = temporal_attention(
        qkv.reshape(frames, 2 * pairs, 3 * head_width),
        grad_heads.reshape(frames, 2 * pairs, head_width),
        times,
    )
    flat_mixed = mixed.reshape(tokens, head_width)
    flat_merged = merged.reshape(tokens, 3 * head_width)

    peaks = jnp.stack([jnp.max(peak_qkv), jnp.max(peak_out)])
    peaks = jnp.maximum(peaks, swap_core(peaks))
    if tensors == 2:
        peaks = jnp.maximum(peaks, swap_x(peaks))
    peaks = jnp.maximum(peaks, swap_y(peaks))
    bit = 1
    while bit < depth:
        peaks = jnp.maximum(peaks, swap_z(peaks, bit))
        bit *= 2
    peaks = jnp.maximum(peaks, 1e-25)
    all_tokens = tokens * depth * (spaces // 2)
    qkv_bound = all_tokens * math.sqrt(features) * jnp.max(jnp.abs(gain)) * peaks[0]
    out_bound = all_tokens * UPSTREAM_TOP * peaks[1]
    norm_bound = 6 * head_width * peaks[0]
    is_out = lax.broadcasted_iota(jnp.int32, (1, width), 1) >= 3 * head_width
    encoding = jnp.where(is_out, WIRE_TOP / out_bound, WIRE_TOP / qkv_bound)
    decoding = jnp.where(is_out, out_bound / WIRE_TOP, qkv_bound / WIRE_TOP)

    def weight_part(k, row, earlier):
        start = after((z - 1 - k) % depth * (2 * block_rows) + row * block_rows, earlier)
        normed_cut = lax.dynamic_slice_in_dim(all_normed, start, block_rows, 1)
        upstream_cut = lax.dynamic_slice_in_dim(all_upstream, start, block_rows, 1)
        return jnp.concatenate(
            [dot_tn(normed_cut, flat_merged), dot_tn(upstream_cut, flat_mixed)], 1
        )

    def away_part(k, earlier):
        return (weight_part(k, 1 - y, earlier) * encoding).astype(WIRE)

    def norm_part(rows):
        flat = rows.reshape(frames * pairs, 3 * head_width)
        return dot_nt(flat, weight_qkv).reshape(frames, pairs, features)

    norm_away = norm_part(merged[:, pairs:])
    away = [away_part(0, norm_away)]
    norm_here = norm_part(after(merged[:, :pairs], away[0]))
    away.append(away_part(1, norm_here))
    here = [weight_part(0, y, away[1])]
    for k in range(2, depth):
        away.append(away_part(k, here[-1]))
        here.append(weight_part(k - 1, y, away[-1]))
    here.append(weight_part(depth - 1, y, here[-1]))
    partial_norm = norm_here + swap_core(norm_away)
    row_dot = jnp.sum(partial_norm * gain * (hidden * inverse), -1, keepdims=True)
    if tensors == 2:
        row_dot = row_dot + swap_x(row_dot)
        sent = (cut_x(partial_norm, 1 - x) * (WIRE_TOP / norm_bound)).astype(WIRE)
        grad_norm = cut_x(partial_norm) + swap_x(sent).astype(jnp.float32) * (
            norm_bound / WIRE_TOP
        )
    else:
        row_dot = lax.psum(row_dot, "tensor")
        grad_norm = lax.psum_scatter(partial_norm, "tensor", scatter_dimension=2, tiled=True)
    unit_rows = (cut_x(own_inputs).astype(jnp.float32) + cut_x(embedded)[:, None, :]) * inverse
    grad_hidden = cut_x(own_upstream).astype(jnp.float32) + inverse * (
        grad_norm * cut_x(gain) - unit_rows * (row_dot / features)
    )
    grad_rows = grad_hidden.astype(jnp.bfloat16)
    grad_inputs = jnp.zeros(inputs.shape, jnp.bfloat16)
    for k in range(depth):
        piece = grad_rows[k * local_frames : (k + 1) * local_frames]
        if k:
            piece = ring(piece, depth - k)
        target, first = place((z + k) % depth)
        grad_inputs = lax.dynamic_update_slice(
            grad_inputs, join_x(piece)[None], (target, 0, first, 0)
        )

    gain_term = jnp.sum(grad_norm * unit_rows, (0, 1))
    action_term = jnp.dot(
        onehot.T, jnp.sum(grad_hidden, 1), precision=lax.Precision.HIGHEST
    )
    small = jnp.concatenate([action_term, gain_term[None, :]], 0)
    small = small + swap_core(small)
    small = small + swap_y(small)
    bit = 1
    while bit < depth:
        small = small + swap_z(small, bit)
        bit *= 2
    small = join_x(small)

    for k in range(depth):
        total = here[k] + swap_y(away[k]).astype(jnp.float32) * decoding
        if k:
            total = total + arriving.astype(jnp.float32) * decoding
        if k < depth - 1:
            arriving = ring((total * encoding).astype(WIRE), 1)
    mine = lax.dynamic_slice_in_dim(total, core * shard_rows, shard_rows, 0)
    other = swap_core(lax.dynamic_slice_in_dim(total, (1 - core) * shard_rows, shard_rows, 0))
    first = jnp.where(core == 0, mine, other).reshape(shard_rows, 4, head_width)
    second = jnp.where(core == 0, other, mine).reshape(shard_rows, 4, head_width)
    joined = jnp.concatenate([first, second], 2)
    return (grad_inputs, joined[:, :3], joined[:, 3], small[actions], small[:actions])


def solution(mesh):
    sizes = mesh.shape
    return jax.shard_map(
        functools.partial(on_device, sizes["frame"], sizes["space"], sizes["tensor"]),
        mesh=mesh,
        in_specs=(
            P(None, "frame", "space", None),
            P(None, "frame", "space", None),
            P(None, "frame"),
            P(),
            P(),
            P(),
            P(("frame", "space"), None, "tensor"),
            P(("frame", "space"), "tensor"),
        ),
        out_specs=(
            P(None, "frame", "space", None),
            P(("frame", "space"), None, "tensor"),
            P(("frame", "space"), "tensor"),
            P(),
            P(),
        ),
        check_vma=False,
    )
```

profile of v0, /device:TPU:0, one launch (start us, length us, event | category | flops | bytes accessed | tf_op | source)
XLA Modules:
  0.0 436.8 jit_solution(13356753700108946042)
XLA Ops:
  20.1 10.9 %collective-permute-done = bf16[2,2,72,1024]{3,2,1,0:T(8,128)(2,1)S(1)} collective-permute-done((bf16[2,2,72,1024]{3,2,1,0:T(8,128)(2,1)S(1)}, bf16[2,2,72,1024]{3,2,1,0:T(8,128)(2,1)S(1)}, u32[]{:S(2)}, u32[]{:S(2)}) %collective-permute-start) | collective-permute-done | bytes 589856 | tf_op jit(solution)/shard_map/ppermute | solution.py:158
  33.7 22.1 %collective-permute-done.2 = bf16[2,2,72,1024]{3,2,1,0:T(8,128)(2,1)S(1)} collective-permute-done((bf16[2,2,72,1024]{3,2,1,0:T(8,128)(2,1)}, bf16[2,2,72,1024]{3,2,1,0:T(8,128)(2,1)S(1)}, u32[]{:S(2)}, u32[]{:S(2)}) %collective-permute-start.2) | collective-permute-done | bytes 589856 | tf_op jit(solution)/shard_map/ppermute | solution.py:158
  59.5 9.3 %collective-permute-start.12 = (bf16[256,2048]{1,0:T(8,128)(2,1)}, bf16[256,2048]{1,0:T(8,128)(2,1)}, u32[]{:S(2)}, u32[]{:S(2)}) collective-permute-start(bf16[256,2048]{1,0:T(8,128)(2,1)} %get-tuple-element.65), channel_id=1, source_target_pairs={{0,8},{8,16},{16,24},{24,0},{1,9},{9,17},{17,25},{25,1},{2,10},{10... | collective-permute-start | bytes 3145736 | tf_op jit(solution)/shard_map/ppermute | solution.py:158
  71.6 12.1 %collective-permute-done.5 = bf16[2,2,72,1024]{3,2,1,0:T(8,128)(2,1)S(1)} collective-permute-done((bf16[2,2,72,1024]{3,2,1,0:T(8,128)(2,1)S(1)}, bf16[2,2,72,1024]{3,2,1,0:T(8,128)(2,1)S(1)}, u32[]{:S(2)}, u32[]{:S(2)}) %collective-permute-start.5) | collective-permute-done | bytes 589856 | tf_op jit(solution)/shard_map/ppermute | solution.py:170
  89.7 5.0 %collective-permute-done.12 = bf16[256,2048]{1,0:T(8,128)(2,1)} collective-permute-done((bf16[256,2048]{1,0:T(8,128)(2,1)}, bf16[256,2048]{1,0:T(8,128)(2,1)}, u32[]{:S(2)}, u32[]{:S(2)}) %collective-permute-start.12) | collective-permute-done | bytes 1048608 | tf_op jit(solution)/shard_map/ppermute | solution.py:158
  94.7 4.1 collective-permute-start.14
  101.5 23.9 %collective-permute-done.14 = bf16[256,2048]{1,0:T(8,128)(2,1)} collective-permute-done((bf16[256,2048]{1,0:T(8,128)(2,1)}, bf16[256,2048]{1,0:T(8,128)(2,1)}, u32[]{:S(2)}, u32[]{:S(2)}) %collective-permute-start.14) | collective-permute-done | bytes 1048608 | tf_op jit(solution)/shard_map/ppermute | solution.py:158
  132.4 4.5 %collective-permute-done.13 = bf16[256,2048]{1,0:T(8,128)(2,1)} collective-permute-done((bf16[256,2048]{1,0:T(8,128)(2,1)}, bf16[256,2048]{1,0:T(8,128)(2,1)}, u32[]{:S(2)}, u32[]{:S(2)}) %collective-permute-start.13) | collective-permute-done | bytes 1048608 | tf_op jit(solution)/shard_map/ppermute | solution.py:167
  141.6 10.8 %collective-permute-done.16 = bf16[256,2048]{1,0:T(8,128)(2,1)} collective-permute-done((bf16[256,2048]{1,0:T(8,128)(2,1)}, bf16[256,2048]{1,0:T(8,128)(2,1)}, u32[]{:S(2)}, u32[]{:S(2)}) %collective-permute-start.16) | collective-permute-done | bytes 1048608 | tf_op jit(solution)/shard_map/ppermute | solution.py:158
  162.9 18.4 %collective-permute-done.17 = bf16[256,2048]{1,0:T(8,128)(2,1)S(1)} collective-permute-done((bf16[256,2048]{1,0:T(8,128)(2,1)}, bf16[256,2048]{1,0:T(8,128)(2,1)S(1)}, u32[]{:S(2)}, u32[]{:S(2)}) %collective-permute-start.17) | collective-permute-done | bytes 1048608 | tf_op jit(solution)/shard_map/ppermute | solution.py:167
  184.2 7.8 %convolution_convert_fusion = bf16[1152,1536]{1,0:T(8,128)(2,1)S(1)} fusion(bf16[1152,2048]{1,0:T(8,128)(2,1)S(1)} %bitcast.130, bf16[2048,2048]{1,0:T(8,128)(2,1)S(1)} %constant_dynamic-update-slice_fusion), kind=kOutput, calls=%fused_computation | convolution fusion | flops 7249526784 | bytes 14548992 | tf_op jit(solution)/shard_map/dot_general | solution.py:27
  191.9 7.8 %temporal_attention.1 = (bf16[8,144,512]{2,1,0:T(8,128)(2,1)S(1)}, bf16[8,144,1536]{2,1,0:T(8,128)(2,1)S(1)}, f32[8,128]{1,0:T(8,128)S(1)}, f32[8,128]{1,0:T(8,128)S(1)}) custom-call(f32[128,1]{1,0:T(8,128)S(1)} %broadcast_in_dim_reshape.9.late_ref, f32[1,128]{1,0:T(1,128)S(1)} %broadcast_in_dim_reshape.8.early_ref, bf16[8,144,1536]{2,1,0:T(8,128)(2,1)S(1)} %bitcast.107, ...), custom_call_target="tpu_custom_call" | custom-call | flops 1207959552 | bytes 9437184 | tf_op jit(solution)/shard_map/temporal_attention/pallas_call | solution.py:108
  201.5 5.8 %fusion.2 = f32[8,72,2048]{2,1,0:T(8,128)} fusion(bf16[2048,2048]{1,0:T(8,128)(2,1)S(1)} %constant_dynamic-update-slice_fusion, bf16[8,144,1536]{2,1,0:T(8,128)(2,1)S(1)} %get-tuple-element.20), kind=kOutput, calls=%fused_computation.3 | convolution fusion | flops 3623878656 | bytes 12779520 | tf_op jit(solution)/shard_map/dot_general | solution.py:23
  210.2 4.6 %fusion.58 = f32[256,1536]{1,0:T(8,128)} fusion(bf16[1152,1536]{1,0:T(8,128)(2,1)} %bitcast.109, bf16[1152,2048]{1,0:T(8,128)(2,1)} %bitcast.131, s32[]{:T(128)S(6)} %select_n.487), kind=kOutput, calls=%fused_computation.105 | convolution fusion | flops 905969664 | bytes 5701636 | tf_op jit(solution)/shard_map/dot_general | solution.py:31
  241.9 9.4 %collective-permute-start.22 = (f32[2]{0:T(128)S(1)}, f32[2]{0:T(128)S(1)}, u32[]{:S(2)}, u32[]{:S(2)}) collective-permute-start(f32[2]{0:T(128)S(1)} %max.20), channel_id=1, source_target_pairs={{0,8},{8,0},{16,24},{24,16},{1,9},{9,1},{17,25},{25,17},{2,10},{10... | collective-permute-start | bytes 32 | tf_op jit(solution)/shard_map/ppermute | solution.py:161
  262.1 8.2 %fusion = f32[8,72,2048]{2,1,0:T(8,128)} fusion(bf16[8,72,1536]{2,1,0:T(8,128)(2,1)S(1)} %copy-done.15, bf16[2048,2048]{1,0:T(8,128)(2,1)} %copy-done.12), kind=kOutput, calls=%fused_computation.1 | convolution fusion | flops 3623878656 | bytes 12779520 | tf_op jit(solution)/shard_map/dot_general | solution.py:23
  286.5 16.1 %collective-permute-done.37 = f16[256,2048]{1,0:T(8,128)(2,1)} collective-permute-done((f16[256,2048]{1,0:T(8,128)(2,1)}, f16[256,2048]{1,0:T(8,128)(2,1)}, u32[]{:S(2)}, u32[]{:S(2)}) %collective-permute-start.37) | collective-permute-done | bytes 1048608 | tf_op jit(solution)/shard_map/ppermute | solution.py:167
  314.7 10.3 %collective-permute-done.36 = f16[256,2048]{1,0:T(8,128)(2,1)} collective-permute-done((f16[256,2048]{1,0:T(8,128)(2,1)}, f16[256,2048]{1,0:T(8,128)(2,1)}, u32[]{:S(2)}, u32[]{:S(2)}) %collective-permute-start.36) | collective-permute-done | bytes 1048608 | tf_op jit(solution)/shard_map/ppermute | solution.py:167
  330.1 4.7 %fusion.30 = f32[256,1536]{1,0:T(8,128)} fusion(bf16[1152,1536]{1,0:T(8,128)(2,1)} %bitcast.113, bf16[1152,2048]{1,0:T(8,128)(2,1)} %bitcast.137, s32[]{:T(128)S(6)} %select_n.505), kind=kOutput, calls=%fused_computation.77 | convolution fusion | flops 905969664 | bytes 5701636 | tf_op jit(solution)/shard_map/dot_general | solution.py:31
  343.2 4.2 collective-permute-done.35
  359.8 5.4 %collective-permute-done.34 = f16[256,2048]{1,0:T(8,128)(2,1)} collective-permute-done((f16[256,2048]{1,0:T(8,128)(2,1)}, f16[256,2048]{1,0:T(8,128)(2,1)}, u32[]{:S(2)}, u32[]{:S(2)}) %collective-permute-start.34) | collective-permute-done | bytes 1048608 | tf_op jit(solution)/shard_map/ppermute | solution.py:167
  386.7 4.2 collective-permute-done.44
  403.5 14.4 %collective-permute-done.30 = bf16[2,72,1024]{2,1,0:T(8,128)(2,1)S(1)} collective-permute-done((bf16[2,72,1024]{2,1,0:T(8,128)(2,1)S(1)}, bf16[2,72,1024]{2,1,0:T(8,128)(2,1)S(1)}, u32[]{:S(2)}, u32[]{:S(2)}) %collective-permute-start.30) | collective-permute-done | bytes 294944 | tf_op jit(solution)/shard_map/ppermute | solution.py:158
  421.6 6.2 %collective-permute-done.31 = bf16[2,72,1024]{2,1,0:T(8,128)(2,1)S(1)} collective-permute-done((bf16[2,72,1024]{2,1,0:T(8,128)(2,1)S(1)}, bf16[2,72,1024]{2,1,0:T(8,128)(2,1)S(1)}, u32[]{:S(2)}, u32[]{:S(2)}) %collective-permute-start.31) | collective-permute-done | bytes 294944 | tf_op jit(solution)/shard_map/ppermute | solution.py:170
  (247 shorter events, 200.5 us)
Async XLA Ops:
  10.5 22.0 %collective-permute-start.10 = (bf16[128,2048]{1,0:T(8,128)(2,1)}, bf16[128,2048]{1,0:T(8,128)(2,1)}, u32[]{:S(2)}, u32[]{:S(2)}) collective-permute-start(bf16[128,2048]{1,0:T(8,128)(2,1)} %pad_maximum_fusion.14), channel_id=1, source_target_pairs={{0,2},{2,0},{4,6},{6,4},{1,3},{3,1},{5,7},{7,5},{8,10},{10,8},{12,... | collective-permute-start | bytes 1572872 | tf_op jit(solution)/shard_map/ppermute | solution.py:164
  16.5 39.4 %collective-permute-start.2 = (bf16[2,2,72,1024]{3,2,1,0:T(8,128)(2,1)}, bf16[2,2,72,1024]{3,2,1,0:T(8,128)(2,1)S(1)}, u32[]{:S(2)}, u32[]{:S(2)}) collective-permute-start(bf16[2,2,72,1024]{3,2,1,0:T(8,128)(2,1)} %pad_maximum_fusion.12), channel_id=1, source_target_pairs={{0,16},{8,24},{16,0},{24,8},{1,17},{9,25},{17,1},{25,9},{2,18},{10... | collective-permute-start | bytes 1769480 | tf_op jit(solution)/shard_map/ppermute | solution.py:158
  16.9 51.9 %collective-permute-start.4 = (bf16[2,2,72,1024]{3,2,1,0:T(8,128)(2,1)}, bf16[2,2,72,1024]{3,2,1,0:T(8,128)(2,1)S(1)}, u32[]{:S(2)}, u32[]{:S(2)}) collective-permute-start(bf16[2,2,72,1024]{3,2,1,0:T(8,128)(2,1)} %pad_maximum_fusion.13), channel_id=1, source_target_pairs={{0,24},{8,0},{16,8},{24,16},{1,25},{9,1},{17,9},{25,17},{2,26},{10... | collective-permute-start | bytes 1769480 | tf_op jit(solution)/shard_map/ppermute | solution.py:158
  31.0 38.4 %collective-permute-start.1 = (bf16[2,2,72,1024]{3,2,1,0:T(8,128)(2,1)S(1)}, bf16[2,2,72,1024]{3,2,1,0:T(8,128)(2,1)S(1)}, u32[]{:S(2)}, u32[]{:S(2)}) collective-permute-start(bf16[2,2,72,1024]{3,2,1,0:T(8,128)(2,1)S(1)} %collective-permute-done), channel_id=1, source_target_pairs={{0,1},{1,0},{2,3},{3,2},{4,5},{5,4},{6,7},{7,6},{8,9},{9,8},{10,11... | collective-permute-start | bytes 1769480 | tf_op jit(solution)/shard_map/ppermute | solution.py:170
  59.5 35.2 %collective-permute-start.12 = (bf16[256,2048]{1,0:T(8,128)(2,1)}, bf16[256,2048]{1,0:T(8,128)(2,1)}, u32[]{:S(2)}, u32[]{:S(2)}) collective-permute-start(bf16[256,2048]{1,0:T(8,128)(2,1)} %get-tuple-element.65), channel_id=1, source_target_pairs={{0,8},{8,16},{16,24},{24,0},{1,9},{9,17},{17,25},{25,1},{2,10},{10... | collective-permute-start | bytes 3145736 | tf_op jit(solution)/shard_map/ppermute | solution.py:158
  87.0 66.0 %collective-permute-start.9 = (bf16[8,72,2048]{2,1,0:T(8,128)(2,1)}, bf16[8,72,2048]{2,1,0:T(8,128)(2,1)}, u32[]{:S(2)}, u32[]{:S(2)}) collective-permute-start(bf16[8,72,2048]{2,1,0:T(8,128)(2,1)} %multiply_convert_fusion), channel_id=1, source_target_pairs={{0,2},{2,0},{4,6},{6,4},{1,3},{3,1},{5,7},{7,5},{8,10},{10,8},{12,... | collective-permute-start | bytes 7077896 | tf_op jit(solution)/shard_map/ppermute | solution.py:164
  88.1 39.0 %collective-permute-start.11 = (bf16[256,2048]{1,0:T(8,128)(2,1)}, bf16[256,2048]{1,0:T(8,128)(2,1)}, u32[]{:S(2)}, u32[]{:S(2)}) collective-permute-start(bf16[256,2048]{1,0:T(8,128)(2,1)} %get-tuple-element.65), channel_id=1, source_target_pairs={{0,4},{2,6},{4,0},{6,2},{1,5},{3,7},{5,1},{7,3},{8,12},{10,14},{12... | collective-permute-start | bytes 3145736 | tf_op jit(solution)/shard_map/ppermute | solution.py:167
  94.7 30.7 %collective-permute-start.14 = (bf16[256,2048]{1,0:T(8,128)(2,1)}, bf16[256,2048]{1,0:T(8,128)(2,1)}, u32[]{:S(2)}, u32[]{:S(2)}) collective-permute-start(bf16[256,2048]{1,0:T(8,128)(2,1)} %collective-permute-done.12), channel_id=1, source_target_pairs={{0,8},{8,16},{16,24},{24,0},{1,9},{9,17},{17,25},{25,1},{2,10},{10... | collective-permute-start | bytes 3145736 | tf_op jit(solution)/shard_map/ppermute | solution.py:158
  100.5 55.7 %collective-permute-start.18 = (bf16[8,72,2048]{2,1,0:T(8,128)(2,1)}, bf16[8,72,2048]{2,1,0:T(8,128)(2,1)}, u32[]{:S(2)}, u32[]{:S(2)}) collective-permute-start(bf16[8,72,2048]{2,1,0:T(8,128)(2,1)} %pad_maximum_fusion.2), channel_id=1, source_target_pairs={{0,2},{2,0},{4,6},{6,4},{1,3},{3,1},{5,7},{7,5},{8,10},{10,8},{12,... | collective-permute-start | bytes 7077896 | tf_op jit(solution)/shard_map/ppermute | solution.py:164
  100.6 36.3 %collective-permute-start.13 = (bf16[256,2048]{1,0:T(8,128)(2,1)}, bf16[256,2048]{1,0:T(8,128)(2,1)}, u32[]{:S(2)}, u32[]{:S(2)}) collective-permute-start(bf16[256,2048]{1,0:T(8,128)(2,1)} %collective-permute-done.12), channel_id=1, source_target_pairs={{0,4},{2,6},{4,0},{6,2},{1,5},{3,7},{5,1},{7,3},{8,12},{10,14},{12... | collective-permute-start | bytes 3145736 | tf_op jit(solution)/shard_map/ppermute | solution.py:167
  125.4 27.1 %collective-permute-start.16 = (bf16[256,2048]{1,0:T(8,128)(2,1)}, bf16[256,2048]{1,0:T(8,128)(2,1)}, u32[]{:S(2)}, u32[]{:S(2)}) collective-permute-start(bf16[256,2048]{1,0:T(8,128)(2,1)} %collective-permute-done.14), channel_id=1, source_target_pairs={{0,8},{8,16},{16,24},{24,0},{1,9},{9,17},{17,25},{25,1},{2,10},{10... | collective-permute-start | bytes 3145736 | tf_op jit(solution)/shard_map/ppermute | solution.py:158
  131.8 28.2 %collective-permute-start.15 = (bf16[256,2048]{1,0:T(8,128)(2,1)}, bf16[256,2048]{1,0:T(8,128)(2,1)S(1)}, u32[]{:S(2)}, u32[]{:S(2)}) collective-permute-start(bf16[256,2048]{1,0:T(8,128)(2,1)} %collective-permute-done.14), channel_id=1, source_target_pairs={{0,4},{2,6},{4,0},{6,2},{1,5},{3,7},{5,1},{7,3},{8,12},{10,14},{12... | collective-permute-start | bytes 3145736 | tf_op jit(solution)/shard_map/ppermute | solution.py:167
  152.4 28.9 %collective-permute-start.17 = (bf16[256,2048]{1,0:T(8,128)(2,1)}, bf16[256,2048]{1,0:T(8,128)(2,1)S(1)}, u32[]{:S(2)}, u32[]{:S(2)}) collective-permute-start(bf16[256,2048]{1,0:T(8,128)(2,1)} %collective-permute-done.16), channel_id=1, source_target_pairs={{0,4},{2,6},{4,0},{6,2},{1,5},{3,7},{5,1},{7,3},{8,12},{10,14},{12... | collective-permute-start | bytes 3145736 | tf_op jit(solution)/shard_map/ppermute | solution.py:167
  210.1 141.1 %collective-permute-start.24 = (f32[8,72,2048]{2,1,0:T(8,128)}, f32[8,72,2048]{2,1,0:T(8,128)}, u32[]{:S(2)}, u32[]{:S(2)}) collective-permute-start(f32[8,72,2048]{2,1,0:T(8,128)} %fusion.2), channel_id=1, source_target_pairs={{0,2},{2,0},{4,6},{6,4},{1,3},{3,1},{5,7},{7,5},{8,10},{10,8},{12,... | collective-permute-start | bytes 14155784 | tf_op jit(solution)/shard_map/ppermute | solution.py:164
  276.1 26.5 %collective-permute-start.37 = (f16[256,2048]{1,0:T(8,128)(2,1)}, f16[256,2048]{1,0:T(8,128)(2,1)}, u32[]{:S(2)}, u32[]{:S(2)}) collective-permute-start(f16[256,2048]{1,0:T(8,128)(2,1)} %fusion.9), channel_id=1, source_target_pairs={{0,4},{2,6},{4,0},{6,2},{1,5},{3,7},{5,1},{7,3},{8,12},{10,14},{12... | collective-permute-start | bytes 3145736 | tf_op jit(solution)/shard_map/ppermute | solution.py:167
  279.9 45.1 %collective-permute-start.36 = (f16[256,2048]{1,0:T(8,128)(2,1)}, f16[256,2048]{1,0:T(8,128)(2,1)}, u32[]{:S(2)}, u32[]{:S(2)}) collective-permute-start(f16[256,2048]{1,0:T(8,128)(2,1)} %get-tuple-element.89), channel_id=1, source_target_pairs={{0,4},{2,6},{4,0},{6,2},{1,5},{3,7},{5,1},{7,3},{8,12},{10,14},{12... | collective-permute-start | bytes 3145736 | tf_op jit(solution)/shard_map/ppermute | solution.py:167
  305.2 19.8 %collective-permute-start.38 = (f16[256,2048]{1,0:T(8,128)(2,1)}, f16[256,2048]{1,0:T(8,128)(2,1)}, u32[]{:S(2)}, u32[]{:S(2)}) collective-permute-start(f16[256,2048]{1,0:T(8,128)(2,1)} %multiply_convert_fusion.4), channel_id=1, source_target_pairs={{0,8},{8,16},{16,24},{24,0},{1,9},{9,17},{17,25},{25,1},{2,10},{10... | collective-permute-start | bytes 3145736 | tf_op jit(solution)/shard_map/ppermute | solution.py:158
  307.3 40.1 %collective-permute-start.35 = (f16[256,2048]{1,0:T(8,128)(2,1)}, f16[256,2048]{1,0:T(8,128)(2,1)S(1)}, u32[]{:S(2)}, u32[]{:S(2)}) collective-permute-start(f16[256,2048]{1,0:T(8,128)(2,1)} %get-tuple-element.90), channel_id=1, source_target_pairs={{0,4},{2,6},{4,0},{6,2},{1,5},{3,7},{5,1},{7,3},{8,12},{10,14},{12... | collective-permute-start | bytes 3145736 | tf_op jit(solution)/shard_map/ppermute | solution.py:167
  328.3 19.2 %collective-permute-start.39 = (f16[256,2048]{1,0:T(8,128)(2,1)}, f16[256,2048]{1,0:T(8,128)(2,1)}, u32[]{:S(2)}, u32[]{:S(2)}) collective-permute-start(f16[256,2048]{1,0:T(8,128)(2,1)} %multiply_convert_fusion.3), channel_id=1, source_target_pairs={{0,8},{8,16},{16,24},{24,0},{1,9},{9,17},{17,25},{25,1},{2,10},{10... | collective-permute-start | bytes 3145736 | tf_op jit(solution)/shard_map/ppermute | solution.py:158
  334.8 30.4 %collective-permute-start.34 = (f16[256,2048]{1,0:T(8,128)(2,1)}, f16[256,2048]{1,0:T(8,128)(2,1)}, u32[]{:S(2)}, u32[]{:S(2)}) collective-permute-start(f16[256,2048]{1,0:T(8,128)(2,1)} %get-tuple-element.88), channel_id=1, source_target_pairs={{0,4},{2,6},{4,0},{6,2},{1,5},{3,7},{5,1},{7,3},{8,12},{10,14},{12... | collective-permute-start | bytes 3145736 | tf_op jit(solution)/shard_map/ppermute | solution.py:167
  349.4 19.1 %collective-permute-start.40 = (f16[256,2048]{1,0:T(8,128)(2,1)S(1)}, f16[256,2048]{1,0:T(8,128)(2,1)S(1)}, u32[]{:S(2)}, u32[]{:S(2)}) collective-permute-start(f16[256,2048]{1,0:T(8,128)(2,1)S(1)} %multiply_convert_fusion.2), channel_id=1, source_target_pairs={{0,8},{8,16},{16,24},{24,0},{1,9},{9,17},{17,25},{25,1},{2,10},{10... | collective-permute-start | bytes 3145736 | tf_op jit(solution)/shard_map/ppermute | solution.py:158
  356.4 19.9 %collective-permute-start.25 = (f16[8,72,1024]{2,1,0:T(8,128)(2,1)}, f16[8,72,1024]{2,1,0:T(8,128)(2,1)}, u32[]{:S(2)}, u32[]{:S(2)}) collective-permute-start(f16[8,72,1024]{2,1,0:T(8,128)(2,1)} %multiply_convert_fusion.1), channel_id=1, source_target_pairs={{0,1},{1,0},{2,3},{3,2},{4,5},{5,4},{6,7},{7,6},{8,9},{9,8},{10,11... | collective-permute-start | bytes 3538952 | tf_op jit(solution)/shard_map/ppermute | solution.py:170
  397.8 20.1 %collective-permute-start.30 = (bf16[2,72,1024]{2,1,0:T(8,128)(2,1)S(1)}, bf16[2,72,1024]{2,1,0:T(8,128)(2,1)S(1)}, u32[]{:S(2)}, u32[]{:S(2)}) collective-permute-start(bf16[2,72,1024]{2,1,0:T(8,128)(2,1)S(1)} %get-tuple-element.51), channel_id=1, source_target_pairs={{0,16},{8,24},{16,0},{24,8},{1,17},{9,25},{17,1},{25,9},{2,18},{10... | collective-permute-start | bytes 884744 | tf_op jit(solution)/shard_map/ppermute | solution.py:158
  400.6 18.5 %collective-permute-start.28 = (bf16[2,72,1024]{2,1,0:T(8,128)(2,1)S(1)}, bf16[2,72,1024]{2,1,0:T(8,128)(2,1)S(1)}, u32[]{:S(2)}, u32[]{:S(2)}) collective-permute-start(bf16[2,72,1024]{2,1,0:T(8,128)(2,1)S(1)} %get-tuple-element.52), channel_id=1, source_target_pairs={{0,24},{8,0},{16,8},{24,16},{1,25},{9,1},{17,9},{25,17},{2,26},{10... | collective-permute-start | bytes 884744 | tf_op jit(solution)/shard_map/ppermute | solution.py:158
  (51 other events, 461.6 us)
where the time goes:
time: 444 us; the launch traced here: 437 us
  waiting for transfers between devices  196 us (44%)
  starting transfers between devices  73.3 us (17%)
  matrix products  72.2 us (16%)
  other arithmetic  50.8 us (11%)
  local copies, waits for them, and re-layouts  31.2 us (7%)
  Pallas kernels  7.78 us (2%)
  between operations  5.97 us (1%)
    ppermute x15, waiting for transfers between devices, ring(): lax.ppermute(value, 'frame', [(i, (i + shift) % depth) for i in range(dep...  90.3 us
    ppermute x10, waiting for transfers between devices, swap_y(): return lax.ppermute(value, 'space', [(i, i ^ 2) for i in range(spaces)])  62.1 us
    dot_general x16, matrix products, dot_tn(): lax.dot_general(a, b, (((0,), (0,)), ((), ())), preferred_element_type=jn...  47.3 us
    ppermute x15, starting transfers between devices, ring(): lax.ppermute(value, 'frame', [(i, (i + shift) % depth) for i in range(dep...  33.4 us
    ppermute x11, waiting for transfers between devices, swap_x(): return lax.ppermute(value, 'tensor', [(0, 1), (1, 0)])  32.7 us
    dot_general x2, matrix products, dot_nt(): lax.dot_general(a, b, (((1,), (1,)), ((), ())), preferred_element_type=jn...  14 us
    ppermute x11, starting transfers between devices, swap_x(): return lax.ppermute(value, 'tensor', [(0, 1), (1, 0)])  13.3 us
    ppermute x4, starting transfers between devices, swap_z(): return lax.ppermute(value, 'frame', [(i, i ^ bit) for i in range(depth)])  13.3 us
  transfers between devices with their start and end apart: 47, of which 28 were waited for; matrix products, arithmetic and copies ran while one was open for 30% of the time, Pallas kernels for 0%

commit v1 on v0

--- a/solution.py
+++ b/solution.py
@@ -16,7 +16,7 @@
 
 
 def after(value, *earlier):
-    return lax.optimization_barrier((value, *earlier))[0]
+    return lax.optimization_barrier((value, earlier))[0]
 
 
 def dot_nt(a, b):
@@ -169,9 +169,9 @@
     def swap_x(value):
         return lax.ppermute(value, "tensor", [(0, 1), (1, 0)])
 
-    def join_x(own):
+    def join_x(own, other=None):
         if tensors == 2:
-            other = swap_x(own)
+            other = swap_x(own) if other is None else other
             first = jnp.where(x == 0, own, other)
             second = jnp.where(x == 0, other, own)
             return jnp.concatenate([first, second], -1)
@@ -203,38 +203,51 @@
             rows, (rollout, 0, first, start), (1, local_frames, pairs, size)
         )[0]
 
-    collected = []
-    for k in range(depth):
-        if k == 0:
-            collected.append([pieces(rows, k, 0, features) for rows in (inputs, upstream)])
-            continue
-        start = x * slice_width
-        if k > 1:
-            start = after(start, sent)
+    def collect(k, start):
         piece = jnp.stack([pieces(rows, k, start, slice_width) for rows in (inputs, upstream)])
-        piece = join_x(ring(piece, k))
-        collected.append([piece[0], piece[1]])
-    own_inputs = jnp.concatenate([both_rows[0] for both_rows in collected], 0)
-    own_upstream = jnp.concatenate([both_rows[1] for both_rows in collected], 0)
+        return ring(piece, k)
 
     block_rows = 2 * shard_rows
+    arrived = collect(1, x * slice_width)
+    block = after(block, arrived)
+    blocks, across, joined, all_ids = [], [], [], [action_ids]
+    for k in range(1, depth):
+        blocks.append(block)
+        across.append(swap_y(block))
+        crossed = swap_x(arrived) if tensors == 2 else None
+        joined.append(join_x(arrived, crossed))
+        following = ring(block, 1)
+        earlier = [across[-1], joined[-1] if crossed is None else crossed]
+        if k + 1 < depth:
+            arrived = collect(k + 1, after(x * slice_width, block))
+            earlier.append(arrived)
+            all_ids.append(ring(after(action_ids, block), k))
+            earlier.append(all_ids[-1])
+            following, arrived = lax.optimization_barrier((following, arrived, earlier))[:2]
+        block = following
+    all_ids.append(ring(after(action_ids, blocks[-1]), depth - 1))
+    blocks.append(block)
+    across.append(swap_y(block))
     weights = jnp.zeros((features, width), jnp.bfloat16)
-    for k in range(depth):
-        if k:
-            block = ring(block, 1)
-        start = (z - k) % depth * (2 * block_rows)
-        weights = lax.dynamic_update_slice(weights, block, (start + y * block_rows, 0))
-        weights = lax.dynamic_update_slice(
-            weights, swap_y(block), (start + (1 - y) * block_rows, 0)
-        )
-    weight_qkv, weight_out = weights[:, : 3 * head_width], weights[:, 3 * head_width :]
+
+    def settle(weights, k, arrived, row):
+        start = (z - k) % depth * (2 * block_rows) + row * block_rows
+        return lax.dynamic_update_slice(weights, arrived, (start, 0))
+
+    for k in range(depth - 1):
+        weights = settle(weights, k, blocks[k], y)
+        if k + 2 < depth:
+            weights = settle(weights, k, across[k], 1 - y)
+    joined[-1], weights, block, all_ids, across[-2] = lax.optimization_barrier(
+        (joined[-1], weights, blocks[-1], all_ids, across[-2])
+    )
+    locals_ = [pieces(rows, 0, 0, features) for rows in (inputs, upstream)]
+    own_inputs = jnp.concatenate([locals_[0]] + [both_rows[0] for both_rows in joined], 0)
+    own_upstream = jnp.concatenate([locals_[1]] + [both_rows[1] for both_rows in joined], 0)
     rollout, _ = place(z)
     ids = jnp.concatenate(
         [
-            lax.dynamic_index_in_dim(
-                ring(action_ids, k) if k else action_ids, rollout, 0, keepdims=False
-            )
-            for k in range(depth)
+            lax.dynamic_index_in_dim(each, rollout, 0, keepdims=False) for each in all_ids
         ]
     )
     order = (
@@ -259,6 +272,12 @@
 
     all_upstream = both(own_upstream)
     all_normed = both(normed)
+    normed_t, upstream_t = lax.optimization_barrier((all_normed.T, all_upstream.T))
+
+    weights = settle(weights, depth - 2, across[-2], 1 - y)
+    weights = settle(weights, depth - 1, block, y)
+    weights = settle(weights, depth - 1, after(across[-1], normed_t, upstream_t), 1 - y)
+    weight_qkv, weight_out = weights[:, : 3 * head_width], weights[:, 3 * head_width :]
     qkv = dot_nn(all_normed, weight_qkv).astype(jnp.bfloat16)
     grad_heads = dot_nn(all_upstream, weight_out).astype(jnp.bfloat16)
     mixed, merged, peak_qkv, peak_out = temporal_attention(
@@ -269,69 +288,91 @@
     flat_mixed = mixed.reshape(tokens, head_width)
     flat_merged = merged.reshape(tokens, 3 * head_width)
 
-    peaks = jnp.stack([jnp.max(peak_qkv), jnp.max(peak_out)])
-    peaks = jnp.maximum(peaks, swap_core(peaks))
-    if tensors == 2:
-        peaks = jnp.maximum(peaks, swap_x(peaks))
-    peaks = jnp.maximum(peaks, swap_y(peaks))
-    bit = 1
-    while bit < depth:
-        peaks = jnp.maximum(peaks, swap_z(peaks, bit))
-        bit *= 2
-    peaks = jnp.maximum(peaks, 1e-25)
-    all_tokens = tokens * depth * (spaces // 2)
-    qkv_bound = all_tokens * math.sqrt(features) * jnp.max(jnp.abs(gain)) * peaks[0]
-    out_bound = all_tokens * UPSTREAM_TOP * peaks[1]
-    norm_bound = 6 * head_width * peaks[0]
-    is_out = lax.broadcasted_iota(jnp.int32, (1, width), 1) >= 3 * head_width
-    encoding = jnp.where(is_out, WIRE_TOP / out_bound, WIRE_TOP / qkv_bound)
-    decoding = jnp.where(is_out, out_bound / WIRE_TOP, qkv_bound / WIRE_TOP)
-
-    def weight_part(k, row, earlier):
-        start = after((z - 1 - k) % depth * (2 * block_rows) + row * block_rows, earlier)
-        normed_cut = lax.dynamic_slice_in_dim(all_normed, start, block_rows, 1)
-        upstream_cut = lax.dynamic_slice_in_dim(all_upstream, start, block_rows, 1)
+    own_bound = tokens * jnp.where(
+        lax.broadcasted_iota(jnp.int32, (1, width), 1) < 3 * head_width,
+        math.sqrt(features) * jnp.max(jnp.abs(gain)) * jnp.max(peak_qkv),
+        UPSTREAM_TOP * jnp.max(peak_out),
+    )
+    own_bound = jnp.maximum(own_bound, 1e-20)
+
+    def pack(value, bound):
+        exponent = jnp.ceil(jnp.log2(bound / WIRE_TOP))
         return jnp.concatenate(
-            [dot_tn(normed_cut, flat_merged), dot_tn(upstream_cut, flat_mixed)], 1
+            [value * jnp.exp2(-exponent), jnp.broadcast_to(exponent, (8, width))], 0
+        ).astype(WIRE)
+
+    def unpack(sent):
+        scale = jnp.exp2(sent[block_rows : block_rows + 1].astype(jnp.float32))
+        return sent[:block_rows].astype(jnp.float32) * scale, scale * WIRE_TOP
+
+    def weight_part(k, earlier):
+        start = after((z - 1 - k) % depth * (2 * block_rows), earlier)
+        cuts = [
+            lax.dynamic_slice_in_dim(rows, start, 2 * block_rows, 0)
+            for rows in (normed_t, upstream_t)
+        ]
+        part = jnp.concatenate([dot_nn(cuts[0], flat_merged), dot_nn(cuts[1], flat_mixed)], 1)
+        return (
+            lax.dynamic_slice_in_dim(part, y * block_rows, block_rows, 0),
+            pack(
+                lax.dynamic_slice_in_dim(part, (1 - y) * block_rows, block_rows, 0), own_bound
+            ),
         )
-
-    def away_part(k, earlier):
-        return (weight_part(k, 1 - y, earlier) * encoding).astype(WIRE)
 
     def norm_part(rows):
         flat = rows.reshape(frames * pairs, 3 * head_width)
         return dot_nt(flat, weight_qkv).reshape(frames, pairs, features)
 
     norm_away = norm_part(merged[:, pairs:])
-    away = [away_part(0, norm_away)]
-    norm_here = norm_part(after(merged[:, :pairs], away[0]))
-    away.append(away_part(1, norm_here))
-    here = [weight_part(0, y, away[1])]
-    for k in range(2, depth):
-        away.append(away_part(k, here[-1]))
-        here.append(weight_part(k - 1, y, away[-1]))
-    here.append(weight_part(depth - 1, y, here[-1]))
+    weight_parts = [weight_part(0, norm_away)]
+    norm_here = norm_part(after(merged[:, :pairs], weight_parts[0][1]))
     partial_norm = norm_here + swap_core(norm_away)
     row_dot = jnp.sum(partial_norm * gain * (hidden * inverse), -1, keepdims=True)
     if tensors == 2:
-        row_dot = row_dot + swap_x(row_dot)
-        sent = (cut_x(partial_norm, 1 - x) * (WIRE_TOP / norm_bound)).astype(WIRE)
-        grad_norm = cut_x(partial_norm) + swap_x(sent).astype(jnp.float32) * (
-            norm_bound / WIRE_TOP
-        )
+        x_away = cut_x(partial_norm, 1 - x)
+        row_scale = jnp.max(jnp.abs(partial_norm), -1, keepdims=True)
+        row_scale = jnp.maximum(row_scale, 1e-20) / WIRE_TOP
+        sent = (x_away / row_scale).astype(WIRE)
+        row_terms = swap_x(jnp.concatenate([row_dot, row_scale], -1))
+        x_terms = swap_x(sent)
     else:
         row_dot = lax.psum(row_dot, "tensor")
         grad_norm = lax.psum_scatter(partial_norm, "tensor", scatter_dimension=2, tiled=True)
+        sent = partial_norm
+
+    def chip_sum(k, earlier):
+        term, bound = unpack(after(swap_y(weight_parts[k][1]), earlier))
+        return weight_parts[k][0] + term, bound + own_bound
+
+    def ring_sum(k, arriving, earlier):
+        total, bound = chip_sum(k, earlier)
+        term, ring_bound = unpack(arriving)
+        return total + term, bound + ring_bound
+
+    weight_parts.append(weight_part(1, sent))
+    payload = pack(*chip_sum(0, weight_parts[1][1]))
+    weight_parts.append(weight_part(2, payload))
+    if tensors == 2:
+        x_terms, row_terms = after((x_terms, row_terms), weight_parts[2][1])
+        row_dot = row_dot + row_terms[..., :1]
+        grad_norm = cut_x(partial_norm) + x_terms.astype(jnp.float32) * row_terms[..., 1:]
     unit_rows = (cut_x(own_inputs).astype(jnp.float32) + cut_x(embedded)[:, None, :]) * inverse
     grad_hidden = cut_x(own_upstream).astype(jnp.float32) + inverse * (
         grad_norm * cut_x(gain) - unit_rows * (row_dot / features)
     )
     grad_rows = grad_hidden.astype(jnp.bfloat16)
+    returned = [grad_rows[:local_frames]]
+    for k in range(1, depth):
+        returned.append(
+            ring(grad_rows[k * local_frames : (k + 1) * local_frames], depth - k)
+        )
+    for k in range(1, depth - 1):
+        if k + 2 < depth:
+            weight_parts.append(weight_part(k + 2, (payload, grad_rows)))
+        payload = pack(*ring_sum(k, ring(payload, 1), weight_parts[-1][1]))
     grad_inputs = jnp.zeros(inputs.shape, jnp.bfloat16)
     for k in range(depth):
-        piece = grad_rows[k * local_frames : (k + 1) * local_frames]
-        if k:
-            piece = ring(piece, depth - k)
+        piece = after(returned[k], payload) if k else returned[k]
         target, first = place((z + k) % depth)
         grad_inputs = lax.dynamic_update_slice(
             grad_inputs, join_x(piece)[None], (target, 0, first, 0)
@@ -342,20 +383,16 @@
         onehot.T, jnp.sum(grad_hidden, 1), precision=lax.Precision.HIGHEST
     )
     small = jnp.concatenate([action_term, gain_term[None, :]], 0)
+    last_sum, last_bound = chip_sum(depth - 1, payload)
+    small = after(small, last_sum)
     small = small + swap_core(small)
-    small = small + swap_y(small)
+    small = join_x(small + swap_y(small))
     bit = 1
     while bit < depth:
         small = small + swap_z(small, bit)
         bit *= 2
-    small = join_x(small)
-
-    for k in range(depth):
-        total = here[k] + swap_y(away[k]).astype(jnp.float32) * decoding
-        if k:
-            total = total + arriving.astype(jnp.float32) * decoding
-        if k < depth - 1:
-            arriving = ring((total * encoding).astype(WIRE), 1)
+
+    total = last_sum + unpack(ring(payload, 1))[0]
     mine = lax.dynamic_slice_in_dim(total, core * shard_rows, shard_rows, 0)
     other = swap_core(lax.dynamic_slice_in_dim(total, (1 - core) * shard_rows, shard_rows, 0))
     first = jnp.where(core == 0, mine, other).reshape(shard_rows, 4, head_width)

time: 444 us -> 416 us (0.937)
  starting transfers between devices: 73.3 us -> 57.3 us
  local copies, waits for them, and re-layouts: 31.2 us -> 43.7 us
  matrix products: 72.2 us -> 61.8 us
  other arithmetic: 50.8 us -> 42.5 us
    dot_general x16 -> x0, matrix products: 47.3 us -> none  [dot_tn(): lax.dot_general(a, b, (((0,), (0,)), ((), ())), preferred_element_type=jn...]
    ppermute x10 -> x9, waiting for transfers between devices: 62.1 us -> 21.8 us  [swap_y(): return lax.ppermute(value, 'space', [(i, i ^ 2) for i in range(spaces)])]
    dot_general x2 -> x10, matrix products: 10.4 us -> 43.1 us  [dot_nn(): lax.dot_general(a, b, (((1,), (0,)), ((), ())), preferred_element_type=jn...]
    ppermute x15, waiting for transfers between devices: 90.3 us -> 120 us  [ring(): lax.ppermute(value, 'frame', [(i, (i + shift) % depth) for i in range(dep...]
    ppermute x15, starting transfers between devices: 33.4 us -> 19.4 us  [ring(): lax.ppermute(value, 'frame', [(i, (i + shift) % depth) for i in range(dep...]
    convert_element_type x6 -> x1, other arithmetic: 13.9 us -> 1.41 us  [on_device(): sent = (x_away / row_scale).astype(WIRE)]
    ppermute x11 -> x10, waiting for transfers between devices: 32.7 us -> 41.5 us  [swap_x(): return lax.ppermute(value, 'tensor', [(0, 1), (1, 0)])]
    concatenate x2 -> x10, other arithmetic: 1.79 us -> 9.57 us  [the longest x7 7.78 us: pack(): jnp.concatenate([value * jnp.exp2(-exponent), jnp.broadcast_to(exponent,...]
  transfers between devices with their start and end apart: 47 -> 42, of which waited for: 28 -> 25; matrix products, arithmetic and copies ran while one was open for 30% -> 25% of each run, Pallas kernels for 0% -> 0%
where the time goes in v1:
time: 416 us; the launch traced here: 411 us
  waiting for transfers between devices  193 us (46%)
  matrix products  61.8 us (15%)
  starting transfers between devices  57.3 us (14%)
  local copies, waits for them, and re-layouts  43.7 us (11%)
  other arithmetic  42.5 us (10%)
  Pallas kernels  7.78 us (2%)
  between operations  4.51 us (1%)
    ppermute x15, waiting for transfers between devices, ring(): lax.ppermute(value, 'frame', [(i, (i + shift) % depth) for i in range(dep...  120 us
    dot_general x10, matrix products, dot_nn(): lax.dot_general(a, b, (((1,), (0,)), ((), ())), preferred_element_type=jn...  43.1 us
    ppermute x10, waiting for transfers between devices, swap_x(): return lax.ppermute(value, 'tensor', [(0, 1), (1, 0)])  41.5 us
    ppermute x9, waiting for transfers between devices, swap_y(): return lax.ppermute(value, 'space', [(i, i ^ 2) for i in range(spaces)])  21.8 us
    ppermute x15, starting transfers between devices, ring(): lax.ppermute(value, 'frame', [(i, (i + shift) % depth) for i in range(dep...  19.4 us
    dot_general x2, matrix products, dot_nt(): lax.dot_general(a, b, (((1,), (1,)), ((), ())), preferred_element_type=jn...  18.2 us
    ppermute x2, starting transfers between devices, swap_z(): return lax.ppermute(value, 'frame', [(i, i ^ bit) for i in range(depth)])  14.4 us
    dynamic_update_slice x8, local copies, waits for them, and re-layouts, settle(): return lax.dynamic_update_slice(weights, arrived, (start, 0))  13.7 us
  transfers between devices with their start and end apart: 42, of which 25 were waited for; matrix products, arithmetic and copies ran while one was open for 25% of the time, Pallas kernels for 0%

profile of v1, /device:TPU:0, one launch (start us, length us, event | category | flops | bytes accessed | tf_op | source)
XLA Modules:
  0.0 411.0 jit_solution(3349336113039034579)
XLA Ops:
  9.1 15.1 %collective-permute-done = bf16[2,2,72,1024]{3,2,1,0:T(8,128)(2,1)} collective-permute-done((bf16[2,2,72,1024]{3,2,1,0:T(8,128)(2,1)}, bf16[2,2,72,1024]{3,2,1,0:T(8,128)(2,1)}, u32[]{:S(2)}, u32[]{:S(2)}) %collective-permute-start) | collective-permute-done | bytes 589856 | tf_op jit(solution)/shard_map/ppermute | solution.py:158
  33.1 4.4 %broadcast_in_dim.102 = bf16[2048,2048]{1,0:T(8,128)(2,1)} broadcast(bf16[]{:T(256)} %constant.249.clone.1), dimensions={} | broadcast | bytes 8388610 | tf_op jit(solution)/shard_map/broadcast_in_dim | solution.py:231
  42.8 22.1 %collective-permute-done.6 = s32[2,2]{1,0:T(2,128)S(1)} collective-permute-done((s32[2,2]{1,0:T(2,128)S(1)}, s32[2,2]{1,0:T(2,128)S(1)}, u32[]{:S(2)}, u32[]{:S(2)}) %collective-permute-start.6) | collective-permute-done | bytes 48 | tf_op jit(solution)/shard_map/ppermute | solution.py:158
  64.9 12.5 %collective-permute-done.4 = bf16[2,2,72,1024]{3,2,1,0:T(8,128)(2,1)S(1)} collective-permute-done((bf16[2,2,72,1024]{3,2,1,0:T(8,128)(2,1)S(1)}, bf16[2,2,72,1024]{3,2,1,0:T(8,128)(2,1)S(1)}, u32[]{:S(2)}, u32[]{:S(2)}) %collective-permute-start.4) | collective-permute-done | bytes 589856 | tf_op jit(solution)/shard_map/ppermute | solution.py:158
  81.8 3.9 collective-permute-start.9
  94.3 23.3 %collective-permute-done.11 = s32[2,2]{1,0:T(2,128)S(1)} collective-permute-done((s32[2,2]{1,0:T(2,128)S(1)}, s32[2,2]{1,0:T(2,128)S(1)}, u32[]{:S(2)}, u32[]{:S(2)}) %collective-permute-start.11) | collective-permute-done | bytes 48 | tf_op jit(solution)/shard_map/ppermute | solution.py:158
  128.1 6.1 %collective-permute-done.12 = bf16[2,2,72,1024]{3,2,1,0:T(8,128)(2,1)S(1)} collective-permute-done((bf16[2,2,72,1024]{3,2,1,0:T(8,128)(2,1)S(1)}, bf16[2,2,72,1024]{3,2,1,0:T(8,128)(2,1)S(1)}, u32[]{:S(2)}, u32[]{:S(2)}) %collective-permute-start.12) | collective-permute-done | bytes 589856 | tf_op jit(solution)/shard_map/ppermute | solution.py:170
  134.4 6.6 %collective-permute-done.14 = s32[2,2]{1,0:T(2,128)S(1)} collective-permute-done((s32[2,2]{1,0:T(2,128)S(1)}, s32[2,2]{1,0:T(2,128)S(1)}, u32[]{:S(2)}, u32[]{:S(2)}) %collective-permute-start.14) | collective-permute-done | bytes 48 | tf_op jit(solution)/shard_map/ppermute | solution.py:158
  163.6 14.7 %collective-permute-done.17 = bf16[256,2048]{1,0:T(8,128)(2,1)S(1)} collective-permute-done((bf16[256,2048]{1,0:T(8,128)(2,1)}, bf16[256,2048]{1,0:T(8,128)(2,1)S(1)}, u32[]{:S(2)}, u32[]{:S(2)}) %collective-permute-start.17) | collective-permute-done | bytes 1048608 | tf_op jit(solution)/shard_map/ppermute | solution.py:167
  179.4 4.2 %convolution_convert_fusion.1 = bf16[1152,512]{1,0:T(8,128)(2,1)S(1)} fusion(bf16[1152,2048]{1,0:T(8,128)(2,1)S(1)} %bitcast.125, bf16[2048,2048]{1,0:T(8,128)(2,1)} %constant_dynamic-update-slice_fusion), kind=kOutput, calls=%fused_computation.33 | convolution fusion | flops 2416508928 | bytes 7995392 | tf_op jit(solution)/shard_map/dot_general | solution.py:27
  183.7 9.7 %convolution_convert_fusion = bf16[1152,1536]{1,0:T(8,128)(2,1)S(1)} fusion(bf16[1152,2048]{1,0:T(8,128)(2,1)S(1)} %bitcast.120, bf16[2048,2048]{1,0:T(8,128)(2,1)} %constant_dynamic-update-slice_fusion), kind=kOutput, calls=%fused_computation | convolution fusion | flops 7249526784 | bytes 14548992 | tf_op jit(solution)/shard_map/dot_general | solution.py:27
  193.4 7.8 %temporal_attention.1 = (bf16[8,144,512]{2,1,0:T(8,128)(2,1)S(1)}, bf16[8,144,1536]{2,1,0:T(8,128)(2,1)S(1)}, f32[8,128]{1,0:T(8,128)S(1)}, f32[8,128]{1,0:T(8,128)S(1)}) custom-call(f32[128,1]{1,0:T(8,128)S(1)} %copy-done.2, f32[1,128]{1,0:T(1,128)S(1)} %broadcast_in_dim_reshape.8.early_ref, bf16[8,144,1536]{2,1,0:T(8,128)(2,1)S(1)} %bitcast.108, ...), custom_call_target="tpu_custom_call" | custom-call | flops 1207959552 | bytes 9437184 | tf_op jit(solution)/shard_map/temporal_attention/pallas_call | solution.py:108
  201.2 8.9 %fusion.2 = f32[8,72,2048]{2,1,0:T(8,128)} fusion(bf16[2048,2048]{1,0:T(8,128)(2,1)} %constant_dynamic-update-slice_fusion, bf16[8,144,1536]{2,1,0:T(8,128)(2,1)S(1)} %get-tuple-element.66), kind=kOutput, calls=%fused_computation.3 | convolution fusion | flops 3623878656 | bytes 12779520 | tf_op jit(solution)/shard_map/dot_general | solution.py:23
  219.8 4.0 fusion.55
  228.2 9.3 %multiply_reduce_fusion = (f32[8,72]{1,0:T(8,128)}, f32[8,72]{1,0:T(8,128)S(1)}, f32[8,72,2048]{2,1,0:T(8,128)S(1)}) fusion(bf16[8,72,2048]{2,1,0:T(8,128)(2,1)S(1)} %copy-done.7, f32[2048]{0:T(1024)S(1)} %copy-done.49, f32[8,72]{1,0:T(8,128)S(1)} %copy-done.51, f32[8,2048]{1,0:T(8,128)S(1)} %copy-done.44, f32[8,72,2048]{2,1,0:T(8,128)} %collective-permute-done.19, ...), kind=kOutput, calls=%fused_computation.18 | convolution fusion | flops 3634494464 | bytes 19938048 | tf_op jit(solution)/shard_map/dot_general | solution.py:23
  271.5 13.6 %collective-permute-done.21 = f32[8,72,2]{1,0,2:T(8,128)S(1)} collective-permute-done((f32[8,72,2]{1,0,2:T(8,128)S(1)}, f32[8,72,2]{1,0,2:T(8,128)S(1)}, u32[]{:S(2)}, u32[]{:S(2)}) %collective-permute-start.21) | collective-permute-done | bytes 4640 | tf_op jit(solution)/shard_map/ppermute | solution.py:170
  285.1 4.2 %fusion.97 = (f32[8,1024]{1,0:T(8,128)}, f32[1024]{0:T(1024)S(1)}, bf16[8,72,1024]{2,1,0:T(8,128)(2,1)}) fusion(f32[8,72]{1,0:T(8,128)S(1)} %get-tuple-element.146, f32[8,1024]{1,0:T(8,128)S(1)} %copy-done.46, bf16[8,72,2048]{2,1,0:T(8,128)(2,1)S(1)} %copy-done.8, s32[]{:T(128)} %select_n.440, f32[1024]{0:T(1024)S(1)} %dynamic-slice-done, ...), kind=kLoop, calls=%fused_computation.247 | loop fusion | flops 9427968 | bytes 7158532 | tf_op jit(solution)/shard_map/reduce_sum | solution.py:383
  309.0 6.4 %collective-permute-done.23 = bf16[2,72,1024]{2,1,0:T(8,128)(2,1)S(1)} collective-permute-done((bf16[2,72,1024]{2,1,0:T(8,128)(2,1)S(1)}, bf16[2,72,1024]{2,1,0:T(8,128)(2,1)S(1)}, u32[]{:S(2)}, u32[]{:S(2)}) %collective-permute-start.23) | collective-permute-done | bytes 294944 | tf_op jit(solution)/shard_map/ppermute | solution.py:170
  320.6 12.3 %collective-permute-done.28 = f16[264,2048]{1,0:T(8,128)(2,1)} collective-permute-done((f16[264,2048]{1,0:T(8,128)(2,1)}, f16[264,2048]{1,0:T(8,128)(2,1)}, u32[]{:S(2)}, u32[]{:S(2)}) %collective-permute-start.28) | collective-permute-done | bytes 1081376 | tf_op jit(solution)/shard_map/ppermute | solution.py:158
  340.3 11.3 %collective-permute-done.30 = bf16[2,72,1024]{2,1,0:T(8,128)(2,1)S(1)} collective-permute-done((bf16[2,72,1024]{2,1,0:T(8,128)(2,1)S(1)}, bf16[2,72,1024]{2,1,0:T(8,128)(2,1)S(1)}, u32[]{:S(2)}, u32[]{:S(2)}) %collective-permute-start.30) | collective-permute-done | bytes 294944 | tf_op jit(solution)/shard_map/ppermute | solution.py:158
  353.8 7.7 %collective-permute-done.31 = bf16[2,72,1024]{2,1,0:T(8,128)(2,1)S(1)} collective-permute-done((bf16[2,72,1024]{2,1,0:T(8,128)(2,1)S(1)}, bf16[2,72,1024]{2,1,0:T(8,128)(2,1)S(1)}, u32[]{:S(2)}, u32[]{:S(2)}) %collective-permute-start.31) | collective-permute-done | bytes 294944 | tf_op jit(solution)/shard_map/ppermute | solution.py:170
  361.6 11.1 %collective-permute-done.35 = f16[264,2048]{1,0:T(8,128)(2,1)S(1)} collective-permute-done((f16[264,2048]{1,0:T(8,128)(2,1)S(1)}, f16[264,2048]{1,0:T(8,128)(2,1)S(1)}, u32[]{:S(2)}, u32[]{:S(2)}) %collective-permute-start.35) | collective-permute-done | bytes 1081376 | tf_op jit(solution)/shard_map/ppermute | solution.py:158
  383.3 13.9 %collective-permute-start.40 = (f32[9,2048]{1,0:T(8,128)S(1)}, f32[9,2048]{1,0:T(8,128)S(1)}, u32[]{:S(2)}, u32[]{:S(2)}) collective-permute-start(f32[9,2048]{1,0:T(8,128)S(1)} %pad_maximum_fusion.20), channel_id=1, source_target_pairs={{0,8},{8,0},{16,24},{24,16},{1,9},{9,1},{17,25},{25,17},{2,10},{10... | collective-permute-start | bytes 221192 | tf_op jit(solution)/shard_map/ppermute | solution.py:161
  401.3 5.4 %collective-permute-done.41 = f32[9,2048]{1,0:T(8,128)S(1)} collective-permute-done((f32[9,2048]{1,0:T(8,128)S(1)}, f32[9,2048]{1,0:T(8,128)S(1)}, u32[]{:S(2)}, u32[]{:S(2)}) %collective-permute-start.41) | collective-permute-done | bytes 73760 | tf_op jit(solution)/shard_map/ppermute | solution.py:161
  (314 shorter events, 167.8 us)
Async XLA Ops:
  24.2 53.2 %collective-permute-start.5 = (bf16[256,2048]{1,0:T(8,128)(2,1)S(1)}, bf16[256,2048]{1,0:T(8,128)(2,1)}, u32[]{:S(2)}, u32[]{:S(2)}) collective-permute-start(bf16[256,2048]{1,0:T(8,128)(2,1)S(1)} %pad_maximum_fusion.12), channel_id=1, source_target_pairs={{0,4},{2,6},{4,0},{6,2},{1,5},{3,7},{5,1},{7,3},{8,12},{10,14},{12... | collective-permute-start | bytes 3145736 | tf_op jit(solution)/shard_map/ppermute | solution.py:167
  25.7 51.7 %collective-permute-start.3 = (bf16[256,2048]{1,0:T(8,128)(2,1)S(1)}, bf16[256,2048]{1,0:T(8,128)(2,1)}, u32[]{:S(2)}, u32[]{:S(2)}) collective-permute-start(bf16[256,2048]{1,0:T(8,128)(2,1)S(1)} %pad_maximum_fusion.12), channel_id=1, source_target_pairs={{0,8},{8,16},{16,24},{24,0},{1,9},{9,17},{17,25},{25,1},{2,10},{10... | collective-permute-start | bytes 3145736 | tf_op jit(solution)/shard_map/ppermute | solution.py:158
  28.6 48.8 %collective-permute-start.4 = (bf16[2,2,72,1024]{3,2,1,0:T(8,128)(2,1)S(1)}, bf16[2,2,72,1024]{3,2,1,0:T(8,128)(2,1)S(1)}, u32[]{:S(2)}, u32[]{:S(2)}) collective-permute-start(bf16[2,2,72,1024]{3,2,1,0:T(8,128)(2,1)S(1)} %pad_maximum_fusion.16), channel_id=1, source_target_pairs={{0,16},{8,24},{16,0},{24,8},{1,17},{9,25},{17,1},{25,9},{2,18},{10... | collective-permute-start | bytes 1769480 | tf_op jit(solution)/shard_map/ppermute | solution.py:158
  31.0 33.9 %collective-permute-start.6 = (s32[2,2]{1,0:T(2,128)S(1)}, s32[2,2]{1,0:T(2,128)S(1)}, u32[]{:S(2)}, u32[]{:S(2)}) collective-permute-start(s32[2,2]{1,0:T(2,128)S(1)} %copy-done.56), channel_id=1, source_target_pairs={{0,8},{8,16},{16,24},{24,0},{1,9},{9,17},{17,25},{25,1},{2,10},{10... | collective-permute-start | bytes 56 | tf_op jit(solution)/shard_map/ppermute | solution.py:158
  77.4 40.2 %collective-permute-start.10 = (bf16[256,2048]{1,0:T(8,128)(2,1)}, bf16[256,2048]{1,0:T(8,128)(2,1)S(1)}, u32[]{:S(2)}, u32[]{:S(2)}) collective-permute-start(bf16[256,2048]{1,0:T(8,128)(2,1)} %collective-permute-done.3), channel_id=1, source_target_pairs={{0,4},{2,6},{4,0},{6,2},{1,5},{3,7},{5,1},{7,3},{8,12},{10,14},{12... | collective-permute-start | bytes 3145736 | tf_op jit(solution)/shard_map/ppermute | solution.py:167
  78.1 39.5 %collective-permute-start.8 = (bf16[256,2048]{1,0:T(8,128)(2,1)}, bf16[256,2048]{1,0:T(8,128)(2,1)}, u32[]{:S(2)}, u32[]{:S(2)}) collective-permute-start(bf16[256,2048]{1,0:T(8,128)(2,1)} %collective-permute-done.3), channel_id=1, source_target_pairs={{0,8},{8,16},{16,24},{24,0},{1,9},{9,17},{17,25},{25,1},{2,10},{10... | collective-permute-start | bytes 3145736 | tf_op jit(solution)/shard_map/ppermute | solution.py:158
  81.8 35.8 %collective-permute-start.9 = (bf16[2,2,72,1024]{3,2,1,0:T(8,128)(2,1)S(1)}, bf16[2,2,72,1024]{3,2,1,0:T(8,128)(2,1)S(1)}, u32[]{:S(2)}, u32[]{:S(2)}) collective-permute-start(bf16[2,2,72,1024]{3,2,1,0:T(8,128)(2,1)S(1)} %pad_maximum_fusion.17), channel_id=1, source_target_pairs={{0,24},{8,0},{16,8},{24,16},{1,25},{9,1},{17,9},{25,17},{2,26},{10... | collective-permute-start | bytes 1769480 | tf_op jit(solution)/shard_map/ppermute | solution.py:158
  85.7 31.9 %collective-permute-start.11 = (s32[2,2]{1,0:T(2,128)S(1)}, s32[2,2]{1,0:T(2,128)S(1)}, u32[]{:S(2)}, u32[]{:S(2)}) collective-permute-start(s32[2,2]{1,0:T(2,128)S(1)} %copy-done.56), channel_id=1, source_target_pairs={{0,16},{8,24},{16,0},{24,8},{1,17},{9,25},{17,1},{25,9},{2,18},{10... | collective-permute-start | bytes 56 | tf_op jit(solution)/shard_map/ppermute | solution.py:158
  117.6 27.1 %collective-permute-start.13 = (bf16[256,2048]{1,0:T(8,128)(2,1)}, bf16[256,2048]{1,0:T(8,128)(2,1)S(1)}, u32[]{:S(2)}, u32[]{:S(2)}) collective-permute-start(bf16[256,2048]{1,0:T(8,128)(2,1)} %collective-permute-done.8), channel_id=1, source_target_pairs={{0,8},{8,16},{16,24},{24,0},{1,9},{9,17},{17,25},{25,1},{2,10},{10... | collective-permute-start | bytes 3145736 | tf_op jit(solution)/shard_map/ppermute | solution.py:158
  118.2 26.5 %collective-permute-start.15 = (bf16[256,2048]{1,0:T(8,128)(2,1)}, bf16[256,2048]{1,0:T(8,128)(2,1)S(1)}, u32[]{:S(2)}, u32[]{:S(2)}) collective-permute-start(bf16[256,2048]{1,0:T(8,128)(2,1)} %collective-permute-done.8), channel_id=1, source_target_pairs={{0,4},{2,6},{4,0},{6,2},{1,5},{3,7},{5,1},{7,3},{8,12},{10,14},{12... | collective-permute-start | bytes 3145736 | tf_op jit(solution)/shard_map/ppermute | solution.py:167
  153.0 25.3 %collective-permute-start.17 = (bf16[256,2048]{1,0:T(8,128)(2,1)}, bf16[256,2048]{1,0:T(8,128)(2,1)S(1)}, u32[]{:S(2)}, u32[]{:S(2)}) collective-permute-start(bf16[256,2048]{1,0:T(8,128)(2,1)} %copy-done.35), channel_id=1, source_target_pairs={{0,4},{2,6},{4,0},{6,2},{1,5},{3,7},{5,1},{7,3},{8,12},{10,14},{12... | collective-permute-start | bytes 3145736 | tf_op jit(solution)/shard_map/ppermute | solution.py:167
  226.8 26.5 %collective-permute-start.22 = (f16[264,2048]{1,0:T(8,128)(2,1)}, f16[264,2048]{1,0:T(8,128)(2,1)}, u32[]{:S(2)}, u32[]{:S(2)}) collective-permute-start(f16[264,2048]{1,0:T(8,128)(2,1)} %pad_maximum_fusion.7), channel_id=1, source_target_pairs={{0,4},{2,6},{4,0},{6,2},{1,5},{3,7},{5,1},{7,3},{8,12},{10,14},{12... | collective-permute-start | bytes 3244040 | tf_op jit(solution)/shard_map/ppermute | solution.py:167
  257.1 27.9 %collective-permute-start.20 = (f16[8,72,1024]{2,1,0:T(8,128)(2,1)}, f16[8,72,1024]{2,1,0:T(8,128)(2,1)}, u32[]{:S(2)}, u32[]{:S(2)}) collective-permute-start(f16[8,72,1024]{2,1,0:T(8,128)(2,1)} %divide_convert_fusion), channel_id=1, source_target_pairs={{0,1},{1,0},{2,3},{3,2},{4,5},{5,4},{6,7},{7,6},{8,9},{9,8},{10,11... | collective-permute-start | bytes 3538952 | tf_op jit(solution)/shard_map/ppermute | solution.py:170
  258.5 40.9 %collective-permute-start.26 = (f16[264,2048]{1,0:T(8,128)(2,1)}, f16[264,2048]{1,0:T(8,128)(2,1)}, u32[]{:S(2)}, u32[]{:S(2)}) collective-permute-start(f16[264,2048]{1,0:T(8,128)(2,1)} %pad_maximum_fusion.6), channel_id=1, source_target_pairs={{0,4},{2,6},{4,0},{6,2},{1,5},{3,7},{5,1},{7,3},{8,12},{10,14},{12... | collective-permute-start | bytes 3244040 | tf_op jit(solution)/shard_map/ppermute | solution.py:167
  260.0 39.4 %collective-permute-start.27 = (f16[264,2048]{1,0:T(8,128)(2,1)}, f16[264,2048]{1,0:T(8,128)(2,1)}, u32[]{:S(2)}, u32[]{:S(2)}) collective-permute-start(f16[264,2048]{1,0:T(8,128)(2,1)} %pad_maximum_fusion.9), channel_id=1, source_target_pairs={{0,8},{8,16},{16,24},{24,0},{1,9},{9,17},{17,25},{25,1},{2,10},{10... | collective-permute-start | bytes 3244040 | tf_op jit(solution)/shard_map/ppermute | solution.py:158
  263.5 21.6 %collective-permute-start.21 = (f32[8,72,2]{1,0,2:T(8,128)S(1)}, f32[8,72,2]{1,0,2:T(8,128)S(1)}, u32[]{:S(2)}, u32[]{:S(2)}) collective-permute-start(f32[8,72,2]{1,0,2:T(8,128)S(1)} %pad_maximum_fusion.22), channel_id=1, source_target_pairs={{0,1},{1,0},{2,3},{3,2},{4,5},{5,4},{6,7},{7,6},{8,9},{9,8},{10,11... | collective-permute-start | bytes 13832 | tf_op jit(solution)/shard_map/ppermute | solution.py:170
  270.8 37.9 %collective-permute-start.25 = (f16[264,2048]{1,0:T(8,128)(2,1)}, f16[264,2048]{1,0:T(8,128)(2,1)}, u32[]{:S(2)}, u32[]{:S(2)}) collective-permute-start(f16[264,2048]{1,0:T(8,128)(2,1)} %pad_maximum_fusion.5), channel_id=1, source_target_pairs={{0,4},{2,6},{4,0},{6,2},{1,5},{3,7},{5,1},{7,3},{8,12},{10,14},{12... | collective-permute-start | bytes 3244040 | tf_op jit(solution)/shard_map/ppermute | solution.py:167
  303.7 29.1 %collective-permute-start.28 = (f16[264,2048]{1,0:T(8,128)(2,1)}, f16[264,2048]{1,0:T(8,128)(2,1)}, u32[]{:S(2)}, u32[]{:S(2)}) collective-permute-start(f16[264,2048]{1,0:T(8,128)(2,1)} %pad_maximum_fusion.10), channel_id=1, source_target_pairs={{0,8},{8,16},{16,24},{24,0},{1,9},{9,17},{17,25},{25,1},{2,10},{10... | collective-permute-start | bytes 3244040 | tf_op jit(solution)/shard_map/ppermute | solution.py:158
  303.7 33.3 %collective-permute-start.34 = (f16[264,2048]{1,0:T(8,128)(2,1)}, f16[264,2048]{1,0:T(8,128)(2,1)S(1)}, u32[]{:S(2)}, u32[]{:S(2)}) collective-permute-start(f16[264,2048]{1,0:T(8,128)(2,1)} %pad_maximum_fusion.4), channel_id=1, source_target_pairs={{0,4},{2,6},{4,0},{6,2},{1,5},{3,7},{5,1},{7,3},{8,12},{10,14},{12... | collective-permute-start | bytes 3244040 | tf_op jit(solution)/shard_map/ppermute | solution.py:167
  316.7 22.3 %collective-permute-start.32 = (bf16[2,72,1024]{2,1,0:T(8,128)(2,1)S(1)}, bf16[2,72,1024]{2,1,0:T(8,128)(2,1)S(1)}, u32[]{:S(2)}, u32[]{:S(2)}) collective-permute-start(bf16[2,72,1024]{2,1,0:T(8,128)(2,1)S(1)} %get-tuple-element.105), channel_id=1, source_target_pairs={{0,8},{8,16},{16,24},{24,0},{1,9},{9,17},{17,25},{25,1},{2,10},{10... | collective-permute-start | bytes 884744 | tf_op jit(solution)/shard_map/ppermute | solution.py:158
  316.8 34.9 %collective-permute-start.30 = (bf16[2,72,1024]{2,1,0:T(8,128)(2,1)S(1)}, bf16[2,72,1024]{2,1,0:T(8,128)(2,1)S(1)}, u32[]{:S(2)}, u32[]{:S(2)}) collective-permute-start(bf16[2,72,1024]{2,1,0:T(8,128)(2,1)S(1)} %get-tuple-element.106), channel_id=1, source_target_pairs={{0,16},{8,24},{16,0},{24,8},{1,17},{9,25},{17,1},{25,9},{2,18},{10... | collective-permute-start | bytes 884744 | tf_op jit(solution)/shard_map/ppermute | solution.py:158
  319.1 33.9 %collective-permute-start.24 = (bf16[2,72,1024]{2,1,0:T(8,128)(2,1)S(1)}, bf16[2,72,1024]{2,1,0:T(8,128)(2,1)S(1)}, u32[]{:S(2)}, u32[]{:S(2)}) collective-permute-start(bf16[2,72,1024]{2,1,0:T(8,128)(2,1)S(1)} %get-tuple-element.107), channel_id=1, source_target_pairs={{0,24},{8,0},{16,8},{24,16},{1,25},{9,1},{17,9},{25,17},{2,26},{10... | collective-permute-start | bytes 884744 | tf_op jit(solution)/shard_map/ppermute | solution.py:158
  336.3 36.3 %collective-permute-start.35 = (f16[264,2048]{1,0:T(8,128)(2,1)S(1)}, f16[264,2048]{1,0:T(8,128)(2,1)S(1)}, u32[]{:S(2)}, u32[]{:S(2)}) collective-permute-start(f16[264,2048]{1,0:T(8,128)(2,1)S(1)} %pad_maximum_fusion.11), channel_id=1, source_target_pairs={{0,8},{8,16},{16,24},{24,0},{1,9},{9,17},{17,25},{25,1},{2,10},{10... | collective-permute-start | bytes 3244040 | tf_op jit(solution)/shard_map/ppermute | solution.py:158
  380.4 27.5 %collective-permute-start.36 = (f32[128,2048]{1,0:T(8,128)S(1)}, f32[128,2048]{1,0:T(8,128)S(1)}, u32[]{:S(2)}, u32[]{:S(2)}) collective-permute-start(f32[128,2048]{1,0:T(8,128)S(1)} %constant_dynamic-slice_fusion), channel_id=1, source_target_pairs={{0,2},{2,0},{4,6},{6,4},{1,3},{3,1},{5,7},{7,5},{8,10},{10,8},{12,... | collective-permute-start | bytes 3145736 | tf_op jit(solution)/shard_map/ppermute | solution.py:164
  (79 other events, 816.1 us)

commit v2 on v1

--- a/solution.py
+++ b/solution.py
@@ -136,6 +136,121 @@
     )(per_row[:, None], per_row[None, :], qkv, grad_heads)
 
 
+def weight_kernel(
+    place_ref, norm_near, norm_far, up_near, up_far, merged_ref, mixed_ref, near_ref, far_ref, turned
+):
+    step = pl.program_id(0)
+    rows = near_ref.shape[0]
+
+    @pl.when(step == 0)
+    def _():
+        turned[:rows] = norm_near[...].T
+        turned[rows:] = norm_far[...].T
+
+    @pl.when(step < 3)
+    def _():
+        near_ref[...] = dot_nn(turned[:rows], merged_ref[...])
+        far_ref[...] = dot_nn(turned[rows:], merged_ref[...])
+
+    @pl.when(step == 3)
+    def _():
+        near_ref[...] = dot_tn(up_near[...], mixed_ref[...])
+        far_ref[...] = dot_tn(up_far[...], mixed_ref[...])
+
+
+def weight_product(places, rows, normed, upstream, merged, mixed):
+    tokens, width = mixed.shape
+    near = pl.BlockSpec((tokens, rows), lambda i, at: (0, at[0]))
+    far = pl.BlockSpec((tokens, rows), lambda i, at: (0, at[1]))
+    out = pl.BlockSpec((rows, width), lambda i, at: (0, i))
+    return pl.pallas_call(
+        weight_kernel,
+        grid_spec=pltpu.PrefetchScalarGridSpec(
+            num_scalar_prefetch=1,
+            grid=(4,),
+            in_specs=[
+                near,
+                far,
+                near,
+                far,
+                pl.BlockSpec((tokens, width), lambda i, at: (0, jnp.minimum(i, 2))),
+                pl.BlockSpec((tokens, width), lambda i, at: (0, 0)),
+            ],
+            out_specs=[out, out],
+            scratch_shapes=[pltpu.VMEM((2 * rows, tokens), jnp.bfloat16)],
+        ),
+        out_shape=[jax.ShapeDtypeStruct((rows, 4 * width), jnp.float32)] * 2,
+        compiler_params=pltpu.CompilerParams(vmem_limit_bytes=40 * 1024 * 1024),
+        cost_estimate=pl.CostEstimate(flops=1, bytes_accessed=1, transcendentals=0),
+        name="weight_product",
+    )(places, normed, normed, upstream, upstream, merged, mixed)
+
+
+def project_kernel(normed_ref, up_ref, weight_ref, qkv_ref, grad_ref):
+    @pl.when(pl.program_id(0) < 3)
+    def _():
+        qkv_ref[...] = dot_nn(normed_ref[...], weight_ref[...]).astype(jnp.bfloat16)
+
+    @pl.when(pl.program_id(0) == 3)
+    def _():
+        grad_ref[...] = dot_nn(up_ref[...], weight_ref[...]).astype(jnp.bfloat16)
+
+
+def project(normed, upstream, weights):
+    tokens, features = normed.shape
+    width = weights.shape[1] // 4
+    rows = tokens // 2
+    return pl.pallas_call(
+        project_kernel,
+        grid=(4, 2),
+        in_specs=[
+            pl.BlockSpec((rows, features), lambda i, j: (jnp.where(i < 3, j, 1), 0)),
+            pl.BlockSpec((rows, features), lambda i, j: (jnp.where(i < 3, 0, j), 0)),
+            pl.BlockSpec((features, width), lambda i, j: (0, i)),
+        ],
+        out_specs=[
+            pl.BlockSpec(
+                (rows, width), lambda i, j: (jnp.where(i < 3, j, 1), jnp.minimum(i, 2))
+            ),
+            pl.BlockSpec((rows, width), lambda i, j: (jnp.where(i < 3, 0, j), 0)),
+        ],
+        out_shape=[
+            jax.ShapeDtypeStruct((tokens, 3 * width), jnp.bfloat16),
+            jax.ShapeDtypeStruct((tokens, width), jnp.bfloat16),
+        ],
+        compiler_params=pltpu.CompilerParams(vmem_limit_bytes=40 * 1024 * 1024),
+        cost_estimate=pl.CostEstimate(
+            flops=2 * tokens * features * 4 * width,
+            bytes_accessed=8 * tokens * features,
+            transcendentals=0,
+        ),
+        name="project",
+    )(normed, upstream, weights)
+
+
+def norm_kernel(merged_ref, weight_ref, out_ref):
+    out_ref[...] = dot_nt(merged_ref[...], weight_ref[...])
+
+
+def norm_product(merged, weights):
+    rows, depth = merged.shape
+    features = weights.shape[0]
+    tile = features // 4
+    return pl.pallas_call(
+        norm_kernel,
+        grid=(4,),
+        in_specs=[
+            pl.BlockSpec((rows, depth), lambda i: (0, 0)),
+            pl.BlockSpec((tile, depth), lambda i: (i, 0)),
+        ],
+        out_specs=pl.BlockSpec((rows, tile), lambda i: (0, i)),
+        out_shape=jax.ShapeDtypeStruct((rows, features), jnp.float32),
+        compiler_params=pltpu.CompilerParams(vmem_limit_bytes=40 * 1024 * 1024),
+        cost_estimate=pl.CostEstimate(flops=1, bytes_accessed=1, transcendentals=0),
+        name="norm_product",
+    )(merged, weights)
+
+
 def on_device(
     depth, spaces, tensors, inputs, upstream, action_ids, frame_time, action_table, gain, w_qkv, w_out
 ):
@@ -207,40 +322,35 @@
         piece = jnp.stack([pieces(rows, k, start, slice_width) for rows in (inputs, upstream)])
         return ring(piece, k)
 
+    def settle(weights, k, arrived, row):
+        start = (z - k) % depth * (2 * block_rows) + row * block_rows
+        return lax.dynamic_update_slice(weights, arrived, (start, 0))
+
     block_rows = 2 * shard_rows
     arrived = collect(1, x * slice_width)
     block = after(block, arrived)
     blocks, across, joined, all_ids = [], [], [], [action_ids]
+    weights = jnp.zeros((features, width), jnp.bfloat16)
     for k in range(1, depth):
         blocks.append(block)
         across.append(swap_y(block))
         crossed = swap_x(arrived) if tensors == 2 else None
         joined.append(join_x(arrived, crossed))
         following = ring(block, 1)
+        weights = settle(weights, k - 1, block, y)
+        if k > 1:
+            weights = settle(weights, k - 2, across[k - 2], 1 - y)
         earlier = [across[-1], joined[-1] if crossed is None else crossed]
         if k + 1 < depth:
             arrived = collect(k + 1, after(x * slice_width, block))
             earlier.append(arrived)
             all_ids.append(ring(after(action_ids, block), k))
             earlier.append(all_ids[-1])
-            following, arrived = lax.optimization_barrier((following, arrived, earlier))[:2]
+            following, arrived, weights = lax.optimization_barrier(
+                (following, arrived, weights, earlier)
+            )[:3]
         block = following
     all_ids.append(ring(after(action_ids, blocks[-1]), depth - 1))
-    blocks.append(block)
-    across.append(swap_y(block))
-    weights = jnp.zeros((features, width), jnp.bfloat16)
-
-    def settle(weights, k, arrived, row):
-        start = (z - k) % depth * (2 * block_rows) + row * block_rows
-        return lax.dynamic_update_slice(weights, arrived, (start, 0))
-
-    for k in range(depth - 1):
-        weights = settle(weights, k, blocks[k], y)
-        if k + 2 < depth:
-            weights = settle(weights, k, across[k], 1 - y)
-    joined[-1], weights, block, all_ids, across[-2] = lax.optimization_barrier(
-        (joined[-1], weights, blocks[-1], all_ids, across[-2])
-    )
     locals_ = [pieces(rows, 0, 0, features) for rows in (inputs, upstream)]
     own_inputs = jnp.concatenate([locals_[0]] + [both_rows[0] for both_rows in joined], 0)
     own_upstream = jnp.concatenate([locals_[1]] + [both_rows[1] for both_rows in joined], 0)
@@ -267,19 +377,20 @@
     inverse = lax.rsqrt(jnp.mean(hidden * hidden, -1, keepdims=True) + NORM_EPSILON)
     normed = (hidden * inverse * gain).astype(jnp.bfloat16)
 
+    block, normed, own_upstream, weights, near = lax.optimization_barrier(
+        (block, normed, own_upstream, weights, across[-1])
+    )
+    far = swap_y(block)
+
     def both(own):
         return jnp.concatenate([own, swap_core(own)], 1).reshape(tokens, features)
 
     all_upstream = both(own_upstream)
     all_normed = both(normed)
-    normed_t, upstream_t = lax.optimization_barrier((all_normed.T, all_upstream.T))
-
-    weights = settle(weights, depth - 2, across[-2], 1 - y)
+    weights = settle(weights, depth - 2, near, 1 - y)
     weights = settle(weights, depth - 1, block, y)
-    weights = settle(weights, depth - 1, after(across[-1], normed_t, upstream_t), 1 - y)
-    weight_qkv, weight_out = weights[:, : 3 * head_width], weights[:, 3 * head_width :]
-    qkv = dot_nn(all_normed, weight_qkv).astype(jnp.bfloat16)
-    grad_heads = dot_nn(all_upstream, weight_out).astype(jnp.bfloat16)
+    weights = settle(weights, depth - 1, after(far, all_normed, all_upstream), 1 - y)
+    qkv, grad_heads = project(all_normed, all_upstream, weights)
     mixed, merged, peak_qkv, peak_out = temporal_attention(
         qkv.reshape(frames, 2 * pairs, 3 * head_width),
         grad_heads.reshape(frames, 2 * pairs, head_width),
@@ -306,26 +417,31 @@
         return sent[:block_rows].astype(jnp.float32) * scale, scale * WIRE_TOP
 
     def weight_part(k, earlier):
-        start = after((z - 1 - k) % depth * (2 * block_rows), earlier)
-        cuts = [
-            lax.dynamic_slice_in_dim(rows, start, 2 * block_rows, 0)
-            for rows in (normed_t, upstream_t)
-        ]
-        part = jnp.concatenate([dot_nn(cuts[0], flat_merged), dot_nn(cuts[1], flat_mixed)], 1)
-        return (
-            lax.dynamic_slice_in_dim(part, y * block_rows, block_rows, 0),
-            pack(
-                lax.dynamic_slice_in_dim(part, (1 - y) * block_rows, block_rows, 0), own_bound
-            ),
+        block_at = after((z - 1 - k) % depth * 2, earlier)
+        places = jnp.stack([block_at + y, block_at + 1 - y])
+        near, far = weight_product(
+            places, block_rows, all_normed, all_upstream, flat_merged, flat_mixed
         )
+        return near, pack(far, own_bound)
 
     def norm_part(rows):
         flat = rows.reshape(frames * pairs, 3 * head_width)
-        return dot_nt(flat, weight_qkv).reshape(frames, pairs, features)
-
-    norm_away = norm_part(merged[:, pairs:])
-    weight_parts = [weight_part(0, norm_away)]
-    norm_here = norm_part(after(merged[:, :pairs], weight_parts[0][1]))
+        return norm_product(flat, weights).reshape(frames, pairs, features)
+
+    def chip_sum(k, earlier):
+        term, bound = unpack(after(swap_y(weight_parts[k][1]), earlier))
+        return weight_parts[k][0] + term, bound + own_bound
+
+    def ring_sum(k, arriving, earlier):
+        total, bound = chip_sum(k, earlier)
+        term, ring_bound = unpack(arriving)
+        return total + term, bound + ring_bound
+
+    weight_parts = [weight_part(0, flat_merged)]
+    norm_away = norm_part(after(merged[:, pairs:], weight_parts[0][1]))
+    weight_parts.append(weight_part(1, norm_away))
+    payload = pack(*chip_sum(0, weight_parts[1][1]))
+    norm_here = norm_part(after(merged[:, :pairs], payload))
     partial_norm = norm_here + swap_core(norm_away)
     row_dot = jnp.sum(partial_norm * gain * (hidden * inverse), -1, keepdims=True)
     if tensors == 2:
@@ -339,21 +455,11 @@
         row_dot = lax.psum(row_dot, "tensor")
         grad_norm = lax.psum_scatter(partial_norm, "tensor", scatter_dimension=2, tiled=True)
         sent = partial_norm
-
-    def chip_sum(k, earlier):
-        term, bound = unpack(after(swap_y(weight_parts[k][1]), earlier))
-        return weight_parts[k][0] + term, bound + own_bound
-
-    def ring_sum(k, arriving, earlier):
-        total, bound = chip_sum(k, earlier)
-        term, ring_bound = unpack(arriving)
-        return total + term, bound + ring_bound
-
-    weight_parts.append(weight_part(1, sent))
-    payload = pack(*chip_sum(0, weight_parts[1][1]))
-    weight_parts.append(weight_part(2, payload))
+    weight_parts.append(weight_part(2, sent))
+    payload = pack(*ring_sum(1, ring(payload, 1), weight_parts[2][1]))
+    weight_parts.append(weight_part(3, payload))
     if tensors == 2:
-        x_terms, row_terms = after((x_terms, row_terms), weight_parts[2][1])
+        x_terms, row_terms = after((x_terms, row_terms), weight_parts[3][1])
         row_dot = row_dot + row_terms[..., :1]
         grad_norm = cut_x(partial_norm) + x_terms.astype(jnp.float32) * row_terms[..., 1:]
     unit_rows = (cut_x(own_inputs).astype(jnp.float32) + cut_x(embedded)[:, None, :]) * inverse
@@ -366,10 +472,22 @@
         returned.append(
             ring(grad_rows[k * local_frames : (k + 1) * local_frames], depth - k)
         )
-    for k in range(1, depth - 1):
+
+    gain_term = jnp.sum(grad_norm * unit_rows, (0, 1))
+    action_term = jnp.dot(
+        onehot.T, jnp.sum(grad_hidden, 1), precision=lax.Precision.HIGHEST
+    )
+    small = jnp.concatenate([action_term, gain_term[None, :]], 0)
+    small = small + swap_core(small)
+    bit = 1
+    while bit < depth:
+        small = small + swap_z(small, bit)
+        bit *= 2
+
+    for k in range(2, depth - 1):
+        payload = pack(*ring_sum(k, ring(payload, 1), (small, weight_parts[k + 1][1])))
         if k + 2 < depth:
-            weight_parts.append(weight_part(k + 2, (payload, grad_rows)))
-        payload = pack(*ring_sum(k, ring(payload, 1), weight_parts[-1][1]))
+            weight_parts.append(weight_part(k + 2, payload))
     grad_inputs = jnp.zeros(inputs.shape, jnp.bfloat16)
     for k in range(depth):
         piece = after(returned[k], payload) if k else returned[k]
@@ -377,22 +495,9 @@
         grad_inputs = lax.dynamic_update_slice(
             grad_inputs, join_x(piece)[None], (target, 0, first, 0)
         )
-
-    gain_term = jnp.sum(grad_norm * unit_rows, (0, 1))
-    action_term = jnp.dot(
-        onehot.T, jnp.sum(grad_hidden, 1), precision=lax.Precision.HIGHEST
-    )
-    small = jnp.concatenate([action_term, gain_term[None, :]], 0)
-    last_sum, last_bound = chip_sum(depth - 1, payload)
-    small = after(small, last_sum)
-    small = small + swap_core(small)
+    small = after(small, payload)
     small = join_x(small + swap_y(small))
-    bit = 1
-    while bit < depth:
-        small = small + swap_z(small, bit)
-        bit *= 2
-
-    total = last_sum + unpack(ring(payload, 1))[0]
+    total = chip_sum(depth - 1, payload)[0] + unpack(after(ring(payload, 1), small))[0]
     mine = lax.dynamic_slice_in_dim(total, core * shard_rows, shard_rows, 0)
     other = swap_core(lax.dynamic_slice_in_dim(total, (1 - core) * shard_rows, shard_rows, 0))
     first = jnp.where(core == 0, mine, other).reshape(shard_rows, 4, head_width)

time: 416 us -> 401 us (0.964)
  matrix products: 61.8 us -> 0.48 us
  Pallas kernels: 7.78 us -> 62 us
  local copies, waits for them, and re-layouts: 43.7 us -> 59.9 us
  waiting for transfers between devices: 193 us -> 180 us
  starting transfers between devices: 57.3 us -> 48.2 us
    dot_general x12 -> x0, matrix products: 61.3 us -> none  [the longest x10 43.1 us: dot_nn(): lax.dot_general(a, b, (((1,), (0,)), ((), ())), preferred_element_type=jn...]
    pallas_call x0 -> x7, Pallas kernels: none -> 54.2 us  [the longest x4 26 us: weight_product(): pl.pallas_call(weight_kernel, grid_spec=pltpu.PrefetchScalarGridSpec(num_...]
    ppermute x10, waiting for transfers between devices: 41.5 us -> 19.6 us  [swap_x(): return lax.ppermute(value, 'tensor', [(0, 1), (1, 0)])]
    ppermute x9, waiting for transfers between devices: 21.8 us -> 42 us  [swap_y(): return lax.ppermute(value, 'space', [(i, i ^ 2) for i in range(spaces)])]
    unnamed x121 -> x117, local copies, waits for them, and re-layouts: 9.02 us -> 27.1 us
    ppermute x15, waiting for transfers between devices: 120 us -> 108 us  [ring(): lax.ppermute(value, 'frame', [(i, (i + shift) % depth) for i in range(dep...]
    ppermute x2, starting transfers between devices: 14.4 us -> 2.91 us  [swap_z(): return lax.ppermute(value, 'frame', [(i, i ^ bit) for i in range(depth)])]
    reduce_sum x0 -> x1, other arithmetic: none -> 4.71 us  [on_device(): jnp.sum(partial_norm * gain * (hidden * inverse), -1, keepdims=True)]
  transfers between devices with their start and end apart: 42 -> 42, of which waited for: 25 -> 19; matrix products, arithmetic and copies ran while one was open for 25% -> 16% of each run, Pallas kernels for 0% -> 7%
where the time goes in v2:
time: 401 us; the launch traced here: 399 us
  waiting for transfers between devices  180 us (45%)
  Pallas kernels  62 us (15%)
  local copies, waits for them, and re-layouts  59.9 us (15%)
  starting transfers between devices  48.2 us (12%)
  other arithmetic  44.7 us (11%)
    ppermute x15, waiting for transfers between devices, ring(): lax.ppermute(value, 'frame', [(i, (i + shift) % depth) for i in range(dep...  108 us
    ppermute x9, waiting for transfers between devices, swap_y(): return lax.ppermute(value, 'space', [(i, i ^ 2) for i in range(spaces)])  42 us
    unnamed x117, local copies, waits for them, and re-layouts  27.1 us
    pallas_call x4, Pallas kernels, weight_product(): pl.pallas_call(weight_kernel, grid_spec=pltpu.PrefetchScalarGridSpec(num_...  26 us
    ppermute x15, starting transfers between devices, ring(): lax.ppermute(value, 'frame', [(i, (i + shift) % depth) for i in range(dep...  23.5 us
    ppermute x10, waiting for transfers between devices, swap_x(): return lax.ppermute(value, 'tensor', [(0, 1), (1, 0)])  19.6 us
    pallas_call x2, Pallas kernels, norm_product(): pl.pallas_call(norm_kernel, grid=(4,), in_specs=[pl.BlockSpec((rows, dept...  14.6 us
    pallas_call x1, Pallas kernels, project(): pl.pallas_call(project_kernel, grid=(4, 2), in_specs=[pl.BlockSpec((rows,...  13.6 us
  transfers between devices with their start and end apart: 42, of which 19 were waited for; matrix products, arithmetic and copies ran while one was open for 16% of the time, Pallas kernels for 7%

profile of v2, /device:TPU:0, one launch (start us, length us, event | category | flops | bytes accessed | tf_op | source)
XLA Modules:
  0.0 399.3 jit_solution(7826527333468725644)
XLA Ops:
  9.9 11.5 %collective-permute-done.1 = bf16[2,2,72,1024]{3,2,1,0:T(8,128)(2,1)S(1)} collective-permute-done((bf16[2,2,72,1024]{3,2,1,0:T(8,128)(2,1)}, bf16[2,2,72,1024]{3,2,1,0:T(8,128)(2,1)S(1)}, u32[]{:S(2)}, u32[]{:S(2)}) %collective-permute-start.1) | collective-permute-done | bytes 589856 | tf_op jit(solution)/shard_map/ppermute | solution.py:273
  31.2 4.3 %broadcast_in_dim.102 = bf16[2048,2048]{1,0:T(8,128)(2,1)} broadcast(bf16[]{:T(256)} %constant.249.clone.1), dimensions={} | broadcast | bytes 8388610 | tf_op jit(solution)/shard_map/broadcast_in_dim | solution.py:333
  36.6 23.6 %collective-permute-done.6 = s32[2,2]{1,0:T(2,128)S(1)} collective-permute-done((s32[2,2]{1,0:T(2,128)S(1)}, s32[2,2]{1,0:T(2,128)S(1)}, u32[]{:S(2)}, u32[]{:S(2)}) %collective-permute-start.6) | collective-permute-done | bytes 48 | tf_op jit(solution)/shard_map/ppermute | solution.py:273
  61.3 11.5 %collective-permute-done.3 = bf16[2,2,72,1024]{3,2,1,0:T(8,128)(2,1)S(1)} collective-permute-done((bf16[2,2,72,1024]{3,2,1,0:T(8,128)(2,1)S(1)}, bf16[2,2,72,1024]{3,2,1,0:T(8,128)(2,1)S(1)}, u32[]{:S(2)}, u32[]{:S(2)}) %collective-permute-start.3) | collective-permute-done | bytes 589856 | tf_op jit(solution)/shard_map/ppermute | solution.py:273
  87.4 26.8 %collective-permute-done.11 = s32[2,2]{1,0:T(2,128)S(1)} collective-permute-done((s32[2,2]{1,0:T(2,128)S(1)}, s32[2,2]{1,0:T(2,128)S(1)}, u32[]{:S(2)}, u32[]{:S(2)}) %collective-permute-start.11) | collective-permute-done | bytes 48 | tf_op jit(solution)/shard_map/ppermute | solution.py:273
  123.0 15.2 %collective-permute-done.14 = s32[2,2]{1,0:T(2,128)S(1)} collective-permute-done((s32[2,2]{1,0:T(2,128)S(1)}, s32[2,2]{1,0:T(2,128)S(1)}, u32[]{:S(2)}, u32[]{:S(2)}) %collective-permute-start.14) | collective-permute-done | bytes 48 | tf_op jit(solution)/shard_map/ppermute | solution.py:273
  156.6 4.8 %pad_maximum_fusion = bf16[8,144,2048]{2,1,0:T(8,128)(2,1)S(1)} fusion(bf16[8,72,2048]{2,1,0:T(8,128)(2,1)} %collective-permute-done.16, bf16[8,72,2048]{2,1,0:T(8,128)(2,1)} %multiply_convert_fusion), kind=kLoop, calls=%fused_computation | loop fusion | flops 9437184 | bytes 9437184 | tf_op jit(solution)/shard_map/concatenate | solution.py:386
  161.4 13.2 %collective-permute-done.18 = bf16[256,2048]{1,0:T(8,128)(2,1)S(1)} collective-permute-done((bf16[256,2048]{1,0:T(8,128)(2,1)}, bf16[256,2048]{1,0:T(8,128)(2,1)S(1)}, u32[]{:S(2)}, u32[]{:S(2)}) %collective-permute-start.18) | collective-permute-done | bytes 1048608 | tf_op jit(solution)/shard_map/ppermute | solution.py:282
  175.7 13.6 %project.1 = (bf16[1152,1536]{1,0:T(8,128)(2,1)S(1)}, bf16[1152,512]{1,0:T(8,128)(2,1)S(1)}) custom-call(bf16[1152,2048]{1,0:T(8,128)(2,1)S(1)} %bitcast.105, bf16[1152,2048]{1,0:T(8,128)(2,1)S(1)} %bitcast.96, bf16[2048,2048]{1,0:T(8,128)(2,1)} %constant_dynamic-update-slice_fusion.weight_ref), custom_call_target="tpu_custom_call" | custom-call | flops 9663676416 | bytes 18874368 | tf_op jit(solution)/shard_map/project/pallas_call | solution.py:203
  189.3 7.8 %temporal_attention.1 = (bf16[8,144,512]{2,1,0:T(8,128)(2,1)S(1)}, bf16[8,144,1536]{2,1,0:T(8,128)(2,1)S(1)}, f32[8,128]{1,0:T(8,128)S(1)}, f32[8,128]{1,0:T(8,128)S(1)}) custom-call(f32[128,1]{1,0:T(8,128)S(1)} %copy-done.23, f32[1,128]{1,0:T(1,128)S(1)} %broadcast_in_dim_reshape.8.early_ref, bf16[8,144,1536]{2,1,0:T(8,128)(2,1)S(1)} %bitcast.125, ...), custom_call_target="tpu_custom_call" | custom-call | flops 1207959552 | bytes 9437184 | tf_op jit(solution)/shard_map/temporal_attention/pallas_call | solution.py:108
  206.6 6.4 %weight_product.4 = (f32[256,2048]{1,0:T(8,128)S(1)}, f32[256,2048]{1,0:T(8,128)S(1)}) custom-call(s32[2]{0:T(128)S(1)} %pad_add_fusion.1.place_ref, bf16[1152,2048]{1,0:T(8,128)(2,1)S(1)} %bitcast.106, bf16[1152,2048]{1,0:T(8,128)(2,1)S(1)} %bitcast.107, bf16[1152,2048]{1,0:T(8,128)(2,1)} %bitcast.97, bf16[1152,2048]{1,0:T(8,128)(2,1)} %bitcast.98, ...), custom_call_target="tpu_custom_call" | custom-call | flops 1 | bytes 1 | tf_op jit(solution)/shard_map/weight_product/pallas_call | solution.py:166
  215.7 7.8 %norm_product.2 = f32[576,2048]{1,0:T(8,128)} custom-call(bf16[576,1536]{1,0:T(8,128)(2,1)S(1)} %bitcast.124, bf16[2048,2048]{1,0:T(8,128)(2,1)} %constant_dynamic-update-slice_fusion.weight_ref), custom_call_target="tpu_custom_call" | custom-call | flops 1 | bytes 1 | tf_op jit(solution)/shard_map/norm_product/pallas_call | solution.py:239
  229.8 6.4 %weight_product.5 = (f32[256,2048]{1,0:T(8,128)S(1)}, f32[256,2048]{1,0:T(8,128)S(1)}) custom-call(s32[2]{0:T(128)S(1)} %pad_add_fusion.2.place_ref, bf16[1152,2048]{1,0:T(8,128)(2,1)S(1)} %bitcast.108, bf16[1152,2048]{1,0:T(8,128)(2,1)S(1)} %bitcast.109, bf16[1152,2048]{1,0:T(8,128)(2,1)} %bitcast.99, bf16[1152,2048]{1,0:T(8,128)(2,1)} %bitcast.100, ...), custom_call_target="tpu_custom_call" | custom-call | flops 1 | bytes 1 | tf_op jit(solution)/shard_map/weight_product/pallas_call | solution.py:166
  239.0 11.4 %collective-permute-done.19 = f16[264,2048]{1,0:T(8,128)(2,1)} collective-permute-done((f16[264,2048]{1,0:T(8,128)(2,1)}, f16[264,2048]{1,0:T(8,128)(2,1)}, u32[]{:S(2)}, u32[]{:S(2)}) %collective-permute-start.19) | collective-permute-done | bytes 1081376 | tf_op jit(solution)/shard_map/ppermute | solution.py:282
  254.9 6.8 %norm_product.3 = f32[576,2048]{1,0:T(8,128)S(1)} custom-call(bf16[576,1536]{1,0:T(8,128)(2,1)S(1)} %bitcast.123, bf16[2048,2048]{1,0:T(8,128)(2,1)} %constant_dynamic-update-slice_fusion.weight_ref), custom_call_target="tpu_custom_call" | custom-call | flops 1 | bytes 1 | tf_op jit(solution)/shard_map/norm_product/pallas_call | solution.py:239
  261.7 4.7 %multiply_reduce_fusion = (f32[8,72]{1,0:T(8,128)}, f32[8,72]{1,0:T(8,128)S(1)}, f32[8,72,2048]{2,1,0:T(8,128)S(1)}) fusion(bf16[8,72,2048]{2,1,0:T(8,128)(2,1)S(1)} %copy-done.25, f32[2048]{0:T(1024)S(1)} %copy-done.49, f32[8,72]{1,0:T(8,128)S(1)} %copy-done.51, f32[8,2048]{1,0:T(8,128)S(1)} %copy-done.35, f32[8,72,2048]{2,1,0:T(8,128)S(1)} %bitcast.122, ...), kind=kLoop, calls=%fused_computation.2 | loop fusion | flops 10615680 | bytes 16595712 | tf_op jit(solution)/shard_map/reduce_sum | solution.py:446
  274.9 6.4 %weight_product.6 = (f32[256,2048]{1,0:T(8,128)S(1)}, f32[256,2048]{1,0:T(8,128)S(1)}) custom-call(s32[2]{0:T(128)S(1)} %pad_add_fusion.3.place_ref, bf16[1152,2048]{1,0:T(8,128)(2,1)S(1)} %bitcast.110, bf16[1152,2048]{1,0:T(8,128)(2,1)S(1)} %bitcast.111, bf16[1152,2048]{1,0:T(8,128)(2,1)} %bitcast.101, bf16[1152,2048]{1,0:T(8,128)(2,1)} %bitcast.102, ...), custom_call_target="tpu_custom_call" | custom-call | flops 1 | bytes 1 | tf_op jit(solution)/shard_map/weight_product/pallas_call | solution.py:166
  295.6 6.8 %weight_product.7 = (f32[256,2048]{1,0:T(8,128)S(1)}, f32[256,2048]{1,0:T(8,128)S(1)}) custom-call(s32[2]{0:T(128)S(1)} %pad_add_fusion.4.place_ref, bf16[1152,2048]{1,0:T(8,128)(2,1)S(1)} %bitcast.112, bf16[1152,2048]{1,0:T(8,128)(2,1)S(1)} %bitcast.113, bf16[1152,2048]{1,0:T(8,128)(2,1)} %bitcast.103, bf16[1152,2048]{1,0:T(8,128)(2,1)} %bitcast.104, ...), custom_call_target="tpu_custom_call" | custom-call | flops 1 | bytes 1 | tf_op jit(solution)/shard_map/weight_product/pallas_call | solution.py:166
  313.0 5.1 %collective-permute-done.29 = f32[9,1024]{1,0:T(8,128)S(1)} collective-permute-done((f32[9,1024]{1,0:T(8,128)S(1)}, f32[9,1024]{1,0:T(8,128)S(1)}, u32[]{:S(2)}, u32[]{:S(2)}) %collective-permute-start.29) | collective-permute-done | bytes 36896 | tf_op jit(solution)/shard_map/ppermute | solution.py:276
  328.4 16.6 %collective-permute-done.37 = f16[264,2048]{1,0:T(8,128)(2,1)S(1)} collective-permute-done((f16[264,2048]{1,0:T(8,128)(2,1)}, f16[264,2048]{1,0:T(8,128)(2,1)S(1)}, u32[]{:S(2)}, u32[]{:S(2)}) %collective-permute-start.37) | collective-permute-done | bytes 1081376 | tf_op jit(solution)/shard_map/ppermute | solution.py:282
  350.7 3.8 collective-permute-start.26
  354.5 19.3 %collective-permute-done.33 = bf16[2,72,1024]{2,1,0:T(8,128)(2,1)S(1)} collective-permute-done((bf16[2,72,1024]{2,1,0:T(8,128)(2,1)S(1)}, bf16[2,72,1024]{2,1,0:T(8,128)(2,1)S(1)}, u32[]{:S(2)}, u32[]{:S(2)}) %collective-permute-start.33) | collective-permute-done | bytes 294944 | tf_op jit(solution)/shard_map/ppermute | solution.py:273
  377.4 6.2 %collective-permute-done.34 = bf16[2,72,1024]{2,1,0:T(8,128)(2,1)S(1)} collective-permute-done((bf16[2,72,1024]{2,1,0:T(8,128)(2,1)S(1)}, bf16[2,72,1024]{2,1,0:T(8,128)(2,1)S(1)}, u32[]{:S(2)}, u32[]{:S(2)}) %collective-permute-start.34) | collective-permute-done | bytes 294944 | tf_op jit(solution)/shard_map/ppermute | solution.py:285
  384.5 10.8 %collective-permute-done.32 = bf16[2,72,1024]{2,1,0:T(8,128)(2,1)S(1)} collective-permute-done((bf16[2,72,1024]{2,1,0:T(8,128)(2,1)S(1)}, bf16[2,72,1024]{2,1,0:T(8,128)(2,1)S(1)}, u32[]{:S(2)}, u32[]{:S(2)}) %collective-permute-start.32) | collective-permute-done | bytes 294944 | tf_op jit(solution)/shard_map/ppermute | solution.py:285
  (307 shorter events, 144.7 us)
Async XLA Ops:
  21.4 51.5 %collective-permute-start.2 = (bf16[256,2048]{1,0:T(8,128)(2,1)S(1)}, bf16[256,2048]{1,0:T(8,128)(2,1)}, u32[]{:S(2)}, u32[]{:S(2)}) collective-permute-start(bf16[256,2048]{1,0:T(8,128)(2,1)S(1)} %pad_maximum_fusion.11), channel_id=1, source_target_pairs={{0,8},{8,16},{16,24},{24,0},{1,9},{9,17},{17,25},{25,1},{2,10},{10... | collective-permute-start | bytes 3145736 | tf_op jit(solution)/shard_map/ppermute | solution.py:273
  21.4 52.3 %collective-permute-start.4 = (bf16[256,2048]{1,0:T(8,128)(2,1)S(1)}, bf16[256,2048]{1,0:T(8,128)(2,1)}, u32[]{:S(2)}, u32[]{:S(2)}) collective-permute-start(bf16[256,2048]{1,0:T(8,128)(2,1)S(1)} %pad_maximum_fusion.11), channel_id=1, source_target_pairs={{0,4},{2,6},{4,0},{6,2},{1,5},{3,7},{5,1},{7,3},{8,12},{10,14},{12... | collective-permute-start | bytes 3145736 | tf_op jit(solution)/shard_map/ppermute | solution.py:282
  24.0 36.2 %collective-permute-start.5 = (bf16[2,2,72,1024]{3,2,1,0:T(8,128)(2,1)S(1)}, bf16[2,2,72,1024]{3,2,1,0:T(8,128)(2,1)S(1)}, u32[]{:S(2)}, u32[]{:S(2)}) collective-permute-start(bf16[2,2,72,1024]{3,2,1,0:T(8,128)(2,1)S(1)} %collective-permute-done.1), channel_id=1, source_target_pairs={{0,1},{1,0},{2,3},{3,2},{4,5},{5,4},{6,7},{7,6},{8,9},{9,8},{10,11... | collective-permute-start | bytes 1769480 | tf_op jit(solution)/shard_map/ppermute | solution.py:285
  26.8 46.0 %collective-permute-start.3 = (bf16[2,2,72,1024]{3,2,1,0:T(8,128)(2,1)S(1)}, bf16[2,2,72,1024]{3,2,1,0:T(8,128)(2,1)S(1)}, u32[]{:S(2)}, u32[]{:S(2)}) collective-permute-start(bf16[2,2,72,1024]{3,2,1,0:T(8,128)(2,1)S(1)} %pad_maximum_fusion.16), channel_id=1, source_target_pairs={{0,16},{8,24},{16,0},{24,8},{1,17},{9,25},{17,1},{25,9},{2,18},{10... | collective-permute-start | bytes 1769480 | tf_op jit(solution)/shard_map/ppermute | solution.py:273
  29.2 31.1 %collective-permute-start.6 = (s32[2,2]{1,0:T(2,128)S(1)}, s32[2,2]{1,0:T(2,128)S(1)}, u32[]{:S(2)}, u32[]{:S(2)}) collective-permute-start(s32[2,2]{1,0:T(2,128)S(1)} %copy-done.56), channel_id=1, source_target_pairs={{0,8},{8,16},{16,24},{24,0},{1,9},{9,17},{17,25},{25,1},{2,10},{10... | collective-permute-start | bytes 56 | tf_op jit(solution)/shard_map/ppermute | solution.py:273
  76.0 39.0 %collective-permute-start.7 = (bf16[256,2048]{1,0:T(8,128)(2,1)}, bf16[256,2048]{1,0:T(8,128)(2,1)S(1)}, u32[]{:S(2)}, u32[]{:S(2)}) collective-permute-start(bf16[256,2048]{1,0:T(8,128)(2,1)} %collective-permute-done.2), channel_id=1, source_target_pairs={{0,8},{8,16},{16,24},{24,0},{1,9},{9,17},{17,25},{25,1},{2,10},{10... | collective-permute-start | bytes 3145736 | tf_op jit(solution)/shard_map/ppermute | solution.py:273
  76.1 38.9 %collective-permute-start.9 = (bf16[256,2048]{1,0:T(8,128)(2,1)}, bf16[256,2048]{1,0:T(8,128)(2,1)S(1)}, u32[]{:S(2)}, u32[]{:S(2)}) collective-permute-start(bf16[256,2048]{1,0:T(8,128)(2,1)} %collective-permute-done.2), channel_id=1, source_target_pairs={{0,4},{2,6},{4,0},{6,2},{1,5},{3,7},{5,1},{7,3},{8,12},{10,14},{12... | collective-permute-start | bytes 3145736 | tf_op jit(solution)/shard_map/ppermute | solution.py:282
  77.5 37.5 %collective-permute-start.8 = (bf16[2,2,72,1024]{3,2,1,0:T(8,128)(2,1)S(1)}, bf16[2,2,72,1024]{3,2,1,0:T(8,128)(2,1)S(1)}, u32[]{:S(2)}, u32[]{:S(2)}) collective-permute-start(bf16[2,2,72,1024]{3,2,1,0:T(8,128)(2,1)S(1)} %pad_maximum_fusion.17), channel_id=1, source_target_pairs={{0,24},{8,0},{16,8},{24,16},{1,25},{9,1},{17,9},{25,17},{2,26},{10... | collective-permute-start | bytes 1769480 | tf_op jit(solution)/shard_map/ppermute | solution.py:273
  81.3 32.9 %collective-permute-start.10 = (bf16[2,2,72,1024]{3,2,1,0:T(8,128)(2,1)S(1)}, bf16[2,2,72,1024]{3,2,1,0:T(8,128)(2,1)S(1)}, u32[]{:S(2)}, u32[]{:S(2)}) collective-permute-start(bf16[2,2,72,1024]{3,2,1,0:T(8,128)(2,1)S(1)} %copy-done.45), channel_id=1, source_target_pairs={{0,1},{1,0},{2,3},{3,2},{4,5},{5,4},{6,7},{7,6},{8,9},{9,8},{10,11... | collective-permute-start | bytes 1769480 | tf_op jit(solution)/shard_map/ppermute | solution.py:285
  82.7 31.4 %collective-permute-start.11 = (s32[2,2]{1,0:T(2,128)S(1)}, s32[2,2]{1,0:T(2,128)S(1)}, u32[]{:S(2)}, u32[]{:S(2)}) collective-permute-start(s32[2,2]{1,0:T(2,128)S(1)} %copy-done.56), channel_id=1, source_target_pairs={{0,16},{8,24},{16,0},{24,8},{1,17},{9,25},{17,1},{25,9},{2,18},{10... | collective-permute-start | bytes 56 | tf_op jit(solution)/shard_map/ppermute | solution.py:273
  115.0 29.2 %collective-permute-start.12 = (bf16[256,2048]{1,0:T(8,128)(2,1)S(1)}, bf16[256,2048]{1,0:T(8,128)(2,1)S(1)}, u32[]{:S(2)}, u32[]{:S(2)}) collective-permute-start(bf16[256,2048]{1,0:T(8,128)(2,1)S(1)} %collective-permute-done.7), channel_id=1, source_target_pairs={{0,8},{8,16},{16,24},{24,0},{1,9},{9,17},{17,25},{25,1},{2,10},{10... | collective-permute-start | bytes 3145736 | tf_op jit(solution)/shard_map/ppermute | solution.py:273
  116.7 28.5 %collective-permute-start.15 = (bf16[256,2048]{1,0:T(8,128)(2,1)S(1)}, bf16[256,2048]{1,0:T(8,128)(2,1)S(1)}, u32[]{:S(2)}, u32[]{:S(2)}) collective-permute-start(bf16[256,2048]{1,0:T(8,128)(2,1)S(1)} %collective-permute-done.7), channel_id=1, source_target_pairs={{0,4},{2,6},{4,0},{6,2},{1,5},{3,7},{5,1},{7,3},{8,12},{10,14},{12... | collective-permute-start | bytes 3145736 | tf_op jit(solution)/shard_map/ppermute | solution.py:282
  223.5 38.2 %collective-permute-start.20 = (f32[8,72,2048]{2,1,0:T(8,128)}, f32[8,72,2048]{2,1,0:T(8,128)}, u32[]{:S(2)}, u32[]{:S(2)}) collective-permute-start(f32[8,72,2048]{2,1,0:T(8,128)} %bitcast.25), channel_id=1, source_target_pairs={{0,2},{2,0},{4,6},{6,4},{1,3},{3,1},{5,7},{7,5},{8,10},{10,8},{12,... | collective-permute-start | bytes 14155784 | tf_op jit(solution)/shard_map/ppermute | solution.py:279
  223.5 27.0 %collective-permute-start.19 = (f16[264,2048]{1,0:T(8,128)(2,1)}, f16[264,2048]{1,0:T(8,128)(2,1)}, u32[]{:S(2)}, u32[]{:S(2)}) collective-permute-start(f16[264,2048]{1,0:T(8,128)(2,1)} %pad_maximum_fusion.7), channel_id=1, source_target_pairs={{0,4},{2,6},{4,0},{6,2},{1,5},{3,7},{5,1},{7,3},{8,12},{10,14},{12... | collective-permute-start | bytes 3244040 | tf_op jit(solution)/shard_map/ppermute | solution.py:282
  238.3 45.1 %collective-permute-start.23 = (f16[264,2048]{1,0:T(8,128)(2,1)}, f16[264,2048]{1,0:T(8,128)(2,1)}, u32[]{:S(2)}, u32[]{:S(2)}) collective-permute-start(f16[264,2048]{1,0:T(8,128)(2,1)} %pad_maximum_fusion.6), channel_id=1, source_target_pairs={{0,4},{2,6},{4,0},{6,2},{1,5},{3,7},{5,1},{7,3},{8,12},{10,14},{12... | collective-permute-start | bytes 3244040 | tf_op jit(solution)/shard_map/ppermute | solution.py:282
  254.3 29.2 %collective-permute-start.24 = (f16[264,2048]{1,0:T(8,128)(2,1)}, f16[264,2048]{1,0:T(8,128)(2,1)}, u32[]{:S(2)}, u32[]{:S(2)}) collective-permute-start(f16[264,2048]{1,0:T(8,128)(2,1)} %pad_maximum_fusion.8), channel_id=1, source_target_pairs={{0,8},{8,16},{16,24},{24,0},{1,9},{9,17},{17,25},{25,1},{2,10},{10... | collective-permute-start | bytes 3244040 | tf_op jit(solution)/shard_map/ppermute | solution.py:273
  270.1 36.1 %collective-permute-start.21 = (f16[8,72,1024]{2,1,0:T(8,128)(2,1)}, f16[8,72,1024]{2,1,0:T(8,128)(2,1)}, u32[]{:S(2)}, u32[]{:S(2)}) collective-permute-start(f16[8,72,1024]{2,1,0:T(8,128)(2,1)} %divide_convert_fusion), channel_id=1, source_target_pairs={{0,1},{1,0},{2,3},{3,2},{4,5},{5,4},{6,7},{7,6},{8,9},{9,8},{10,11... | collective-permute-start | bytes 3538952 | tf_op jit(solution)/shard_map/ppermute | solution.py:285
  287.8 36.0 %collective-permute-start.27 = (f16[264,2048]{1,0:T(8,128)(2,1)}, f16[264,2048]{1,0:T(8,128)(2,1)}, u32[]{:S(2)}, u32[]{:S(2)}) collective-permute-start(f16[264,2048]{1,0:T(8,128)(2,1)} %pad_maximum_fusion.5), channel_id=1, source_target_pairs={{0,4},{2,6},{4,0},{6,2},{1,5},{3,7},{5,1},{7,3},{8,12},{10,14},{12... | collective-permute-start | bytes 3244040 | tf_op jit(solution)/shard_map/ppermute | solution.py:282
  289.4 34.4 %collective-permute-start.31 = (f16[264,2048]{1,0:T(8,128)(2,1)}, f16[264,2048]{1,0:T(8,128)(2,1)}, u32[]{:S(2)}, u32[]{:S(2)}) collective-permute-start(f16[264,2048]{1,0:T(8,128)(2,1)} %pad_maximum_fusion.9), channel_id=1, source_target_pairs={{0,8},{8,16},{16,24},{24,0},{1,9},{9,17},{17,25},{25,1},{2,10},{10... | collective-permute-start | bytes 3244040 | tf_op jit(solution)/shard_map/ppermute | solution.py:273
  318.7 26.3 %collective-permute-start.37 = (f16[264,2048]{1,0:T(8,128)(2,1)}, f16[264,2048]{1,0:T(8,128)(2,1)S(1)}, u32[]{:S(2)}, u32[]{:S(2)}) collective-permute-start(f16[264,2048]{1,0:T(8,128)(2,1)} %pad_maximum_fusion.4), channel_id=1, source_target_pairs={{0,4},{2,6},{4,0},{6,2},{1,5},{3,7},{5,1},{7,3},{8,12},{10,14},{12... | collective-permute-start | bytes 3244040 | tf_op jit(solution)/shard_map/ppermute | solution.py:282
  319.3 27.1 %collective-permute-start.25 = (bf16[2,72,1024]{2,1,0:T(8,128)(2,1)S(1)}, bf16[2,72,1024]{2,1,0:T(8,128)(2,1)S(1)}, u32[]{:S(2)}, u32[]{:S(2)}) collective-permute-start(bf16[2,72,1024]{2,1,0:T(8,128)(2,1)S(1)} %slice.194), channel_id=1, source_target_pairs={{0,1},{1,0},{2,3},{3,2},{4,5},{5,4},{6,7},{7,6},{8,9},{9,8},{10,11... | collective-permute-start | bytes 884744 | tf_op jit(solution)/shard_map/ppermute | solution.py:285
  327.2 56.5 %collective-permute-start.38 = (f16[264,2048]{1,0:T(8,128)(2,1)S(1)}, f16[264,2048]{1,0:T(8,128)(2,1)S(1)}, u32[]{:S(2)}, u32[]{:S(2)}) collective-permute-start(f16[264,2048]{1,0:T(8,128)(2,1)S(1)} %pad_maximum_fusion.10), channel_id=1, source_target_pairs={{0,8},{8,16},{16,24},{24,0},{1,9},{9,17},{17,25},{25,1},{2,10},{10... | collective-permute-start | bytes 3244040 | tf_op jit(solution)/shard_map/ppermute | solution.py:273
  346.5 27.3 %collective-permute-start.33 = (bf16[2,72,1024]{2,1,0:T(8,128)(2,1)S(1)}, bf16[2,72,1024]{2,1,0:T(8,128)(2,1)S(1)}, u32[]{:S(2)}, u32[]{:S(2)}) collective-permute-start(bf16[2,72,1024]{2,1,0:T(8,128)(2,1)S(1)} %get-tuple-element.125), channel_id=1, source_target_pairs={{0,16},{8,24},{16,0},{24,8},{1,17},{9,25},{17,1},{25,9},{2,18},{10... | collective-permute-start | bytes 884744 | tf_op jit(solution)/shard_map/ppermute | solution.py:273
  350.7 26.1 %collective-permute-start.26 = (bf16[2,72,1024]{2,1,0:T(8,128)(2,1)S(1)}, bf16[2,72,1024]{2,1,0:T(8,128)(2,1)S(1)}, u32[]{:S(2)}, u32[]{:S(2)}) collective-permute-start(bf16[2,72,1024]{2,1,0:T(8,128)(2,1)S(1)} %get-tuple-element.126), channel_id=1, source_target_pairs={{0,24},{8,0},{16,8},{24,16},{1,25},{9,1},{17,9},{25,17},{2,26},{10... | collective-permute-start | bytes 884744 | tf_op jit(solution)/shard_map/ppermute | solution.py:273
  (77 other events, 638.1 us)

commit v3 on v2

--- a/solution.py
+++ b/solution.py
@@ -13,6 +13,7 @@
 UPSTREAM_TOP = 6.0
 WIRE = jnp.float16
 WIRE_TOP = 32768.0
+VMEM = 58 * 1024 * 1024
 
 
 def after(value, *earlier):
@@ -126,7 +127,7 @@
             jax.ShapeDtypeStruct((8, HEAD), jnp.float32),
             jax.ShapeDtypeStruct((8, HEAD), jnp.float32),
         ],
-        compiler_params=pltpu.CompilerParams(vmem_limit_bytes=40 * 1024 * 1024),
+        compiler_params=pltpu.CompilerParams(vmem_limit_bytes=VMEM),
         cost_estimate=pl.CostEstimate(
             flops=16 * work * HEAD,
             bytes_accessed=16 * frames * pairs * width,
@@ -180,7 +181,7 @@
             scratch_shapes=[pltpu.VMEM((2 * rows, tokens), jnp.bfloat16)],
         ),
         out_shape=[jax.ShapeDtypeStruct((rows, 4 * width), jnp.float32)] * 2,
-        compiler_params=pltpu.CompilerParams(vmem_limit_bytes=40 * 1024 * 1024),
+        compiler_params=pltpu.CompilerParams(vmem_limit_bytes=VMEM),
         cost_estimate=pl.CostEstimate(flops=1, bytes_accessed=1, transcendentals=0),
         name="weight_product",
     )(places, normed, normed, upstream, upstream, merged, mixed)
@@ -218,7 +219,7 @@
             jax.ShapeDtypeStruct((tokens, 3 * width), jnp.bfloat16),
             jax.ShapeDtypeStruct((tokens, width), jnp.bfloat16),
         ],
-        compiler_params=pltpu.CompilerParams(vmem_limit_bytes=40 * 1024 * 1024),
+        compiler_params=pltpu.CompilerParams(vmem_limit_bytes=VMEM),
         cost_estimate=pl.CostEstimate(
             flops=2 * tokens * features * 4 * width,
             bytes_accessed=8 * tokens * features,
@@ -245,7 +246,7 @@
         ],
         out_specs=pl.BlockSpec((rows, tile), lambda i: (0, i)),
         out_shape=jax.ShapeDtypeStruct((rows, features), jnp.float32),
-        compiler_params=pltpu.CompilerParams(vmem_limit_bytes=40 * 1024 * 1024),
+        compiler_params=pltpu.CompilerParams(vmem_limit_bytes=VMEM),
         cost_estimate=pl.CostEstimate(flops=1, bytes_accessed=1, transcendentals=0),
         name="norm_product",
     )(merged, weights)
@@ -322,35 +323,37 @@
         piece = jnp.stack([pieces(rows, k, start, slice_width) for rows in (inputs, upstream)])
         return ring(piece, k)
 
-    def settle(weights, k, arrived, row):
-        start = (z - k) % depth * (2 * block_rows) + row * block_rows
+    def settle(weights, k, arrived, row, offset=0):
+        start = (z - k) % depth * (2 * block_rows) + row * block_rows + offset
         return lax.dynamic_update_slice(weights, arrived, (start, 0))
 
     block_rows = 2 * shard_rows
     arrived = collect(1, x * slice_width)
-    block = after(block, arrived)
     blocks, across, joined, all_ids = [], [], [], [action_ids]
     weights = jnp.zeros((features, width), jnp.bfloat16)
     for k in range(1, depth):
         blocks.append(block)
         across.append(swap_y(block))
-        crossed = swap_x(arrived) if tensors == 2 else None
-        joined.append(join_x(arrived, crossed))
-        following = ring(block, 1)
+        if k + 1 < depth:
+            following = ring(block, 1)
+            earlier = [across[-1]]
+        else:
+            following = [ring(block[:shard_rows], 1), ring(block[shard_rows:], 1)]
+            earlier = [across[-1], swap_y(following[0])]
         weights = settle(weights, k - 1, block, y)
         if k > 1:
+            crossed = swap_x(arrived) if tensors == 2 else None
+            joined.append(join_x(arrived, crossed))
+            earlier.append(joined[-1] if crossed is None else crossed)
+            arrived = collect(k, after(x * slice_width, block))
             weights = settle(weights, k - 2, across[k - 2], 1 - y)
-        earlier = [across[-1], joined[-1] if crossed is None else crossed]
-        if k + 1 < depth:
-            arrived = collect(k + 1, after(x * slice_width, block))
-            earlier.append(arrived)
-            all_ids.append(ring(after(action_ids, block), k))
-            earlier.append(all_ids[-1])
-            following, arrived, weights = lax.optimization_barrier(
-                (following, arrived, weights, earlier)
-            )[:3]
-        block = following
-    all_ids.append(ring(after(action_ids, blocks[-1]), depth - 1))
+        all_ids.append(ring(after(action_ids, block), k))
+        block, arrived, weights, all_ids[-1], earlier = lax.optimization_barrier(
+            (following, arrived, weights, all_ids[-1], earlier)
+        )
+    joined.append(join_x(arrived))
+    near = earlier[0]
+    last = [*block, earlier[1], swap_y(block[1])]
     locals_ = [pieces(rows, 0, 0, features) for rows in (inputs, upstream)]
     own_inputs = jnp.concatenate([locals_[0]] + [both_rows[0] for both_rows in joined], 0)
     own_upstream = jnp.concatenate([locals_[1]] + [both_rows[1] for both_rows in joined], 0)
@@ -377,19 +380,17 @@
     inverse = lax.rsqrt(jnp.mean(hidden * hidden, -1, keepdims=True) + NORM_EPSILON)
     normed = (hidden * inverse * gain).astype(jnp.bfloat16)
 
-    block, normed, own_upstream, weights, near = lax.optimization_barrier(
-        (block, normed, own_upstream, weights, across[-1])
-    )
-    far = swap_y(block)
-
     def both(own):
         return jnp.concatenate([own, swap_core(own)], 1).reshape(tokens, features)
 
     all_upstream = both(own_upstream)
     all_normed = both(normed)
     weights = settle(weights, depth - 2, near, 1 - y)
-    weights = settle(weights, depth - 1, block, y)
-    weights = settle(weights, depth - 1, after(far, all_normed, all_upstream), 1 - y)
+    last[3] = after(last[3], all_normed, all_upstream)
+    for i, part in enumerate(last):
+        weights = settle(
+            weights, depth - 1, part, 1 - y if i >= 2 else y, offset=i % 2 * shard_rows
+        )
     qkv, grad_heads = project(all_normed, all_upstream, weights)
     mixed, merged, peak_qkv, peak_out = temporal_attention(
         qkv.reshape(frames, 2 * pairs, 3 * head_width),
@@ -442,7 +443,7 @@
     weight_parts.append(weight_part(1, norm_away))
     payload = pack(*chip_sum(0, weight_parts[1][1]))
     norm_here = norm_part(after(merged[:, :pairs], payload))
-    partial_norm = norm_here + swap_core(norm_away)
+    partial_norm = norm_here + swap_core(after(norm_away, payload))
     row_dot = jnp.sum(partial_norm * gain * (hidden * inverse), -1, keepdims=True)
     if tensors == 2:
         x_away = cut_x(partial_norm, 1 - x)
@@ -479,25 +480,26 @@
     )
     small = jnp.concatenate([action_term, gain_term[None, :]], 0)
     small = small + swap_core(small)
+    for k in range(2, depth - 1):
+        payload = pack(*ring_sum(k, ring(payload, 1), (small, returned[1:])))
+        if k + 2 < depth:
+            weight_parts.append(weight_part(k + 2, payload))
+    grad_inputs = jnp.zeros(inputs.shape, jnp.bfloat16)
+    for k in range(depth):
+        piece = after(returned[k], payload)
+        target, first = place((z + k) % depth)
+        grad_inputs = lax.dynamic_update_slice(
+            grad_inputs, join_x(piece)[None], (target, 0, first, 0)
+        )
+    total = chip_sum(depth - 1, payload)[0]
+    small = after(small, total)
+    small = join_x(small + swap_y(small))
+    arriving, small = lax.optimization_barrier((ring(payload, 1), small))
+    total = total + unpack(arriving)[0]
     bit = 1
     while bit < depth:
         small = small + swap_z(small, bit)
         bit *= 2
-
-    for k in range(2, depth - 1):
-        payload = pack(*ring_sum(k, ring(payload, 1), (small, weight_parts[k + 1][1])))
-        if k + 2 < depth:
-            weight_parts.append(weight_part(k + 2, payload))
-    grad_inputs = jnp.zeros(inputs.shape, jnp.bfloat16)
-    for k in range(depth):
-        piece = after(returned[k], payload) if k else returned[k]
-        target, first = place((z + k) % depth)
-        grad_inputs = lax.dynamic_update_slice(
-            grad_inputs, join_x(piece)[None], (target, 0, first, 0)
-        )
-    small = after(small, payload)
-    small = join_x(small + swap_y(small))
-    total = chip_sum(depth - 1, payload)[0] + unpack(after(ring(payload, 1), small))[0]
     mine = lax.dynamic_slice_in_dim(total, core * shard_rows, shard_rows, 0)
     other = swap_core(lax.dynamic_slice_in_dim(total, (1 - core) * shard_rows, shard_rows, 0))
     first = jnp.where(core == 0, mine, other).reshape(shard_rows, 4, head_width)

time: 401 us -> 410 us (1.022)
  Pallas kernels: 62 us -> 80.9 us
  local copies, waits for them, and re-layouts: 59.9 us -> 42.4 us
  other arithmetic: 44.7 us -> 53.4 us
    ppermute x9 -> x10, waiting for transfers between devices: 42 us -> 6.32 us  [swap_y(): return lax.ppermute(value, 'space', [(i, i ^ 2) for i in range(spaces)])]
    ppermute x10, waiting for transfers between devices: 19.6 us -> 43.3 us  [swap_x(): return lax.ppermute(value, 'tensor', [(0, 1), (1, 0)])]
    unnamed x117 -> x77, local copies, waits for them, and re-layouts: 27.1 us -> 5.8 us
    ppermute x15 -> x16, waiting for transfers between devices: 108 us -> 119 us  [ring(): lax.ppermute(value, 'frame', [(i, (i + shift) % depth) for i in range(dep...]
    pallas_call x4, Pallas kernels: 26 us -> 34.9 us  [weight_product(): pl.pallas_call(weight_kernel, grid_spec=pltpu.PrefetchScalarGridSpec(num_...]
    another operation x11, other arithmetic: 7.05 us -> 12.4 us
    pallas_call x1, Pallas kernels: 13.6 us -> 18.3 us  [project(): pl.pallas_call(project_kernel, grid=(4, 2), in_specs=[pl.BlockSpec((rows,...]
    ppermute x15 -> x16, starting transfers between devices: 23.5 us -> 20.5 us  [ring(): lax.ppermute(value, 'frame', [(i, (i + shift) % depth) for i in range(dep...]
  transfers between devices with their start and end apart: 42 -> 44, of which waited for: 19 -> 18; matrix products, arithmetic and copies ran while one was open for 16% -> 16% of each run, Pallas kernels for 7% -> 11%
where the time goes in v3:
time: 410 us; the launch traced here: 409 us
  waiting for transfers between devices  182 us (44%)
  Pallas kernels  80.9 us (20%)
  other arithmetic  53.4 us (13%)
  starting transfers between devices  46.1 us (11%)
  local copies, waits for them, and re-layouts  42.4 us (10%)
    ppermute x16, waiting for transfers between devices, ring(): lax.ppermute(value, 'frame', [(i, (i + shift) % depth) for i in range(dep...  119 us
    ppermute x10, waiting for transfers between devices, swap_x(): return lax.ppermute(value, 'tensor', [(0, 1), (1, 0)])  43.3 us
    pallas_call x4, Pallas kernels, weight_product(): pl.pallas_call(weight_kernel, grid_spec=pltpu.PrefetchScalarGridSpec(num_...  34.9 us
    ppermute x16, starting transfers between devices, ring(): lax.ppermute(value, 'frame', [(i, (i + shift) % depth) for i in range(dep...  20.5 us
    pallas_call x1, Pallas kernels, project(): pl.pallas_call(project_kernel, grid=(4, 2), in_specs=[pl.BlockSpec((rows,...  18.3 us
    pallas_call x2, Pallas kernels, norm_product(): pl.pallas_call(norm_kernel, grid=(4,), in_specs=[pl.BlockSpec((rows, dept...  16.8 us
    dynamic_update_slice x9, local copies, waits for them, and re-layouts, settle(): return lax.dynamic_update_slice(weights, arrived, (start, 0))  13.4 us
    another operation x11, other arithmetic  12.4 us
  transfers between devices with their start and end apart: 44, of which 18 were waited for; matrix products, arithmetic and copies ran while one was open for 16% of the time, Pallas kernels for 11%

profile of v3, /device:TPU:0, one launch (start us, length us, event | category | flops | bytes accessed | tf_op | source)
XLA Modules:
  0.0 408.7 jit_solution(12967400180631821984)
XLA Ops:
  4.3 4.4 %broadcast_in_dim.102 = bf16[2048,2048]{1,0:T(8,128)(2,1)} broadcast(bf16[]{:T(256)} %constant.255.clone.1), dimensions={} | broadcast | bytes 8388610 | tf_op jit(solution)/shard_map/broadcast_in_dim | solution.py:333
  21.2 30.5 %collective-permute-done.3 = s32[2,2]{1,0:T(2,128)S(1)} collective-permute-done((s32[2,2]{1,0:T(2,128)S(1)}, s32[2,2]{1,0:T(2,128)S(1)}, u32[]{:S(2)}, u32[]{:S(2)}) %collective-permute-start.3) | collective-permute-done | bytes 48 | tf_op jit(solution)/shard_map/ppermute | solution.py:274
  62.7 7.7 %collective-permute-done.5 = bf16[2,2,72,1024]{3,2,1,0:T(8,128)(2,1)S(1)} collective-permute-done((bf16[2,2,72,1024]{3,2,1,0:T(8,128)(2,1)S(1)}, bf16[2,2,72,1024]{3,2,1,0:T(8,128)(2,1)S(1)}, u32[]{:S(2)}, u32[]{:S(2)}) %collective-permute-start.5) | collective-permute-done | bytes 589856 | tf_op jit(solution)/shard_map/ppermute | solution.py:286
  71.4 34.8 %collective-permute-done.8 = s32[2,2]{1,0:T(2,128)S(1)} collective-permute-done((s32[2,2]{1,0:T(2,128)S(1)}, s32[2,2]{1,0:T(2,128)S(1)}, u32[]{:S(2)}, u32[]{:S(2)}) %collective-permute-start.8) | collective-permute-done | bytes 48 | tf_op jit(solution)/shard_map/ppermute | solution.py:274
  113.4 3.9 collective-permute-start.13
  118.3 8.1 %collective-permute-done.11 = bf16[128,2048]{1,0:T(8,128)(2,1)} collective-permute-done((bf16[128,2048]{1,0:T(8,128)(2,1)}, bf16[128,2048]{1,0:T(8,128)(2,1)}, u32[]{:S(2)}, u32[]{:S(2)}) %collective-permute-start.11) | collective-permute-done | bytes 524320 | tf_op jit(solution)/shard_map/ppermute | solution.py:274
  130.5 14.5 %collective-permute-done.14 = s32[2,2]{1,0:T(2,128)S(1)} collective-permute-done((s32[2,2]{1,0:T(2,128)S(1)}, s32[2,2]{1,0:T(2,128)S(1)}, u32[]{:S(2)}, u32[]{:S(2)}) %collective-permute-start.14) | collective-permute-done | bytes 48 | tf_op jit(solution)/shard_map/ppermute | solution.py:274
  145.0 4.0 collective-permute-done.12
  150.9 12.2 %collective-permute-done.17 = bf16[2,2,72,1024]{3,2,1,0:T(8,128)(2,1)S(1)} collective-permute-done((bf16[2,2,72,1024]{3,2,1,0:T(8,128)(2,1)S(1)}, bf16[2,2,72,1024]{3,2,1,0:T(8,128)(2,1)S(1)}, u32[]{:S(2)}, u32[]{:S(2)}) %collective-permute-start.17) | collective-permute-done | bytes 589856 | tf_op jit(solution)/shard_map/ppermute | solution.py:286
  179.7 4.7 %pad_maximum_fusion = bf16[8,144,2048]{2,1,0:T(8,128)(2,1)} fusion(bf16[8,72,2048]{2,1,0:T(8,128)(2,1)} %collective-permute-done.18, bf16[8,72,2048]{2,1,0:T(8,128)(2,1)S(1)} %multiply_convert_fusion), kind=kLoop, calls=%fused_computation | loop fusion | flops 9437184 | bytes 9437184 | tf_op jit(solution)/shard_map/concatenate | solution.py:384
  189.1 18.3 %project.1 = (bf16[1152,1536]{1,0:T(8,128)(2,1)}, bf16[1152,512]{1,0:T(8,128)(2,1)}) custom-call(bf16[1152,2048]{1,0:T(8,128)(2,1)} %bitcast.96, bf16[1152,2048]{1,0:T(8,128)(2,1)} %bitcast.105, bf16[2048,2048]{1,0:T(8,128)(2,1)} %constant_dynamic-update-slice_fusion.weight_ref), custom_call_target="tpu_custom_call" | custom-call | flops 9663676416 | bytes 18874368 | tf_op jit(solution)/shard_map/project/pallas_call | solution.py:204
  207.4 10.8 %temporal_attention.1 = (bf16[8,144,512]{2,1,0:T(8,128)(2,1)}, bf16[8,144,1536]{2,1,0:T(8,128)(2,1)}, f32[8,128]{1,0:T(8,128)}, f32[8,128]{1,0:T(8,128)}) custom-call(f32[128,1]{1,0:T(8,128)} %broadcast_in_dim_reshape.9.late_ref, f32[1,128]{1,0:T(1,128)} %broadcast_in_dim_reshape.8.early_ref, bf16[8,144,1536]{2,1,0:T(8,128)(2,1)} %bitcast.127, ...), custom_call_target="tpu_custom_call" | custom-call | flops 1207959552 | bytes 9437184 | tf_op jit(solution)/shard_map/temporal_attention/pallas_call | solution.py:109
  222.7 8.7 %weight_product.4 = (f32[256,2048]{1,0:T(8,128)}, f32[256,2048]{1,0:T(8,128)}) custom-call(s32[2]{0:T(128)} %pad_add_fusion.1.place_ref, bf16[1152,2048]{1,0:T(8,128)(2,1)} %bitcast.97, bf16[1152,2048]{1,0:T(8,128)(2,1)} %bitcast.98, bf16[1152,2048]{1,0:T(8,128)(2,1)} %bitcast.106, bf16[1152,2048]{1,0:T(8,128)(2,1)} %bitcast.107, ...), custom_call_target="tpu_custom_call" | custom-call | flops 1 | bytes 1 | tf_op jit(solution)/shard_map/weight_product/pallas_call | solution.py:167
  237.3 8.3 %norm_product.2 = f32[576,2048]{1,0:T(8,128)} custom-call(bf16[576,1536]{1,0:T(8,128)(2,1)} %bitcast.124, bf16[2048,2048]{1,0:T(8,128)(2,1)} %constant_dynamic-update-slice_fusion.weight_ref), custom_call_target="tpu_custom_call" | custom-call | flops 1 | bytes 1 | tf_op jit(solution)/shard_map/norm_product/pallas_call | solution.py:240
  246.2 8.8 %weight_product.5 = (f32[256,2048]{1,0:T(8,128)}, f32[256,2048]{1,0:T(8,128)}) custom-call(s32[2]{0:T(128)} %pad_add_fusion.2.place_ref, bf16[1152,2048]{1,0:T(8,128)(2,1)} %bitcast.99, bf16[1152,2048]{1,0:T(8,128)(2,1)} %bitcast.100, bf16[1152,2048]{1,0:T(8,128)(2,1)} %bitcast.108, bf16[1152,2048]{1,0:T(8,128)(2,1)} %bitcast.109, ...), custom_call_target="tpu_custom_call" | custom-call | flops 1 | bytes 1 | tf_op jit(solution)/shard_map/weight_product/pallas_call | solution.py:167
  262.5 8.4 %norm_product.3 = f32[576,2048]{1,0:T(8,128)} custom-call(bf16[576,1536]{1,0:T(8,128)(2,1)} %bitcast.123, bf16[2048,2048]{1,0:T(8,128)(2,1)} %constant_dynamic-update-slice_fusion.weight_ref), custom_call_target="tpu_custom_call" | custom-call | flops 1 | bytes 1 | tf_op jit(solution)/shard_map/norm_product/pallas_call | solution.py:240
  271.0 5.4 %multiply_reduce_fusion = (f32[8,72]{1,0:T(8,128)S(1)}, f32[8,72]{1,0:T(8,128)S(1)}, f32[8,72,2048]{2,1,0:T(8,128)S(1)}) fusion(bf16[8,72,2048]{2,1,0:T(8,128)(2,1)S(1)} %copy-done.4, f32[2048]{0:T(1024)S(1)} %copy-done.35, f32[8,72]{1,0:T(8,128)S(1)} %add_rsqrt_fusion, f32[8,2048]{1,0:T(8,128)S(1)} %fusion.22, f32[8,72,2048]{2,1,0:T(8,128)} %bitcast.122, ...), kind=kLoop, calls=%fused_computation.2 | loop fusion | flops 10615680 | bytes 16595712 | tf_op jit(solution)/shard_map/reduce_sum | solution.py:447
  281.9 8.7 %weight_product.6 = (f32[256,2048]{1,0:T(8,128)}, f32[256,2048]{1,0:T(8,128)}) custom-call(s32[2]{0:T(128)} %pad_add_fusion.3.place_ref, bf16[1152,2048]{1,0:T(8,128)(2,1)} %bitcast.101, bf16[1152,2048]{1,0:T(8,128)(2,1)} %bitcast.102, bf16[1152,2048]{1,0:T(8,128)(2,1)} %bitcast.110, bf16[1152,2048]{1,0:T(8,128)(2,1)} %bitcast.111, ...), custom_call_target="tpu_custom_call" | custom-call | flops 1 | bytes 1 | tf_op jit(solution)/shard_map/weight_product/pallas_call | solution.py:167
  300.3 8.7 %weight_product.7 = (f32[256,2048]{1,0:T(8,128)}, f32[256,2048]{1,0:T(8,128)}) custom-call(s32[2]{0:T(128)} %pad_add_fusion.4.place_ref, bf16[1152,2048]{1,0:T(8,128)(2,1)} %bitcast.103, bf16[1152,2048]{1,0:T(8,128)(2,1)} %bitcast.104, bf16[1152,2048]{1,0:T(8,128)(2,1)} %bitcast.112, bf16[1152,2048]{1,0:T(8,128)(2,1)} %bitcast.113, ...), custom_call_target="tpu_custom_call" | custom-call | flops 1 | bytes 1 | tf_op jit(solution)/shard_map/weight_product/pallas_call | solution.py:167
  324.8 8.3 %collective-permute-done.29 = bf16[2,72,1024]{2,1,0:T(8,128)(2,1)S(1)} collective-permute-done((bf16[2,72,1024]{2,1,0:T(8,128)(2,1)S(1)}, bf16[2,72,1024]{2,1,0:T(8,128)(2,1)S(1)}, u32[]{:S(2)}, u32[]{:S(2)}) %collective-permute-start.29) | collective-permute-done | bytes 294944 | tf_op jit(solution)/shard_map/ppermute | solution.py:274
  333.1 19.0 %collective-permute-done.30 = bf16[2,72,1024]{2,1,0:T(8,128)(2,1)S(1)} collective-permute-done((bf16[2,72,1024]{2,1,0:T(8,128)(2,1)S(1)}, bf16[2,72,1024]{2,1,0:T(8,128)(2,1)S(1)}, u32[]{:S(2)}, u32[]{:S(2)}) %collective-permute-start.30) | collective-permute-done | bytes 294944 | tf_op jit(solution)/shard_map/ppermute | solution.py:274
  368.1 21.5 %collective-permute-done.33 = bf16[2,72,1024]{2,1,0:T(8,128)(2,1)S(1)} collective-permute-done((bf16[2,72,1024]{2,1,0:T(8,128)(2,1)S(1)}, bf16[2,72,1024]{2,1,0:T(8,128)(2,1)S(1)}, u32[]{:S(2)}, u32[]{:S(2)}) %collective-permute-start.33) | collective-permute-done | bytes 294944 | tf_op jit(solution)/shard_map/ppermute | solution.py:286
  391.8 5.1 %collective-permute-done.42 = f32[9,2048]{1,0:T(8,128)S(1)} collective-permute-done((f32[9,2048]{1,0:T(8,128)S(1)}, f32[9,2048]{1,0:T(8,128)S(1)}, u32[]{:S(2)}, u32[]{:S(2)}) %collective-permute-start.42) | collective-permute-done | bytes 73760 | tf_op jit(solution)/shard_map/ppermute | solution.py:277
  398.7 6.3 %collective-permute-done.43 = f32[9,2048]{1,0:T(8,128)S(1)} collective-permute-done((f32[9,2048]{1,0:T(8,128)S(1)}, f32[9,2048]{1,0:T(8,128)S(1)}, u32[]{:S(2)}, u32[]{:S(2)}) %collective-permute-start.43) | collective-permute-done | bytes 73760 | tf_op jit(solution)/shard_map/ppermute | solution.py:277
  (275 shorter events, 133.8 us)
Async XLA Ops:
  10.3 41.4 %collective-permute-start.1 = (bf16[256,2048]{1,0:T(8,128)(2,1)}, bf16[256,2048]{1,0:T(8,128)(2,1)S(1)}, u32[]{:S(2)}, u32[]{:S(2)}) collective-permute-start(bf16[256,2048]{1,0:T(8,128)(2,1)} %get-tuple-element.157), channel_id=1, source_target_pairs={{0,8},{8,16},{16,24},{24,0},{1,9},{9,17},{17,25},{25,1},{2,10},{10... | collective-permute-start | bytes 3145736 | tf_op jit(solution)/shard_map/ppermute | solution.py:274
  13.3 38.5 %collective-permute-start.4 = (bf16[256,2048]{1,0:T(8,128)(2,1)}, bf16[256,2048]{1,0:T(8,128)(2,1)S(1)}, u32[]{:S(2)}, u32[]{:S(2)}) collective-permute-start(bf16[256,2048]{1,0:T(8,128)(2,1)} %get-tuple-element.157), channel_id=1, source_target_pairs={{0,4},{2,6},{4,0},{6,2},{1,5},{3,7},{5,1},{7,3},{8,12},{10,14},{12... | collective-permute-start | bytes 3145736 | tf_op jit(solution)/shard_map/ppermute | solution.py:283
  15.9 35.8 %collective-permute-start.2 = (bf16[2,2,72,1024]{3,2,1,0:T(8,128)(2,1)S(1)}, bf16[2,2,72,1024]{3,2,1,0:T(8,128)(2,1)S(1)}, u32[]{:S(2)}, u32[]{:S(2)}) collective-permute-start(bf16[2,2,72,1024]{3,2,1,0:T(8,128)(2,1)S(1)} %pad_maximum_fusion.15), channel_id=1, source_target_pairs={{0,8},{8,16},{16,24},{24,0},{1,9},{9,17},{17,25},{25,1},{2,10},{10... | collective-permute-start | bytes 1769480 | tf_op jit(solution)/shard_map/ppermute | solution.py:274
  19.5 32.2 %collective-permute-start.3 = (s32[2,2]{1,0:T(2,128)S(1)}, s32[2,2]{1,0:T(2,128)S(1)}, u32[]{:S(2)}, u32[]{:S(2)}) collective-permute-start(s32[2,2]{1,0:T(2,128)S(1)} %copy-done.36), channel_id=1, source_target_pairs={{0,8},{8,16},{16,24},{24,0},{1,9},{9,17},{17,25},{25,1},{2,10},{10... | collective-permute-start | bytes 56 | tf_op jit(solution)/shard_map/ppermute | solution.py:274
  54.4 51.9 %collective-permute-start.6 = (bf16[256,2048]{1,0:T(8,128)(2,1)S(1)}, bf16[256,2048]{1,0:T(8,128)(2,1)S(1)}, u32[]{:S(2)}, u32[]{:S(2)}) collective-permute-start(bf16[256,2048]{1,0:T(8,128)(2,1)S(1)} %collective-permute-done.1), channel_id=1, source_target_pairs={{0,8},{8,16},{16,24},{24,0},{1,9},{9,17},{17,25},{25,1},{2,10},{10... | collective-permute-start | bytes 3145736 | tf_op jit(solution)/shard_map/ppermute | solution.py:274
  54.4 52.6 %collective-permute-start.9 = (bf16[256,2048]{1,0:T(8,128)(2,1)S(1)}, bf16[256,2048]{1,0:T(8,128)(2,1)}, u32[]{:S(2)}, u32[]{:S(2)}) collective-permute-start(bf16[256,2048]{1,0:T(8,128)(2,1)S(1)} %collective-permute-done.1), channel_id=1, source_target_pairs={{0,4},{2,6},{4,0},{6,2},{1,5},{3,7},{5,1},{7,3},{8,12},{10,14},{12... | collective-permute-start | bytes 3145736 | tf_op jit(solution)/shard_map/ppermute | solution.py:283
  57.5 48.7 %collective-permute-start.7 = (bf16[2,2,72,1024]{3,2,1,0:T(8,128)(2,1)S(1)}, bf16[2,2,72,1024]{3,2,1,0:T(8,128)(2,1)S(1)}, u32[]{:S(2)}, u32[]{:S(2)}) collective-permute-start(bf16[2,2,72,1024]{3,2,1,0:T(8,128)(2,1)S(1)} %pad_maximum_fusion.16), channel_id=1, source_target_pairs={{0,16},{8,24},{16,0},{24,8},{1,17},{9,25},{17,1},{25,9},{2,18},{10... | collective-permute-start | bytes 1769480 | tf_op jit(solution)/shard_map/ppermute | solution.py:274
  59.8 46.4 %collective-permute-start.8 = (s32[2,2]{1,0:T(2,128)S(1)}, s32[2,2]{1,0:T(2,128)S(1)}, u32[]{:S(2)}, u32[]{:S(2)}) collective-permute-start(s32[2,2]{1,0:T(2,128)S(1)} %copy-done.36), channel_id=1, source_target_pairs={{0,16},{8,24},{16,0},{24,8},{1,17},{9,25},{17,1},{25,9},{2,18},{10... | collective-permute-start | bytes 56 | tf_op jit(solution)/shard_map/ppermute | solution.py:274
  108.1 40.9 %collective-permute-start.15 = (bf16[256,2048]{1,0:T(8,128)(2,1)S(1)}, bf16[256,2048]{1,0:T(8,128)(2,1)S(1)}, u32[]{:S(2)}, u32[]{:S(2)}) collective-permute-start(bf16[256,2048]{1,0:T(8,128)(2,1)S(1)} %collective-permute-done.6), channel_id=1, source_target_pairs={{0,4},{2,6},{4,0},{6,2},{1,5},{3,7},{5,1},{7,3},{8,12},{10,14},{12... | collective-permute-start | bytes 3145736 | tf_op jit(solution)/shard_map/ppermute | solution.py:283
  113.4 35.6 %collective-permute-start.13 = (bf16[2,2,72,1024]{3,2,1,0:T(8,128)(2,1)S(1)}, bf16[2,2,72,1024]{3,2,1,0:T(8,128)(2,1)S(1)}, u32[]{:S(2)}, u32[]{:S(2)}) collective-permute-start(bf16[2,2,72,1024]{3,2,1,0:T(8,128)(2,1)S(1)} %pad_maximum_fusion.17), channel_id=1, source_target_pairs={{0,24},{8,0},{16,8},{24,16},{1,25},{9,1},{17,9},{25,17},{2,26},{10... | collective-permute-start | bytes 1769480 | tf_op jit(solution)/shard_map/ppermute | solution.py:274
  117.3 31.7 %collective-permute-start.12 = (bf16[128,2048]{1,0:T(8,128)(2,1)S(1)}, bf16[128,2048]{1,0:T(8,128)(2,1)S(1)}, u32[]{:S(2)}, u32[]{:S(2)}) collective-permute-start(bf16[128,2048]{1,0:T(8,128)(2,1)S(1)} %copy-done.27), channel_id=1, source_target_pairs={{0,8},{8,16},{16,24},{24,0},{1,9},{9,17},{17,25},{25,1},{2,10},{10... | collective-permute-start | bytes 1572872 | tf_op jit(solution)/shard_map/ppermute | solution.py:274
  233.8 25.6 %collective-permute-start.21 = (f16[264,2048]{1,0:T(8,128)(2,1)S(1)}, f16[264,2048]{1,0:T(8,128)(2,1)S(1)}, u32[]{:S(2)}, u32[]{:S(2)}) collective-permute-start(f16[264,2048]{1,0:T(8,128)(2,1)S(1)} %pad_maximum_fusion.7), channel_id=1, source_target_pairs={{0,4},{2,6},{4,0},{6,2},{1,5},{3,7},{5,1},{7,3},{8,12},{10,14},{12... | collective-permute-start | bytes 3244040 | tf_op jit(solution)/shard_map/ppermute | solution.py:283
  261.1 32.8 %collective-permute-start.25 = (f16[264,2048]{1,0:T(8,128)(2,1)}, f16[264,2048]{1,0:T(8,128)(2,1)}, u32[]{:S(2)}, u32[]{:S(2)}) collective-permute-start(f16[264,2048]{1,0:T(8,128)(2,1)} %pad_maximum_fusion.6), channel_id=1, source_target_pairs={{0,4},{2,6},{4,0},{6,2},{1,5},{3,7},{5,1},{7,3},{8,12},{10,14},{12... | collective-permute-start | bytes 3244040 | tf_op jit(solution)/shard_map/ppermute | solution.py:283
  262.5 31.4 %collective-permute-start.26 = (f16[264,2048]{1,0:T(8,128)(2,1)}, f16[264,2048]{1,0:T(8,128)(2,1)}, u32[]{:S(2)}, u32[]{:S(2)}) collective-permute-start(f16[264,2048]{1,0:T(8,128)(2,1)} %pad_maximum_fusion.8), channel_id=1, source_target_pairs={{0,8},{8,16},{16,24},{24,0},{1,9},{9,17},{17,25},{25,1},{2,10},{10... | collective-permute-start | bytes 3244040 | tf_op jit(solution)/shard_map/ppermute | solution.py:274
  280.6 32.2 %collective-permute-start.23 = (f16[8,72,1024]{2,1,0:T(8,128)(2,1)}, f16[8,72,1024]{2,1,0:T(8,128)(2,1)}, u32[]{:S(2)}, u32[]{:S(2)}) collective-permute-start(f16[8,72,1024]{2,1,0:T(8,128)(2,1)} %divide_convert_fusion), channel_id=1, source_target_pairs={{0,1},{1,0},{2,3},{3,2},{4,5},{5,4},{6,7},{7,6},{8,9},{9,8},{10,11... | collective-permute-start | bytes 3538952 | tf_op jit(solution)/shard_map/ppermute | solution.py:286
  298.3 26.0 %collective-permute-start.27 = (f16[264,2048]{1,0:T(8,128)(2,1)}, f16[264,2048]{1,0:T(8,128)(2,1)}, u32[]{:S(2)}, u32[]{:S(2)}) collective-permute-start(f16[264,2048]{1,0:T(8,128)(2,1)} %pad_maximum_fusion.5), channel_id=1, source_target_pairs={{0,4},{2,6},{4,0},{6,2},{1,5},{3,7},{5,1},{7,3},{8,12},{10,14},{12... | collective-permute-start | bytes 3244040 | tf_op jit(solution)/shard_map/ppermute | solution.py:283
  299.4 52.8 %collective-permute-start.32 = (f16[264,2048]{1,0:T(8,128)(2,1)}, f16[264,2048]{1,0:T(8,128)(2,1)S(1)}, u32[]{:S(2)}, u32[]{:S(2)}) collective-permute-start(f16[264,2048]{1,0:T(8,128)(2,1)} %pad_maximum_fusion.9), channel_id=1, source_target_pairs={{0,8},{8,16},{16,24},{24,0},{1,9},{9,17},{17,25},{25,1},{2,10},{10... | collective-permute-start | bytes 3244040 | tf_op jit(solution)/shard_map/ppermute | solution.py:274
  319.3 32.8 %collective-permute-start.30 = (bf16[2,72,1024]{2,1,0:T(8,128)(2,1)S(1)}, bf16[2,72,1024]{2,1,0:T(8,128)(2,1)S(1)}, u32[]{:S(2)}, u32[]{:S(2)}) collective-permute-start(bf16[2,72,1024]{2,1,0:T(8,128)(2,1)S(1)} %get-tuple-element.135), channel_id=1, source_target_pairs={{0,16},{8,24},{16,0},{24,8},{1,17},{9,25},{17,1},{25,9},{2,18},{10... | collective-permute-start | bytes 884744 | tf_op jit(solution)/shard_map/ppermute | solution.py:274
  319.9 32.2 %collective-permute-start.31 = (bf16[2,72,1024]{2,1,0:T(8,128)(2,1)S(1)}, bf16[2,72,1024]{2,1,0:T(8,128)(2,1)S(1)}, u32[]{:S(2)}, u32[]{:S(2)}) collective-permute-start(bf16[2,72,1024]{2,1,0:T(8,128)(2,1)S(1)} %get-tuple-element.134), channel_id=1, source_target_pairs={{0,8},{8,16},{16,24},{24,0},{1,9},{9,17},{17,25},{25,1},{2,10},{10... | collective-permute-start | bytes 884744 | tf_op jit(solution)/shard_map/ppermute | solution.py:274
  324.3 31.0 %collective-permute-start.37 = (f16[264,2048]{1,0:T(8,128)(2,1)S(1)}, f16[264,2048]{1,0:T(8,128)(2,1)S(1)}, u32[]{:S(2)}, u32[]{:S(2)}) collective-permute-start(f16[264,2048]{1,0:T(8,128)(2,1)S(1)} %pad_maximum_fusion.4), channel_id=1, source_target_pairs={{0,4},{2,6},{4,0},{6,2},{1,5},{3,7},{5,1},{7,3},{8,12},{10,14},{12... | collective-permute-start | bytes 3244040 | tf_op jit(solution)/shard_map/ppermute | solution.py:283
  362.1 28.0 %collective-permute-start.38 = (f16[264,2048]{1,0:T(8,128)(2,1)S(1)}, f16[264,2048]{1,0:T(8,128)(2,1)S(1)}, u32[]{:S(2)}, u32[]{:S(2)}) collective-permute-start(f16[264,2048]{1,0:T(8,128)(2,1)S(1)} %pad_maximum_fusion.10), channel_id=1, source_target_pairs={{0,8},{8,16},{16,24},{24,0},{1,9},{9,17},{17,25},{25,1},{2,10},{10... | collective-permute-start | bytes 3244040 | tf_op jit(solution)/shard_map/ppermute | solution.py:274
  362.1 28.6 %collective-permute-start.36 = (bf16[2,72,1024]{2,1,0:T(8,128)(2,1)}, bf16[2,72,1024]{2,1,0:T(8,128)(2,1)S(1)}, u32[]{:S(2)}, u32[]{:S(2)}) collective-permute-start(bf16[2,72,1024]{2,1,0:T(8,128)(2,1)} %copy-done.30), channel_id=1, source_target_pairs={{0,1},{1,0},{2,3},{3,2},{4,5},{5,4},{6,7},{7,6},{8,9},{9,8},{10,11... | collective-permute-start | bytes 884744 | tf_op jit(solution)/shard_map/ppermute | solution.py:286
  363.4 28.1 %collective-permute-start.35 = (bf16[2,72,1024]{2,1,0:T(8,128)(2,1)}, bf16[2,72,1024]{2,1,0:T(8,128)(2,1)S(1)}, u32[]{:S(2)}, u32[]{:S(2)}) collective-permute-start(bf16[2,72,1024]{2,1,0:T(8,128)(2,1)} %copy-done.28), channel_id=1, source_target_pairs={{0,1},{1,0},{2,3},{3,2},{4,5},{5,4},{6,7},{7,6},{8,9},{9,8},{10,11... | collective-permute-start | bytes 884744 | tf_op jit(solution)/shard_map/ppermute | solution.py:286
  364.2 25.8 %collective-permute-start.34 = (bf16[2,72,1024]{2,1,0:T(8,128)(2,1)}, bf16[2,72,1024]{2,1,0:T(8,128)(2,1)S(1)}, u32[]{:S(2)}, u32[]{:S(2)}) collective-permute-start(bf16[2,72,1024]{2,1,0:T(8,128)(2,1)} %copy-done.32), channel_id=1, source_target_pairs={{0,1},{1,0},{2,3},{3,2},{4,5},{5,4},{6,7},{7,6},{8,9},{9,8},{10,11... | collective-permute-start | bytes 884744 | tf_op jit(solution)/shard_map/ppermute | solution.py:286
  (59 other events, 660.7 us)

commit v4 on v2

--- a/solution.py
+++ b/solution.py
@@ -13,6 +13,7 @@
 UPSTREAM_TOP = 6.0
 WIRE = jnp.float16
 WIRE_TOP = 32768.0
+MIB = 1024 * 1024
 
 
 def after(value, *earlier):
@@ -32,7 +33,7 @@
 
 
 def attention_kernel(
-    late_ref, early_ref, qkv_ref, grad_ref, mixed_ref, merged_ref, peak_qkv_ref, peak_out_ref
+    late_ref, early_ref, qkv_ref, grad_ref, mixed_ref, merged_ref, peak_ref
 ):
     frames, group, width = grad_ref.shape
     rows = frames * group
@@ -59,8 +60,7 @@
 
     @pl.when(pl.program_id(0) == 0)
     def _():
-        peak_qkv_ref[...] = jnp.zeros_like(peak_qkv_ref)
-        peak_out_ref[...] = jnp.zeros_like(peak_out_ref)
+        peak_ref[...] = jnp.zeros_like(peak_ref)
 
     row_id = lax.broadcasted_iota(jnp.int32, (rows, rows), 0)
     col_id = lax.broadcasted_iota(jnp.int32, (rows, rows), 1)
@@ -84,7 +84,7 @@
     low = [(grad_scores[h] - high[h].astype(jnp.float32)).astype(jnp.bfloat16) for h in heads]
     grad_query = [(dot_nn(high[h], key[h]) + dot_nn(low[h], key[h])) * scale for h in heads]
     grad_key = [(dot_tn(high[h], query[h]) + dot_tn(low[h], query[h])) * scale for h in heads]
-    top_out, top_qkv = peak_out_ref[...], peak_qkv_ref[...]
+    top_out, top_qkv = peak_ref[0], peak_ref[1]
     for h, start in enumerate(starts):
         store(mixed_ref, start, mixed[h])
         store(merged_ref, start, grad_query[h])
@@ -93,8 +93,8 @@
         top_out = jnp.maximum(top_out, peak(mixed[h]))
         for term in (grad_query[h], grad_key[h], grad_value[h]):
             top_qkv = jnp.maximum(top_qkv, peak(term))
-    peak_out_ref[...] = top_out
-    peak_qkv_ref[...] = top_qkv
+    peak_ref[0] = top_out
+    peak_ref[1] = top_qkv
 
 
 def temporal_attention(qkv, grad_heads, times):
@@ -117,16 +117,14 @@
         out_specs=[
             pl.BlockSpec((frames, group, width), moving),
             pl.BlockSpec((frames, group, 3 * width), moving),
-            pl.BlockSpec((8, HEAD), fixed),
-            pl.BlockSpec((8, HEAD), fixed),
+            pl.BlockSpec((2, 8, HEAD), lambda i: (0, 0, 0)),
         ],
         out_shape=[
             jax.ShapeDtypeStruct((frames, pairs, width), jnp.bfloat16),
             jax.ShapeDtypeStruct((frames, pairs, 3 * width), jnp.bfloat16),
-            jax.ShapeDtypeStruct((8, HEAD), jnp.float32),
-            jax.ShapeDtypeStruct((8, HEAD), jnp.float32),
-        ],
-        compiler_params=pltpu.CompilerParams(vmem_limit_bytes=40 * 1024 * 1024),
+            jax.ShapeDtypeStruct((2, 8, HEAD), jnp.float32),
+        ],
+        compiler_params=pltpu.CompilerParams(vmem_limit_bytes=16 * MIB),
         cost_estimate=pl.CostEstimate(
             flops=16 * work * HEAD,
             bytes_accessed=16 * frames * pairs * width,
@@ -136,32 +134,45 @@
     )(per_row[:, None], per_row[None, :], qkv, grad_heads)
 
 
+def turn_kernel(rows_ref, out_ref):
+    out_ref[...] = rows_ref[...].T
+
+
+def turn(rows):
+    tokens, features = rows.shape
+    tile = features // 8
+    return pl.pallas_call(
+        turn_kernel,
+        grid=(8,),
+        in_specs=[pl.BlockSpec((tokens, tile), lambda i: (0, i))],
+        out_specs=pl.BlockSpec((tile, tokens), lambda i: (i, 0)),
+        out_shape=jax.ShapeDtypeStruct((features, tokens), rows.dtype),
+        compiler_params=pltpu.CompilerParams(vmem_limit_bytes=12 * MIB),
+        cost_estimate=pl.CostEstimate(flops=1, bytes_accessed=1, transcendentals=0),
+        name="turn",
+    )(rows)
+
+
 def weight_kernel(
-    place_ref, norm_near, norm_far, up_near, up_far, merged_ref, mixed_ref, near_ref, far_ref, turned
+    place_ref, norm_near, norm_far, up_near, up_far, merged_ref, mixed_ref, near_ref, far_ref
 ):
     step = pl.program_id(0)
-    rows = near_ref.shape[0]
-
-    @pl.when(step == 0)
-    def _():
-        turned[:rows] = norm_near[...].T
-        turned[rows:] = norm_far[...].T
 
     @pl.when(step < 3)
     def _():
-        near_ref[...] = dot_nn(turned[:rows], merged_ref[...])
-        far_ref[...] = dot_nn(turned[rows:], merged_ref[...])
+        near_ref[...] = dot_nn(norm_near[...], merged_ref[...])
+        far_ref[...] = dot_nn(norm_far[...], merged_ref[...])
 
     @pl.when(step == 3)
     def _():
-        near_ref[...] = dot_tn(up_near[...], mixed_ref[...])
-        far_ref[...] = dot_tn(up_far[...], mixed_ref[...])
+        near_ref[...] = dot_nn(up_near[...], mixed_ref[...])
+        far_ref[...] = dot_nn(up_far[...], mixed_ref[...])
 
 
 def weight_product(places, rows, normed, upstream, merged, mixed):
     tokens, width = mixed.shape
-    near = pl.BlockSpec((tokens, rows), lambda i, at: (0, at[0]))
-    far = pl.BlockSpec((tokens, rows), lambda i, at: (0, at[1]))
+    near = pl.BlockSpec((rows, tokens), lambda i, at: (at[0], 0))
+    far = pl.BlockSpec((rows, tokens), lambda i, at: (at[1], 0))
     out = pl.BlockSpec((rows, width), lambda i, at: (0, i))
     return pl.pallas_call(
         weight_kernel,
@@ -177,10 +188,9 @@
                 pl.BlockSpec((tokens, width), lambda i, at: (0, 0)),
             ],
             out_specs=[out, out],
-            scratch_shapes=[pltpu.VMEM((2 * rows, tokens), jnp.bfloat16)],
         ),
         out_shape=[jax.ShapeDtypeStruct((rows, 4 * width), jnp.float32)] * 2,
-        compiler_params=pltpu.CompilerParams(vmem_limit_bytes=40 * 1024 * 1024),
+        compiler_params=pltpu.CompilerParams(vmem_limit_bytes=20 * MIB),
         cost_estimate=pl.CostEstimate(flops=1, bytes_accessed=1, transcendentals=0),
         name="weight_product",
     )(places, normed, normed, upstream, upstream, merged, mixed)
@@ -218,7 +228,7 @@
             jax.ShapeDtypeStruct((tokens, 3 * width), jnp.bfloat16),
             jax.ShapeDtypeStruct((tokens, width), jnp.bfloat16),
         ],
-        compiler_params=pltpu.CompilerParams(vmem_limit_bytes=40 * 1024 * 1024),
+        compiler_params=pltpu.CompilerParams(vmem_limit_bytes=26 * MIB),
         cost_estimate=pl.CostEstimate(
             flops=2 * tokens * features * 4 * width,
             bytes_accessed=8 * tokens * features,
@@ -245,7 +255,7 @@
         ],
         out_specs=pl.BlockSpec((rows, tile), lambda i: (0, i)),
         out_shape=jax.ShapeDtypeStruct((rows, features), jnp.float32),
-        compiler_params=pltpu.CompilerParams(vmem_limit_bytes=40 * 1024 * 1024),
+        compiler_params=pltpu.CompilerParams(vmem_limit_bytes=18 * MIB),
         cost_estimate=pl.CostEstimate(flops=1, bytes_accessed=1, transcendentals=0),
         name="norm_product",
     )(merged, weights)
@@ -328,9 +338,9 @@
 
     block_rows = 2 * shard_rows
     arrived = collect(1, x * slice_width)
-    block = after(block, arrived)
-    blocks, across, joined, all_ids = [], [], [], [action_ids]
-    weights = jnp.zeros((features, width), jnp.bfloat16)
+    blocks, across, joined = [], [], []
+    all_ids = [action_ids] + [ring(after(action_ids, block), k) for k in range(1, depth)]
+    weights = after(jnp.zeros((features, width), jnp.bfloat16), arrived)
     for k in range(1, depth):
         blocks.append(block)
         across.append(swap_y(block))
@@ -343,14 +353,10 @@
         earlier = [across[-1], joined[-1] if crossed is None else crossed]
         if k + 1 < depth:
             arrived = collect(k + 1, after(x * slice_width, block))
-            earlier.append(arrived)
-            all_ids.append(ring(after(action_ids, block), k))
-            earlier.append(all_ids[-1])
-            following, arrived, weights = lax.optimization_barrier(
-                (following, arrived, weights, earlier)
-            )[:3]
+            following, arrived, weights, all_ids, earlier = lax.optimization_barrier(
+                (following, arrived, weights, all_ids, earlier)
+            )
         block = following
-    all_ids.append(ring(after(action_ids, blocks[-1]), depth - 1))
     locals_ = [pieces(rows, 0, 0, features) for rows in (inputs, upstream)]
     own_inputs = jnp.concatenate([locals_[0]] + [both_rows[0] for both_rows in joined], 0)
     own_upstream = jnp.concatenate([locals_[1]] + [both_rows[1] for both_rows in joined], 0)
@@ -387,11 +393,12 @@
 
     all_upstream = both(own_upstream)
     all_normed = both(normed)
+    normed_t, upstream_t = turn(all_normed), turn(all_upstream)
     weights = settle(weights, depth - 2, near, 1 - y)
     weights = settle(weights, depth - 1, block, y)
-    weights = settle(weights, depth - 1, after(far, all_normed, all_upstream), 1 - y)
+    weights = settle(weights, depth - 1, after(far, normed_t, upstream_t), 1 - y)
     qkv, grad_heads = project(all_normed, all_upstream, weights)
-    mixed, merged, peak_qkv, peak_out = temporal_attention(
+    mixed, merged, peaks = temporal_attention(
         qkv.reshape(frames, 2 * pairs, 3 * head_width),
         grad_heads.reshape(frames, 2 * pairs, head_width),
         times,
@@ -399,10 +406,11 @@
     flat_mixed = mixed.reshape(tokens, head_width)
     flat_merged = merged.reshape(tokens, 3 * head_width)
 
+    peaks = jnp.max(peaks, (1, 2))
     own_bound = tokens * jnp.where(
         lax.broadcasted_iota(jnp.int32, (1, width), 1) < 3 * head_width,
-        math.sqrt(features) * jnp.max(jnp.abs(gain)) * jnp.max(peak_qkv),
-        UPSTREAM_TOP * jnp.max(peak_out),
+        math.sqrt(features) * jnp.max(jnp.abs(gain)) * peaks[1],
+        UPSTREAM_TOP * peaks[0],
     )
     own_bound = jnp.maximum(own_bound, 1e-20)
 
@@ -420,7 +428,7 @@
         block_at = after((z - 1 - k) % depth * 2, earlier)
         places = jnp.stack([block_at + y, block_at + 1 - y])
         near, far = weight_product(
-            places, block_rows, all_normed, all_upstream, flat_merged, flat_mixed
+            places, block_rows, normed_t, upstream_t, flat_merged, flat_mixed
         )
         return near, pack(far, own_bound)
 
@@ -442,7 +450,7 @@
     weight_parts.append(weight_part(1, norm_away))
     payload = pack(*chip_sum(0, weight_parts[1][1]))
     norm_here = norm_part(after(merged[:, :pairs], payload))
-    partial_norm = norm_here + swap_core(norm_away)
+    partial_norm = norm_here + swap_core(after(norm_away, payload))
     row_dot = jnp.sum(partial_norm * gain * (hidden * inverse), -1, keepdims=True)
     if tensors == 2:
         x_away = cut_x(partial_norm, 1 - x)
@@ -467,12 +475,6 @@
         grad_norm * cut_x(gain) - unit_rows * (row_dot / features)
     )
     grad_rows = grad_hidden.astype(jnp.bfloat16)
-    returned = [grad_rows[:local_frames]]
-    for k in range(1, depth):
-        returned.append(
-            ring(grad_rows[k * local_frames : (k + 1) * local_frames], depth - k)
-        )
-
     gain_term = jnp.sum(grad_norm * unit_rows, (0, 1))
     action_term = jnp.dot(
         onehot.T, jnp.sum(grad_hidden, 1), precision=lax.Precision.HIGHEST
@@ -483,21 +485,29 @@
     while bit < depth:
         small = small + swap_z(small, bit)
         bit *= 2
+    grad_rows, small = lax.optimization_barrier((grad_rows, small))
+    returned = [grad_rows[:local_frames]]
+    for k in range(1, depth):
+        returned.append(
+            ring(grad_rows[k * local_frames : (k + 1) * local_frames], depth - k)
+        )
 
     for k in range(2, depth - 1):
-        payload = pack(*ring_sum(k, ring(payload, 1), (small, weight_parts[k + 1][1])))
+        payload = pack(*ring_sum(k, ring(payload, 1), returned[1:]))
         if k + 2 < depth:
             weight_parts.append(weight_part(k + 2, payload))
     grad_inputs = jnp.zeros(inputs.shape, jnp.bfloat16)
     for k in range(depth):
-        piece = after(returned[k], payload) if k else returned[k]
+        piece = after(returned[k], payload)
         target, first = place((z + k) % depth)
         grad_inputs = lax.dynamic_update_slice(
             grad_inputs, join_x(piece)[None], (target, 0, first, 0)
         )
-    small = after(small, payload)
+    arriving, grad_inputs, small = lax.optimization_barrier(
+        (ring(payload, 1), grad_inputs, small)
+    )
     small = join_x(small + swap_y(small))
-    total = chip_sum(depth - 1, payload)[0] + unpack(after(ring(payload, 1), small))[0]
+    total = chip_sum(depth - 1, arriving)[0] + unpack(arriving)[0]
     mine = lax.dynamic_slice_in_dim(total, core * shard_rows, shard_rows, 0)
     other = swap_core(lax.dynamic_slice_in_dim(total, (1 - core) * shard_rows, shard_rows, 0))
     first = jnp.where(core == 0, mine, other).reshape(shard_rows, 4, head_width)

time: 401 us -> 391 us (0.975)
  waiting for transfers between devices: 180 us -> 158 us
  local copies, waits for them, and re-layouts: 59.9 us -> 70.8 us
    ppermute x9, waiting for transfers between devices: 42 us -> 12.6 us  [swap_y(): return lax.ppermute(value, 'space', [(i, i ^ 2) for i in range(spaces)])]
    ppermute x15, waiting for transfers between devices: 108 us -> 88.4 us  [ring(): lax.ppermute(value, 'frame', [(i, (i + shift) % depth) for i in range(dep...]
    ppermute x10, waiting for transfers between devices: 19.6 us -> 39.7 us  [swap_x(): return lax.ppermute(value, 'tensor', [(0, 1), (1, 0)])]
    unnamed x117 -> x113, local copies, waits for them, and re-layouts: 27.1 us -> 38.7 us
    pallas_call x4, Pallas kernels: 26 us -> 18.2 us  [weight_product(): pl.pallas_call(weight_kernel, grid_spec=pltpu.PrefetchScalarGridSpec(num_...]
    ppermute x15, starting transfers between devices: 23.5 us -> 29.4 us  [ring(): lax.ppermute(value, 'frame', [(i, (i + shift) % depth) for i in range(dep...]
    pallas_call x0 -> x2, Pallas kernels: none -> 4.76 us  [turn(): pl.pallas_call(turn_kernel, grid=(8,), in_specs=[pl.BlockSpec((tokens, ti...]
    ppermute x2, waiting for transfers between devices: 8.76 us -> 13.3 us  [swap_z(): return lax.ppermute(value, 'frame', [(i, i ^ bit) for i in range(depth)])]
  transfers between devices with their start and end apart: 42 -> 42, of which waited for: 19 -> 24; matrix products, arithmetic and copies ran while one was open for 16% -> 15% of each run, Pallas kernels for 7% -> 8%
where the time goes in v4:
time: 391 us; the launch traced here: 388 us
  waiting for transfers between devices  158 us (40%)
  local copies, waits for them, and re-layouts  70.8 us (18%)
  Pallas kernels  58.7 us (15%)
  starting transfers between devices  50.8 us (13%)
  other arithmetic  45.3 us (12%)
    ppermute x15, waiting for transfers between devices, ring(): lax.ppermute(value, 'frame', [(i, (i + shift) % depth) for i in range(dep...  88.4 us
    ppermute x10, waiting for transfers between devices, swap_x(): return lax.ppermute(value, 'tensor', [(0, 1), (1, 0)])  39.7 us
    unnamed x113, local copies, waits for them, and re-layouts  38.7 us
    ppermute x15, starting transfers between devices, ring(): lax.ppermute(value, 'frame', [(i, (i + shift) % depth) for i in range(dep...  29.4 us
    pallas_call x4, Pallas kernels, weight_product(): pl.pallas_call(weight_kernel, grid_spec=pltpu.PrefetchScalarGridSpec(num_...  18.2 us
    pallas_call x2, Pallas kernels, norm_product(): pl.pallas_call(norm_kernel, grid=(4,), in_specs=[pl.BlockSpec((rows, dept...  14.4 us
    pallas_call x1, Pallas kernels, project(): pl.pallas_call(project_kernel, grid=(4, 2), in_specs=[pl.BlockSpec((rows,...  13.6 us
    ppermute x2, waiting for transfers between devices, swap_z(): return lax.ppermute(value, 'frame', [(i, i ^ bit) for i in range(depth)])  13.3 us
  transfers between devices with their start and end apart: 42, of which 24 were waited for; matrix products, arithmetic and copies ran while one was open for 15% of the time, Pallas kernels for 8%

profile of v4, /device:TPU:0, one launch (start us, length us, event | category | flops | bytes accessed | tf_op | source)
XLA Modules:
  0.0 387.7 jit_solution(11212870668264583374)
XLA Ops:
  16.2 11.0 %collective-permute-done.3 = bf16[2,2,72,1024]{3,2,1,0:T(8,128)(2,1)S(1)} collective-permute-done((bf16[2,2,72,1024]{3,2,1,0:T(8,128)(2,1)S(1)}, bf16[2,2,72,1024]{3,2,1,0:T(8,128)(2,1)S(1)}, u32[]{:S(2)}, u32[]{:S(2)}) %collective-permute-start.3) | collective-permute-done | bytes 589856 | tf_op jit(solution)/shard_map/ppermute | solution.py:283
  31.4 4.4 %broadcast_in_dim.105 = bf16[2048,2048]{1,0:T(8,128)(2,1)} broadcast(bf16[]{:T(256)} %constant.263.clone.1), dimensions={} | broadcast | bytes 8388610 | tf_op jit(solution)/shard_map/broadcast_in_dim | solution.py:343
  36.8 25.1 %collective-permute-done.4 = s32[2,2]{1,0:T(2,128)S(1)} collective-permute-done((s32[2,2]{1,0:T(2,128)S(1)}, s32[2,2]{1,0:T(2,128)S(1)}, u32[]{:S(2)}, u32[]{:S(2)}) %collective-permute-start.4) | collective-permute-done | bytes 48 | tf_op jit(solution)/shard_map/ppermute | solution.py:283
  61.9 13.3 %collective-permute-start.5 = (s32[2,2]{1,0:T(2,128)S(1)}, s32[2,2]{1,0:T(2,128)S(1)}, u32[]{:S(2)}, u32[]{:S(2)}) collective-permute-start(s32[2,2]{1,0:T(2,128)S(1)} %copy-done.54), channel_id=1, source_target_pairs={{0,16},{8,24},{16,0},{24,8},{1,17},{9,25},{17,1},{25,9},{2,18},{10... | collective-permute-start | bytes 56 | tf_op jit(solution)/shard_map/ppermute | solution.py:283
  100.9 19.0 %collective-permute-done.10 = bf16[2,2,72,1024]{3,2,1,0:T(8,128)(2,1)S(1)} collective-permute-done((bf16[2,2,72,1024]{3,2,1,0:T(8,128)(2,1)S(1)}, bf16[2,2,72,1024]{3,2,1,0:T(8,128)(2,1)S(1)}, u32[]{:S(2)}, u32[]{:S(2)}) %collective-permute-start.10) | collective-permute-done | bytes 589856 | tf_op jit(solution)/shard_map/ppermute | solution.py:283
  125.7 10.7 %collective-permute-done.14 = bf16[2,2,72,1024]{3,2,1,0:T(8,128)(2,1)S(1)} collective-permute-done((bf16[2,2,72,1024]{3,2,1,0:T(8,128)(2,1)S(1)}, bf16[2,2,72,1024]{3,2,1,0:T(8,128)(2,1)S(1)}, u32[]{:S(2)}, u32[]{:S(2)}) %collective-permute-start.14) | collective-permute-done | bytes 589856 | tf_op jit(solution)/shard_map/ppermute | solution.py:295
  141.1 4.9 %collective-permute-done.13 = bf16[256,2048]{1,0:T(8,128)(2,1)S(1)} collective-permute-done((bf16[256,2048]{1,0:T(8,128)(2,1)S(1)}, bf16[256,2048]{1,0:T(8,128)(2,1)S(1)}, u32[]{:S(2)}, u32[]{:S(2)}) %collective-permute-start.13) | collective-permute-done | bytes 1048608 | tf_op jit(solution)/shard_map/ppermute | solution.py:283
  170.5 5.8 %collective-permute-done.18 = bf16[256,2048]{1,0:T(8,128)(2,1)S(1)} collective-permute-done((bf16[256,2048]{1,0:T(8,128)(2,1)}, bf16[256,2048]{1,0:T(8,128)(2,1)S(1)}, u32[]{:S(2)}, u32[]{:S(2)}) %collective-permute-start.18) | collective-permute-done | bytes 1048608 | tf_op jit(solution)/shard_map/ppermute | solution.py:292
  177.4 13.6 %project.1 = (bf16[1152,1536]{1,0:T(8,128)(2,1)S(1)}, bf16[1152,512]{1,0:T(8,128)(2,1)S(1)}) custom-call(bf16[1152,2048]{1,0:T(8,128)(2,1)S(1)} %bitcast.109, bf16[1152,2048]{1,0:T(8,128)(2,1)S(1)} %bitcast.107, bf16[2048,2048]{1,0:T(8,128)(2,1)} %constant_dynamic-update-slice_fusion.weight_ref), custom_call_target="tpu_custom_call" | custom-call | flops 9663676416 | bytes 18874368 | tf_op jit(solution)/shard_map/project/pallas_call | solution.py:213
  191.1 7.8 %temporal_attention.1 = (bf16[8,144,512]{2,1,0:T(8,128)(2,1)S(1)}, bf16[8,144,1536]{2,1,0:T(8,128)(2,1)S(1)}, f32[2,8,128]{2,1,0:T(8,128)S(1)}) custom-call(f32[128,1]{1,0:T(8,128)S(1)} %copy-done.26, f32[1,128]{1,0:T(1,128)S(1)} %broadcast_in_dim_reshape.8.early_ref, bf16[8,144,1536]{2,1,0:T(8,128)(2,1)S(1)} %bitcast.113, bf16[8,144,512]{2,1,0:T(8,128)(2,1)S(1)} %bitcast.114), custom_call_target="tpu_custom_call" | custom-call | flops 1207959552 | bytes 9437184 | tf_op jit(solution)/shard_map/temporal_attention/pallas_call | solution.py:108
  207.9 4.6 %weight_product.4 = (f32[256,2048]{1,0:T(8,128)S(1)}, f32[256,2048]{1,0:T(8,128)S(1)}) custom-call(s32[2]{0:T(128)S(1)} %pad_add_fusion.1.place_ref, bf16[2048,1152]{1,0:T(8,128)(2,1)S(1)} %copy-done.8, bf16[2048,1152]{1,0:T(8,128)(2,1)S(1)} %copy-done.8, bf16[2048,1152]{1,0:T(8,128)(2,1)S(1)} %copy-done.3, bf16[2048,1152]{1,0:T(8,128)(2,1)S(1)} %copy-done.3, ...), custom_call_target="tpu_custom_call" | custom-call | flops 1 | bytes 1 | tf_op jit(solution)/shard_map/weight_product/pallas_call | solution.py:177
  216.2 7.8 %norm_product.2 = f32[576,2048]{1,0:T(8,128)} custom-call(bf16[576,1536]{1,0:T(8,128)(2,1)S(1)} %bitcast.112, bf16[2048,2048]{1,0:T(8,128)(2,1)} %constant_dynamic-update-slice_fusion.weight_ref), custom_call_target="tpu_custom_call" | custom-call | flops 1 | bytes 1 | tf_op jit(solution)/shard_map/norm_product/pallas_call | solution.py:249
  230.0 4.6 %weight_product.5 = (f32[256,2048]{1,0:T(8,128)S(1)}, f32[256,2048]{1,0:T(8,128)S(1)}) custom-call(s32[2]{0:T(128)S(1)} %pad_add_fusion.2.place_ref, bf16[2048,1152]{1,0:T(8,128)(2,1)S(1)} %copy-done.9, bf16[2048,1152]{1,0:T(8,128)(2,1)S(1)} %copy-done.9, bf16[2048,1152]{1,0:T(8,128)(2,1)S(1)} %copy-done.4, bf16[2048,1152]{1,0:T(8,128)(2,1)S(1)} %copy-done.4, ...), custom_call_target="tpu_custom_call" | custom-call | flops 1 | bytes 1 | tf_op jit(solution)/shard_map/weight_product/pallas_call | solution.py:177
  246.8 6.6 %norm_product.3 = f32[576,2048]{1,0:T(8,128)S(1)} custom-call(bf16[576,1536]{1,0:T(8,128)(2,1)S(1)} %bitcast.111, bf16[2048,2048]{1,0:T(8,128)(2,1)} %constant_dynamic-update-slice_fusion.weight_ref), custom_call_target="tpu_custom_call" | custom-call | flops 1 | bytes 1 | tf_op jit(solution)/shard_map/norm_product/pallas_call | solution.py:249
  253.4 4.7 %multiply_reduce_fusion = (f32[8,72]{1,0:T(8,128)}, f32[8,72]{1,0:T(8,128)S(1)}, f32[8,72,2048]{2,1,0:T(8,128)S(1)}) fusion(bf16[8,72,2048]{2,1,0:T(8,128)(2,1)S(1)} %copy-done.28, f32[2048]{0:T(1024)S(1)} %copy-done.47, f32[8,72]{1,0:T(8,128)S(1)} %copy-done.49, f32[8,2048]{1,0:T(8,128)S(1)} %copy-done.36, f32[8,72,2048]{2,1,0:T(8,128)S(1)} %bitcast.110, ...), kind=kLoop, calls=%fused_computation.2 | loop fusion | flops 10615680 | bytes 16595712 | tf_op jit(solution)/shard_map/reduce_sum | solution.py:454
  269.2 4.6 %weight_product.6 = (f32[256,2048]{1,0:T(8,128)S(1)}, f32[256,2048]{1,0:T(8,128)S(1)}) custom-call(s32[2]{0:T(128)S(1)} %pad_add_fusion.3.place_ref, bf16[2048,1152]{1,0:T(8,128)(2,1)S(1)} %copy-done.10, bf16[2048,1152]{1,0:T(8,128)(2,1)S(1)} %copy-done.10, bf16[2048,1152]{1,0:T(8,128)(2,1)S(1)} %copy-done.5, bf16[2048,1152]{1,0:T(8,128)(2,1)S(1)} %copy-done.5, ...), custom_call_target="tpu_custom_call" | custom-call | flops 1 | bytes 1 | tf_op jit(solution)/shard_map/weight_product/pallas_call | solution.py:177
  288.0 4.6 %weight_product.7 = (f32[256,2048]{1,0:T(8,128)S(1)}, f32[256,2048]{1,0:T(8,128)S(1)}) custom-call(s32[2]{0:T(128)S(1)} %pad_add_fusion.4.place_ref, bf16[2048,1152]{1,0:T(8,128)(2,1)S(1)} %copy-done.11, bf16[2048,1152]{1,0:T(8,128)(2,1)S(1)} %copy-done.11, bf16[2048,1152]{1,0:T(8,128)(2,1)S(1)} %copy-done.6, bf16[2048,1152]{1,0:T(8,128)(2,1)S(1)} %copy-done.6, ...), custom_call_target="tpu_custom_call" | custom-call | flops 1 | bytes 1 | tf_op jit(solution)/shard_map/weight_product/pallas_call | solution.py:177
  302.0 8.3 %collective-permute-done.27 = f32[9,1024]{1,0:T(8,128)S(1)} collective-permute-done((f32[9,1024]{1,0:T(8,128)S(1)}, f32[9,1024]{1,0:T(8,128)S(1)}, u32[]{:S(2)}, u32[]{:S(2)}) %collective-permute-start.27) | collective-permute-done | bytes 36896 | tf_op jit(solution)/shard_map/ppermute | solution.py:286
  311.0 5.0 %collective-permute-done.28 = f32[9,1024]{1,0:T(8,128)S(1)} collective-permute-done((f32[9,1024]{1,0:T(8,128)S(1)}, f32[9,1024]{1,0:T(8,128)S(1)}, u32[]{:S(2)}, u32[]{:S(2)}) %collective-permute-start.28) | collective-permute-done | bytes 36896 | tf_op jit(solution)/shard_map/ppermute | solution.py:286
  318.6 8.0 %collective-permute-done.29 = bf16[2,72,1024]{2,1,0:T(8,128)(2,1)S(1)} collective-permute-done((bf16[2,72,1024]{2,1,0:T(8,128)(2,1)S(1)}, bf16[2,72,1024]{2,1,0:T(8,128)(2,1)S(1)}, u32[]{:S(2)}, u32[]{:S(2)}) %collective-permute-start.29) | collective-permute-done | bytes 294944 | tf_op jit(solution)/shard_map/ppermute | solution.py:283
  326.6 15.1 %collective-permute-done.30 = bf16[2,72,1024]{2,1,0:T(8,128)(2,1)S(1)} collective-permute-done((bf16[2,72,1024]{2,1,0:T(8,128)(2,1)S(1)}, bf16[2,72,1024]{2,1,0:T(8,128)(2,1)S(1)}, u32[]{:S(2)}, u32[]{:S(2)}) %collective-permute-start.30) | collective-permute-done | bytes 294944 | tf_op jit(solution)/shard_map/ppermute | solution.py:283
  349.4 5.4 %collective-permute-done.36 = bf16[2,72,1024]{2,1,0:T(8,128)(2,1)} collective-permute-done((bf16[2,72,1024]{2,1,0:T(8,128)(2,1)S(1)}, bf16[2,72,1024]{2,1,0:T(8,128)(2,1)}, u32[]{:S(2)}, u32[]{:S(2)}) %collective-permute-start.36) | collective-permute-done | bytes 294944 | tf_op jit(solution)/shard_map/ppermute | solution.py:295
  356.4 4.7 %collective-permute-done.35 = bf16[2,72,1024]{2,1,0:T(8,128)(2,1)} collective-permute-done((bf16[2,72,1024]{2,1,0:T(8,128)(2,1)S(1)}, bf16[2,72,1024]{2,1,0:T(8,128)(2,1)}, u32[]{:S(2)}, u32[]{:S(2)}) %collective-permute-start.35) | collective-permute-done | bytes 294944 | tf_op jit(solution)/shard_map/ppermute | solution.py:295
  362.1 8.5 %collective-permute-done.34 = bf16[2,72,1024]{2,1,0:T(8,128)(2,1)S(1)} collective-permute-done((bf16[2,72,1024]{2,1,0:T(8,128)(2,1)S(1)}, bf16[2,72,1024]{2,1,0:T(8,128)(2,1)S(1)}, u32[]{:S(2)}, u32[]{:S(2)}) %collective-permute-start.34) | collective-permute-done | bytes 294944 | tf_op jit(solution)/shard_map/ppermute | solution.py:295
  (303 shorter events, 176.0 us)
Async XLA Ops:
  8.0 19.2 %collective-permute-start.3 = (bf16[2,2,72,1024]{3,2,1,0:T(8,128)(2,1)S(1)}, bf16[2,2,72,1024]{3,2,1,0:T(8,128)(2,1)S(1)}, u32[]{:S(2)}, u32[]{:S(2)}) collective-permute-start(bf16[2,2,72,1024]{3,2,1,0:T(8,128)(2,1)S(1)} %pad_maximum_fusion.16), channel_id=1, source_target_pairs={{0,8},{8,16},{16,24},{24,0},{1,9},{9,17},{17,25},{25,1},{2,10},{10... | collective-permute-start | bytes 1769480 | tf_op jit(solution)/shard_map/ppermute | solution.py:283
  11.0 69.3 %collective-permute-start.1 = (bf16[256,2048]{1,0:T(8,128)(2,1)}, bf16[256,2048]{1,0:T(8,128)(2,1)}, u32[]{:S(2)}, u32[]{:S(2)}) collective-permute-start(bf16[256,2048]{1,0:T(8,128)(2,1)} %pad_maximum_fusion.11), channel_id=1, source_target_pairs={{0,8},{8,16},{16,24},{24,0},{1,9},{9,17},{17,25},{25,1},{2,10},{10... | collective-permute-start | bytes 3145736 | tf_op jit(solution)/shard_map/ppermute | solution.py:283
  12.6 67.7 %collective-permute-start.7 = (bf16[256,2048]{1,0:T(8,128)(2,1)}, bf16[256,2048]{1,0:T(8,128)(2,1)}, u32[]{:S(2)}, u32[]{:S(2)}) collective-permute-start(bf16[256,2048]{1,0:T(8,128)(2,1)} %pad_maximum_fusion.11), channel_id=1, source_target_pairs={{0,4},{2,6},{4,0},{6,2},{1,5},{3,7},{5,1},{7,3},{8,12},{10,14},{12... | collective-permute-start | bytes 3145736 | tf_op jit(solution)/shard_map/ppermute | solution.py:292
  15.0 65.3 %collective-permute-start.2 = (bf16[2,2,72,1024]{3,2,1,0:T(8,128)(2,1)}, bf16[2,2,72,1024]{3,2,1,0:T(8,128)(2,1)}, u32[]{:S(2)}, u32[]{:S(2)}) collective-permute-start(bf16[2,2,72,1024]{3,2,1,0:T(8,128)(2,1)} %pad_maximum_fusion.15), channel_id=1, source_target_pairs={{0,16},{8,24},{16,0},{24,8},{1,17},{9,25},{17,1},{25,9},{2,18},{10... | collective-permute-start | bytes 1769480 | tf_op jit(solution)/shard_map/ppermute | solution.py:283
  27.3 53.1 %collective-permute-start.8 = (bf16[2,2,72,1024]{3,2,1,0:T(8,128)(2,1)S(1)}, bf16[2,2,72,1024]{3,2,1,0:T(8,128)(2,1)}, u32[]{:S(2)}, u32[]{:S(2)}) collective-permute-start(bf16[2,2,72,1024]{3,2,1,0:T(8,128)(2,1)S(1)} %collective-permute-done.3), channel_id=1, source_target_pairs={{0,1},{1,0},{2,3},{3,2},{4,5},{5,4},{6,7},{7,6},{8,9},{9,8},{10,11... | collective-permute-start | bytes 1769480 | tf_op jit(solution)/shard_map/ppermute | solution.py:295
  31.4 30.5 %collective-permute-start.4 = (s32[2,2]{1,0:T(2,128)S(1)}, s32[2,2]{1,0:T(2,128)S(1)}, u32[]{:S(2)}, u32[]{:S(2)}) collective-permute-start(s32[2,2]{1,0:T(2,128)S(1)} %copy-done.54), channel_id=1, source_target_pairs={{0,8},{8,16},{16,24},{24,0},{1,9},{9,17},{17,25},{25,1},{2,10},{10... | collective-permute-start | bytes 56 | tf_op jit(solution)/shard_map/ppermute | solution.py:283
  82.7 37.3 %collective-permute-start.11 = (bf16[256,2048]{1,0:T(8,128)(2,1)}, bf16[256,2048]{1,0:T(8,128)(2,1)S(1)}, u32[]{:S(2)}, u32[]{:S(2)}) collective-permute-start(bf16[256,2048]{1,0:T(8,128)(2,1)} %collective-permute-done.1), channel_id=1, source_target_pairs={{0,4},{2,6},{4,0},{6,2},{1,5},{3,7},{5,1},{7,3},{8,12},{10,14},{12... | collective-permute-start | bytes 3145736 | tf_op jit(solution)/shard_map/ppermute | solution.py:292
  84.2 35.7 %collective-permute-start.9 = (bf16[256,2048]{1,0:T(8,128)(2,1)}, bf16[256,2048]{1,0:T(8,128)(2,1)S(1)}, u32[]{:S(2)}, u32[]{:S(2)}) collective-permute-start(bf16[256,2048]{1,0:T(8,128)(2,1)} %collective-permute-done.1), channel_id=1, source_target_pairs={{0,8},{8,16},{16,24},{24,0},{1,9},{9,17},{17,25},{25,1},{2,10},{10... | collective-permute-start | bytes 3145736 | tf_op jit(solution)/shard_map/ppermute | solution.py:283
  85.8 34.2 %collective-permute-start.10 = (bf16[2,2,72,1024]{3,2,1,0:T(8,128)(2,1)S(1)}, bf16[2,2,72,1024]{3,2,1,0:T(8,128)(2,1)S(1)}, u32[]{:S(2)}, u32[]{:S(2)}) collective-permute-start(bf16[2,2,72,1024]{3,2,1,0:T(8,128)(2,1)S(1)} %pad_maximum_fusion.17), channel_id=1, source_target_pairs={{0,24},{8,0},{16,8},{24,16},{1,25},{9,1},{17,9},{25,17},{2,26},{10... | collective-permute-start | bytes 1769480 | tf_op jit(solution)/shard_map/ppermute | solution.py:283
  120.0 26.1 %collective-permute-start.13 = (bf16[256,2048]{1,0:T(8,128)(2,1)S(1)}, bf16[256,2048]{1,0:T(8,128)(2,1)S(1)}, u32[]{:S(2)}, u32[]{:S(2)}) collective-permute-start(bf16[256,2048]{1,0:T(8,128)(2,1)S(1)} %collective-permute-done.9), channel_id=1, source_target_pairs={{0,8},{8,16},{16,24},{24,0},{1,9},{9,17},{17,25},{25,1},{2,10},{10... | collective-permute-start | bytes 3145736 | tf_op jit(solution)/shard_map/ppermute | solution.py:283
  121.2 25.8 %collective-permute-start.15 = (bf16[256,2048]{1,0:T(8,128)(2,1)S(1)}, bf16[256,2048]{1,0:T(8,128)(2,1)S(1)}, u32[]{:S(2)}, u32[]{:S(2)}) collective-permute-start(bf16[256,2048]{1,0:T(8,128)(2,1)S(1)} %collective-permute-done.9), channel_id=1, source_target_pairs={{0,4},{2,6},{4,0},{6,2},{1,5},{3,7},{5,1},{7,3},{8,12},{10,14},{12... | collective-permute-start | bytes 3145736 | tf_op jit(solution)/shard_map/ppermute | solution.py:292
  151.0 25.3 %collective-permute-start.18 = (bf16[256,2048]{1,0:T(8,128)(2,1)}, bf16[256,2048]{1,0:T(8,128)(2,1)S(1)}, u32[]{:S(2)}, u32[]{:S(2)}) collective-permute-start(bf16[256,2048]{1,0:T(8,128)(2,1)} %copy-done.37), channel_id=1, source_target_pairs={{0,4},{2,6},{4,0},{6,2},{1,5},{3,7},{5,1},{7,3},{8,12},{10,14},{12... | collective-permute-start | bytes 3145736 | tf_op jit(solution)/shard_map/ppermute | solution.py:292
  214.2 25.2 %collective-permute-start.19 = (f16[264,2048]{1,0:T(8,128)(2,1)}, f16[264,2048]{1,0:T(8,128)(2,1)}, u32[]{:S(2)}, u32[]{:S(2)}) collective-permute-start(f16[264,2048]{1,0:T(8,128)(2,1)} %pad_maximum_fusion.7), channel_id=1, source_target_pairs={{0,4},{2,6},{4,0},{6,2},{1,5},{3,7},{5,1},{7,3},{8,12},{10,14},{12... | collective-permute-start | bytes 3244040 | tf_op jit(solution)/shard_map/ppermute | solution.py:292
  244.5 31.3 %collective-permute-start.24 = (f16[264,2048]{1,0:T(8,128)(2,1)}, f16[264,2048]{1,0:T(8,128)(2,1)}, u32[]{:S(2)}, u32[]{:S(2)}) collective-permute-start(f16[264,2048]{1,0:T(8,128)(2,1)} %pad_maximum_fusion.6), channel_id=1, source_target_pairs={{0,4},{2,6},{4,0},{6,2},{1,5},{3,7},{5,1},{7,3},{8,12},{10,14},{12... | collective-permute-start | bytes 3244040 | tf_op jit(solution)/shard_map/ppermute | solution.py:292
  245.0 30.8 %collective-permute-start.25 = (f16[264,2048]{1,0:T(8,128)(2,1)}, f16[264,2048]{1,0:T(8,128)(2,1)}, u32[]{:S(2)}, u32[]{:S(2)}) collective-permute-start(f16[264,2048]{1,0:T(8,128)(2,1)} %pad_maximum_fusion.8), channel_id=1, source_target_pairs={{0,8},{8,16},{16,24},{24,0},{1,9},{9,17},{17,25},{25,1},{2,10},{10... | collective-permute-start | bytes 3244040 | tf_op jit(solution)/shard_map/ppermute | solution.py:283
  261.8 34.5 %collective-permute-start.22 = (f16[8,72,1024]{2,1,0:T(8,128)(2,1)}, f16[8,72,1024]{2,1,0:T(8,128)(2,1)}, u32[]{:S(2)}, u32[]{:S(2)}) collective-permute-start(f16[8,72,1024]{2,1,0:T(8,128)(2,1)} %divide_convert_fusion), channel_id=1, source_target_pairs={{0,1},{1,0},{2,3},{3,2},{4,5},{5,4},{6,7},{7,6},{8,9},{9,8},{10,11... | collective-permute-start | bytes 3538952 | tf_op jit(solution)/shard_map/ppermute | solution.py:295
  280.2 38.4 %collective-permute-start.21 = (f16[264,2048]{1,0:T(8,128)(2,1)}, f16[264,2048]{1,0:T(8,128)(2,1)}, u32[]{:S(2)}, u32[]{:S(2)}) collective-permute-start(f16[264,2048]{1,0:T(8,128)(2,1)} %pad_maximum_fusion.5), channel_id=1, source_target_pairs={{0,4},{2,6},{4,0},{6,2},{1,5},{3,7},{5,1},{7,3},{8,12},{10,14},{12... | collective-permute-start | bytes 3244040 | tf_op jit(solution)/shard_map/ppermute | solution.py:292
  281.8 59.9 %collective-permute-start.32 = (f16[264,2048]{1,0:T(8,128)(2,1)}, f16[264,2048]{1,0:T(8,128)(2,1)S(1)}, u32[]{:S(2)}, u32[]{:S(2)}) collective-permute-start(f16[264,2048]{1,0:T(8,128)(2,1)} %pad_maximum_fusion.9), channel_id=1, source_target_pairs={{0,8},{8,16},{16,24},{24,0},{1,9},{9,17},{17,25},{25,1},{2,10},{10... | collective-permute-start | bytes 3244040 | tf_op jit(solution)/shard_map/ppermute | solution.py:283
  317.9 23.7 %collective-permute-start.30 = (bf16[2,72,1024]{2,1,0:T(8,128)(2,1)S(1)}, bf16[2,72,1024]{2,1,0:T(8,128)(2,1)S(1)}, u32[]{:S(2)}, u32[]{:S(2)}) collective-permute-start(bf16[2,72,1024]{2,1,0:T(8,128)(2,1)S(1)} %get-tuple-element.148), channel_id=1, source_target_pairs={{0,16},{8,24},{16,0},{24,8},{1,17},{9,25},{17,1},{25,9},{2,18},{10... | collective-permute-start | bytes 884744 | tf_op jit(solution)/shard_map/ppermute | solution.py:283
  317.9 23.7 %collective-permute-start.31 = (bf16[2,72,1024]{2,1,0:T(8,128)(2,1)S(1)}, bf16[2,72,1024]{2,1,0:T(8,128)(2,1)S(1)}, u32[]{:S(2)}, u32[]{:S(2)}) collective-permute-start(bf16[2,72,1024]{2,1,0:T(8,128)(2,1)S(1)} %get-tuple-element.147), channel_id=1, source_target_pairs={{0,8},{8,16},{16,24},{24,0},{1,9},{9,17},{17,25},{25,1},{2,10},{10... | collective-permute-start | bytes 884744 | tf_op jit(solution)/shard_map/ppermute | solution.py:283
  346.8 25.3 %collective-permute-start.38 = (f16[264,2048]{1,0:T(8,128)(2,1)S(1)}, f16[264,2048]{1,0:T(8,128)(2,1)S(1)}, u32[]{:S(2)}, u32[]{:S(2)}) collective-permute-start(f16[264,2048]{1,0:T(8,128)(2,1)S(1)} %pad_maximum_fusion.4), channel_id=1, source_target_pairs={{0,4},{2,6},{4,0},{6,2},{1,5},{3,7},{5,1},{7,3},{8,12},{10,14},{12... | collective-permute-start | bytes 3244040 | tf_op jit(solution)/shard_map/ppermute | solution.py:292
  347.3 24.8 %collective-permute-start.33 = (f16[264,2048]{1,0:T(8,128)(2,1)S(1)}, f16[264,2048]{1,0:T(8,128)(2,1)S(1)}, u32[]{:S(2)}, u32[]{:S(2)}) collective-permute-start(f16[264,2048]{1,0:T(8,128)(2,1)S(1)} %pad_maximum_fusion.10), channel_id=1, source_target_pairs={{0,8},{8,16},{16,24},{24,0},{1,9},{9,17},{17,25},{25,1},{2,10},{10... | collective-permute-start | bytes 3244040 | tf_op jit(solution)/shard_map/ppermute | solution.py:283
  348.8 22.4 %collective-permute-start.37 = (bf16[2,72,1024]{2,1,0:T(8,128)(2,1)S(1)}, bf16[2,72,1024]{2,1,0:T(8,128)(2,1)S(1)}, u32[]{:S(2)}, u32[]{:S(2)}) collective-permute-start(bf16[2,72,1024]{2,1,0:T(8,128)(2,1)S(1)} %collective-permute-done.31), channel_id=1, source_target_pairs={{0,1},{1,0},{2,3},{3,2},{4,5},{5,4},{6,7},{7,6},{8,9},{9,8},{10,11... | collective-permute-start | bytes 884744 | tf_op jit(solution)/shard_map/ppermute | solution.py:295
  354.8 15.9 %collective-permute-start.34 = (bf16[2,72,1024]{2,1,0:T(8,128)(2,1)S(1)}, bf16[2,72,1024]{2,1,0:T(8,128)(2,1)S(1)}, u32[]{:S(2)}, u32[]{:S(2)}) collective-permute-start(bf16[2,72,1024]{2,1,0:T(8,128)(2,1)S(1)} %get-tuple-element.113), channel_id=1, source_target_pairs={{0,1},{1,0},{2,3},{3,2},{4,5},{5,4},{6,7},{7,6},{8,9},{9,8},{10,11... | collective-permute-start | bytes 884744 | tf_op jit(solution)/shard_map/ppermute | solution.py:295
  (75 other events, 532.6 us)

commit v5 on v4

--- a/solution.py
+++ b/solution.py
@@ -190,7 +190,7 @@
             out_specs=[out, out],
         ),
         out_shape=[jax.ShapeDtypeStruct((rows, 4 * width), jnp.float32)] * 2,
-        compiler_params=pltpu.CompilerParams(vmem_limit_bytes=20 * MIB),
+        compiler_params=pltpu.CompilerParams(vmem_limit_bytes=58 * MIB),
         cost_estimate=pl.CostEstimate(flops=1, bytes_accessed=1, transcendentals=0),
         name="weight_product",
     )(places, normed, normed, upstream, upstream, merged, mixed)
@@ -330,7 +330,20 @@
 
     def collect(k, start):
         piece = jnp.stack([pieces(rows, k, start, slice_width) for rows in (inputs, upstream)])
-        return ring(piece, k)
+        target, _ = place((z + k) % depth)
+        ids = lax.dynamic_index_in_dim(action_ids, target, 0, keepdims=False)
+        ids = jnp.broadcast_to(ids.astype(piece.dtype)[:, None], (local_frames, slice_width))
+        ids = jnp.pad(ids, ((0, -local_frames % 8), (0, 0)))
+        return ring(jnp.concatenate([piece.reshape(-1, slice_width), ids], 0), k)
+
+    piece_shape = (2, local_frames, pairs, slice_width)
+    piece_rows = 2 * local_frames * pairs
+
+    def join_piece(own, other):
+        ids = own[piece_rows : piece_rows + local_frames, 0].astype(jnp.int32)
+        if other is not None:
+            other = other[:piece_rows].reshape(piece_shape)
+        return join_x(own[:piece_rows].reshape(piece_shape), other), ids
 
     def settle(weights, k, arrived, row):
         start = (z - k) % depth * (2 * block_rows) + row * block_rows
@@ -339,13 +352,16 @@
     block_rows = 2 * shard_rows
     arrived = collect(1, x * slice_width)
     blocks, across, joined = [], [], []
-    all_ids = [action_ids] + [ring(after(action_ids, block), k) for k in range(1, depth)]
+    rollout, _ = place(z)
+    all_ids = [lax.dynamic_index_in_dim(action_ids, rollout, 0, keepdims=False)]
     weights = after(jnp.zeros((features, width), jnp.bfloat16), arrived)
     for k in range(1, depth):
         blocks.append(block)
         across.append(swap_y(block))
         crossed = swap_x(arrived) if tensors == 2 else None
-        joined.append(join_x(arrived, crossed))
+        piece, ids = join_piece(arrived, crossed)
+        joined.append(piece)
+        all_ids.append(ids)
         following = ring(block, 1)
         weights = settle(weights, k - 1, block, y)
         if k > 1:
@@ -353,19 +369,14 @@
         earlier = [across[-1], joined[-1] if crossed is None else crossed]
         if k + 1 < depth:
             arrived = collect(k + 1, after(x * slice_width, block))
-            following, arrived, weights, all_ids, earlier = lax.optimization_barrier(
-                (following, arrived, weights, all_ids, earlier)
+            following, arrived, weights, earlier = lax.optimization_barrier(
+                (following, arrived, weights, earlier)
             )
         block = following
     locals_ = [pieces(rows, 0, 0, features) for rows in (inputs, upstream)]
     own_inputs = jnp.concatenate([locals_[0]] + [both_rows[0] for both_rows in joined], 0)
     own_upstream = jnp.concatenate([locals_[1]] + [both_rows[1] for both_rows in joined], 0)
-    rollout, _ = place(z)
-    ids = jnp.concatenate(
-        [
-            lax.dynamic_index_in_dim(each, rollout, 0, keepdims=False) for each in all_ids
-        ]
-    )
+    ids = jnp.concatenate(all_ids)
     order = (
         (z - jnp.arange(depth, dtype=jnp.int32)[:, None]) % depth * local_frames
         + jnp.arange(local_frames, dtype=jnp.int32)[None, :]
@@ -481,11 +492,7 @@
     )
     small = jnp.concatenate([action_term, gain_term[None, :]], 0)
     small = small + swap_core(small)
-    bit = 1
-    while bit < depth:
-        small = small + swap_z(small, bit)
-        bit *= 2
-    grad_rows, small = lax.optimization_barrier((grad_rows, small))
+    small = small + swap_z(small, 1)
     returned = [grad_rows[:local_frames]]
     for k in range(1, depth):
         returned.append(
@@ -493,7 +500,7 @@
         )
 
     for k in range(2, depth - 1):
-        payload = pack(*ring_sum(k, ring(payload, 1), returned[1:]))
+        payload = pack(*ring_sum(k, ring(payload, 1), (returned[1:], small)))
         if k + 2 < depth:
             weight_parts.append(weight_part(k + 2, payload))
     grad_inputs = jnp.zeros(inputs.shape, jnp.bfloat16)
@@ -503,6 +510,11 @@
         grad_inputs = lax.dynamic_update_slice(
             grad_inputs, join_x(piece)[None], (target, 0, first, 0)
         )
+    small = after(small, payload)
+    bit = 2
+    while bit < depth:
+        small = small + swap_z(small, bit)
+        bit *= 2
     arriving, grad_inputs, small = lax.optimization_barrier(
         (ring(payload, 1), grad_inputs, small)
     )

time: 391 us -> 390 us (level)
  local copies, waits for them, and re-layouts: 70.8 us -> 42.9 us
  waiting for transfers between devices: 158 us -> 176 us
  Pallas kernels: 58.7 us -> 74.4 us
  starting transfers between devices: 50.8 us -> 36.7 us
  other arithmetic: 45.3 us -> 54.7 us
    unnamed x113 -> x53, local copies, waits for them, and re-layouts: 38.7 us -> 12.7 us
    ppermute x2, waiting for transfers between devices: 13.3 us -> 33.3 us  [swap_z(): return lax.ppermute(value, 'frame', [(i, i ^ bit) for i in range(depth)])]
    ppermute x15 -> x12, starting transfers between devices: 29.4 us -> 13.5 us  [ring(): lax.ppermute(value, 'frame', [(i, (i + shift) % depth) for i in range(dep...]
    pallas_call x4, Pallas kernels: 18.2 us -> 33.9 us  [weight_product(): pl.pallas_call(weight_kernel, grid_spec=pltpu.PrefetchScalarGridSpec(num_...]
    ppermute x10, waiting for transfers between devices: 39.7 us -> 27.1 us  [swap_x(): return lax.ppermute(value, 'tensor', [(0, 1), (1, 0)])]
    ppermute x15 -> x12, waiting for transfers between devices: 88.4 us -> 98.9 us  [ring(): lax.ppermute(value, 'frame', [(i, (i + shift) % depth) for i in range(dep...]
    another operation x11, other arithmetic: 6.69 us -> 12.8 us
  transfers between devices with their start and end apart: 42 -> 39, of which waited for: 24 -> 19; matrix products, arithmetic and copies ran while one was open for 15% -> 16% of each run, Pallas kernels for 8% -> 12%
where the time goes in v5:
time: 390 us; the launch traced here: 388 us
  waiting for transfers between devices  176 us (45%)
  Pallas kernels  74.4 us (19%)
  other arithmetic  54.7 us (14%)
  local copies, waits for them, and re-layouts  42.9 us (11%)
  starting transfers between devices  36.7 us (9%)
    ppermute x12, waiting for transfers between devices, ring(): lax.ppermute(value, 'frame', [(i, (i + shift) % depth) for i in range(dep...  98.9 us
    pallas_call x4, Pallas kernels, weight_product(): pl.pallas_call(weight_kernel, grid_spec=pltpu.PrefetchScalarGridSpec(num_...  33.9 us
    ppermute x2, waiting for transfers between devices, swap_z(): return lax.ppermute(value, 'frame', [(i, i ^ bit) for i in range(depth)])  33.3 us
    ppermute x10, waiting for transfers between devices, swap_x(): return lax.ppermute(value, 'tensor', [(0, 1), (1, 0)])  27.1 us
    pallas_call x2, Pallas kernels, norm_product(): pl.pallas_call(norm_kernel, grid=(4,), in_specs=[pl.BlockSpec((rows, dept...  14.4 us
    pallas_call x1, Pallas kernels, project(): pl.pallas_call(project_kernel, grid=(4, 2), in_specs=[pl.BlockSpec((rows,...  13.6 us
    ppermute x12, starting transfers between devices, ring(): lax.ppermute(value, 'frame', [(i, (i + shift) % depth) for i in range(dep...  13.5 us
    another operation x11, other arithmetic  12.8 us
  transfers between devices with their start and end apart: 39, of which 19 were waited for; matrix products, arithmetic and copies ran while one was open for 16% of the time, Pallas kernels for 12%

profile of v5, /device:TPU:0, one launch (start us, length us, event | category | flops | bytes accessed | tf_op | source)
XLA Modules:
  0.0 388.3 jit_solution(8891392783824382577)
XLA Ops:
  18.5 10.4 %collective-permute-done.3 = bf16[296,1024]{1,0:T(8,128)(2,1)} collective-permute-done((bf16[296,1024]{1,0:T(8,128)(2,1)}, bf16[296,1024]{1,0:T(8,128)(2,1)}, u32[]{:S(2)}, u32[]{:S(2)}) %collective-permute-start.3) | collective-permute-done | bytes 606240 | tf_op jit(solution)/shard_map/ppermute | solution.py:283
  32.5 4.4 %broadcast_in_dim.62 = bf16[2048,2048]{1,0:T(8,128)(2,1)} broadcast(bf16[]{:T(256)} %constant.276.clone.1), dimensions={} | broadcast | bytes 8388610 | tf_op jit(solution)/shard_map/broadcast_in_dim | solution.py:357
  38.0 38.7 %collective-permute-done.2 = bf16[296,1024]{1,0:T(8,128)(2,1)} collective-permute-done((bf16[296,1024]{1,0:T(8,128)(2,1)}, bf16[296,1024]{1,0:T(8,128)(2,1)}, u32[]{:S(2)}, u32[]{:S(2)}) %collective-permute-start.2) | collective-permute-done | bytes 606240 | tf_op jit(solution)/shard_map/ppermute | solution.py:283
  80.9 3.8 collective-permute-start.7
  91.7 8.0 %collective-permute-done.9 = bf16[296,1024]{1,0:T(8,128)(2,1)S(1)} collective-permute-done((bf16[296,1024]{1,0:T(8,128)(2,1)}, bf16[296,1024]{1,0:T(8,128)(2,1)S(1)}, u32[]{:S(2)}, u32[]{:S(2)}) %collective-permute-start.9) | collective-permute-done | bytes 606240 | tf_op jit(solution)/shard_map/ppermute | solution.py:295
  101.0 17.8 %collective-permute-done.7 = bf16[296,1024]{1,0:T(8,128)(2,1)S(1)} collective-permute-done((bf16[296,1024]{1,0:T(8,128)(2,1)S(1)}, bf16[296,1024]{1,0:T(8,128)(2,1)S(1)}, u32[]{:S(2)}, u32[]{:S(2)}) %collective-permute-start.7) | collective-permute-done | bytes 606240 | tf_op jit(solution)/shard_map/ppermute | solution.py:283
  123.8 10.3 %collective-permute-done.11 = bf16[296,1024]{1,0:T(8,128)(2,1)S(1)} collective-permute-done((bf16[296,1024]{1,0:T(8,128)(2,1)S(1)}, bf16[296,1024]{1,0:T(8,128)(2,1)S(1)}, u32[]{:S(2)}, u32[]{:S(2)}) %collective-permute-start.11) | collective-permute-done | bytes 606240 | tf_op jit(solution)/shard_map/ppermute | solution.py:295
  138.8 8.2 %collective-permute-done.10 = bf16[256,2048]{1,0:T(8,128)(2,1)} collective-permute-done((bf16[256,2048]{1,0:T(8,128)(2,1)S(1)}, bf16[256,2048]{1,0:T(8,128)(2,1)}, u32[]{:S(2)}, u32[]{:S(2)}) %collective-permute-start.10) | collective-permute-done | bytes 1048608 | tf_op jit(solution)/shard_map/ppermute | solution.py:283
  169.4 5.4 %collective-permute-done.15 = bf16[256,2048]{1,0:T(8,128)(2,1)S(1)} collective-permute-done((bf16[256,2048]{1,0:T(8,128)(2,1)}, bf16[256,2048]{1,0:T(8,128)(2,1)S(1)}, u32[]{:S(2)}, u32[]{:S(2)}) %collective-permute-start.15) | collective-permute-done | bytes 1048608 | tf_op jit(solution)/shard_map/ppermute | solution.py:292
  175.8 13.6 %project.1 = (bf16[1152,1536]{1,0:T(8,128)(2,1)S(1)}, bf16[1152,512]{1,0:T(8,128)(2,1)S(1)}) custom-call(bf16[1152,2048]{1,0:T(8,128)(2,1)S(1)} %bitcast.118, bf16[1152,2048]{1,0:T(8,128)(2,1)S(1)} %bitcast.116, bf16[2048,2048]{1,0:T(8,128)(2,1)} %constant_dynamic-update-slice_fusion.weight_ref), custom_call_target="tpu_custom_call" | custom-call | flops 9663676416 | bytes 18874368 | tf_op jit(solution)/shard_map/project/pallas_call | solution.py:213
  189.4 7.8 %temporal_attention.1 = (bf16[8,144,512]{2,1,0:T(8,128)(2,1)S(1)}, bf16[8,144,1536]{2,1,0:T(8,128)(2,1)S(1)}, f32[2,8,128]{2,1,0:T(8,128)S(1)}) custom-call(f32[128,1]{1,0:T(8,128)S(1)} %broadcast_in_dim_reshape.9.late_ref, f32[1,128]{1,0:T(1,128)S(1)} %broadcast_in_dim_reshape.8.early_ref, bf16[8,144,1536]{2,1,0:T(8,128)(2,1)S(1)} %bitcast.122, ...), custom_call_target="tpu_custom_call" | custom-call | flops 1207959552 | bytes 9437184 | tf_op jit(solution)/shard_map/temporal_attention/pallas_call | solution.py:108
  202.8 8.4 %weight_product.4 = (f32[256,2048]{1,0:T(8,128)}, f32[256,2048]{1,0:T(8,128)}) custom-call(s32[2]{0:T(128)} %pad_add_fusion.1.place_ref, bf16[2048,1152]{1,0:T(8,128)(2,1)} %copy-done.3, bf16[2048,1152]{1,0:T(8,128)(2,1)} %copy-done.3, bf16[2048,1152]{1,0:T(8,128)(2,1)} %copy-done.2, bf16[2048,1152]{1,0:T(8,128)(2,1)} %copy-done.2, ...), custom_call_target="tpu_custom_call" | custom-call | flops 1 | bytes 1 | tf_op jit(solution)/shard_map/weight_product/pallas_call | solution.py:177
  215.3 7.8 %norm_product.2 = f32[576,2048]{1,0:T(8,128)} custom-call(bf16[576,1536]{1,0:T(8,128)(2,1)S(1)} %bitcast.121, bf16[2048,2048]{1,0:T(8,128)(2,1)} %constant_dynamic-update-slice_fusion.weight_ref), custom_call_target="tpu_custom_call" | custom-call | flops 1 | bytes 1 | tf_op jit(solution)/shard_map/norm_product/pallas_call | solution.py:249
  223.7 8.3 %weight_product.5 = (f32[256,2048]{1,0:T(8,128)}, f32[256,2048]{1,0:T(8,128)}) custom-call(s32[2]{0:T(128)} %pad_add_fusion.2.place_ref, bf16[2048,1152]{1,0:T(8,128)(2,1)} %copy-done.3, bf16[2048,1152]{1,0:T(8,128)(2,1)} %copy-done.3, bf16[2048,1152]{1,0:T(8,128)(2,1)} %copy-done.2, bf16[2048,1152]{1,0:T(8,128)(2,1)} %copy-done.2, ...), custom_call_target="tpu_custom_call" | custom-call | flops 1 | bytes 1 | tf_op jit(solution)/shard_map/weight_product/pallas_call | solution.py:177
  240.8 6.6 %norm_product.3 = f32[576,2048]{1,0:T(8,128)S(1)} custom-call(bf16[576,1536]{1,0:T(8,128)(2,1)S(1)} %bitcast.120, bf16[2048,2048]{1,0:T(8,128)(2,1)} %constant_dynamic-update-slice_fusion.weight_ref), custom_call_target="tpu_custom_call" | custom-call | flops 1 | bytes 1 | tf_op jit(solution)/shard_map/norm_product/pallas_call | solution.py:249
  248.5 4.2 %multiply_reduce_fusion = (f32[8,72]{1,0:T(8,128)S(1)}, f32[8,72]{1,0:T(8,128)S(1)}, f32[8,72,2048]{2,1,0:T(8,128)S(1)}) fusion(bf16[8,72,2048]{2,1,0:T(8,128)(2,1)S(1)} %copy-done.9, f32[2048]{0:T(1024)S(1)} %copy-done.21, f32[8,72]{1,0:T(8,128)S(1)} %add_rsqrt_fusion, f32[8,2048]{1,0:T(8,128)S(1)} %fusion.22, f32[8,72,2048]{2,1,0:T(8,128)S(1)} %bitcast.119, ...), kind=kLoop, calls=%fused_computation.2 | loop fusion | flops 10615680 | bytes 16595712 | tf_op jit(solution)/shard_map/reduce_sum | solution.py:465
  257.4 8.3 %weight_product.6 = (f32[256,2048]{1,0:T(8,128)}, f32[256,2048]{1,0:T(8,128)}) custom-call(s32[2]{0:T(128)} %pad_add_fusion.3.place_ref, bf16[2048,1152]{1,0:T(8,128)(2,1)} %copy-done.3, bf16[2048,1152]{1,0:T(8,128)(2,1)} %copy-done.3, bf16[2048,1152]{1,0:T(8,128)(2,1)} %copy-done.2, bf16[2048,1152]{1,0:T(8,128)(2,1)} %copy-done.2, ...), custom_call_target="tpu_custom_call" | custom-call | flops 1 | bytes 1 | tf_op jit(solution)/shard_map/weight_product/pallas_call | solution.py:177
  275.4 8.9 %weight_product.7 = (f32[256,2048]{1,0:T(8,128)}, f32[256,2048]{1,0:T(8,128)}) custom-call(s32[2]{0:T(128)} %pad_add_fusion.4.place_ref, bf16[2048,1152]{1,0:T(8,128)(2,1)} %copy-done.3, bf16[2048,1152]{1,0:T(8,128)(2,1)} %copy-done.3, bf16[2048,1152]{1,0:T(8,128)(2,1)} %copy-done.2, bf16[2048,1152]{1,0:T(8,128)(2,1)} %copy-done.2, ...), custom_call_target="tpu_custom_call" | custom-call | flops 1 | bytes 1 | tf_op jit(solution)/shard_map/weight_product/pallas_call | solution.py:177
  297.0 6.2 %collective-permute-done.27 = f32[9,1024]{1,0:T(8,128)S(1)} collective-permute-done((f32[9,1024]{1,0:T(8,128)S(1)}, f32[9,1024]{1,0:T(8,128)S(1)}, u32[]{:S(2)}, u32[]{:S(2)}) %collective-permute-start.27) | collective-permute-done | bytes 36896 | tf_op jit(solution)/shard_map/ppermute | solution.py:286
  303.8 7.1 %collective-permute-done.23 = bf16[2,72,1024]{2,1,0:T(8,128)(2,1)S(1)} collective-permute-done((bf16[2,72,1024]{2,1,0:T(8,128)(2,1)S(1)}, bf16[2,72,1024]{2,1,0:T(8,128)(2,1)S(1)}, u32[]{:S(2)}, u32[]{:S(2)}) %collective-permute-start.23) | collective-permute-done | bytes 294944 | tf_op jit(solution)/shard_map/ppermute | solution.py:283
  310.9 16.7 %collective-permute-done.24 = bf16[2,72,1024]{2,1,0:T(8,128)(2,1)S(1)} collective-permute-done((bf16[2,72,1024]{2,1,0:T(8,128)(2,1)S(1)}, bf16[2,72,1024]{2,1,0:T(8,128)(2,1)S(1)}, u32[]{:S(2)}, u32[]{:S(2)}) %collective-permute-start.24) | collective-permute-done | bytes 294944 | tf_op jit(solution)/shard_map/ppermute | solution.py:283
  334.3 27.1 %collective-permute-done.34 = f32[9,1024]{1,0:T(8,128)S(1)} collective-permute-done((f32[9,1024]{1,0:T(8,128)S(1)}, f32[9,1024]{1,0:T(8,128)S(1)}, u32[]{:S(2)}, u32[]{:S(2)}) %collective-permute-start.34) | collective-permute-done | bytes 36896 | tf_op jit(solution)/shard_map/ppermute | solution.py:286
  365.6 5.7 %collective-permute-done.30 = bf16[2,72,1024]{2,1,0:T(8,128)(2,1)S(1)} collective-permute-done((bf16[2,72,1024]{2,1,0:T(8,128)(2,1)S(1)}, bf16[2,72,1024]{2,1,0:T(8,128)(2,1)S(1)}, u32[]{:S(2)}, u32[]{:S(2)}) %collective-permute-start.30) | collective-permute-done | bytes 294944 | tf_op jit(solution)/shard_map/ppermute | solution.py:295
  376.9 3.3 collective-permute-done.37
  (245 shorter events, 137.9 us)
Async XLA Ops:
  9.0 19.8 %collective-permute-start.3 = (bf16[296,1024]{1,0:T(8,128)(2,1)}, bf16[296,1024]{1,0:T(8,128)(2,1)}, u32[]{:S(2)}, u32[]{:S(2)}) collective-permute-start(bf16[296,1024]{1,0:T(8,128)(2,1)} %pad_maximum_fusion.13), channel_id=1, source_target_pairs={{0,8},{8,16},{16,24},{24,0},{1,9},{9,17},{17,25},{25,1},{2,10},{10... | collective-permute-start | bytes 1818632 | tf_op jit(solution)/shard_map/ppermute | solution.py:283
  13.0 63.7 %collective-permute-start.1 = (bf16[256,2048]{1,0:T(8,128)(2,1)}, bf16[256,2048]{1,0:T(8,128)(2,1)S(1)}, u32[]{:S(2)}, u32[]{:S(2)}) collective-permute-start(bf16[256,2048]{1,0:T(8,128)(2,1)} %pad_maximum_fusion.11), channel_id=1, source_target_pairs={{0,8},{8,16},{16,24},{24,0},{1,9},{9,17},{17,25},{25,1},{2,10},{10... | collective-permute-start | bytes 3145736 | tf_op jit(solution)/shard_map/ppermute | solution.py:283
  14.7 62.0 %collective-permute-start.4 = (bf16[256,2048]{1,0:T(8,128)(2,1)}, bf16[256,2048]{1,0:T(8,128)(2,1)}, u32[]{:S(2)}, u32[]{:S(2)}) collective-permute-start(bf16[256,2048]{1,0:T(8,128)(2,1)} %pad_maximum_fusion.11), channel_id=1, source_target_pairs={{0,4},{2,6},{4,0},{6,2},{1,5},{3,7},{5,1},{7,3},{8,12},{10,14},{12... | collective-permute-start | bytes 3145736 | tf_op jit(solution)/shard_map/ppermute | solution.py:292
  17.2 59.5 %collective-permute-start.2 = (bf16[296,1024]{1,0:T(8,128)(2,1)}, bf16[296,1024]{1,0:T(8,128)(2,1)}, u32[]{:S(2)}, u32[]{:S(2)}) collective-permute-start(bf16[296,1024]{1,0:T(8,128)(2,1)} %pad_maximum_fusion.12), channel_id=1, source_target_pairs={{0,16},{8,24},{16,0},{24,8},{1,17},{9,25},{17,1},{25,9},{2,18},{10... | collective-permute-start | bytes 1818632 | tf_op jit(solution)/shard_map/ppermute | solution.py:283
  28.8 47.9 %collective-permute-start.5 = (bf16[296,1024]{1,0:T(8,128)(2,1)}, bf16[296,1024]{1,0:T(8,128)(2,1)}, u32[]{:S(2)}, u32[]{:S(2)}) collective-permute-start(bf16[296,1024]{1,0:T(8,128)(2,1)} %collective-permute-done.3), channel_id=1, source_target_pairs={{0,1},{1,0},{2,3},{3,2},{4,5},{5,4},{6,7},{7,6},{8,9},{9,8},{10,11... | collective-permute-start | bytes 1818632 | tf_op jit(solution)/shard_map/ppermute | solution.py:295
  79.1 39.7 %collective-permute-start.6 = (bf16[256,2048]{1,0:T(8,128)(2,1)S(1)}, bf16[256,2048]{1,0:T(8,128)(2,1)S(1)}, u32[]{:S(2)}, u32[]{:S(2)}) collective-permute-start(bf16[256,2048]{1,0:T(8,128)(2,1)S(1)} %collective-permute-done.1), channel_id=1, source_target_pairs={{0,8},{8,16},{16,24},{24,0},{1,9},{9,17},{17,25},{25,1},{2,10},{10... | collective-permute-start | bytes 3145736 | tf_op jit(solution)/shard_map/ppermute | solution.py:283
  79.1 39.7 %collective-permute-start.8 = (bf16[256,2048]{1,0:T(8,128)(2,1)S(1)}, bf16[256,2048]{1,0:T(8,128)(2,1)S(1)}, u32[]{:S(2)}, u32[]{:S(2)}) collective-permute-start(bf16[256,2048]{1,0:T(8,128)(2,1)S(1)} %collective-permute-done.1), channel_id=1, source_target_pairs={{0,4},{2,6},{4,0},{6,2},{1,5},{3,7},{5,1},{7,3},{8,12},{10,14},{12... | collective-permute-start | bytes 3145736 | tf_op jit(solution)/shard_map/ppermute | solution.py:292
  80.9 37.8 %collective-permute-start.7 = (bf16[296,1024]{1,0:T(8,128)(2,1)S(1)}, bf16[296,1024]{1,0:T(8,128)(2,1)S(1)}, u32[]{:S(2)}, u32[]{:S(2)}) collective-permute-start(bf16[296,1024]{1,0:T(8,128)(2,1)S(1)} %pad_maximum_fusion.14), channel_id=1, source_target_pairs={{0,24},{8,0},{16,8},{24,16},{1,25},{9,1},{17,9},{25,17},{2,26},{10... | collective-permute-start | bytes 1818632 | tf_op jit(solution)/shard_map/ppermute | solution.py:283
  120.4 26.6 %collective-permute-start.10 = (bf16[256,2048]{1,0:T(8,128)(2,1)S(1)}, bf16[256,2048]{1,0:T(8,128)(2,1)}, u32[]{:S(2)}, u32[]{:S(2)}) collective-permute-start(bf16[256,2048]{1,0:T(8,128)(2,1)S(1)} %collective-permute-done.6), channel_id=1, source_target_pairs={{0,8},{8,16},{16,24},{24,0},{1,9},{9,17},{17,25},{25,1},{2,10},{10... | collective-permute-start | bytes 3145736 | tf_op jit(solution)/shard_map/ppermute | solution.py:283
  120.6 26.4 %collective-permute-start.12 = (bf16[256,2048]{1,0:T(8,128)(2,1)S(1)}, bf16[256,2048]{1,0:T(8,128)(2,1)}, u32[]{:S(2)}, u32[]{:S(2)}) collective-permute-start(bf16[256,2048]{1,0:T(8,128)(2,1)S(1)} %collective-permute-done.6), channel_id=1, source_target_pairs={{0,4},{2,6},{4,0},{6,2},{1,5},{3,7},{5,1},{7,3},{8,12},{10,14},{12... | collective-permute-start | bytes 3145736 | tf_op jit(solution)/shard_map/ppermute | solution.py:292
  149.4 25.3 %collective-permute-start.15 = (bf16[256,2048]{1,0:T(8,128)(2,1)}, bf16[256,2048]{1,0:T(8,128)(2,1)S(1)}, u32[]{:S(2)}, u32[]{:S(2)}) collective-permute-start(bf16[256,2048]{1,0:T(8,128)(2,1)} %collective-permute-done.10), channel_id=1, source_target_pairs={{0,4},{2,6},{4,0},{6,2},{1,5},{3,7},{5,1},{7,3},{8,12},{10,14},{12... | collective-permute-start | bytes 3145736 | tf_op jit(solution)/shard_map/ppermute | solution.py:292
  213.4 25.0 %collective-permute-start.16 = (f16[264,2048]{1,0:T(8,128)(2,1)S(1)}, f16[264,2048]{1,0:T(8,128)(2,1)S(1)}, u32[]{:S(2)}, u32[]{:S(2)}) collective-permute-start(f16[264,2048]{1,0:T(8,128)(2,1)S(1)} %pad_maximum_fusion.7), channel_id=1, source_target_pairs={{0,4},{2,6},{4,0},{6,2},{1,5},{3,7},{5,1},{7,3},{8,12},{10,14},{12... | collective-permute-start | bytes 3244040 | tf_op jit(solution)/shard_map/ppermute | solution.py:292
  240.2 28.9 %collective-permute-start.21 = (f16[264,2048]{1,0:T(8,128)(2,1)}, f16[264,2048]{1,0:T(8,128)(2,1)}, u32[]{:S(2)}, u32[]{:S(2)}) collective-permute-start(f16[264,2048]{1,0:T(8,128)(2,1)} %pad_maximum_fusion.6), channel_id=1, source_target_pairs={{0,4},{2,6},{4,0},{6,2},{1,5},{3,7},{5,1},{7,3},{8,12},{10,14},{12... | collective-permute-start | bytes 3244040 | tf_op jit(solution)/shard_map/ppermute | solution.py:292
  240.8 28.2 %collective-permute-start.22 = (f16[264,2048]{1,0:T(8,128)(2,1)}, f16[264,2048]{1,0:T(8,128)(2,1)}, u32[]{:S(2)}, u32[]{:S(2)}) collective-permute-start(f16[264,2048]{1,0:T(8,128)(2,1)} %pad_maximum_fusion.8), channel_id=1, source_target_pairs={{0,8},{8,16},{16,24},{24,0},{1,9},{9,17},{17,25},{25,1},{2,10},{10... | collective-permute-start | bytes 3244040 | tf_op jit(solution)/shard_map/ppermute | solution.py:283
  256.9 31.5 %collective-permute-start.19 = (f16[8,72,1024]{2,1,0:T(8,128)(2,1)}, f16[8,72,1024]{2,1,0:T(8,128)(2,1)S(1)}, u32[]{:S(2)}, u32[]{:S(2)}) collective-permute-start(f16[8,72,1024]{2,1,0:T(8,128)(2,1)} %divide_convert_fusion), channel_id=1, source_target_pairs={{0,1},{1,0},{2,3},{3,2},{4,5},{5,4},{6,7},{7,6},{8,9},{9,8},{10,11... | collective-permute-start | bytes 3538952 | tf_op jit(solution)/shard_map/ppermute | solution.py:295
  273.5 30.3 %collective-permute-start.18 = (f16[264,2048]{1,0:T(8,128)(2,1)}, f16[264,2048]{1,0:T(8,128)(2,1)}, u32[]{:S(2)}, u32[]{:S(2)}) collective-permute-start(f16[264,2048]{1,0:T(8,128)(2,1)} %pad_maximum_fusion.5), channel_id=1, source_target_pairs={{0,4},{2,6},{4,0},{6,2},{1,5},{3,7},{5,1},{7,3},{8,12},{10,14},{12... | collective-permute-start | bytes 3244040 | tf_op jit(solution)/shard_map/ppermute | solution.py:292
  275.4 52.2 %collective-permute-start.28 = (f16[264,2048]{1,0:T(8,128)(2,1)}, f16[264,2048]{1,0:T(8,128)(2,1)}, u32[]{:S(2)}, u32[]{:S(2)}) collective-permute-start(f16[264,2048]{1,0:T(8,128)(2,1)} %pad_maximum_fusion.9), channel_id=1, source_target_pairs={{0,8},{8,16},{16,24},{24,0},{1,9},{9,17},{17,25},{25,1},{2,10},{10... | collective-permute-start | bytes 3244040 | tf_op jit(solution)/shard_map/ppermute | solution.py:283
  297.0 30.6 %collective-permute-start.24 = (bf16[2,72,1024]{2,1,0:T(8,128)(2,1)S(1)}, bf16[2,72,1024]{2,1,0:T(8,128)(2,1)S(1)}, u32[]{:S(2)}, u32[]{:S(2)}) collective-permute-start(bf16[2,72,1024]{2,1,0:T(8,128)(2,1)S(1)} %get-tuple-element.134), channel_id=1, source_target_pairs={{0,16},{8,24},{16,0},{24,8},{1,17},{9,25},{17,1},{25,9},{2,18},{10... | collective-permute-start | bytes 884744 | tf_op jit(solution)/shard_map/ppermute | solution.py:283
  303.2 24.4 %collective-permute-start.25 = (bf16[2,72,1024]{2,1,0:T(8,128)(2,1)S(1)}, bf16[2,72,1024]{2,1,0:T(8,128)(2,1)S(1)}, u32[]{:S(2)}, u32[]{:S(2)}) collective-permute-start(bf16[2,72,1024]{2,1,0:T(8,128)(2,1)S(1)} %get-tuple-element.133), channel_id=1, source_target_pairs={{0,8},{8,16},{16,24},{24,0},{1,9},{9,17},{17,25},{25,1},{2,10},{10... | collective-permute-start | bytes 884744 | tf_op jit(solution)/shard_map/ppermute | solution.py:283
  331.0 31.7 %collective-permute-start.32 = (bf16[2,72,1024]{2,1,0:T(8,128)(2,1)S(1)}, bf16[2,72,1024]{2,1,0:T(8,128)(2,1)}, u32[]{:S(2)}, u32[]{:S(2)}) collective-permute-start(bf16[2,72,1024]{2,1,0:T(8,128)(2,1)S(1)} %collective-permute-done.24), channel_id=1, source_target_pairs={{0,1},{1,0},{2,3},{3,2},{4,5},{5,4},{6,7},{7,6},{8,9},{9,8},{10,11... | collective-permute-start | bytes 884744 | tf_op jit(solution)/shard_map/ppermute | solution.py:295
  332.3 32.3 %collective-permute-start.31 = (bf16[2,72,1024]{2,1,0:T(8,128)(2,1)S(1)}, bf16[2,72,1024]{2,1,0:T(8,128)(2,1)}, u32[]{:S(2)}, u32[]{:S(2)}) collective-permute-start(bf16[2,72,1024]{2,1,0:T(8,128)(2,1)S(1)} %collective-permute-done.23), channel_id=1, source_target_pairs={{0,1},{1,0},{2,3},{3,2},{4,5},{5,4},{6,7},{7,6},{8,9},{9,8},{10,11... | collective-permute-start | bytes 884744 | tf_op jit(solution)/shard_map/ppermute | solution.py:295
  333.1 28.3 %collective-permute-start.34 = (f32[9,1024]{1,0:T(8,128)S(1)}, f32[9,1024]{1,0:T(8,128)S(1)}, u32[]{:S(2)}, u32[]{:S(2)}) collective-permute-start(f32[9,1024]{1,0:T(8,128)S(1)} %add.449), channel_id=1, source_target_pairs={{0,16},{8,24},{16,0},{24,8},{1,17},{9,25},{17,1},{25,9},{2,18},{10... | collective-permute-start | bytes 110600 | tf_op jit(solution)/shard_map/ppermute | solution.py:286
  333.1 39.0 %collective-permute-start.35 = (f16[264,2048]{1,0:T(8,128)(2,1)S(1)}, f16[264,2048]{1,0:T(8,128)(2,1)S(1)}, u32[]{:S(2)}, u32[]{:S(2)}) collective-permute-start(f16[264,2048]{1,0:T(8,128)(2,1)S(1)} %copy-done.19), channel_id=1, source_target_pairs={{0,4},{2,6},{4,0},{6,2},{1,5},{3,7},{5,1},{7,3},{8,12},{10,14},{12... | collective-permute-start | bytes 3244040 | tf_op jit(solution)/shard_map/ppermute | solution.py:292
  334.3 37.7 %collective-permute-start.29 = (f16[264,2048]{1,0:T(8,128)(2,1)S(1)}, f16[264,2048]{1,0:T(8,128)(2,1)S(1)}, u32[]{:S(2)}, u32[]{:S(2)}) collective-permute-start(f16[264,2048]{1,0:T(8,128)(2,1)S(1)} %pad_maximum_fusion.10), channel_id=1, source_target_pairs={{0,8},{8,16},{16,24},{24,0},{1,9},{9,17},{17,25},{25,1},{2,10},{10... | collective-permute-start | bytes 3244040 | tf_op jit(solution)/shard_map/ppermute | solution.py:283
  (42 other events, 409.5 us)

commit v6 on v5

--- a/solution.py
+++ b/solution.py
@@ -156,40 +156,41 @@
 def weight_kernel(
     place_ref, norm_near, norm_far, up_near, up_far, merged_ref, mixed_ref, near_ref, far_ref
 ):
-    step = pl.program_id(0)
+    step = pl.program_id(1)
 
     @pl.when(step < 3)
     def _():
-        near_ref[...] = dot_nn(norm_near[...], merged_ref[...])
-        far_ref[...] = dot_nn(norm_far[...], merged_ref[...])
+        near_ref[0] = dot_nn(norm_near[...], merged_ref[...])
+        far_ref[0] = dot_nn(norm_far[...], merged_ref[...])
 
     @pl.when(step == 3)
     def _():
-        near_ref[...] = dot_nn(up_near[...], mixed_ref[...])
-        far_ref[...] = dot_nn(up_far[...], mixed_ref[...])
+        near_ref[0] = dot_nn(up_near[...], mixed_ref[...])
+        far_ref[0] = dot_nn(up_far[...], mixed_ref[...])
 
 
 def weight_product(places, rows, normed, upstream, merged, mixed):
     tokens, width = mixed.shape
-    near = pl.BlockSpec((rows, tokens), lambda i, at: (at[0], 0))
-    far = pl.BlockSpec((rows, tokens), lambda i, at: (at[1], 0))
-    out = pl.BlockSpec((rows, width), lambda i, at: (0, i))
+    count = places.shape[0] // 2
+    near = pl.BlockSpec((rows, tokens), lambda b, i, at: (at[2 * b], 0))
+    far = pl.BlockSpec((rows, tokens), lambda b, i, at: (at[2 * b + 1], 0))
+    out = pl.BlockSpec((1, rows, width), lambda b, i, at: (b, 0, i))
     return pl.pallas_call(
         weight_kernel,
         grid_spec=pltpu.PrefetchScalarGridSpec(
             num_scalar_prefetch=1,
-            grid=(4,),
+            grid=(count, 4),
             in_specs=[
                 near,
                 far,
                 near,
                 far,
-                pl.BlockSpec((tokens, width), lambda i, at: (0, jnp.minimum(i, 2))),
-                pl.BlockSpec((tokens, width), lambda i, at: (0, 0)),
+                pl.BlockSpec((tokens, width), lambda b, i, at: (0, jnp.minimum(i, 2))),
+                pl.BlockSpec((tokens, width), lambda b, i, at: (0, 0)),
             ],
             out_specs=[out, out],
         ),
-        out_shape=[jax.ShapeDtypeStruct((rows, 4 * width), jnp.float32)] * 2,
+        out_shape=[jax.ShapeDtypeStruct((count, rows, 4 * width), jnp.float32)] * 2,
         compiler_params=pltpu.CompilerParams(vmem_limit_bytes=58 * MIB),
         cost_estimate=pl.CostEstimate(flops=1, bytes_accessed=1, transcendentals=0),
         name="weight_product",
@@ -238,14 +239,19 @@
     )(normed, upstream, weights)
 
 
-def norm_kernel(merged_ref, weight_ref, out_ref):
-    out_ref[...] = dot_nt(merged_ref[...], weight_ref[...])
-
-
-def norm_product(merged, weights):
+def norm_kernel(merged_ref, weight_ref, own_ref, other_ref):
+    frames, pairs, tile = own_ref.shape
+    rows = dot_nt(merged_ref[...], weight_ref[...]).reshape(frames, 2 * pairs, tile)
+    own_ref[...] = rows[:, :pairs]
+    other_ref[...] = rows[:, pairs:]
+
+
+def norm_product(merged, weights, frames):
     rows, depth = merged.shape
     features = weights.shape[0]
     tile = features // 4
+    pairs = rows // frames // 2
+    out = pl.BlockSpec((frames, pairs, tile), lambda i: (0, 0, i))
     return pl.pallas_call(
         norm_kernel,
         grid=(4,),
@@ -253,9 +259,9 @@
             pl.BlockSpec((rows, depth), lambda i: (0, 0)),
             pl.BlockSpec((tile, depth), lambda i: (i, 0)),
         ],
-        out_specs=pl.BlockSpec((rows, tile), lambda i: (0, i)),
-        out_shape=jax.ShapeDtypeStruct((rows, features), jnp.float32),
-        compiler_params=pltpu.CompilerParams(vmem_limit_bytes=18 * MIB),
+        out_specs=[out, out],
+        out_shape=[jax.ShapeDtypeStruct((frames, pairs, features), jnp.float32)] * 2,
+        compiler_params=pltpu.CompilerParams(vmem_limit_bytes=26 * MIB),
         cost_estimate=pl.CostEstimate(flops=1, bytes_accessed=1, transcendentals=0),
         name="norm_product",
     )(merged, weights)
@@ -435,20 +441,16 @@
         scale = jnp.exp2(sent[block_rows : block_rows + 1].astype(jnp.float32))
         return sent[:block_rows].astype(jnp.float32) * scale, scale * WIRE_TOP
 
-    def weight_part(k, earlier):
-        block_at = after((z - 1 - k) % depth * 2, earlier)
-        places = jnp.stack([block_at + y, block_at + 1 - y])
+    def weight_parts_of(steps, earlier):
+        at = after(z, earlier)
+        places = [(at - 1 - k) % depth * 2 + row for k in steps for row in (y, 1 - y)]
         near, far = weight_product(
-            places, block_rows, normed_t, upstream_t, flat_merged, flat_mixed
+            jnp.stack(places), block_rows, normed_t, upstream_t, flat_merged, flat_mixed
         )
-        return near, pack(far, own_bound)
-
-    def norm_part(rows):
-        flat = rows.reshape(frames * pairs, 3 * head_width)
-        return norm_product(flat, weights).reshape(frames, pairs, features)
+        return [(near[i], far[i]) for i in range(len(steps))]
 
     def chip_sum(k, earlier):
-        term, bound = unpack(after(swap_y(weight_parts[k][1]), earlier))
+        term, bound = unpack(after(swap_y(away[k]), earlier))
         return weight_parts[k][0] + term, bound + own_bound
 
     def ring_sum(k, arriving, earlier):
@@ -456,11 +458,12 @@
         term, ring_bound = unpack(arriving)
         return total + term, bound + ring_bound
 
-    weight_parts = [weight_part(0, flat_merged)]
-    norm_away = norm_part(after(merged[:, pairs:], weight_parts[0][1]))
-    weight_parts.append(weight_part(1, norm_away))
-    payload = pack(*chip_sum(0, weight_parts[1][1]))
-    norm_here = norm_part(after(merged[:, :pairs], payload))
+    weight_parts = weight_parts_of([0], flat_merged)
+    away = [pack(weight_parts[0][1], own_bound)]
+    norm_here, norm_away = norm_product(after(flat_merged, away[0]), weights, frames)
+    weight_parts += weight_parts_of(range(1, depth), norm_away)
+    away.append(pack(weight_parts[1][1], own_bound))
+    payload = pack(*chip_sum(0, away[1]))
     partial_norm = norm_here + swap_core(after(norm_away, payload))
     row_dot = jnp.sum(partial_norm * gain * (hidden * inverse), -1, keepdims=True)
     if tensors == 2:
@@ -474,11 +477,11 @@
         row_dot = lax.psum(row_dot, "tensor")
         grad_norm = lax.psum_scatter(partial_norm, "tensor", scatter_dimension=2, tiled=True)
         sent = partial_norm
-    weight_parts.append(weight_part(2, sent))
-    payload = pack(*ring_sum(1, ring(payload, 1), weight_parts[2][1]))
-    weight_parts.append(weight_part(3, payload))
+    away.append(pack(after(weight_parts[2][1], sent), own_bound))
+    payload = pack(*ring_sum(1, ring(payload, 1), away[2]))
+    away.append(pack(after(weight_parts[3][1], payload), own_bound))
     if tensors == 2:
-        x_terms, row_terms = after((x_terms, row_terms), weight_parts[3][1])
+        x_terms, row_terms = after((x_terms, row_terms), away[3])
         row_dot = row_dot + row_terms[..., :1]
         grad_norm = cut_x(partial_norm) + x_terms.astype(jnp.float32) * row_terms[..., 1:]
     unit_rows = (cut_x(own_inputs).astype(jnp.float32) + cut_x(embedded)[:, None, :]) * inverse
@@ -493,6 +496,7 @@
     small = jnp.concatenate([action_term, gain_term[None, :]], 0)
     small = small + swap_core(small)
     small = small + swap_z(small, 1)
+    small = join_x(small + swap_y(small))
     returned = [grad_rows[:local_frames]]
     for k in range(1, depth):
         returned.append(
@@ -502,7 +506,7 @@
     for k in range(2, depth - 1):
         payload = pack(*ring_sum(k, ring(payload, 1), (returned[1:], small)))
         if k + 2 < depth:
-            weight_parts.append(weight_part(k + 2, payload))
+            away.append(pack(after(weight_parts[k + 2][1], payload), own_bound))
     grad_inputs = jnp.zeros(inputs.shape, jnp.bfloat16)
     for k in range(depth):
         piece = after(returned[k], payload)
@@ -513,12 +517,11 @@
     small = after(small, payload)
     bit = 2
     while bit < depth:
-        small = small + swap_z(small, bit)
+        small = small + after(swap_z(small, bit), grad_inputs)
         bit *= 2
     arriving, grad_inputs, small = lax.optimization_barrier(
         (ring(payload, 1), grad_inputs, small)
     )
-    small = join_x(small + swap_y(small))
     total = chip_sum(depth - 1, arriving)[0] + unpack(arriving)[0]
     mine = lax.dynamic_slice_in_dim(total, core * shard_rows, shard_rows, 0)
     other = swap_core(lax.dynamic_slice_in_dim(total, (1 - core) * shard_rows, shard_rows, 0))

time: 390 us -> 395 us (1.013)
  waiting for transfers between devices: 176 us -> 198 us
  other arithmetic: 54.7 us -> 45.6 us
  Pallas kernels: 74.4 us -> 66.1 us
    ppermute x10, waiting for transfers between devices: 27.1 us -> 37.3 us  [swap_x(): return lax.ppermute(value, 'tensor', [(0, 1), (1, 0)])]
    ppermute x9, waiting for transfers between devices: 11.9 us -> 20.8 us  [swap_y(): return lax.ppermute(value, 'space', [(i, i ^ 2) for i in range(spaces)])]
    ppermute x2, waiting for transfers between devices: 33.3 us -> 27.7 us  [swap_z(): return lax.ppermute(value, 'frame', [(i, i ^ bit) for i in range(depth)])]
    pallas_call x4 -> x2, Pallas kernels: 33.9 us -> 29 us  [weight_product(): pl.pallas_call(weight_kernel, grid_spec=pltpu.PrefetchScalarGridSpec(num_...]
    ppermute x12, waiting for transfers between devices: 98.9 us -> 104 us  [ring(): lax.ppermute(value, 'frame', [(i, (i + shift) % depth) for i in range(dep...]
    concatenate x7, other arithmetic: 6.93 us -> 2.91 us  [pack(): jnp.concatenate([value * jnp.exp2(-exponent), jnp.broadcast_to(exponent,...]
    another operation x15 -> x12, other arithmetic: 15.2 us -> 11.5 us
    pallas_call x2 -> x1, Pallas kernels: 14.4 us -> 10.9 us  [norm_product(): pl.pallas_call(norm_kernel, grid=(4,), in_specs=[pl.BlockSpec((rows, dept...]
  transfers between devices with their start and end apart: 39 -> 39, of which waited for: 19 -> 25; matrix products, arithmetic and copies ran while one was open for 16% -> 14% of each run, Pallas kernels for 12% -> 9%
where the time goes in v6:
time: 395 us; the launch traced here: 394 us
  waiting for transfers between devices  198 us (50%)
  Pallas kernels  66.1 us (17%)
  other arithmetic  45.6 us (12%)
  local copies, waits for them, and re-layouts  45.1 us (11%)
  starting transfers between devices  35.1 us (9%)
    ppermute x12, waiting for transfers between devices, ring(): lax.ppermute(value, 'frame', [(i, (i + shift) % depth) for i in range(dep...  104 us
    ppermute x10, waiting for transfers between devices, swap_x(): return lax.ppermute(value, 'tensor', [(0, 1), (1, 0)])  37.3 us
    pallas_call x2, Pallas kernels, weight_product(): pl.pallas_call(weight_kernel, grid_spec=pltpu.PrefetchScalarGridSpec(num_...  29 us
    ppermute x2, waiting for transfers between devices, swap_z(): return lax.ppermute(value, 'frame', [(i, i ^ bit) for i in range(depth)])  27.7 us
    ppermute x9, waiting for transfers between devices, swap_y(): return lax.ppermute(value, 'space', [(i, i ^ 2) for i in range(spaces)])  20.8 us
    pallas_call x1, Pallas kernels, project(): pl.pallas_call(project_kernel, grid=(4, 2), in_specs=[pl.BlockSpec((rows,...  13.6 us
    dynamic_update_slice x7, local copies, waits for them, and re-layouts, settle(): return lax.dynamic_update_slice(weights, arrived, (start, 0))  12.6 us
    ppermute x12, starting transfers between devices, ring(): lax.ppermute(value, 'frame', [(i, (i + shift) % depth) for i in range(dep...  12 us
  transfers between devices with their start and end apart: 39, of which 25 were waited for; matrix products, arithmetic and copies ran while one was open for 14% of the time, Pallas kernels for 9%

profile of v6, /device:TPU:0, one launch (start us, length us, event | category | flops | bytes accessed | tf_op | source)
XLA Modules:
  0.0 393.6 jit_solution(14009902059708373590)
XLA Ops:
  17.7 11.1 %collective-permute-done.3 = bf16[296,1024]{1,0:T(8,128)(2,1)} collective-permute-done((bf16[296,1024]{1,0:T(8,128)(2,1)}, bf16[296,1024]{1,0:T(8,128)(2,1)}, u32[]{:S(2)}, u32[]{:S(2)}) %collective-permute-start.3) | collective-permute-done | bytes 606240 | tf_op jit(solution)/shard_map/ppermute | solution.py:289
  32.5 4.4 %broadcast_in_dim.62 = bf16[2048,2048]{1,0:T(8,128)(2,1)} broadcast(bf16[]{:T(256)} %constant.287.clone.1), dimensions={} | broadcast | bytes 8388610 | tf_op jit(solution)/shard_map/broadcast_in_dim | solution.py:363
  38.0 38.7 %collective-permute-done.2 = bf16[296,1024]{1,0:T(8,128)(2,1)} collective-permute-done((bf16[296,1024]{1,0:T(8,128)(2,1)S(1)}, bf16[296,1024]{1,0:T(8,128)(2,1)}, u32[]{:S(2)}, u32[]{:S(2)}) %collective-permute-start.2) | collective-permute-done | bytes 606240 | tf_op jit(solution)/shard_map/ppermute | solution.py:289
  80.9 3.8 collective-permute-start.7
  93.0 6.7 %collective-permute-done.9 = bf16[296,1024]{1,0:T(8,128)(2,1)S(1)} collective-permute-done((bf16[296,1024]{1,0:T(8,128)(2,1)}, bf16[296,1024]{1,0:T(8,128)(2,1)S(1)}, u32[]{:S(2)}, u32[]{:S(2)}) %collective-permute-start.9) | collective-permute-done | bytes 606240 | tf_op jit(solution)/shard_map/ppermute | solution.py:301
  101.0 17.8 %collective-permute-done.7 = bf16[296,1024]{1,0:T(8,128)(2,1)S(1)} collective-permute-done((bf16[296,1024]{1,0:T(8,128)(2,1)S(1)}, bf16[296,1024]{1,0:T(8,128)(2,1)S(1)}, u32[]{:S(2)}, u32[]{:S(2)}) %collective-permute-start.7) | collective-permute-done | bytes 606240 | tf_op jit(solution)/shard_map/ppermute | solution.py:289
  123.5 10.3 %collective-permute-done.11 = bf16[296,1024]{1,0:T(8,128)(2,1)S(1)} collective-permute-done((bf16[296,1024]{1,0:T(8,128)(2,1)S(1)}, bf16[296,1024]{1,0:T(8,128)(2,1)S(1)}, u32[]{:S(2)}, u32[]{:S(2)}) %collective-permute-start.11) | collective-permute-done | bytes 606240 | tf_op jit(solution)/shard_map/ppermute | solution.py:301
  138.7 7.9 %collective-permute-done.10 = bf16[256,2048]{1,0:T(8,128)(2,1)} collective-permute-done((bf16[256,2048]{1,0:T(8,128)(2,1)S(1)}, bf16[256,2048]{1,0:T(8,128)(2,1)}, u32[]{:S(2)}, u32[]{:S(2)}) %collective-permute-start.10) | collective-permute-done | bytes 1048608 | tf_op jit(solution)/shard_map/ppermute | solution.py:289
  168.8 5.5 %collective-permute-done.15 = bf16[256,2048]{1,0:T(8,128)(2,1)S(1)} collective-permute-done((bf16[256,2048]{1,0:T(8,128)(2,1)}, bf16[256,2048]{1,0:T(8,128)(2,1)S(1)}, u32[]{:S(2)}, u32[]{:S(2)}) %collective-permute-start.15) | collective-permute-done | bytes 1048608 | tf_op jit(solution)/shard_map/ppermute | solution.py:298
  175.4 13.6 %project.1 = (bf16[1152,1536]{1,0:T(8,128)(2,1)S(1)}, bf16[1152,512]{1,0:T(8,128)(2,1)S(1)}) custom-call(bf16[1152,2048]{1,0:T(8,128)(2,1)S(1)} %bitcast.147, bf16[1152,2048]{1,0:T(8,128)(2,1)S(1)} %bitcast.145, bf16[2048,2048]{1,0:T(8,128)(2,1)} %constant_dynamic-update-slice_fusion.weight_ref), custom_call_target="tpu_custom_call" | custom-call | flops 9663676416 | bytes 18874368 | tf_op jit(solution)/shard_map/project/pallas_call | solution.py:214
  189.0 7.8 %temporal_attention.1 = (bf16[8,144,512]{2,1,0:T(8,128)(2,1)S(1)}, bf16[8,144,1536]{2,1,0:T(8,128)(2,1)S(1)}, f32[2,8,128]{2,1,0:T(8,128)S(1)}) custom-call(f32[128,1]{1,0:T(8,128)S(1)} %broadcast_in_dim_reshape.9.late_ref, f32[1,128]{1,0:T(1,128)S(1)} %broadcast_in_dim_reshape.8.early_ref, bf16[8,144,1536]{2,1,0:T(8,128)(2,1)S(1)} %bitcast.152, ...), custom_call_target="tpu_custom_call" | custom-call | flops 1207959552 | bytes 9437184 | tf_op jit(solution)/shard_map/temporal_attention/pallas_call | solution.py:108
  202.2 8.4 %weight_product.2 = (f32[1,256,2048]{2,1,0:T(8,128)}, f32[1,256,2048]{2,1,0:T(8,128)}) custom-call(s32[2]{0:T(128)} %pad_add_fusion.1.place_ref, bf16[2048,1152]{1,0:T(8,128)(2,1)} %copy-done.3, bf16[2048,1152]{1,0:T(8,128)(2,1)} %copy-done.3, bf16[2048,1152]{1,0:T(8,128)(2,1)} %copy-done.2, bf16[2048,1152]{1,0:T(8,128)(2,1)} %copy-done.2, ...), custom_call_target="tpu_custom_call" | custom-call | flops 1 | bytes 1 | tf_op jit(solution)/shard_map/weight_product/pallas_call | solution.py:178
  213.2 10.9 %norm_product.1 = (f32[8,72,2048]{2,1,0:T(8,128)S(1)}, f32[8,72,2048]{2,1,0:T(8,128)}) custom-call(bf16[1152,1536]{1,0:T(8,128)(2,1)S(1)} %bitcast.143, bf16[2048,2048]{1,0:T(8,128)(2,1)} %constant_dynamic-update-slice_fusion.weight_ref), custom_call_target="tpu_custom_call" | custom-call | flops 1 | bytes 1 | tf_op jit(solution)/shard_map/norm_product/pallas_call | solution.py:255
  227.0 20.6 %weight_product.3 = (f32[3,256,2048]{2,1,0:T(8,128)}, f32[3,256,2048]{2,1,0:T(8,128)}) custom-call(s32[6]{0:T(128)} %stack.51.place_ref, bf16[2048,1152]{1,0:T(8,128)(2,1)} %copy-done.3, bf16[2048,1152]{1,0:T(8,128)(2,1)} %copy-done.3, bf16[2048,1152]{1,0:T(8,128)(2,1)} %copy-done.2, bf16[2048,1152]{1,0:T(8,128)(2,1)} %copy-done.2, ...), custom_call_target="tpu_custom_call" | custom-call | flops 1 | bytes 1 | tf_op jit(solution)/shard_map/weight_product/pallas_call | solution.py:178
  262.0 4.1 %multiply_reduce_fusion = (f32[8,72]{1,0:T(8,128)S(1)}, f32[8,72]{1,0:T(8,128)S(1)}, f32[8,72,2048]{2,1,0:T(8,128)S(1)}) fusion(bf16[8,72,2048]{2,1,0:T(8,128)(2,1)S(1)} %copy-done.9, f32[2048]{0:T(1024)S(1)} %copy-done.16, f32[8,72]{1,0:T(8,128)S(1)} %add_rsqrt_fusion, f32[8,2048]{1,0:T(8,128)S(1)} %fusion.33, f32[8,72,2048]{2,1,0:T(8,128)S(1)} %bitcast.151, ...), kind=kLoop, calls=%fused_computation.2 | loop fusion | flops 10615680 | bytes 16595712 | tf_op jit(solution)/shard_map/reduce_sum | solution.py:468
  269.4 11.1 %collective-permute-done.21 = f16[264,2048]{1,0:T(8,128)(2,1)S(1)} collective-permute-done((f16[264,2048]{1,0:T(8,128)(2,1)S(1)}, f16[264,2048]{1,0:T(8,128)(2,1)S(1)}, u32[]{:S(2)}, u32[]{:S(2)}) %collective-permute-start.21) | collective-permute-done | bytes 1081376 | tf_op jit(solution)/shard_map/ppermute | solution.py:298
  280.5 6.4 %collective-permute-done.22 = f16[264,2048]{1,0:T(8,128)(2,1)} collective-permute-done((f16[264,2048]{1,0:T(8,128)(2,1)S(1)}, f16[264,2048]{1,0:T(8,128)(2,1)}, u32[]{:S(2)}, u32[]{:S(2)}) %collective-permute-start.22) | collective-permute-done | bytes 1081376 | tf_op jit(solution)/shard_map/ppermute | solution.py:289
  298.5 20.8 %collective-permute-done.27 = f32[9,1024]{1,0:T(8,128)S(1)} collective-permute-done((f32[9,1024]{1,0:T(8,128)S(1)}, f32[9,1024]{1,0:T(8,128)S(1)}, u32[]{:S(2)}, u32[]{:S(2)}) %collective-permute-start.27) | collective-permute-done | bytes 36896 | tf_op jit(solution)/shard_map/ppermute | solution.py:292
  319.4 4.3 %collective-permute-done.28 = f32[9,1024]{1,0:T(8,128)S(1)} collective-permute-done((f32[9,1024]{1,0:T(8,128)S(1)}, f32[9,1024]{1,0:T(8,128)S(1)}, u32[]{:S(2)}, u32[]{:S(2)}) %collective-permute-start.28) | collective-permute-done | bytes 36896 | tf_op jit(solution)/shard_map/ppermute | solution.py:298
  328.0 4.9 %collective-permute-done.23 = bf16[2,72,1024]{2,1,0:T(8,128)(2,1)S(1)} collective-permute-done((bf16[2,72,1024]{2,1,0:T(8,128)(2,1)S(1)}, bf16[2,72,1024]{2,1,0:T(8,128)(2,1)S(1)}, u32[]{:S(2)}, u32[]{:S(2)}) %collective-permute-start.23) | collective-permute-done | bytes 294944 | tf_op jit(solution)/shard_map/ppermute | solution.py:289
  332.9 16.8 %collective-permute-done.24 = bf16[2,72,1024]{2,1,0:T(8,128)(2,1)S(1)} collective-permute-done((bf16[2,72,1024]{2,1,0:T(8,128)(2,1)S(1)}, bf16[2,72,1024]{2,1,0:T(8,128)(2,1)S(1)}, u32[]{:S(2)}, u32[]{:S(2)}) %collective-permute-start.24) | collective-permute-done | bytes 294944 | tf_op jit(solution)/shard_map/ppermute | solution.py:289
  357.6 5.0 %collective-permute-done.34 = bf16[2,72,1024]{2,1,0:T(8,128)(2,1)} collective-permute-done((bf16[2,72,1024]{2,1,0:T(8,128)(2,1)S(1)}, bf16[2,72,1024]{2,1,0:T(8,128)(2,1)}, u32[]{:S(2)}, u32[]{:S(2)}) %collective-permute-start.34) | collective-permute-done | bytes 294944 | tf_op jit(solution)/shard_map/ppermute | solution.py:301
  365.0 3.9 collective-permute-done.33
  378.0 6.9 %collective-permute-done.36 = f32[9,2048]{1,0:T(8,128)S(1)} collective-permute-done((f32[9,2048]{1,0:T(8,128)S(1)}, f32[9,2048]{1,0:T(8,128)S(1)}, u32[]{:S(2)}, u32[]{:S(2)}) %collective-permute-start.36) | collective-permute-done | bytes 73760 | tf_op jit(solution)/shard_map/ppermute | solution.py:292
  (231 shorter events, 138.5 us)
Async XLA Ops:
  9.0 19.8 %collective-permute-start.3 = (bf16[296,1024]{1,0:T(8,128)(2,1)}, bf16[296,1024]{1,0:T(8,128)(2,1)}, u32[]{:S(2)}, u32[]{:S(2)}) collective-permute-start(bf16[296,1024]{1,0:T(8,128)(2,1)} %pad_maximum_fusion.13), channel_id=1, source_target_pairs={{0,8},{8,16},{16,24},{24,0},{1,9},{9,17},{17,25},{25,1},{2,10},{10... | collective-permute-start | bytes 1818632 | tf_op jit(solution)/shard_map/ppermute | solution.py:289
  13.0 63.7 %collective-permute-start.1 = (bf16[256,2048]{1,0:T(8,128)(2,1)}, bf16[256,2048]{1,0:T(8,128)(2,1)}, u32[]{:S(2)}, u32[]{:S(2)}) collective-permute-start(bf16[256,2048]{1,0:T(8,128)(2,1)} %pad_maximum_fusion.11), channel_id=1, source_target_pairs={{0,8},{8,16},{16,24},{24,0},{1,9},{9,17},{17,25},{25,1},{2,10},{10... | collective-permute-start | bytes 3145736 | tf_op jit(solution)/shard_map/ppermute | solution.py:289
  14.7 62.0 %collective-permute-start.4 = (bf16[256,2048]{1,0:T(8,128)(2,1)}, bf16[256,2048]{1,0:T(8,128)(2,1)}, u32[]{:S(2)}, u32[]{:S(2)}) collective-permute-start(bf16[256,2048]{1,0:T(8,128)(2,1)} %pad_maximum_fusion.11), channel_id=1, source_target_pairs={{0,4},{2,6},{4,0},{6,2},{1,5},{3,7},{5,1},{7,3},{8,12},{10,14},{12... | collective-permute-start | bytes 3145736 | tf_op jit(solution)/shard_map/ppermute | solution.py:298
  16.4 60.3 %collective-permute-start.2 = (bf16[296,1024]{1,0:T(8,128)(2,1)S(1)}, bf16[296,1024]{1,0:T(8,128)(2,1)}, u32[]{:S(2)}, u32[]{:S(2)}) collective-permute-start(bf16[296,1024]{1,0:T(8,128)(2,1)S(1)} %pad_maximum_fusion.12), channel_id=1, source_target_pairs={{0,16},{8,24},{16,0},{24,8},{1,17},{9,25},{17,1},{25,9},{2,18},{10... | collective-permute-start | bytes 1818632 | tf_op jit(solution)/shard_map/ppermute | solution.py:289
  28.8 47.9 %collective-permute-start.5 = (bf16[296,1024]{1,0:T(8,128)(2,1)}, bf16[296,1024]{1,0:T(8,128)(2,1)}, u32[]{:S(2)}, u32[]{:S(2)}) collective-permute-start(bf16[296,1024]{1,0:T(8,128)(2,1)} %collective-permute-done.3), channel_id=1, source_target_pairs={{0,1},{1,0},{2,3},{3,2},{4,5},{5,4},{6,7},{7,6},{8,9},{9,8},{10,11... | collective-permute-start | bytes 1818632 | tf_op jit(solution)/shard_map/ppermute | solution.py:301
  79.0 39.7 %collective-permute-start.6 = (bf16[256,2048]{1,0:T(8,128)(2,1)}, bf16[256,2048]{1,0:T(8,128)(2,1)S(1)}, u32[]{:S(2)}, u32[]{:S(2)}) collective-permute-start(bf16[256,2048]{1,0:T(8,128)(2,1)} %collective-permute-done.1), channel_id=1, source_target_pairs={{0,8},{8,16},{16,24},{24,0},{1,9},{9,17},{17,25},{25,1},{2,10},{10... | collective-permute-start | bytes 3145736 | tf_op jit(solution)/shard_map/ppermute | solution.py:289
  79.1 39.7 %collective-permute-start.8 = (bf16[256,2048]{1,0:T(8,128)(2,1)}, bf16[256,2048]{1,0:T(8,128)(2,1)S(1)}, u32[]{:S(2)}, u32[]{:S(2)}) collective-permute-start(bf16[256,2048]{1,0:T(8,128)(2,1)} %collective-permute-done.1), channel_id=1, source_target_pairs={{0,4},{2,6},{4,0},{6,2},{1,5},{3,7},{5,1},{7,3},{8,12},{10,14},{12... | collective-permute-start | bytes 3145736 | tf_op jit(solution)/shard_map/ppermute | solution.py:298
  80.9 37.8 %collective-permute-start.7 = (bf16[296,1024]{1,0:T(8,128)(2,1)S(1)}, bf16[296,1024]{1,0:T(8,128)(2,1)S(1)}, u32[]{:S(2)}, u32[]{:S(2)}) collective-permute-start(bf16[296,1024]{1,0:T(8,128)(2,1)S(1)} %pad_maximum_fusion.14), channel_id=1, source_target_pairs={{0,24},{8,0},{16,8},{24,16},{1,25},{9,1},{17,9},{25,17},{2,26},{10... | collective-permute-start | bytes 1818632 | tf_op jit(solution)/shard_map/ppermute | solution.py:289
  118.8 15.1 %collective-permute-start.11 = (bf16[296,1024]{1,0:T(8,128)(2,1)S(1)}, bf16[296,1024]{1,0:T(8,128)(2,1)S(1)}, u32[]{:S(2)}, u32[]{:S(2)}) collective-permute-start(bf16[296,1024]{1,0:T(8,128)(2,1)S(1)} %collective-permute-done.7), channel_id=1, source_target_pairs={{0,1},{1,0},{2,3},{3,2},{4,5},{5,4},{6,7},{7,6},{8,9},{9,8},{10,11... | collective-permute-start | bytes 1818632 | tf_op jit(solution)/shard_map/ppermute | solution.py:301
  120.3 26.2 %collective-permute-start.10 = (bf16[256,2048]{1,0:T(8,128)(2,1)S(1)}, bf16[256,2048]{1,0:T(8,128)(2,1)}, u32[]{:S(2)}, u32[]{:S(2)}) collective-permute-start(bf16[256,2048]{1,0:T(8,128)(2,1)S(1)} %collective-permute-done.6), channel_id=1, source_target_pairs={{0,8},{8,16},{16,24},{24,0},{1,9},{9,17},{17,25},{25,1},{2,10},{10... | collective-permute-start | bytes 3145736 | tf_op jit(solution)/shard_map/ppermute | solution.py:289
  120.4 26.2 %collective-permute-start.12 = (bf16[256,2048]{1,0:T(8,128)(2,1)S(1)}, bf16[256,2048]{1,0:T(8,128)(2,1)}, u32[]{:S(2)}, u32[]{:S(2)}) collective-permute-start(bf16[256,2048]{1,0:T(8,128)(2,1)S(1)} %collective-permute-done.6), channel_id=1, source_target_pairs={{0,4},{2,6},{4,0},{6,2},{1,5},{3,7},{5,1},{7,3},{8,12},{10,14},{12... | collective-permute-start | bytes 3145736 | tf_op jit(solution)/shard_map/ppermute | solution.py:298
  149.0 25.3 %collective-permute-start.15 = (bf16[256,2048]{1,0:T(8,128)(2,1)}, bf16[256,2048]{1,0:T(8,128)(2,1)S(1)}, u32[]{:S(2)}, u32[]{:S(2)}) collective-permute-start(bf16[256,2048]{1,0:T(8,128)(2,1)} %collective-permute-done.10), channel_id=1, source_target_pairs={{0,4},{2,6},{4,0},{6,2},{1,5},{3,7},{5,1},{7,3},{8,12},{10,14},{12... | collective-permute-start | bytes 3145736 | tf_op jit(solution)/shard_map/ppermute | solution.py:298
  212.9 37.0 %collective-permute-start.16 = (f16[264,2048]{1,0:T(8,128)(2,1)S(1)}, f16[264,2048]{1,0:T(8,128)(2,1)}, u32[]{:S(2)}, u32[]{:S(2)}) collective-permute-start(f16[264,2048]{1,0:T(8,128)(2,1)S(1)} %pad_maximum_fusion.7), channel_id=1, source_target_pairs={{0,4},{2,6},{4,0},{6,2},{1,5},{3,7},{5,1},{7,3},{8,12},{10,14},{12... | collective-permute-start | bytes 3244040 | tf_op jit(solution)/shard_map/ppermute | solution.py:298
  253.8 26.7 %collective-permute-start.21 = (f16[264,2048]{1,0:T(8,128)(2,1)S(1)}, f16[264,2048]{1,0:T(8,128)(2,1)S(1)}, u32[]{:S(2)}, u32[]{:S(2)}) collective-permute-start(f16[264,2048]{1,0:T(8,128)(2,1)S(1)} %pad_maximum_fusion.6), channel_id=1, source_target_pairs={{0,4},{2,6},{4,0},{6,2},{1,5},{3,7},{5,1},{7,3},{8,12},{10,14},{12... | collective-permute-start | bytes 3244040 | tf_op jit(solution)/shard_map/ppermute | solution.py:298
  258.5 28.4 %collective-permute-start.22 = (f16[264,2048]{1,0:T(8,128)(2,1)S(1)}, f16[264,2048]{1,0:T(8,128)(2,1)}, u32[]{:S(2)}, u32[]{:S(2)}) collective-permute-start(f16[264,2048]{1,0:T(8,128)(2,1)S(1)} %copy-done.14), channel_id=1, source_target_pairs={{0,8},{8,16},{16,24},{24,0},{1,9},{9,17},{17,25},{25,1},{2,10},{10... | collective-permute-start | bytes 3244040 | tf_op jit(solution)/shard_map/ppermute | solution.py:289
  266.5 28.2 %collective-permute-start.19 = (f16[8,72,1024]{2,1,0:T(8,128)(2,1)S(1)}, f16[8,72,1024]{2,1,0:T(8,128)(2,1)S(1)}, u32[]{:S(2)}, u32[]{:S(2)}) collective-permute-start(f16[8,72,1024]{2,1,0:T(8,128)(2,1)S(1)} %divide_convert_fusion), channel_id=1, source_target_pairs={{0,1},{1,0},{2,3},{3,2},{4,5},{5,4},{6,7},{7,6},{8,9},{9,8},{10,11... | collective-permute-start | bytes 3538952 | tf_op jit(solution)/shard_map/ppermute | solution.py:301
  267.6 60.4 %collective-permute-start.18 = (f16[264,2048]{1,0:T(8,128)(2,1)S(1)}, f16[264,2048]{1,0:T(8,128)(2,1)S(1)}, u32[]{:S(2)}, u32[]{:S(2)}) collective-permute-start(f16[264,2048]{1,0:T(8,128)(2,1)S(1)} %pad_maximum_fusion.5), channel_id=1, source_target_pairs={{0,4},{2,6},{4,0},{6,2},{1,5},{3,7},{5,1},{7,3},{8,12},{10,14},{12... | collective-permute-start | bytes 3244040 | tf_op jit(solution)/shard_map/ppermute | solution.py:298
  290.6 59.2 %collective-permute-start.30 = (f16[264,2048]{1,0:T(8,128)(2,1)S(1)}, f16[264,2048]{1,0:T(8,128)(2,1)S(1)}, u32[]{:S(2)}, u32[]{:S(2)}) collective-permute-start(f16[264,2048]{1,0:T(8,128)(2,1)S(1)} %pad_maximum_fusion.9), channel_id=1, source_target_pairs={{0,8},{8,16},{16,24},{24,0},{1,9},{9,17},{17,25},{25,1},{2,10},{10... | collective-permute-start | bytes 3244040 | tf_op jit(solution)/shard_map/ppermute | solution.py:289
  298.0 21.3 %collective-permute-start.27 = (f32[9,1024]{1,0:T(8,128)S(1)}, f32[9,1024]{1,0:T(8,128)S(1)}, u32[]{:S(2)}, u32[]{:S(2)}) collective-permute-start(f32[9,1024]{1,0:T(8,128)S(1)} %fusion.34), channel_id=1, source_target_pairs={{0,8},{8,0},{16,24},{24,16},{1,9},{9,1},{17,25},{25,17},{2,10},{10... | collective-permute-start | bytes 110600 | tf_op jit(solution)/shard_map/ppermute | solution.py:292
  324.4 25.3 %collective-permute-start.24 = (bf16[2,72,1024]{2,1,0:T(8,128)(2,1)S(1)}, bf16[2,72,1024]{2,1,0:T(8,128)(2,1)S(1)}, u32[]{:S(2)}, u32[]{:S(2)}) collective-permute-start(bf16[2,72,1024]{2,1,0:T(8,128)(2,1)S(1)} %get-tuple-element.130), channel_id=1, source_target_pairs={{0,16},{8,24},{16,0},{24,8},{1,17},{9,25},{17,1},{25,9},{2,18},{10... | collective-permute-start | bytes 884744 | tf_op jit(solution)/shard_map/ppermute | solution.py:289
  328.0 21.8 %collective-permute-start.25 = (bf16[2,72,1024]{2,1,0:T(8,128)(2,1)S(1)}, bf16[2,72,1024]{2,1,0:T(8,128)(2,1)S(1)}, u32[]{:S(2)}, u32[]{:S(2)}) collective-permute-start(bf16[2,72,1024]{2,1,0:T(8,128)(2,1)S(1)} %get-tuple-element.129), channel_id=1, source_target_pairs={{0,8},{8,16},{16,24},{24,0},{1,9},{9,17},{17,25},{25,1},{2,10},{10... | collective-permute-start | bytes 884744 | tf_op jit(solution)/shard_map/ppermute | solution.py:289
  354.5 30.5 %collective-permute-start.37 = (f16[264,2048]{1,0:T(8,128)(2,1)S(1)}, f16[264,2048]{1,0:T(8,128)(2,1)S(1)}, u32[]{:S(2)}, u32[]{:S(2)}) collective-permute-start(f16[264,2048]{1,0:T(8,128)(2,1)S(1)} %pad_maximum_fusion.4), channel_id=1, source_target_pairs={{0,4},{2,6},{4,0},{6,2},{1,5},{3,7},{5,1},{7,3},{8,12},{10,14},{12... | collective-permute-start | bytes 3244040 | tf_op jit(solution)/shard_map/ppermute | solution.py:298
  354.8 30.2 %collective-permute-start.31 = (f16[264,2048]{1,0:T(8,128)(2,1)S(1)}, f16[264,2048]{1,0:T(8,128)(2,1)S(1)}, u32[]{:S(2)}, u32[]{:S(2)}) collective-permute-start(f16[264,2048]{1,0:T(8,128)(2,1)S(1)} %pad_maximum_fusion.10), channel_id=1, source_target_pairs={{0,8},{8,16},{16,24},{24,0},{1,9},{9,17},{17,25},{25,1},{2,10},{10... | collective-permute-start | bytes 3244040 | tf_op jit(solution)/shard_map/ppermute | solution.py:289
  355.7 29.3 %collective-permute-start.36 = (f32[9,2048]{1,0:T(8,128)S(1)}, f32[9,2048]{1,0:T(8,128)S(1)}, u32[]{:S(2)}, u32[]{:S(2)}) collective-permute-start(f32[9,2048]{1,0:T(8,128)S(1)} %pad_maximum_fusion.23), channel_id=1, source_target_pairs={{0,16},{8,24},{16,0},{24,8},{1,17},{9,25},{17,1},{25,9},{2,18},{10... | collective-permute-start | bytes 221192 | tf_op jit(solution)/shard_map/ppermute | solution.py:292
  (37 other events, 338.0 us)

commit v7 on v6

--- a/solution.py
+++ b/solution.py
@@ -153,48 +153,34 @@
     )(rows)
 
 
-def weight_kernel(
-    place_ref, norm_near, norm_far, up_near, up_far, merged_ref, mixed_ref, near_ref, far_ref
-):
-    step = pl.program_id(1)
-
-    @pl.when(step < 3)
+def weight_kernel(normed_ref, up_ref, merged_ref, mixed_ref, out_ref):
+    @pl.when(pl.program_id(1) < 3)
     def _():
-        near_ref[0] = dot_nn(norm_near[...], merged_ref[...])
-        far_ref[0] = dot_nn(norm_far[...], merged_ref[...])
-
-    @pl.when(step == 3)
+        out_ref[...] = dot_nn(normed_ref[...], merged_ref[...])
+
+    @pl.when(pl.program_id(1) == 3)
     def _():
-        near_ref[0] = dot_nn(up_near[...], mixed_ref[...])
-        far_ref[0] = dot_nn(up_far[...], mixed_ref[...])
-
-
-def weight_product(places, rows, normed, upstream, merged, mixed):
+        out_ref[...] = dot_nn(up_ref[...], mixed_ref[...])
+
+
+def weight_product(normed, upstream, merged, mixed):
     tokens, width = mixed.shape
-    count = places.shape[0] // 2
-    near = pl.BlockSpec((rows, tokens), lambda b, i, at: (at[2 * b], 0))
-    far = pl.BlockSpec((rows, tokens), lambda b, i, at: (at[2 * b + 1], 0))
-    out = pl.BlockSpec((1, rows, width), lambda b, i, at: (b, 0, i))
+    rows = normed.shape[0] // 2
     return pl.pallas_call(
         weight_kernel,
-        grid_spec=pltpu.PrefetchScalarGridSpec(
-            num_scalar_prefetch=1,
-            grid=(count, 4),
-            in_specs=[
-                near,
-                far,
-                near,
-                far,
-                pl.BlockSpec((tokens, width), lambda b, i, at: (0, jnp.minimum(i, 2))),
-                pl.BlockSpec((tokens, width), lambda b, i, at: (0, 0)),
-            ],
-            out_specs=[out, out],
-        ),
-        out_shape=[jax.ShapeDtypeStruct((count, rows, 4 * width), jnp.float32)] * 2,
+        grid=(2, 4),
+        in_specs=[
+            pl.BlockSpec((rows, tokens), lambda i, j: (i, 0)),
+            pl.BlockSpec((rows, tokens), lambda i, j: (i, 0)),
+            pl.BlockSpec((tokens, width), lambda i, j: (0, jnp.minimum(j, 2))),
+            pl.BlockSpec((tokens, width), lambda i, j: (0, 0)),
+        ],
+        out_specs=pl.BlockSpec((rows, width), lambda i, j: (i, j)),
+        out_shape=jax.ShapeDtypeStruct((2 * rows, 4 * width), jnp.float32),
         compiler_params=pltpu.CompilerParams(vmem_limit_bytes=58 * MIB),
         cost_estimate=pl.CostEstimate(flops=1, bytes_accessed=1, transcendentals=0),
         name="weight_product",
-    )(places, normed, normed, upstream, upstream, merged, mixed)
+    )(normed, upstream, merged, mixed)
 
 
 def project_kernel(normed_ref, up_ref, weight_ref, qkv_ref, grad_ref):
@@ -441,28 +427,24 @@
         scale = jnp.exp2(sent[block_rows : block_rows + 1].astype(jnp.float32))
         return sent[:block_rows].astype(jnp.float32) * scale, scale * WIRE_TOP
 
-    def weight_parts_of(steps, earlier):
-        at = after(z, earlier)
-        places = [(at - 1 - k) % depth * 2 + row for k in steps for row in (y, 1 - y)]
-        near, far = weight_product(
-            jnp.stack(places), block_rows, normed_t, upstream_t, flat_merged, flat_mixed
-        )
-        return [(near[i], far[i]) for i in range(len(steps))]
+    weight_terms = weight_product(normed_t, upstream_t, flat_merged, flat_mixed)
+
+    def weight_part(k, row):
+        start = ((z - 1 - k) % depth * 2 + row) * block_rows
+        return lax.dynamic_slice_in_dim(weight_terms, start, block_rows, 0)
 
     def chip_sum(k, earlier):
         term, bound = unpack(after(swap_y(away[k]), earlier))
-        return weight_parts[k][0] + term, bound + own_bound
+        return weight_part(k, y) + term, bound + own_bound
 
     def ring_sum(k, arriving, earlier):
         total, bound = chip_sum(k, earlier)
         term, ring_bound = unpack(arriving)
         return total + term, bound + ring_bound
 
-    weight_parts = weight_parts_of([0], flat_merged)
-    away = [pack(weight_parts[0][1], own_bound)]
+    away = [pack(weight_part(0, 1 - y), own_bound)]
     norm_here, norm_away = norm_product(after(flat_merged, away[0]), weights, frames)
-    weight_parts += weight_parts_of(range(1, depth), norm_away)
-    away.append(pack(weight_parts[1][1], own_bound))
+    away.append(pack(after(weight_part(1, 1 - y), norm_away), own_bound))
     payload = pack(*chip_sum(0, away[1]))
     partial_norm = norm_here + swap_core(after(norm_away, payload))
     row_dot = jnp.sum(partial_norm * gain * (hidden * inverse), -1, keepdims=True)
@@ -477,9 +459,9 @@
         row_dot = lax.psum(row_dot, "tensor")
         grad_norm = lax.psum_scatter(partial_norm, "tensor", scatter_dimension=2, tiled=True)
         sent = partial_norm
-    away.append(pack(after(weight_parts[2][1], sent), own_bound))
+    away.append(pack(after(weight_part(2, 1 - y), sent), own_bound))
     payload = pack(*ring_sum(1, ring(payload, 1), away[2]))
-    away.append(pack(after(weight_parts[3][1], payload), own_bound))
+    away.append(pack(after(weight_part(3, 1 - y), payload), own_bound))
     if tensors == 2:
         x_terms, row_terms = after((x_terms, row_terms), away[3])
         row_dot = row_dot + row_terms[..., :1]
@@ -494,19 +476,19 @@
         onehot.T, jnp.sum(grad_hidden, 1), precision=lax.Precision.HIGHEST
     )
     small = jnp.concatenate([action_term, gain_term[None, :]], 0)
-    small = small + swap_core(small)
-    small = small + swap_z(small, 1)
-    small = join_x(small + swap_y(small))
     returned = [grad_rows[:local_frames]]
     for k in range(1, depth):
         returned.append(
             ring(grad_rows[k * local_frames : (k + 1) * local_frames], depth - k)
         )
 
+    small = after(small, returned[1])
+    small = small + swap_core(small)
+    small = join_x(small + swap_y(small))
     for k in range(2, depth - 1):
         payload = pack(*ring_sum(k, ring(payload, 1), (returned[1:], small)))
         if k + 2 < depth:
-            away.append(pack(after(weight_parts[k + 2][1], payload), own_bound))
+            away.append(pack(after(weight_part(k + 2, 1 - y), payload), own_bound))
     grad_inputs = jnp.zeros(inputs.shape, jnp.bfloat16)
     for k in range(depth):
         piece = after(returned[k], payload)
@@ -514,14 +496,14 @@
         grad_inputs = lax.dynamic_update_slice(
             grad_inputs, join_x(piece)[None], (target, 0, first, 0)
         )
-    small = after(small, payload)
+    small = small + after(swap_z(small, 1), grad_inputs)
+    arriving, grad_inputs, small = lax.optimization_barrier(
+        (ring(payload, 1), grad_inputs, small)
+    )
     bit = 2
     while bit < depth:
-        small = small + after(swap_z(small, bit), grad_inputs)
+        small = small + swap_z(small, bit)
         bit *= 2
-    arriving, grad_inputs, small = lax.optimization_barrier(
-        (ring(payload, 1), grad_inputs, small)
-    )
     total = chip_sum(depth - 1, arriving)[0] + unpack(arriving)[0]
     mine = lax.dynamic_slice_in_dim(total, core * shard_rows, shard_rows, 0)
     other = swap_core(lax.dynamic_slice_in_dim(total, (1 - core) * shard_rows, shard_rows, 0))

time: 395 us -> 407 us (1.030)
  waiting for transfers between devices: 198 us -> 211 us
  other arithmetic: 45.6 us -> 55 us
  Pallas kernels: 66.1 us -> 57.7 us
    ppermute x2, waiting for transfers between devices: 27.7 us -> 11.8 us  [swap_z(): return lax.ppermute(value, 'frame', [(i, i ^ bit) for i in range(depth)])]
    ppermute x12, waiting for transfers between devices: 104 us -> 115 us  [ring(): lax.ppermute(value, 'frame', [(i, (i + shift) % depth) for i in range(dep...]
    dynamic_slice x0 -> x2, other arithmetic: none -> 8.9 us  [weight_part(): return lax.dynamic_slice_in_dim(weight_terms, start, block_rows, 0)]
    pallas_call x2 -> x1, Pallas kernels: 29 us -> 20.4 us  [weight_product(): pl.pallas_call(weight_kernel, grid=(2, 4), in_specs=[pl.BlockSpec((rows,...]
    ppermute x10, waiting for transfers between devices: 37.3 us -> 45.8 us  [swap_x(): return lax.ppermute(value, 'tensor', [(0, 1), (1, 0)])]
    ppermute x9, waiting for transfers between devices: 20.8 us -> 27.7 us  [swap_y(): return lax.ppermute(value, 'space', [(i, i ^ 2) for i in range(spaces)])]
    another operation x12 -> x9, other arithmetic: 11.5 us -> 5.95 us
    unnamed x43 -> x67, local copies, waits for them, and re-layouts: 10.4 us -> 11.5 us
  transfers between devices with their start and end apart: 39 -> 39, of which waited for: 25 -> 25; matrix products, arithmetic and copies ran while one was open for 14% -> 14% of each run, Pallas kernels for 9% -> 4%
where the time goes in v7:
time: 407 us; the launch traced here: 405 us
  waiting for transfers between devices  211 us (52%)
  Pallas kernels  57.7 us (14%)
  other arithmetic  55 us (14%)
  local copies, waits for them, and re-layouts  42.7 us (10%)
  starting transfers between devices  35.3 us (9%)
    ppermute x12, waiting for transfers between devices, ring(): lax.ppermute(value, 'frame', [(i, (i + shift) % depth) for i in range(dep...  115 us
    ppermute x10, waiting for transfers between devices, swap_x(): return lax.ppermute(value, 'tensor', [(0, 1), (1, 0)])  45.8 us
    ppermute x9, waiting for transfers between devices, swap_y(): return lax.ppermute(value, 'space', [(i, i ^ 2) for i in range(spaces)])  27.7 us
    pallas_call x1, Pallas kernels, weight_product(): pl.pallas_call(weight_kernel, grid=(2, 4), in_specs=[pl.BlockSpec((rows,...  20.4 us
    ppermute x12, starting transfers between devices, ring(): lax.ppermute(value, 'frame', [(i, (i + shift) % depth) for i in range(dep...  14.6 us
    pallas_call x1, Pallas kernels, project(): pl.pallas_call(project_kernel, grid=(4, 2), in_specs=[pl.BlockSpec((rows,...  13.6 us
    dynamic_update_slice x7, local copies, waits for them, and re-layouts, settle(): return lax.dynamic_update_slice(weights, arrived, (start, 0))  12.7 us
    ppermute x2, waiting for transfers between devices, swap_z(): return lax.ppermute(value, 'frame', [(i, i ^ bit) for i in range(depth)])  11.8 us
  transfers between devices with their start and end apart: 39, of which 25 were waited for; matrix products, arithmetic and copies ran while one was open for 14% of the time, Pallas kernels for 4%

profile of v7, /device:TPU:0, one launch (start us, length us, event | category | flops | bytes accessed | tf_op | source)
XLA Modules:
  0.0 405.4 jit_solution(2539174113657199426)
XLA Ops:
  18.5 10.4 %collective-permute-done.3 = bf16[296,1024]{1,0:T(8,128)(2,1)} collective-permute-done((bf16[296,1024]{1,0:T(8,128)(2,1)}, bf16[296,1024]{1,0:T(8,128)(2,1)}, u32[]{:S(2)}, u32[]{:S(2)}) %collective-permute-start.3) | collective-permute-done | bytes 606240 | tf_op jit(solution)/shard_map/ppermute | solution.py:275
  32.5 4.4 %broadcast_in_dim.58 = bf16[2048,2048]{1,0:T(8,128)(2,1)} broadcast(bf16[]{:T(256)} %constant.283.clone.1), dimensions={} | broadcast | bytes 8388610 | tf_op jit(solution)/shard_map/broadcast_in_dim | solution.py:349
  38.0 38.7 %collective-permute-done.2 = bf16[296,1024]{1,0:T(8,128)(2,1)} collective-permute-done((bf16[296,1024]{1,0:T(8,128)(2,1)}, bf16[296,1024]{1,0:T(8,128)(2,1)}, u32[]{:S(2)}, u32[]{:S(2)}) %collective-permute-start.2) | collective-permute-done | bytes 606240 | tf_op jit(solution)/shard_map/ppermute | solution.py:275
  93.1 6.6 %collective-permute-done.9 = bf16[296,1024]{1,0:T(8,128)(2,1)S(1)} collective-permute-done((bf16[296,1024]{1,0:T(8,128)(2,1)}, bf16[296,1024]{1,0:T(8,128)(2,1)S(1)}, u32[]{:S(2)}, u32[]{:S(2)}) %collective-permute-start.9) | collective-permute-done | bytes 606240 | tf_op jit(solution)/shard_map/ppermute | solution.py:287
  101.0 17.8 %collective-permute-done.7 = bf16[296,1024]{1,0:T(8,128)(2,1)S(1)} collective-permute-done((bf16[296,1024]{1,0:T(8,128)(2,1)S(1)}, bf16[296,1024]{1,0:T(8,128)(2,1)S(1)}, u32[]{:S(2)}, u32[]{:S(2)}) %collective-permute-start.7) | collective-permute-done | bytes 606240 | tf_op jit(solution)/shard_map/ppermute | solution.py:275
  123.8 10.1 %collective-permute-done.11 = bf16[296,1024]{1,0:T(8,128)(2,1)S(1)} collective-permute-done((bf16[296,1024]{1,0:T(8,128)(2,1)S(1)}, bf16[296,1024]{1,0:T(8,128)(2,1)S(1)}, u32[]{:S(2)}, u32[]{:S(2)}) %collective-permute-start.11) | collective-permute-done | bytes 606240 | tf_op jit(solution)/shard_map/ppermute | solution.py:287
  138.5 8.3 %collective-permute-done.10 = bf16[256,2048]{1,0:T(8,128)(2,1)} collective-permute-done((bf16[256,2048]{1,0:T(8,128)(2,1)S(1)}, bf16[256,2048]{1,0:T(8,128)(2,1)}, u32[]{:S(2)}, u32[]{:S(2)}) %collective-permute-start.10) | collective-permute-done | bytes 1048608 | tf_op jit(solution)/shard_map/ppermute | solution.py:275
  169.6 5.0 %collective-permute-done.15 = bf16[256,2048]{1,0:T(8,128)(2,1)S(1)} collective-permute-done((bf16[256,2048]{1,0:T(8,128)(2,1)}, bf16[256,2048]{1,0:T(8,128)(2,1)S(1)}, u32[]{:S(2)}, u32[]{:S(2)}) %collective-permute-start.15) | collective-permute-done | bytes 1048608 | tf_op jit(solution)/shard_map/ppermute | solution.py:284
  175.6 13.6 %project.1 = (bf16[1152,1536]{1,0:T(8,128)(2,1)S(1)}, bf16[1152,512]{1,0:T(8,128)(2,1)S(1)}) custom-call(bf16[1152,2048]{1,0:T(8,128)(2,1)S(1)} %bitcast.98, bf16[1152,2048]{1,0:T(8,128)(2,1)S(1)} %bitcast.96, bf16[2048,2048]{1,0:T(8,128)(2,1)} %constant_dynamic-update-slice_fusion.weight_ref), custom_call_target="tpu_custom_call" | custom-call | flops 9663676416 | bytes 18874368 | tf_op jit(solution)/shard_map/project/pallas_call | solution.py:200
  189.2 7.8 %temporal_attention.1 = (bf16[8,144,512]{2,1,0:T(8,128)(2,1)S(1)}, bf16[8,144,1536]{2,1,0:T(8,128)(2,1)S(1)}, f32[2,8,128]{2,1,0:T(8,128)S(1)}) custom-call(f32[128,1]{1,0:T(8,128)S(1)} %broadcast_in_dim_reshape.9.late_ref, f32[1,128]{1,0:T(1,128)S(1)} %broadcast_in_dim_reshape.8.early_ref, bf16[8,144,1536]{2,1,0:T(8,128)(2,1)S(1)} %bitcast.101, ...), custom_call_target="tpu_custom_call" | custom-call | flops 1207959552 | bytes 9437184 | tf_op jit(solution)/shard_map/temporal_attention/pallas_call | solution.py:108
  201.7 20.4 %weight_product.1 = f32[2048,2048]{1,0:T(8,128)} custom-call(bf16[2048,1152]{1,0:T(8,128)(2,1)} %copy-done.3, bf16[2048,1152]{1,0:T(8,128)(2,1)} %copy-done.2, bf16[1152,1536]{1,0:T(8,128)(2,1)} %bitcast.99, bf16[1152,512]{1,0:T(8,128)(2,1)} %bitcast.103), custom_call_target="tpu_custom_call" | custom-call | flops 1 | bytes 1 | tf_op jit(solution)/shard_map/weight_product/pallas_call | solution.py:169
  222.1 5.9 %constant_dynamic-slice_fusion.4 = (f32[256,2048]{1,0:T(8,128)}, f32[256,2048]{1,0:T(8,128)}, f16[256,2048]{1,0:T(8,128)(2,1)S(1)}) fusion(f32[2048,2048]{1,0:T(8,128)} %weight_product.1, s32[]{:T(128)S(6)} %select_n.526, s32[]{:T(128)S(6)} %select_n.530, f32[2048]{0:T(1024)S(1)} %multiply_exponential_fusion.8, s32[]{:T(128)S(6)} %select_n.527), kind=kLoop, calls=%fused_computation.108 | loop fusion | flops 1048576 | bytes 11542540 | tf_op jit(solution)/shard_map/dynamic_slice | solution.py:434
  229.5 11.2 %norm_product.1 = (f32[8,72,2048]{2,1,0:T(8,128)S(1)}, f32[8,72,2048]{2,1,0:T(8,128)}) custom-call(bf16[1152,1536]{1,0:T(8,128)(2,1)S(1)} %bitcast.100, bf16[2048,2048]{1,0:T(8,128)(2,1)} %constant_dynamic-update-slice_fusion.weight_ref), custom_call_target="tpu_custom_call" | custom-call | flops 1 | bytes 1 | tf_op jit(solution)/shard_map/norm_product/pallas_call | solution.py:241
  243.9 10.5 %collective-permute-done.16 = f16[264,2048]{1,0:T(8,128)(2,1)} collective-permute-done((f16[264,2048]{1,0:T(8,128)(2,1)}, f16[264,2048]{1,0:T(8,128)(2,1)}, u32[]{:S(2)}, u32[]{:S(2)}) %collective-permute-start.16) | collective-permute-done | bytes 1081376 | tf_op jit(solution)/shard_map/ppermute | solution.py:284
  259.7 7.5 %collective-permute-done.17 = f32[8,72,2048]{2,1,0:T(8,128)} collective-permute-done((f32[8,72,2048]{2,1,0:T(8,128)}, f32[8,72,2048]{2,1,0:T(8,128)}, u32[]{:S(2)}, u32[]{:S(2)}) %collective-permute-start.17) | collective-permute-done | bytes 4718624 | tf_op jit(solution)/shard_map/ppermute | solution.py:281
  267.2 5.5 %multiply_reduce_fusion = (f32[8,72]{1,0:T(8,128)S(1)}, f32[8,72]{1,0:T(8,128)S(1)}, f32[8,72,2048]{2,1,0:T(8,128)S(1)}) fusion(bf16[8,72,2048]{2,1,0:T(8,128)(2,1)S(1)} %copy-done.9, f32[2048]{0:T(1024)S(1)} %copy-done.26, f32[8,72]{1,0:T(8,128)} %copy-done.27, f32[8,2048]{1,0:T(8,128)S(1)} %copy-done.16, f32[8,72,2048]{2,1,0:T(8,128)} %copy-done.6, ...), kind=kLoop, calls=%fused_computation.2 | loop fusion | flops 10615680 | bytes 16595712 | tf_op jit(solution)/shard_map/reduce_sum | solution.py:450
  276.3 9.4 %collective-permute-done.21 = f16[264,2048]{1,0:T(8,128)(2,1)S(1)} collective-permute-done((f16[264,2048]{1,0:T(8,128)(2,1)S(1)}, f16[264,2048]{1,0:T(8,128)(2,1)S(1)}, u32[]{:S(2)}, u32[]{:S(2)}) %collective-permute-start.21) | collective-permute-done | bytes 1081376 | tf_op jit(solution)/shard_map/ppermute | solution.py:284
  293.2 8.1 %collective-permute-done.20 = f32[8,72,2]{1,0,2:T(8,128)S(1)} collective-permute-done((f32[8,72,2]{1,0,2:T(8,128)S(1)}, f32[8,72,2]{1,0,2:T(8,128)S(1)}, u32[]{:S(2)}, u32[]{:S(2)}) %collective-permute-start.20) | collective-permute-done | bytes 4640 | tf_op jit(solution)/shard_map/ppermute | solution.py:287
  305.2 20.3 %collective-permute-done.23 = bf16[2,72,1024]{2,1,0:T(8,128)(2,1)S(1)} collective-permute-done((bf16[2,72,1024]{2,1,0:T(8,128)(2,1)S(1)}, bf16[2,72,1024]{2,1,0:T(8,128)(2,1)S(1)}, u32[]{:S(2)}, u32[]{:S(2)}) %collective-permute-start.23) | collective-permute-done | bytes 294944 | tf_op jit(solution)/shard_map/ppermute | solution.py:275
  335.5 17.3 %collective-permute-done.24 = bf16[2,72,1024]{2,1,0:T(8,128)(2,1)S(1)} collective-permute-done((bf16[2,72,1024]{2,1,0:T(8,128)(2,1)S(1)}, bf16[2,72,1024]{2,1,0:T(8,128)(2,1)S(1)}, u32[]{:S(2)}, u32[]{:S(2)}) %collective-permute-start.24) | collective-permute-done | bytes 294944 | tf_op jit(solution)/shard_map/ppermute | solution.py:275
  362.5 4.5 %collective-permute-done.31 = bf16[2,72,1024]{2,1,0:T(8,128)(2,1)} collective-permute-done((bf16[2,72,1024]{2,1,0:T(8,128)(2,1)S(1)}, bf16[2,72,1024]{2,1,0:T(8,128)(2,1)}, u32[]{:S(2)}, u32[]{:S(2)}) %collective-permute-start.31) | collective-permute-done | bytes 294944 | tf_op jit(solution)/shard_map/ppermute | solution.py:287
  374.7 4.8 %collective-permute-done.32 = bf16[2,72,1024]{2,1,0:T(8,128)(2,1)S(1)} collective-permute-done((bf16[2,72,1024]{2,1,0:T(8,128)(2,1)S(1)}, bf16[2,72,1024]{2,1,0:T(8,128)(2,1)S(1)}, u32[]{:S(2)}, u32[]{:S(2)}) %collective-permute-start.32) | collective-permute-done | bytes 294944 | tf_op jit(solution)/shard_map/ppermute | solution.py:287
  379.7 5.2 %collective-permute-done.34 = bf16[2,72,1024]{2,1,0:T(8,128)(2,1)S(1)} collective-permute-done((bf16[2,72,1024]{2,1,0:T(8,128)(2,1)S(1)}, bf16[2,72,1024]{2,1,0:T(8,128)(2,1)S(1)}, u32[]{:S(2)}, u32[]{:S(2)}) %collective-permute-start.34) | collective-permute-done | bytes 294944 | tf_op jit(solution)/shard_map/ppermute | solution.py:287
  392.0 8.8 %collective-permute-done.38 = f32[9,2048]{1,0:T(8,128)S(1)} collective-permute-done((f32[9,2048]{1,0:T(8,128)}, f32[9,2048]{1,0:T(8,128)S(1)}, u32[]{:S(2)}, u32[]{:S(2)}) %collective-permute-start.38) | collective-permute-done | bytes 73760 | tf_op jit(solution)/shard_map/ppermute | solution.py:278
  (250 shorter events, 140.2 us)
Async XLA Ops:
  9.0 19.8 %collective-permute-start.3 = (bf16[296,1024]{1,0:T(8,128)(2,1)}, bf16[296,1024]{1,0:T(8,128)(2,1)}, u32[]{:S(2)}, u32[]{:S(2)}) collective-permute-start(bf16[296,1024]{1,0:T(8,128)(2,1)} %pad_maximum_fusion.13), channel_id=1, source_target_pairs={{0,8},{8,16},{16,24},{24,0},{1,9},{9,17},{17,25},{25,1},{2,10},{10... | collective-permute-start | bytes 1818632 | tf_op jit(solution)/shard_map/ppermute | solution.py:275
  13.0 63.7 %collective-permute-start.1 = (bf16[256,2048]{1,0:T(8,128)(2,1)}, bf16[256,2048]{1,0:T(8,128)(2,1)}, u32[]{:S(2)}, u32[]{:S(2)}) collective-permute-start(bf16[256,2048]{1,0:T(8,128)(2,1)} %pad_maximum_fusion.11), channel_id=1, source_target_pairs={{0,8},{8,16},{16,24},{24,0},{1,9},{9,17},{17,25},{25,1},{2,10},{10... | collective-permute-start | bytes 3145736 | tf_op jit(solution)/shard_map/ppermute | solution.py:275
  14.7 62.0 %collective-permute-start.4 = (bf16[256,2048]{1,0:T(8,128)(2,1)}, bf16[256,2048]{1,0:T(8,128)(2,1)}, u32[]{:S(2)}, u32[]{:S(2)}) collective-permute-start(bf16[256,2048]{1,0:T(8,128)(2,1)} %pad_maximum_fusion.11), channel_id=1, source_target_pairs={{0,4},{2,6},{4,0},{6,2},{1,5},{3,7},{5,1},{7,3},{8,12},{10,14},{12... | collective-permute-start | bytes 3145736 | tf_op jit(solution)/shard_map/ppermute | solution.py:284
  17.2 59.5 %collective-permute-start.2 = (bf16[296,1024]{1,0:T(8,128)(2,1)}, bf16[296,1024]{1,0:T(8,128)(2,1)}, u32[]{:S(2)}, u32[]{:S(2)}) collective-permute-start(bf16[296,1024]{1,0:T(8,128)(2,1)} %pad_maximum_fusion.12), channel_id=1, source_target_pairs={{0,16},{8,24},{16,0},{24,8},{1,17},{9,25},{17,1},{25,9},{2,18},{10... | collective-permute-start | bytes 1818632 | tf_op jit(solution)/shard_map/ppermute | solution.py:275
  28.8 47.9 %collective-permute-start.5 = (bf16[296,1024]{1,0:T(8,128)(2,1)}, bf16[296,1024]{1,0:T(8,128)(2,1)}, u32[]{:S(2)}, u32[]{:S(2)}) collective-permute-start(bf16[296,1024]{1,0:T(8,128)(2,1)} %collective-permute-done.3), channel_id=1, source_target_pairs={{0,1},{1,0},{2,3},{3,2},{4,5},{5,4},{6,7},{7,6},{8,9},{9,8},{10,11... | collective-permute-start | bytes 1818632 | tf_op jit(solution)/shard_map/ppermute | solution.py:287
  79.1 39.7 %collective-permute-start.6 = (bf16[256,2048]{1,0:T(8,128)(2,1)}, bf16[256,2048]{1,0:T(8,128)(2,1)S(1)}, u32[]{:S(2)}, u32[]{:S(2)}) collective-permute-start(bf16[256,2048]{1,0:T(8,128)(2,1)} %collective-permute-done.1), channel_id=1, source_target_pairs={{0,8},{8,16},{16,24},{24,0},{1,9},{9,17},{17,25},{25,1},{2,10},{10... | collective-permute-start | bytes 3145736 | tf_op jit(solution)/shard_map/ppermute | solution.py:275
  79.1 39.7 %collective-permute-start.8 = (bf16[256,2048]{1,0:T(8,128)(2,1)}, bf16[256,2048]{1,0:T(8,128)(2,1)S(1)}, u32[]{:S(2)}, u32[]{:S(2)}) collective-permute-start(bf16[256,2048]{1,0:T(8,128)(2,1)} %collective-permute-done.1), channel_id=1, source_target_pairs={{0,4},{2,6},{4,0},{6,2},{1,5},{3,7},{5,1},{7,3},{8,12},{10,14},{12... | collective-permute-start | bytes 3145736 | tf_op jit(solution)/shard_map/ppermute | solution.py:284
  80.9 37.8 %collective-permute-start.7 = (bf16[296,1024]{1,0:T(8,128)(2,1)S(1)}, bf16[296,1024]{1,0:T(8,128)(2,1)S(1)}, u32[]{:S(2)}, u32[]{:S(2)}) collective-permute-start(bf16[296,1024]{1,0:T(8,128)(2,1)S(1)} %pad_maximum_fusion.14), channel_id=1, source_target_pairs={{0,24},{8,0},{16,8},{24,16},{1,25},{9,1},{17,9},{25,17},{2,26},{10... | collective-permute-start | bytes 1818632 | tf_op jit(solution)/shard_map/ppermute | solution.py:275
  118.8 15.1 %collective-permute-start.11 = (bf16[296,1024]{1,0:T(8,128)(2,1)S(1)}, bf16[296,1024]{1,0:T(8,128)(2,1)S(1)}, u32[]{:S(2)}, u32[]{:S(2)}) collective-permute-start(bf16[296,1024]{1,0:T(8,128)(2,1)S(1)} %collective-permute-done.7), channel_id=1, source_target_pairs={{0,1},{1,0},{2,3},{3,2},{4,5},{5,4},{6,7},{7,6},{8,9},{9,8},{10,11... | collective-permute-start | bytes 1818632 | tf_op jit(solution)/shard_map/ppermute | solution.py:287
  120.3 26.4 %collective-permute-start.10 = (bf16[256,2048]{1,0:T(8,128)(2,1)S(1)}, bf16[256,2048]{1,0:T(8,128)(2,1)}, u32[]{:S(2)}, u32[]{:S(2)}) collective-permute-start(bf16[256,2048]{1,0:T(8,128)(2,1)S(1)} %collective-permute-done.6), channel_id=1, source_target_pairs={{0,8},{8,16},{16,24},{24,0},{1,9},{9,17},{17,25},{25,1},{2,10},{10... | collective-permute-start | bytes 3145736 | tf_op jit(solution)/shard_map/ppermute | solution.py:275
  120.6 26.2 %collective-permute-start.12 = (bf16[256,2048]{1,0:T(8,128)(2,1)S(1)}, bf16[256,2048]{1,0:T(8,128)(2,1)}, u32[]{:S(2)}, u32[]{:S(2)}) collective-permute-start(bf16[256,2048]{1,0:T(8,128)(2,1)S(1)} %collective-permute-done.6), channel_id=1, source_target_pairs={{0,4},{2,6},{4,0},{6,2},{1,5},{3,7},{5,1},{7,3},{8,12},{10,14},{12... | collective-permute-start | bytes 3145736 | tf_op jit(solution)/shard_map/ppermute | solution.py:284
  149.2 25.3 %collective-permute-start.15 = (bf16[256,2048]{1,0:T(8,128)(2,1)}, bf16[256,2048]{1,0:T(8,128)(2,1)S(1)}, u32[]{:S(2)}, u32[]{:S(2)}) collective-permute-start(bf16[256,2048]{1,0:T(8,128)(2,1)} %collective-permute-done.10), channel_id=1, source_target_pairs={{0,4},{2,6},{4,0},{6,2},{1,5},{3,7},{5,1},{7,3},{8,12},{10,14},{12... | collective-permute-start | bytes 3145736 | tf_op jit(solution)/shard_map/ppermute | solution.py:284
  229.2 25.2 %collective-permute-start.16 = (f16[264,2048]{1,0:T(8,128)(2,1)}, f16[264,2048]{1,0:T(8,128)(2,1)}, u32[]{:S(2)}, u32[]{:S(2)}) collective-permute-start(f16[264,2048]{1,0:T(8,128)(2,1)} %pad_maximum_fusion.7), channel_id=1, source_target_pairs={{0,4},{2,6},{4,0},{6,2},{1,5},{3,7},{5,1},{7,3},{8,12},{10,14},{12... | collective-permute-start | bytes 3244040 | tf_op jit(solution)/shard_map/ppermute | solution.py:284
  258.9 26.7 %collective-permute-start.21 = (f16[264,2048]{1,0:T(8,128)(2,1)S(1)}, f16[264,2048]{1,0:T(8,128)(2,1)S(1)}, u32[]{:S(2)}, u32[]{:S(2)}) collective-permute-start(f16[264,2048]{1,0:T(8,128)(2,1)S(1)} %pad_maximum_fusion.6), channel_id=1, source_target_pairs={{0,4},{2,6},{4,0},{6,2},{1,5},{3,7},{5,1},{7,3},{8,12},{10,14},{12... | collective-permute-start | bytes 3244040 | tf_op jit(solution)/shard_map/ppermute | solution.py:284
  259.6 27.9 %collective-permute-start.22 = (f16[264,2048]{1,0:T(8,128)(2,1)}, f16[264,2048]{1,0:T(8,128)(2,1)S(1)}, u32[]{:S(2)}, u32[]{:S(2)}) collective-permute-start(f16[264,2048]{1,0:T(8,128)(2,1)} %pad_maximum_fusion.8), channel_id=1, source_target_pairs={{0,8},{8,16},{16,24},{24,0},{1,9},{9,17},{17,25},{25,1},{2,10},{10... | collective-permute-start | bytes 3244040 | tf_op jit(solution)/shard_map/ppermute | solution.py:275
  273.1 28.3 %collective-permute-start.19 = (f16[8,72,1024]{2,1,0:T(8,128)(2,1)S(1)}, f16[8,72,1024]{2,1,0:T(8,128)(2,1)S(1)}, u32[]{:S(2)}, u32[]{:S(2)}) collective-permute-start(f16[8,72,1024]{2,1,0:T(8,128)(2,1)S(1)} %divide_convert_fusion), channel_id=1, source_target_pairs={{0,1},{1,0},{2,3},{3,2},{4,5},{5,4},{6,7},{7,6},{8,9},{9,8},{10,11... | collective-permute-start | bytes 3538952 | tf_op jit(solution)/shard_map/ppermute | solution.py:287
  275.7 59.8 %collective-permute-start.18 = (f16[264,2048]{1,0:T(8,128)(2,1)}, f16[264,2048]{1,0:T(8,128)(2,1)}, u32[]{:S(2)}, u32[]{:S(2)}) collective-permute-start(f16[264,2048]{1,0:T(8,128)(2,1)} %pad_maximum_fusion.5), channel_id=1, source_target_pairs={{0,4},{2,6},{4,0},{6,2},{1,5},{3,7},{5,1},{7,3},{8,12},{10,14},{12... | collective-permute-start | bytes 3244040 | tf_op jit(solution)/shard_map/ppermute | solution.py:284
  292.0 60.9 %collective-permute-start.29 = (f16[264,2048]{1,0:T(8,128)(2,1)}, f16[264,2048]{1,0:T(8,128)(2,1)}, u32[]{:S(2)}, u32[]{:S(2)}) collective-permute-start(f16[264,2048]{1,0:T(8,128)(2,1)} %pad_maximum_fusion.9), channel_id=1, source_target_pairs={{0,8},{8,16},{16,24},{24,0},{1,9},{9,17},{17,25},{25,1},{2,10},{10... | collective-permute-start | bytes 3244040 | tf_op jit(solution)/shard_map/ppermute | solution.py:275
  303.1 22.4 %collective-permute-start.23 = (bf16[2,72,1024]{2,1,0:T(8,128)(2,1)S(1)}, bf16[2,72,1024]{2,1,0:T(8,128)(2,1)S(1)}, u32[]{:S(2)}, u32[]{:S(2)}) collective-permute-start(bf16[2,72,1024]{2,1,0:T(8,128)(2,1)S(1)} %get-tuple-element.124), channel_id=1, source_target_pairs={{0,24},{8,0},{16,8},{24,16},{1,25},{9,1},{17,9},{25,17},{2,26},{10... | collective-permute-start | bytes 884744 | tf_op jit(solution)/shard_map/ppermute | solution.py:275
  331.8 21.1 %collective-permute-start.24 = (bf16[2,72,1024]{2,1,0:T(8,128)(2,1)S(1)}, bf16[2,72,1024]{2,1,0:T(8,128)(2,1)S(1)}, u32[]{:S(2)}, u32[]{:S(2)}) collective-permute-start(bf16[2,72,1024]{2,1,0:T(8,128)(2,1)S(1)} %get-tuple-element.123), channel_id=1, source_target_pairs={{0,16},{8,24},{16,0},{24,8},{1,17},{9,25},{17,1},{25,9},{2,18},{10... | collective-permute-start | bytes 884744 | tf_op jit(solution)/shard_map/ppermute | solution.py:275
  332.3 20.5 %collective-permute-start.25 = (bf16[2,72,1024]{2,1,0:T(8,128)(2,1)S(1)}, bf16[2,72,1024]{2,1,0:T(8,128)(2,1)S(1)}, u32[]{:S(2)}, u32[]{:S(2)}) collective-permute-start(bf16[2,72,1024]{2,1,0:T(8,128)(2,1)S(1)} %get-tuple-element.122), channel_id=1, source_target_pairs={{0,8},{8,16},{16,24},{24,0},{1,9},{9,17},{17,25},{25,1},{2,10},{10... | collective-permute-start | bytes 884744 | tf_op jit(solution)/shard_map/ppermute | solution.py:275
  358.4 30.2 %collective-permute-start.36 = (f16[264,2048]{1,0:T(8,128)(2,1)S(1)}, f16[264,2048]{1,0:T(8,128)(2,1)S(1)}, u32[]{:S(2)}, u32[]{:S(2)}) collective-permute-start(f16[264,2048]{1,0:T(8,128)(2,1)S(1)} %pad_maximum_fusion.4), channel_id=1, source_target_pairs={{0,4},{2,6},{4,0},{6,2},{1,5},{3,7},{5,1},{7,3},{8,12},{10,14},{12... | collective-permute-start | bytes 3244040 | tf_op jit(solution)/shard_map/ppermute | solution.py:284
  359.9 28.1 %collective-permute-start.35 = (f32[9,2048]{1,0:T(8,128)S(1)}, f32[9,2048]{1,0:T(8,128)S(1)}, u32[]{:S(2)}, u32[]{:S(2)}) collective-permute-start(f32[9,2048]{1,0:T(8,128)S(1)} %pad_maximum_fusion.23), channel_id=1, source_target_pairs={{0,8},{8,0},{16,24},{24,16},{1,9},{9,1},{17,25},{25,17},{2,10},{10... | collective-permute-start | bytes 221192 | tf_op jit(solution)/shard_map/ppermute | solution.py:278
  359.9 28.8 %collective-permute-start.30 = (f16[264,2048]{1,0:T(8,128)(2,1)S(1)}, f16[264,2048]{1,0:T(8,128)(2,1)S(1)}, u32[]{:S(2)}, u32[]{:S(2)}) collective-permute-start(f16[264,2048]{1,0:T(8,128)(2,1)S(1)} %pad_maximum_fusion.10), channel_id=1, source_target_pairs={{0,8},{8,16},{16,24},{24,0},{1,9},{9,17},{17,25},{25,1},{2,10},{10... | collective-permute-start | bytes 3244040 | tf_op jit(solution)/shard_map/ppermute | solution.py:275
  (49 other events, 469.4 us)

commit v8 on v5

--- a/solution.py
+++ b/solution.py
@@ -153,26 +153,27 @@
     )(rows)
 
 
-def weight_kernel(
-    place_ref, norm_near, norm_far, up_near, up_far, merged_ref, mixed_ref, near_ref, far_ref
-):
+def weight_kernel(place_ref, norm_ref, up_ref, merged_ref, mixed_ref, near_ref, far_ref):
     step = pl.program_id(0)
+    rows = near_ref.shape[0]
+    first = place_ref[1] == 0
+
+    def store(both):
+        near_ref[...] = jnp.where(first, both[:rows], both[rows:])
+        far_ref[...] = jnp.where(first, both[rows:], both[:rows])
 
     @pl.when(step < 3)
     def _():
-        near_ref[...] = dot_nn(norm_near[...], merged_ref[...])
-        far_ref[...] = dot_nn(norm_far[...], merged_ref[...])
+        store(dot_nn(norm_ref[...], merged_ref[...]))
 
     @pl.when(step == 3)
     def _():
-        near_ref[...] = dot_nn(up_near[...], mixed_ref[...])
-        far_ref[...] = dot_nn(up_far[...], mixed_ref[...])
+        store(dot_nn(up_ref[...], mixed_ref[...]))
 
 
 def weight_product(places, rows, normed, upstream, merged, mixed):
     tokens, width = mixed.shape
-    near = pl.BlockSpec((rows, tokens), lambda i, at: (at[0], 0))
-    far = pl.BlockSpec((rows, tokens), lambda i, at: (at[1], 0))
+    pair = pl.BlockSpec((2 * rows, tokens), lambda i, at: (at[0], 0))
     out = pl.BlockSpec((rows, width), lambda i, at: (0, i))
     return pl.pallas_call(
         weight_kernel,
@@ -180,10 +181,8 @@
             num_scalar_prefetch=1,
             grid=(4,),
             in_specs=[
-                near,
-                far,
-                near,
-                far,
+                pair,
+                pair,
                 pl.BlockSpec((tokens, width), lambda i, at: (0, jnp.minimum(i, 2))),
                 pl.BlockSpec((tokens, width), lambda i, at: (0, 0)),
             ],
@@ -193,7 +192,7 @@
         compiler_params=pltpu.CompilerParams(vmem_limit_bytes=58 * MIB),
         cost_estimate=pl.CostEstimate(flops=1, bytes_accessed=1, transcendentals=0),
         name="weight_product",
-    )(places, normed, normed, upstream, upstream, merged, mixed)
+    )(places, normed, upstream, merged, mixed)
 
 
 def project_kernel(normed_ref, up_ref, weight_ref, qkv_ref, grad_ref):
@@ -238,14 +237,19 @@
     )(normed, upstream, weights)
 
 
-def norm_kernel(merged_ref, weight_ref, out_ref):
-    out_ref[...] = dot_nt(merged_ref[...], weight_ref[...])
-
-
-def norm_product(merged, weights):
+def norm_kernel(merged_ref, weight_ref, own_ref, other_ref):
+    frames, pairs, tile = own_ref.shape
+    rows = dot_nt(merged_ref[...], weight_ref[...]).reshape(frames, 2 * pairs, tile)
+    own_ref[...] = rows[:, :pairs]
+    other_ref[...] = rows[:, pairs:]
+
+
+def norm_product(merged, weights, frames):
     rows, depth = merged.shape
     features = weights.shape[0]
     tile = features // 4
+    pairs = rows // frames // 2
+    out = pl.BlockSpec((frames, pairs, tile), lambda i: (0, 0, i))
     return pl.pallas_call(
         norm_kernel,
         grid=(4,),
@@ -253,9 +257,9 @@
             pl.BlockSpec((rows, depth), lambda i: (0, 0)),
             pl.BlockSpec((tile, depth), lambda i: (i, 0)),
         ],
-        out_specs=pl.BlockSpec((rows, tile), lambda i: (0, i)),
-        out_shape=jax.ShapeDtypeStruct((rows, features), jnp.float32),
-        compiler_params=pltpu.CompilerParams(vmem_limit_bytes=18 * MIB),
+        out_specs=[out, out],
+        out_shape=[jax.ShapeDtypeStruct((frames, pairs, features), jnp.float32)] * 2,
+        compiler_params=pltpu.CompilerParams(vmem_limit_bytes=26 * MIB),
         cost_estimate=pl.CostEstimate(flops=1, bytes_accessed=1, transcendentals=0),
         name="norm_product",
     )(merged, weights)
@@ -436,17 +440,12 @@
         return sent[:block_rows].astype(jnp.float32) * scale, scale * WIRE_TOP
 
     def weight_part(k, earlier):
-        block_at = after((z - 1 - k) % depth * 2, earlier)
-        places = jnp.stack([block_at + y, block_at + 1 - y])
+        places = jnp.stack([after((z - 1 - k) % depth, earlier), y])
         near, far = weight_product(
             places, block_rows, normed_t, upstream_t, flat_merged, flat_mixed
         )
         return near, pack(far, own_bound)
 
-    def norm_part(rows):
-        flat = rows.reshape(frames * pairs, 3 * head_width)
-        return norm_product(flat, weights).reshape(frames, pairs, features)
-
     def chip_sum(k, earlier):
         term, bound = unpack(after(swap_y(weight_parts[k][1]), earlier))
         return weight_parts[k][0] + term, bound + own_bound
@@ -457,10 +456,11 @@
         return total + term, bound + ring_bound
 
     weight_parts = [weight_part(0, flat_merged)]
-    norm_away = norm_part(after(merged[:, pairs:], weight_parts[0][1]))
+    norm_here, norm_away = norm_product(
+        after(flat_merged, weight_parts[0][1]), weights, frames
+    )
     weight_parts.append(weight_part(1, norm_away))
     payload = pack(*chip_sum(0, weight_parts[1][1]))
-    norm_here = norm_part(after(merged[:, :pairs], payload))
     partial_norm = norm_here + swap_core(after(norm_away, payload))
     row_dot = jnp.sum(partial_norm * gain * (hidden * inverse), -1, keepdims=True)
     if tensors == 2:
@@ -513,7 +513,7 @@
     small = after(small, payload)
     bit = 2
     while bit < depth:
-        small = small + swap_z(small, bit)
+        small = small + after(swap_z(small, bit), grad_inputs)
         bit *= 2
     arriving, grad_inputs, small = lax.optimization_barrier(
         (ring(payload, 1), grad_inputs, small)

time: 390 us -> 380 us (0.974)
  waiting for transfers between devices: 176 us -> 164 us
  Pallas kernels: 74.4 us -> 70.3 us
    ppermute x2, waiting for transfers between devices: 33.3 us -> 12.3 us  [swap_z(): return lax.ppermute(value, 'frame', [(i, i ^ bit) for i in range(depth)])]
    ppermute x10, waiting for transfers between devices: 27.1 us -> 37.1 us  [swap_x(): return lax.ppermute(value, 'tensor', [(0, 1), (1, 0)])]
    ppermute x6, waiting for transfers between devices: 4.53 us -> 10.3 us  [swap_core(): return lax.ppermute(value, 'space', [(i, i ^ 1) for i in range(spaces)])]
    pallas_call x2 -> x1, Pallas kernels: 14.4 us -> 10.9 us  [norm_product(): pl.pallas_call(norm_kernel, grid=(4,), in_specs=[pl.BlockSpec((rows, dept...]
    unnamed x53 -> x39, local copies, waits for them, and re-layouts: 12.7 us -> 12.4 us
  transfers between devices with their start and end apart: 39 -> 39, of which waited for: 19 -> 20; matrix products, arithmetic and copies ran while one was open for 16% -> 18% of each run, Pallas kernels for 12% -> 11%
where the time goes in v8:
time: 380 us; the launch traced here: 379 us
  waiting for transfers between devices  164 us (43%)
  Pallas kernels  70.3 us (18%)
  other arithmetic  56.2 us (15%)
  local copies, waits for them, and re-layouts  44.2 us (12%)
  starting transfers between devices  40 us (11%)
    ppermute x12, waiting for transfers between devices, ring(): lax.ppermute(value, 'frame', [(i, (i + shift) % depth) for i in range(dep...  96.5 us
    ppermute x10, waiting for transfers between devices, swap_x(): return lax.ppermute(value, 'tensor', [(0, 1), (1, 0)])  37.1 us
    pallas_call x4, Pallas kernels, weight_product(): pl.pallas_call(weight_kernel, grid_spec=pltpu.PrefetchScalarGridSpec(num_...  33.2 us
    ppermute x12, starting transfers between devices, ring(): lax.ppermute(value, 'frame', [(i, (i + shift) % depth) for i in range(dep...  14.8 us
    dynamic_update_slice x7, local copies, waits for them, and re-layouts, settle(): return lax.dynamic_update_slice(weights, arrived, (start, 0))  13.8 us
    pallas_call x1, Pallas kernels, project(): pl.pallas_call(project_kernel, grid=(4, 2), in_specs=[pl.BlockSpec((rows,...  13.6 us
    ppermute x10, starting transfers between devices, swap_x(): return lax.ppermute(value, 'tensor', [(0, 1), (1, 0)])  13.2 us
    another operation x11, other arithmetic  12.7 us
  transfers between devices with their start and end apart: 39, of which 20 were waited for; matrix products, arithmetic and copies ran while one was open for 18% of the time, Pallas kernels for 11%

profile of v8, /device:TPU:0, one launch (start us, length us, event | category | flops | bytes accessed | tf_op | source)
XLA Modules:
  0.0 378.7 jit_solution(7451098499145416673)
XLA Ops:
  18.6 10.1 %collective-permute-done.3 = bf16[296,1024]{1,0:T(8,128)(2,1)} collective-permute-done((bf16[296,1024]{1,0:T(8,128)(2,1)S(1)}, bf16[296,1024]{1,0:T(8,128)(2,1)}, u32[]{:S(2)}, u32[]{:S(2)}) %collective-permute-start.3) | collective-permute-done | bytes 606240 | tf_op jit(solution)/shard_map/ppermute | solution.py:287
  32.4 4.4 %broadcast_in_dim.62 = bf16[2048,2048]{1,0:T(8,128)(2,1)} broadcast(bf16[]{:T(256)} %constant.276.clone.1), dimensions={} | broadcast | bytes 8388610 | tf_op jit(solution)/shard_map/broadcast_in_dim | solution.py:361
  37.9 38.7 %collective-permute-done.2 = bf16[296,1024]{1,0:T(8,128)(2,1)} collective-permute-done((bf16[296,1024]{1,0:T(8,128)(2,1)S(1)}, bf16[296,1024]{1,0:T(8,128)(2,1)}, u32[]{:S(2)}, u32[]{:S(2)}) %collective-permute-start.2) | collective-permute-done | bytes 606240 | tf_op jit(solution)/shard_map/ppermute | solution.py:287
  92.8 6.9 %collective-permute-done.9 = bf16[296,1024]{1,0:T(8,128)(2,1)S(1)} collective-permute-done((bf16[296,1024]{1,0:T(8,128)(2,1)}, bf16[296,1024]{1,0:T(8,128)(2,1)S(1)}, u32[]{:S(2)}, u32[]{:S(2)}) %collective-permute-start.9) | collective-permute-done | bytes 606240 | tf_op jit(solution)/shard_map/ppermute | solution.py:299
  101.0 15.8 %collective-permute-done.7 = bf16[296,1024]{1,0:T(8,128)(2,1)S(1)} collective-permute-done((bf16[296,1024]{1,0:T(8,128)(2,1)S(1)}, bf16[296,1024]{1,0:T(8,128)(2,1)S(1)}, u32[]{:S(2)}, u32[]{:S(2)}) %collective-permute-start.7) | collective-permute-done | bytes 606240 | tf_op jit(solution)/shard_map/ppermute | solution.py:287
  124.3 8.3 %collective-permute-done.11 = bf16[296,1024]{1,0:T(8,128)(2,1)S(1)} collective-permute-done((bf16[296,1024]{1,0:T(8,128)(2,1)S(1)}, bf16[296,1024]{1,0:T(8,128)(2,1)S(1)}, u32[]{:S(2)}, u32[]{:S(2)}) %collective-permute-start.11) | collective-permute-done | bytes 606240 | tf_op jit(solution)/shard_map/ppermute | solution.py:299
  137.5 7.9 %collective-permute-done.10 = bf16[256,2048]{1,0:T(8,128)(2,1)} collective-permute-done((bf16[256,2048]{1,0:T(8,128)(2,1)}, bf16[256,2048]{1,0:T(8,128)(2,1)}, u32[]{:S(2)}, u32[]{:S(2)}) %collective-permute-start.10) | collective-permute-done | bytes 1048608 | tf_op jit(solution)/shard_map/ppermute | solution.py:287
  174.2 13.6 %project.1 = (bf16[1152,1536]{1,0:T(8,128)(2,1)S(1)}, bf16[1152,512]{1,0:T(8,128)(2,1)S(1)}) custom-call(bf16[1152,2048]{1,0:T(8,128)(2,1)S(1)} %bitcast.106, bf16[1152,2048]{1,0:T(8,128)(2,1)S(1)} %bitcast.108, bf16[2048,2048]{1,0:T(8,128)(2,1)} %constant_dynamic-update-slice_fusion.weight_ref), custom_call_target="tpu_custom_call" | custom-call | flops 9663676416 | bytes 18874368 | tf_op jit(solution)/shard_map/project/pallas_call | solution.py:212
  187.8 7.8 %temporal_attention.1 = (bf16[8,144,512]{2,1,0:T(8,128)(2,1)S(1)}, bf16[8,144,1536]{2,1,0:T(8,128)(2,1)S(1)}, f32[2,8,128]{2,1,0:T(8,128)S(1)}) custom-call(f32[128,1]{1,0:T(8,128)S(1)} %broadcast_in_dim_reshape.9.late_ref, f32[1,128]{1,0:T(1,128)S(1)} %broadcast_in_dim_reshape.8.early_ref, bf16[8,144,1536]{2,1,0:T(8,128)(2,1)S(1)} %bitcast.113, ...), custom_call_target="tpu_custom_call" | custom-call | flops 1207959552 | bytes 9437184 | tf_op jit(solution)/shard_map/temporal_attention/pallas_call | solution.py:108
  201.1 8.3 %weight_product.4 = (f32[256,2048]{1,0:T(8,128)}, f32[256,2048]{1,0:T(8,128)}) custom-call(s32[2]{0:T(128)} %pad_add_fusion.1.place_ref, bf16[2048,1152]{1,0:T(8,128)(2,1)} %copy-done.2, bf16[2048,1152]{1,0:T(8,128)(2,1)} %copy-done.3, bf16[1152,1536]{1,0:T(8,128)(2,1)} %bitcast.100, bf16[1152,512]{1,0:T(8,128)(2,1)} %bitcast.109), custom_call_target="tpu_custom_call" | custom-call | flops 1 | bytes 1 | tf_op jit(solution)/shard_map/weight_product/pallas_call | solution.py:178
  213.2 10.9 %norm_product.1 = (f32[8,72,2048]{2,1,0:T(8,128)S(1)}, f32[8,72,2048]{2,1,0:T(8,128)}) custom-call(bf16[1152,1536]{1,0:T(8,128)(2,1)S(1)} %bitcast.104, bf16[2048,2048]{1,0:T(8,128)(2,1)} %constant_dynamic-update-slice_fusion.weight_ref), custom_call_target="tpu_custom_call" | custom-call | flops 1 | bytes 1 | tf_op jit(solution)/shard_map/norm_product/pallas_call | solution.py:253
  226.9 8.3 %weight_product.5 = (f32[256,2048]{1,0:T(8,128)}, f32[256,2048]{1,0:T(8,128)}) custom-call(s32[2]{0:T(128)} %pad_add_fusion.2.place_ref, bf16[2048,1152]{1,0:T(8,128)(2,1)} %copy-done.2, bf16[2048,1152]{1,0:T(8,128)(2,1)} %copy-done.3, bf16[1152,1536]{1,0:T(8,128)(2,1)} %bitcast.101, bf16[1152,512]{1,0:T(8,128)(2,1)} %bitcast.110), custom_call_target="tpu_custom_call" | custom-call | flops 1 | bytes 1 | tf_op jit(solution)/shard_map/weight_product/pallas_call | solution.py:178
  240.7 7.7 %collective-permute-done.17 = f32[8,72,2048]{2,1,0:T(8,128)} collective-permute-done((f32[8,72,2048]{2,1,0:T(8,128)}, f32[8,72,2048]{2,1,0:T(8,128)}, u32[]{:S(2)}, u32[]{:S(2)}) %collective-permute-start.17) | collective-permute-done | bytes 4718624 | tf_op jit(solution)/shard_map/ppermute | solution.py:293
  248.5 5.4 %multiply_reduce_fusion = (f32[8,72]{1,0:T(8,128)S(1)}, f32[8,72]{1,0:T(8,128)S(1)}, f32[8,72,2048]{2,1,0:T(8,128)S(1)}) fusion(bf16[8,72,2048]{2,1,0:T(8,128)(2,1)S(1)} %get-tuple-element.120, f32[2048]{0:T(1024)S(1)} %copy-done.16, f32[8,72]{1,0:T(8,128)S(1)} %add_rsqrt_fusion, f32[8,2048]{1,0:T(8,128)S(1)} %fusion.22, f32[8,72,2048]{2,1,0:T(8,128)} %copy-done.7, ...), kind=kLoop, calls=%fused_computation.2 | loop fusion | flops 10615680 | bytes 16595712 | tf_op jit(solution)/shard_map/reduce_sum | solution.py:465
  257.6 8.3 %weight_product.6 = (f32[256,2048]{1,0:T(8,128)}, f32[256,2048]{1,0:T(8,128)}) custom-call(s32[2]{0:T(128)} %pad_add_fusion.3.place_ref, bf16[2048,1152]{1,0:T(8,128)(2,1)} %copy-done.2, bf16[2048,1152]{1,0:T(8,128)(2,1)} %copy-done.3, bf16[1152,1536]{1,0:T(8,128)(2,1)} %bitcast.102, bf16[1152,512]{1,0:T(8,128)(2,1)} %bitcast.111), custom_call_target="tpu_custom_call" | custom-call | flops 1 | bytes 1 | tf_op jit(solution)/shard_map/weight_product/pallas_call | solution.py:178
  276.1 8.3 %weight_product.7 = (f32[256,2048]{1,0:T(8,128)}, f32[256,2048]{1,0:T(8,128)}) custom-call(s32[2]{0:T(128)} %pad_add_fusion.4.place_ref, bf16[2048,1152]{1,0:T(8,128)(2,1)} %copy-done.2, bf16[2048,1152]{1,0:T(8,128)(2,1)} %copy-done.3, bf16[1152,1536]{1,0:T(8,128)(2,1)} %bitcast.103, bf16[1152,512]{1,0:T(8,128)(2,1)} %bitcast.112), custom_call_target="tpu_custom_call" | custom-call | flops 1 | bytes 1 | tf_op jit(solution)/shard_map/weight_product/pallas_call | solution.py:178
  295.8 7.0 %collective-permute-done.27 = f32[9,1024]{1,0:T(8,128)S(1)} collective-permute-done((f32[9,1024]{1,0:T(8,128)S(1)}, f32[9,1024]{1,0:T(8,128)S(1)}, u32[]{:S(2)}, u32[]{:S(2)}) %collective-permute-start.27) | collective-permute-done | bytes 36896 | tf_op jit(solution)/shard_map/ppermute | solution.py:290
  302.8 7.6 %collective-permute-done.23 = bf16[2,72,1024]{2,1,0:T(8,128)(2,1)S(1)} collective-permute-done((bf16[2,72,1024]{2,1,0:T(8,128)(2,1)S(1)}, bf16[2,72,1024]{2,1,0:T(8,128)(2,1)S(1)}, u32[]{:S(2)}, u32[]{:S(2)}) %collective-permute-start.23) | collective-permute-done | bytes 294944 | tf_op jit(solution)/shard_map/ppermute | solution.py:287
  310.5 16.2 %collective-permute-done.24 = bf16[2,72,1024]{2,1,0:T(8,128)(2,1)S(1)} collective-permute-done((bf16[2,72,1024]{2,1,0:T(8,128)(2,1)S(1)}, bf16[2,72,1024]{2,1,0:T(8,128)(2,1)S(1)}, u32[]{:S(2)}, u32[]{:S(2)}) %collective-permute-start.24) | collective-permute-done | bytes 294944 | tf_op jit(solution)/shard_map/ppermute | solution.py:287
  336.1 4.9 %collective-permute-done.30 = bf16[2,72,1024]{2,1,0:T(8,128)(2,1)S(1)} collective-permute-done((bf16[2,72,1024]{2,1,0:T(8,128)(2,1)S(1)}, bf16[2,72,1024]{2,1,0:T(8,128)(2,1)S(1)}, u32[]{:S(2)}, u32[]{:S(2)}) %collective-permute-start.30) | collective-permute-done | bytes 294944 | tf_op jit(solution)/shard_map/ppermute | solution.py:299
  342.5 4.8 %collective-permute-done.31 = bf16[2,72,1024]{2,1,0:T(8,128)(2,1)S(1)} collective-permute-done((bf16[2,72,1024]{2,1,0:T(8,128)(2,1)S(1)}, bf16[2,72,1024]{2,1,0:T(8,128)(2,1)S(1)}, u32[]{:S(2)}, u32[]{:S(2)}) %collective-permute-start.31) | collective-permute-done | bytes 294944 | tf_op jit(solution)/shard_map/ppermute | solution.py:299
  349.0 4.6 %collective-permute-done.32 = bf16[2,72,1024]{2,1,0:T(8,128)(2,1)S(1)} collective-permute-done((bf16[2,72,1024]{2,1,0:T(8,128)(2,1)S(1)}, bf16[2,72,1024]{2,1,0:T(8,128)(2,1)S(1)}, u32[]{:S(2)}, u32[]{:S(2)}) %collective-permute-start.32) | collective-permute-done | bytes 294944 | tf_op jit(solution)/shard_map/ppermute | solution.py:299
  354.2 4.8 %collective-permute-done.33 = bf16[2,72,1024]{2,1,0:T(8,128)(2,1)S(1)} collective-permute-done((bf16[2,72,1024]{2,1,0:T(8,128)(2,1)S(1)}, bf16[2,72,1024]{2,1,0:T(8,128)(2,1)S(1)}, u32[]{:S(2)}, u32[]{:S(2)}) %collective-permute-start.33) | collective-permute-done | bytes 294944 | tf_op jit(solution)/shard_map/ppermute | solution.py:299
  359.1 5.3 %collective-permute-done.34 = f32[9,1024]{1,0:T(8,128)S(1)} collective-permute-done((f32[9,1024]{1,0:T(8,128)S(1)}, f32[9,1024]{1,0:T(8,128)S(1)}, u32[]{:S(2)}, u32[]{:S(2)}) %collective-permute-start.34) | collective-permute-done | bytes 36896 | tf_op jit(solution)/shard_map/ppermute | solution.py:290
  (228 shorter events, 149.4 us)
Async XLA Ops:
  9.0 19.7 %collective-permute-start.3 = (bf16[296,1024]{1,0:T(8,128)(2,1)S(1)}, bf16[296,1024]{1,0:T(8,128)(2,1)}, u32[]{:S(2)}, u32[]{:S(2)}) collective-permute-start(bf16[296,1024]{1,0:T(8,128)(2,1)S(1)} %pad_maximum_fusion.13), channel_id=1, source_target_pairs={{0,8},{8,16},{16,24},{24,0},{1,9},{9,17},{17,25},{25,1},{2,10},{10... | collective-permute-start | bytes 1818632 | tf_op jit(solution)/shard_map/ppermute | solution.py:287
  14.0 62.6 %collective-permute-start.1 = (bf16[256,2048]{1,0:T(8,128)(2,1)}, bf16[256,2048]{1,0:T(8,128)(2,1)}, u32[]{:S(2)}, u32[]{:S(2)}) collective-permute-start(bf16[256,2048]{1,0:T(8,128)(2,1)} %pad_maximum_fusion.11), channel_id=1, source_target_pairs={{0,8},{8,16},{16,24},{24,0},{1,9},{9,17},{17,25},{25,1},{2,10},{10... | collective-permute-start | bytes 3145736 | tf_op jit(solution)/shard_map/ppermute | solution.py:287
  15.6 61.1 %collective-permute-start.4 = (bf16[256,2048]{1,0:T(8,128)(2,1)}, bf16[256,2048]{1,0:T(8,128)(2,1)}, u32[]{:S(2)}, u32[]{:S(2)}) collective-permute-start(bf16[256,2048]{1,0:T(8,128)(2,1)} %pad_maximum_fusion.11), channel_id=1, source_target_pairs={{0,4},{2,6},{4,0},{6,2},{1,5},{3,7},{5,1},{7,3},{8,12},{10,14},{12... | collective-permute-start | bytes 3145736 | tf_op jit(solution)/shard_map/ppermute | solution.py:296
  17.3 59.3 %collective-permute-start.2 = (bf16[296,1024]{1,0:T(8,128)(2,1)S(1)}, bf16[296,1024]{1,0:T(8,128)(2,1)}, u32[]{:S(2)}, u32[]{:S(2)}) collective-permute-start(bf16[296,1024]{1,0:T(8,128)(2,1)S(1)} %pad_maximum_fusion.12), channel_id=1, source_target_pairs={{0,16},{8,24},{16,0},{24,8},{1,17},{9,25},{17,1},{25,9},{2,18},{10... | collective-permute-start | bytes 1818632 | tf_op jit(solution)/shard_map/ppermute | solution.py:287
  28.7 47.9 %collective-permute-start.5 = (bf16[296,1024]{1,0:T(8,128)(2,1)}, bf16[296,1024]{1,0:T(8,128)(2,1)S(1)}, u32[]{:S(2)}, u32[]{:S(2)}) collective-permute-start(bf16[296,1024]{1,0:T(8,128)(2,1)} %collective-permute-done.3), channel_id=1, source_target_pairs={{0,1},{1,0},{2,3},{3,2},{4,5},{5,4},{6,7},{7,6},{8,9},{9,8},{10,11... | collective-permute-start | bytes 1818632 | tf_op jit(solution)/shard_map/ppermute | solution.py:299
  76.6 40.2 %collective-permute-start.6 = (bf16[256,2048]{1,0:T(8,128)(2,1)}, bf16[256,2048]{1,0:T(8,128)(2,1)}, u32[]{:S(2)}, u32[]{:S(2)}) collective-permute-start(bf16[256,2048]{1,0:T(8,128)(2,1)} %collective-permute-done.1), channel_id=1, source_target_pairs={{0,8},{8,16},{16,24},{24,0},{1,9},{9,17},{17,25},{25,1},{2,10},{10... | collective-permute-start | bytes 3145736 | tf_op jit(solution)/shard_map/ppermute | solution.py:287
  79.0 37.8 %collective-permute-start.8 = (bf16[256,2048]{1,0:T(8,128)(2,1)}, bf16[256,2048]{1,0:T(8,128)(2,1)S(1)}, u32[]{:S(2)}, u32[]{:S(2)}) collective-permute-start(bf16[256,2048]{1,0:T(8,128)(2,1)} %collective-permute-done.1), channel_id=1, source_target_pairs={{0,4},{2,6},{4,0},{6,2},{1,5},{3,7},{5,1},{7,3},{8,12},{10,14},{12... | collective-permute-start | bytes 3145736 | tf_op jit(solution)/shard_map/ppermute | solution.py:296
  80.8 36.0 %collective-permute-start.7 = (bf16[296,1024]{1,0:T(8,128)(2,1)S(1)}, bf16[296,1024]{1,0:T(8,128)(2,1)S(1)}, u32[]{:S(2)}, u32[]{:S(2)}) collective-permute-start(bf16[296,1024]{1,0:T(8,128)(2,1)S(1)} %pad_maximum_fusion.14), channel_id=1, source_target_pairs={{0,24},{8,0},{16,8},{24,16},{1,25},{9,1},{17,9},{25,17},{2,26},{10... | collective-permute-start | bytes 1818632 | tf_op jit(solution)/shard_map/ppermute | solution.py:287
  118.5 26.9 %collective-permute-start.10 = (bf16[256,2048]{1,0:T(8,128)(2,1)}, bf16[256,2048]{1,0:T(8,128)(2,1)}, u32[]{:S(2)}, u32[]{:S(2)}) collective-permute-start(bf16[256,2048]{1,0:T(8,128)(2,1)} %collective-permute-done.6), channel_id=1, source_target_pairs={{0,8},{8,16},{16,24},{24,0},{1,9},{9,17},{17,25},{25,1},{2,10},{10... | collective-permute-start | bytes 3145736 | tf_op jit(solution)/shard_map/ppermute | solution.py:287
  119.0 26.4 %collective-permute-start.12 = (bf16[256,2048]{1,0:T(8,128)(2,1)}, bf16[256,2048]{1,0:T(8,128)(2,1)}, u32[]{:S(2)}, u32[]{:S(2)}) collective-permute-start(bf16[256,2048]{1,0:T(8,128)(2,1)} %collective-permute-done.6), channel_id=1, source_target_pairs={{0,4},{2,6},{4,0},{6,2},{1,5},{3,7},{5,1},{7,3},{8,12},{10,14},{12... | collective-permute-start | bytes 3145736 | tf_op jit(solution)/shard_map/ppermute | solution.py:296
  147.8 25.3 %collective-permute-start.15 = (bf16[256,2048]{1,0:T(8,128)(2,1)}, bf16[256,2048]{1,0:T(8,128)(2,1)S(1)}, u32[]{:S(2)}, u32[]{:S(2)}) collective-permute-start(bf16[256,2048]{1,0:T(8,128)(2,1)} %collective-permute-done.10), channel_id=1, source_target_pairs={{0,4},{2,6},{4,0},{6,2},{1,5},{3,7},{5,1},{7,3},{8,12},{10,14},{12... | collective-permute-start | bytes 3145736 | tf_op jit(solution)/shard_map/ppermute | solution.py:296
  211.6 26.8 %collective-permute-start.16 = (f16[264,2048]{1,0:T(8,128)(2,1)S(1)}, f16[264,2048]{1,0:T(8,128)(2,1)S(1)}, u32[]{:S(2)}, u32[]{:S(2)}) collective-permute-start(f16[264,2048]{1,0:T(8,128)(2,1)S(1)} %pad_maximum_fusion.7), channel_id=1, source_target_pairs={{0,4},{2,6},{4,0},{6,2},{1,5},{3,7},{5,1},{7,3},{8,12},{10,14},{12... | collective-permute-start | bytes 3244040 | tf_op jit(solution)/shard_map/ppermute | solution.py:296
  240.2 29.4 %collective-permute-start.21 = (f16[264,2048]{1,0:T(8,128)(2,1)}, f16[264,2048]{1,0:T(8,128)(2,1)}, u32[]{:S(2)}, u32[]{:S(2)}) collective-permute-start(f16[264,2048]{1,0:T(8,128)(2,1)} %pad_maximum_fusion.6), channel_id=1, source_target_pairs={{0,4},{2,6},{4,0},{6,2},{1,5},{3,7},{5,1},{7,3},{8,12},{10,14},{12... | collective-permute-start | bytes 3244040 | tf_op jit(solution)/shard_map/ppermute | solution.py:296
  240.7 28.9 %collective-permute-start.22 = (f16[264,2048]{1,0:T(8,128)(2,1)}, f16[264,2048]{1,0:T(8,128)(2,1)}, u32[]{:S(2)}, u32[]{:S(2)}) collective-permute-start(f16[264,2048]{1,0:T(8,128)(2,1)} %pad_maximum_fusion.8), channel_id=1, source_target_pairs={{0,8},{8,16},{16,24},{24,0},{1,9},{9,17},{17,25},{25,1},{2,10},{10... | collective-permute-start | bytes 3244040 | tf_op jit(solution)/shard_map/ppermute | solution.py:287
  257.1 29.4 %collective-permute-start.19 = (f16[8,72,1024]{2,1,0:T(8,128)(2,1)S(1)}, f16[8,72,1024]{2,1,0:T(8,128)(2,1)S(1)}, u32[]{:S(2)}, u32[]{:S(2)}) collective-permute-start(f16[8,72,1024]{2,1,0:T(8,128)(2,1)S(1)} %divide_convert_fusion), channel_id=1, source_target_pairs={{0,1},{1,0},{2,3},{3,2},{4,5},{5,4},{6,7},{7,6},{8,9},{9,8},{10,11... | collective-permute-start | bytes 3538952 | tf_op jit(solution)/shard_map/ppermute | solution.py:299
  269.1 33.7 %collective-permute-start.18 = (f16[264,2048]{1,0:T(8,128)(2,1)}, f16[264,2048]{1,0:T(8,128)(2,1)}, u32[]{:S(2)}, u32[]{:S(2)}) collective-permute-start(f16[264,2048]{1,0:T(8,128)(2,1)} %pad_maximum_fusion.5), channel_id=1, source_target_pairs={{0,4},{2,6},{4,0},{6,2},{1,5},{3,7},{5,1},{7,3},{8,12},{10,14},{12... | collective-permute-start | bytes 3244040 | tf_op jit(solution)/shard_map/ppermute | solution.py:296
  274.0 52.7 %collective-permute-start.28 = (f16[264,2048]{1,0:T(8,128)(2,1)}, f16[264,2048]{1,0:T(8,128)(2,1)}, u32[]{:S(2)}, u32[]{:S(2)}) collective-permute-start(f16[264,2048]{1,0:T(8,128)(2,1)} %pad_maximum_fusion.9), channel_id=1, source_target_pairs={{0,8},{8,16},{16,24},{24,0},{1,9},{9,17},{17,25},{25,1},{2,10},{10... | collective-permute-start | bytes 3244040 | tf_op jit(solution)/shard_map/ppermute | solution.py:287
  291.3 19.2 %collective-permute-start.23 = (bf16[2,72,1024]{2,1,0:T(8,128)(2,1)S(1)}, bf16[2,72,1024]{2,1,0:T(8,128)(2,1)S(1)}, u32[]{:S(2)}, u32[]{:S(2)}) collective-permute-start(bf16[2,72,1024]{2,1,0:T(8,128)(2,1)S(1)} %get-tuple-element.137), channel_id=1, source_target_pairs={{0,24},{8,0},{16,8},{24,16},{1,25},{9,1},{17,9},{25,17},{2,26},{10... | collective-permute-start | bytes 884744 | tf_op jit(solution)/shard_map/ppermute | solution.py:287
  295.2 31.5 %collective-permute-start.24 = (bf16[2,72,1024]{2,1,0:T(8,128)(2,1)S(1)}, bf16[2,72,1024]{2,1,0:T(8,128)(2,1)S(1)}, u32[]{:S(2)}, u32[]{:S(2)}) collective-permute-start(bf16[2,72,1024]{2,1,0:T(8,128)(2,1)S(1)} %get-tuple-element.136), channel_id=1, source_target_pairs={{0,16},{8,24},{16,0},{24,8},{1,17},{9,25},{17,1},{25,9},{2,18},{10... | collective-permute-start | bytes 884744 | tf_op jit(solution)/shard_map/ppermute | solution.py:287
  302.8 23.9 %collective-permute-start.25 = (bf16[2,72,1024]{2,1,0:T(8,128)(2,1)S(1)}, bf16[2,72,1024]{2,1,0:T(8,128)(2,1)S(1)}, u32[]{:S(2)}, u32[]{:S(2)}) collective-permute-start(bf16[2,72,1024]{2,1,0:T(8,128)(2,1)S(1)} %get-tuple-element.135), channel_id=1, source_target_pairs={{0,8},{8,16},{16,24},{24,0},{1,9},{9,17},{17,25},{25,1},{2,10},{10... | collective-permute-start | bytes 884744 | tf_op jit(solution)/shard_map/ppermute | solution.py:287
  333.1 31.3 %collective-permute-start.35 = (f16[264,2048]{1,0:T(8,128)(2,1)S(1)}, f16[264,2048]{1,0:T(8,128)(2,1)S(1)}, u32[]{:S(2)}, u32[]{:S(2)}) collective-permute-start(f16[264,2048]{1,0:T(8,128)(2,1)S(1)} %pad_maximum_fusion.4), channel_id=1, source_target_pairs={{0,4},{2,6},{4,0},{6,2},{1,5},{3,7},{5,1},{7,3},{8,12},{10,14},{12... | collective-permute-start | bytes 3244040 | tf_op jit(solution)/shard_map/ppermute | solution.py:296
  334.6 29.8 %collective-permute-start.29 = (f16[264,2048]{1,0:T(8,128)(2,1)}, f16[264,2048]{1,0:T(8,128)(2,1)S(1)}, u32[]{:S(2)}, u32[]{:S(2)}) collective-permute-start(f16[264,2048]{1,0:T(8,128)(2,1)} %pad_maximum_fusion.10), channel_id=1, source_target_pairs={{0,8},{8,16},{16,24},{24,0},{1,9},{9,17},{17,25},{25,1},{2,10},{10... | collective-permute-start | bytes 3244040 | tf_op jit(solution)/shard_map/ppermute | solution.py:287
  334.6 19.0 %collective-permute-start.32 = (bf16[2,72,1024]{2,1,0:T(8,128)(2,1)S(1)}, bf16[2,72,1024]{2,1,0:T(8,128)(2,1)S(1)}, u32[]{:S(2)}, u32[]{:S(2)}) collective-permute-start(bf16[2,72,1024]{2,1,0:T(8,128)(2,1)S(1)} %collective-permute-done.24), channel_id=1, source_target_pairs={{0,1},{1,0},{2,3},{3,2},{4,5},{5,4},{6,7},{7,6},{8,9},{9,8},{10,11... | collective-permute-start | bytes 884744 | tf_op jit(solution)/shard_map/ppermute | solution.py:299
  341.0 18.0 %collective-permute-start.33 = (bf16[2,72,1024]{2,1,0:T(8,128)(2,1)S(1)}, bf16[2,72,1024]{2,1,0:T(8,128)(2,1)S(1)}, u32[]{:S(2)}, u32[]{:S(2)}) collective-permute-start(bf16[2,72,1024]{2,1,0:T(8,128)(2,1)S(1)} %collective-permute-done.25), channel_id=1, source_target_pairs={{0,1},{1,0},{2,3},{3,2},{4,5},{5,4},{6,7},{7,6},{8,9},{9,8},{10,11... | collective-permute-start | bytes 884744 | tf_op jit(solution)/shard_map/ppermute | solution.py:299
  (35 other events, 375.4 us)

commit v9 on v8

--- a/solution.py
+++ b/solution.py
@@ -294,6 +294,10 @@
 
     def swap_y(value):
         return lax.ppermute(value, "space", [(i, i ^ 2) for i in range(spaces)])
+
+    def swap_xy(value):
+        pairs_xy = [(i, ((i // 2) ^ 2) * 2 + (i % 2 ^ 1)) for i in range(2 * spaces)]
+        return lax.ppermute(value, ("space", "tensor"), pairs_xy)
 
     def swap_x(value):
         return lax.ppermute(value, "tensor", [(0, 1), (1, 0)])
@@ -444,10 +448,10 @@
         near, far = weight_product(
             places, block_rows, normed_t, upstream_t, flat_merged, flat_mixed
         )
-        return near, pack(far, own_bound)
+        return near, far
 
     def chip_sum(k, earlier):
-        term, bound = unpack(after(swap_y(weight_parts[k][1]), earlier))
+        term, bound = unpack(after(swap_y(away[k]), earlier))
         return weight_parts[k][0] + term, bound + own_bound
 
     def ring_sum(k, arriving, earlier):
@@ -456,11 +460,13 @@
         return total + term, bound + ring_bound
 
     weight_parts = [weight_part(0, flat_merged)]
+    away = [pack(weight_parts[0][1], own_bound)]
     norm_here, norm_away = norm_product(
-        after(flat_merged, weight_parts[0][1]), weights, frames
+        after(flat_merged, away[0]), weights, frames
     )
     weight_parts.append(weight_part(1, norm_away))
-    payload = pack(*chip_sum(0, weight_parts[1][1]))
+    away.append(pack(weight_parts[1][1], own_bound))
+    payload = pack(*chip_sum(0, away[1]))
     partial_norm = norm_here + swap_core(after(norm_away, payload))
     row_dot = jnp.sum(partial_norm * gain * (hidden * inverse), -1, keepdims=True)
     if tensors == 2:
@@ -476,7 +482,8 @@
         sent = partial_norm
     weight_parts.append(weight_part(2, sent))
     payload = pack(*ring_sum(1, ring(payload, 1), weight_parts[2][1]))
-    weight_parts.append(weight_part(3, payload))
+    away.append(pack(after(weight_parts[2][1], payload), own_bound))
+    weight_parts.append(weight_part(3, away[2]))
     if tensors == 2:
         x_terms, row_terms = after((x_terms, row_terms), weight_parts[3][1])
         row_dot = row_dot + row_terms[..., :1]
@@ -493,6 +500,7 @@
     small = jnp.concatenate([action_term, gain_term[None, :]], 0)
     small = small + swap_core(small)
     small = small + swap_z(small, 1)
+    away.append(pack(after(weight_parts[3][1], grad_rows), own_bound))
     returned = [grad_rows[:local_frames]]
     for k in range(1, depth):
         returned.append(
@@ -500,9 +508,10 @@
         )
 
     for k in range(2, depth - 1):
-        payload = pack(*ring_sum(k, ring(payload, 1), (returned[1:], small)))
+        payload = pack(*ring_sum(k, ring(payload, 1), (returned[1:], small, away[-1])))
         if k + 2 < depth:
             weight_parts.append(weight_part(k + 2, payload))
+            away.append(pack(weight_parts[-1][1], own_bound))
     grad_inputs = jnp.zeros(inputs.shape, jnp.bfloat16)
     for k in range(depth):
         piece = after(returned[k], payload)
@@ -518,7 +527,10 @@
     arriving, grad_inputs, small = lax.optimization_barrier(
         (ring(payload, 1), grad_inputs, small)
     )
-    small = join_x(small + swap_y(small))
+    if tensors == 2:
+        small = join_x(small + swap_y(small), swap_x(small) + swap_xy(small))
+    else:
+        small = join_x(small + swap_y(small))
     total = chip_sum(depth - 1, arriving)[0] + unpack(arriving)[0]
     mine = lax.dynamic_slice_in_dim(total, core * shard_rows, shard_rows, 0)
     other = swap_core(lax.dynamic_slice_in_dim(total, (1 - core) * shard_rows, shard_rows, 0))

time: 380 us -> 392 us (1.032)
  waiting for transfers between devices: 164 us -> 184 us
  other arithmetic: 56.2 us -> 50.6 us
    ppermute x2, waiting for transfers between devices: 12.3 us -> 28.3 us  [swap_z(): return lax.ppermute(value, 'frame', [(i, i ^ bit) for i in range(depth)])]
    another operation x11, other arithmetic: 12.7 us -> 7.71 us
    unnamed x39 -> x43, local copies, waits for them, and re-layouts: 12.4 us -> 12.4 us
  transfers between devices with their start and end apart: 39 -> 40, of which waited for: 20 -> 23; matrix products, arithmetic and copies ran while one was open for 18% -> 16% of each run, Pallas kernels for 11% -> 10%
where the time goes in v9:
time: 392 us; the launch traced here: 390 us
  waiting for transfers between devices  184 us (47%)
  Pallas kernels  70.6 us (18%)
  other arithmetic  50.6 us (13%)
  local copies, waits for them, and re-layouts  44.2 us (11%)
  starting transfers between devices  37.3 us (10%)
    ppermute x12, waiting for transfers between devices, ring(): lax.ppermute(value, 'frame', [(i, (i + shift) % depth) for i in range(dep...  97.8 us
    ppermute x10, waiting for transfers between devices, swap_x(): return lax.ppermute(value, 'tensor', [(0, 1), (1, 0)])  40.6 us
    pallas_call x4, Pallas kernels, weight_product(): pl.pallas_call(weight_kernel, grid_spec=pltpu.PrefetchScalarGridSpec(num_...  33.5 us
    ppermute x2, waiting for transfers between devices, swap_z(): return lax.ppermute(value, 'frame', [(i, i ^ bit) for i in range(depth)])  28.3 us
    ppermute x12, starting transfers between devices, ring(): lax.ppermute(value, 'frame', [(i, (i + shift) % depth) for i in range(dep...  14.2 us
    dynamic_update_slice x7, local copies, waits for them, and re-layouts, settle(): return lax.dynamic_update_slice(weights, arrived, (start, 0))  13.8 us
    pallas_call x1, Pallas kernels, project(): pl.pallas_call(project_kernel, grid=(4, 2), in_specs=[pl.BlockSpec((rows,...  13.6 us
    unnamed x43, local copies, waits for them, and re-layouts  12.4 us
  transfers between devices with their start and end apart: 40, of which 23 were waited for; matrix products, arithmetic and copies ran while one was open for 16% of the time, Pallas kernels for 10%

profile of v9, /device:TPU:0, one launch (start us, length us, event | category | flops | bytes accessed | tf_op | source)
XLA Modules:
  0.0 390.4 jit_solution(11539812651095989595)
XLA Ops:
  18.6 10.1 %collective-permute-done.3 = bf16[296,1024]{1,0:T(8,128)(2,1)} collective-permute-done((bf16[296,1024]{1,0:T(8,128)(2,1)S(1)}, bf16[296,1024]{1,0:T(8,128)(2,1)}, u32[]{:S(2)}, u32[]{:S(2)}) %collective-permute-start.3) | collective-permute-done | bytes 606240 | tf_op jit(solution)/shard_map/ppermute | solution.py:287
  32.4 4.4 %broadcast_in_dim.62 = bf16[2048,2048]{1,0:T(8,128)(2,1)} broadcast(bf16[]{:T(256)} %constant.276.clone.1), dimensions={} | broadcast | bytes 8388610 | tf_op jit(solution)/shard_map/broadcast_in_dim | solution.py:365
  37.8 38.8 %collective-permute-done.2 = bf16[296,1024]{1,0:T(8,128)(2,1)} collective-permute-done((bf16[296,1024]{1,0:T(8,128)(2,1)S(1)}, bf16[296,1024]{1,0:T(8,128)(2,1)}, u32[]{:S(2)}, u32[]{:S(2)}) %collective-permute-start.2) | collective-permute-done | bytes 606240 | tf_op jit(solution)/shard_map/ppermute | solution.py:287
  92.8 6.9 %collective-permute-done.9 = bf16[296,1024]{1,0:T(8,128)(2,1)S(1)} collective-permute-done((bf16[296,1024]{1,0:T(8,128)(2,1)}, bf16[296,1024]{1,0:T(8,128)(2,1)S(1)}, u32[]{:S(2)}, u32[]{:S(2)}) %collective-permute-start.9) | collective-permute-done | bytes 606240 | tf_op jit(solution)/shard_map/ppermute | solution.py:303
  101.0 15.8 %collective-permute-done.7 = bf16[296,1024]{1,0:T(8,128)(2,1)S(1)} collective-permute-done((bf16[296,1024]{1,0:T(8,128)(2,1)S(1)}, bf16[296,1024]{1,0:T(8,128)(2,1)S(1)}, u32[]{:S(2)}, u32[]{:S(2)}) %collective-permute-start.7) | collective-permute-done | bytes 606240 | tf_op jit(solution)/shard_map/ppermute | solution.py:287
  124.2 8.3 %collective-permute-done.11 = bf16[296,1024]{1,0:T(8,128)(2,1)S(1)} collective-permute-done((bf16[296,1024]{1,0:T(8,128)(2,1)S(1)}, bf16[296,1024]{1,0:T(8,128)(2,1)S(1)}, u32[]{:S(2)}, u32[]{:S(2)}) %collective-permute-start.11) | collective-permute-done | bytes 606240 | tf_op jit(solution)/shard_map/ppermute | solution.py:303
  137.5 7.9 %collective-permute-done.10 = bf16[256,2048]{1,0:T(8,128)(2,1)} collective-permute-done((bf16[256,2048]{1,0:T(8,128)(2,1)}, bf16[256,2048]{1,0:T(8,128)(2,1)}, u32[]{:S(2)}, u32[]{:S(2)}) %collective-permute-start.10) | collective-permute-done | bytes 1048608 | tf_op jit(solution)/shard_map/ppermute | solution.py:287
  174.2 13.6 %project.1 = (bf16[1152,1536]{1,0:T(8,128)(2,1)S(1)}, bf16[1152,512]{1,0:T(8,128)(2,1)S(1)}) custom-call(bf16[1152,2048]{1,0:T(8,128)(2,1)S(1)} %bitcast.106, bf16[1152,2048]{1,0:T(8,128)(2,1)S(1)} %bitcast.108, bf16[2048,2048]{1,0:T(8,128)(2,1)} %constant_dynamic-update-slice_fusion.weight_ref), custom_call_target="tpu_custom_call" | custom-call | flops 9663676416 | bytes 18874368 | tf_op jit(solution)/shard_map/project/pallas_call | solution.py:212
  187.8 7.8 %temporal_attention.1 = (bf16[8,144,512]{2,1,0:T(8,128)(2,1)S(1)}, bf16[8,144,1536]{2,1,0:T(8,128)(2,1)S(1)}, f32[2,8,128]{2,1,0:T(8,128)S(1)}) custom-call(f32[128,1]{1,0:T(8,128)S(1)} %broadcast_in_dim_reshape.9.late_ref, f32[1,128]{1,0:T(1,128)S(1)} %broadcast_in_dim_reshape.8.early_ref, bf16[8,144,1536]{2,1,0:T(8,128)(2,1)S(1)} %bitcast.113, ...), custom_call_target="tpu_custom_call" | custom-call | flops 1207959552 | bytes 9437184 | tf_op jit(solution)/shard_map/temporal_attention/pallas_call | solution.py:108
  201.1 8.4 %weight_product.4 = (f32[256,2048]{1,0:T(8,128)}, f32[256,2048]{1,0:T(8,128)}) custom-call(s32[2]{0:T(128)} %pad_add_fusion.1.place_ref, bf16[2048,1152]{1,0:T(8,128)(2,1)} %copy-done.2, bf16[2048,1152]{1,0:T(8,128)(2,1)} %copy-done.3, bf16[1152,1536]{1,0:T(8,128)(2,1)} %bitcast.100, bf16[1152,512]{1,0:T(8,128)(2,1)} %bitcast.109), custom_call_target="tpu_custom_call" | custom-call | flops 1 | bytes 1 | tf_op jit(solution)/shard_map/weight_product/pallas_call | solution.py:178
  213.3 11.0 %norm_product.1 = (f32[8,72,2048]{2,1,0:T(8,128)S(1)}, f32[8,72,2048]{2,1,0:T(8,128)}) custom-call(bf16[1152,1536]{1,0:T(8,128)(2,1)S(1)} %bitcast.104, bf16[2048,2048]{1,0:T(8,128)(2,1)} %constant_dynamic-update-slice_fusion.weight_ref), custom_call_target="tpu_custom_call" | custom-call | flops 1 | bytes 1 | tf_op jit(solution)/shard_map/norm_product/pallas_call | solution.py:253
  227.0 8.3 %weight_product.5 = (f32[256,2048]{1,0:T(8,128)}, f32[256,2048]{1,0:T(8,128)}) custom-call(s32[2]{0:T(128)} %pad_add_fusion.2.place_ref, bf16[2048,1152]{1,0:T(8,128)(2,1)} %copy-done.2, bf16[2048,1152]{1,0:T(8,128)(2,1)} %copy-done.3, bf16[1152,1536]{1,0:T(8,128)(2,1)} %bitcast.101, bf16[1152,512]{1,0:T(8,128)(2,1)} %bitcast.110), custom_call_target="tpu_custom_call" | custom-call | flops 1 | bytes 1 | tf_op jit(solution)/shard_map/weight_product/pallas_call | solution.py:178
  240.9 7.8 %collective-permute-done.17 = f32[8,72,2048]{2,1,0:T(8,128)} collective-permute-done((f32[8,72,2048]{2,1,0:T(8,128)}, f32[8,72,2048]{2,1,0:T(8,128)}, u32[]{:S(2)}, u32[]{:S(2)}) %collective-permute-start.17) | collective-permute-done | bytes 4718624 | tf_op jit(solution)/shard_map/ppermute | solution.py:293
  248.6 5.4 %multiply_reduce_fusion = (f32[8,72]{1,0:T(8,128)S(1)}, f32[8,72]{1,0:T(8,128)S(1)}, f32[8,72,2048]{2,1,0:T(8,128)S(1)}) fusion(bf16[8,72,2048]{2,1,0:T(8,128)(2,1)S(1)} %get-tuple-element.124, f32[2048]{0:T(1024)S(1)} %copy-done.18, f32[8,72]{1,0:T(8,128)S(1)} %add_rsqrt_fusion, f32[8,2048]{1,0:T(8,128)S(1)} %fusion.22, f32[8,72,2048]{2,1,0:T(8,128)} %copy-done.7, ...), kind=kLoop, calls=%fused_computation.2 | loop fusion | flops 10615680 | bytes 16595712 | tf_op jit(solution)/shard_map/reduce_sum | solution.py:471
  258.8 8.4 %weight_product.6 = (f32[256,2048]{1,0:T(8,128)}, f32[256,2048]{1,0:T(8,128)}) custom-call(s32[2]{0:T(128)} %pad_add_fusion.3.place_ref, bf16[2048,1152]{1,0:T(8,128)(2,1)} %copy-done.2, bf16[2048,1152]{1,0:T(8,128)(2,1)} %copy-done.3, bf16[1152,1536]{1,0:T(8,128)(2,1)} %bitcast.102, bf16[1152,512]{1,0:T(8,128)(2,1)} %bitcast.111), custom_call_target="tpu_custom_call" | custom-call | flops 1 | bytes 1 | tf_op jit(solution)/shard_map/weight_product/pallas_call | solution.py:178
  275.7 8.4 %weight_product.7 = (f32[256,2048]{1,0:T(8,128)}, f32[256,2048]{1,0:T(8,128)}) custom-call(s32[2]{0:T(128)} %pad_add_fusion.4.place_ref, bf16[2048,1152]{1,0:T(8,128)(2,1)} %copy-done.2, bf16[2048,1152]{1,0:T(8,128)(2,1)} %copy-done.3, bf16[1152,1536]{1,0:T(8,128)(2,1)} %bitcast.103, bf16[1152,512]{1,0:T(8,128)(2,1)} %bitcast.112), custom_call_target="tpu_custom_call" | custom-call | flops 1 | bytes 1 | tf_op jit(solution)/shard_map/weight_product/pallas_call | solution.py:178
  295.5 24.2 %collective-permute-done.27 = f32[9,1024]{1,0:T(8,128)S(1)} collective-permute-done((f32[9,1024]{1,0:T(8,128)S(1)}, f32[9,1024]{1,0:T(8,128)S(1)}, u32[]{:S(2)}, u32[]{:S(2)}) %collective-permute-start.27) | collective-permute-done | bytes 36896 | tf_op jit(solution)/shard_map/ppermute | solution.py:290
  320.2 6.5 %collective-permute-done.23 = bf16[2,72,1024]{2,1,0:T(8,128)(2,1)S(1)} collective-permute-done((bf16[2,72,1024]{2,1,0:T(8,128)(2,1)S(1)}, bf16[2,72,1024]{2,1,0:T(8,128)(2,1)S(1)}, u32[]{:S(2)}, u32[]{:S(2)}) %collective-permute-start.23) | collective-permute-done | bytes 294944 | tf_op jit(solution)/shard_map/ppermute | solution.py:287
  326.8 16.8 %collective-permute-done.24 = bf16[2,72,1024]{2,1,0:T(8,128)(2,1)S(1)} collective-permute-done((bf16[2,72,1024]{2,1,0:T(8,128)(2,1)S(1)}, bf16[2,72,1024]{2,1,0:T(8,128)(2,1)S(1)}, u32[]{:S(2)}, u32[]{:S(2)}) %collective-permute-start.24) | collective-permute-done | bytes 294944 | tf_op jit(solution)/shard_map/ppermute | solution.py:287
  347.8 6.8 %collective-permute-done.30 = bf16[2,72,1024]{2,1,0:T(8,128)(2,1)} collective-permute-done((bf16[2,72,1024]{2,1,0:T(8,128)(2,1)S(1)}, bf16[2,72,1024]{2,1,0:T(8,128)(2,1)}, u32[]{:S(2)}, u32[]{:S(2)}) %collective-permute-start.30) | collective-permute-done | bytes 294944 | tf_op jit(solution)/shard_map/ppermute | solution.py:303
  356.2 4.8 %collective-permute-done.31 = bf16[2,72,1024]{2,1,0:T(8,128)(2,1)} collective-permute-done((bf16[2,72,1024]{2,1,0:T(8,128)(2,1)S(1)}, bf16[2,72,1024]{2,1,0:T(8,128)(2,1)}, u32[]{:S(2)}, u32[]{:S(2)}) %collective-permute-start.31) | collective-permute-done | bytes 294944 | tf_op jit(solution)/shard_map/ppermute | solution.py:303
  362.0 5.2 %collective-permute-done.32 = bf16[2,72,1024]{2,1,0:T(8,128)(2,1)S(1)} collective-permute-done((bf16[2,72,1024]{2,1,0:T(8,128)(2,1)S(1)}, bf16[2,72,1024]{2,1,0:T(8,128)(2,1)S(1)}, u32[]{:S(2)}, u32[]{:S(2)}) %collective-permute-start.32) | collective-permute-done | bytes 294944 | tf_op jit(solution)/shard_map/ppermute | solution.py:303
  367.8 4.8 %collective-permute-done.33 = bf16[2,72,1024]{2,1,0:T(8,128)(2,1)S(1)} collective-permute-done((bf16[2,72,1024]{2,1,0:T(8,128)(2,1)S(1)}, bf16[2,72,1024]{2,1,0:T(8,128)(2,1)S(1)}, u32[]{:S(2)}, u32[]{:S(2)}) %collective-permute-start.33) | collective-permute-done | bytes 294944 | tf_op jit(solution)/shard_map/ppermute | solution.py:303
  372.7 4.1 %collective-permute-done.34 = f32[9,1024]{1,0:T(8,128)S(1)} collective-permute-done((f32[9,1024]{1,0:T(8,128)S(1)}, f32[9,1024]{1,0:T(8,128)S(1)}, u32[]{:S(2)}, u32[]{:S(2)}) %collective-permute-start.34) | collective-permute-done | bytes 36896 | tf_op jit(solution)/shard_map/ppermute | solution.py:290
  (233 shorter events, 142.5 us)
Async XLA Ops:
  9.0 19.7 %collective-permute-start.3 = (bf16[296,1024]{1,0:T(8,128)(2,1)S(1)}, bf16[296,1024]{1,0:T(8,128)(2,1)}, u32[]{:S(2)}, u32[]{:S(2)}) collective-permute-start(bf16[296,1024]{1,0:T(8,128)(2,1)S(1)} %pad_maximum_fusion.13), channel_id=1, source_target_pairs={{0,8},{8,16},{16,24},{24,0},{1,9},{9,17},{17,25},{25,1},{2,10},{10... | collective-permute-start | bytes 1818632 | tf_op jit(solution)/shard_map/ppermute | solution.py:287
  14.0 62.6 %collective-permute-start.1 = (bf16[256,2048]{1,0:T(8,128)(2,1)}, bf16[256,2048]{1,0:T(8,128)(2,1)}, u32[]{:S(2)}, u32[]{:S(2)}) collective-permute-start(bf16[256,2048]{1,0:T(8,128)(2,1)} %pad_maximum_fusion.11), channel_id=1, source_target_pairs={{0,8},{8,16},{16,24},{24,0},{1,9},{9,17},{17,25},{25,1},{2,10},{10... | collective-permute-start | bytes 3145736 | tf_op jit(solution)/shard_map/ppermute | solution.py:287
  15.6 61.1 %collective-permute-start.4 = (bf16[256,2048]{1,0:T(8,128)(2,1)}, bf16[256,2048]{1,0:T(8,128)(2,1)}, u32[]{:S(2)}, u32[]{:S(2)}) collective-permute-start(bf16[256,2048]{1,0:T(8,128)(2,1)} %pad_maximum_fusion.11), channel_id=1, source_target_pairs={{0,4},{2,6},{4,0},{6,2},{1,5},{3,7},{5,1},{7,3},{8,12},{10,14},{12... | collective-permute-start | bytes 3145736 | tf_op jit(solution)/shard_map/ppermute | solution.py:296
  17.3 59.3 %collective-permute-start.2 = (bf16[296,1024]{1,0:T(8,128)(2,1)S(1)}, bf16[296,1024]{1,0:T(8,128)(2,1)}, u32[]{:S(2)}, u32[]{:S(2)}) collective-permute-start(bf16[296,1024]{1,0:T(8,128)(2,1)S(1)} %pad_maximum_fusion.12), channel_id=1, source_target_pairs={{0,16},{8,24},{16,0},{24,8},{1,17},{9,25},{17,1},{25,9},{2,18},{10... | collective-permute-start | bytes 1818632 | tf_op jit(solution)/shard_map/ppermute | solution.py:287
  28.7 47.9 %collective-permute-start.5 = (bf16[296,1024]{1,0:T(8,128)(2,1)}, bf16[296,1024]{1,0:T(8,128)(2,1)S(1)}, u32[]{:S(2)}, u32[]{:S(2)}) collective-permute-start(bf16[296,1024]{1,0:T(8,128)(2,1)} %collective-permute-done.3), channel_id=1, source_target_pairs={{0,1},{1,0},{2,3},{3,2},{4,5},{5,4},{6,7},{7,6},{8,9},{9,8},{10,11... | collective-permute-start | bytes 1818632 | tf_op jit(solution)/shard_map/ppermute | solution.py:303
  76.6 40.2 %collective-permute-start.6 = (bf16[256,2048]{1,0:T(8,128)(2,1)}, bf16[256,2048]{1,0:T(8,128)(2,1)}, u32[]{:S(2)}, u32[]{:S(2)}) collective-permute-start(bf16[256,2048]{1,0:T(8,128)(2,1)} %collective-permute-done.1), channel_id=1, source_target_pairs={{0,8},{8,16},{16,24},{24,0},{1,9},{9,17},{17,25},{25,1},{2,10},{10... | collective-permute-start | bytes 3145736 | tf_op jit(solution)/shard_map/ppermute | solution.py:287
  79.0 37.8 %collective-permute-start.8 = (bf16[256,2048]{1,0:T(8,128)(2,1)}, bf16[256,2048]{1,0:T(8,128)(2,1)S(1)}, u32[]{:S(2)}, u32[]{:S(2)}) collective-permute-start(bf16[256,2048]{1,0:T(8,128)(2,1)} %collective-permute-done.1), channel_id=1, source_target_pairs={{0,4},{2,6},{4,0},{6,2},{1,5},{3,7},{5,1},{7,3},{8,12},{10,14},{12... | collective-permute-start | bytes 3145736 | tf_op jit(solution)/shard_map/ppermute | solution.py:296
  80.8 36.0 %collective-permute-start.7 = (bf16[296,1024]{1,0:T(8,128)(2,1)S(1)}, bf16[296,1024]{1,0:T(8,128)(2,1)S(1)}, u32[]{:S(2)}, u32[]{:S(2)}) collective-permute-start(bf16[296,1024]{1,0:T(8,128)(2,1)S(1)} %pad_maximum_fusion.14), channel_id=1, source_target_pairs={{0,24},{8,0},{16,8},{24,16},{1,25},{9,1},{17,9},{25,17},{2,26},{10... | collective-permute-start | bytes 1818632 | tf_op jit(solution)/shard_map/ppermute | solution.py:287
  118.5 26.9 %collective-permute-start.10 = (bf16[256,2048]{1,0:T(8,128)(2,1)}, bf16[256,2048]{1,0:T(8,128)(2,1)}, u32[]{:S(2)}, u32[]{:S(2)}) collective-permute-start(bf16[256,2048]{1,0:T(8,128)(2,1)} %collective-permute-done.6), channel_id=1, source_target_pairs={{0,8},{8,16},{16,24},{24,0},{1,9},{9,17},{17,25},{25,1},{2,10},{10... | collective-permute-start | bytes 3145736 | tf_op jit(solution)/shard_map/ppermute | solution.py:287
  119.0 26.4 %collective-permute-start.12 = (bf16[256,2048]{1,0:T(8,128)(2,1)}, bf16[256,2048]{1,0:T(8,128)(2,1)}, u32[]{:S(2)}, u32[]{:S(2)}) collective-permute-start(bf16[256,2048]{1,0:T(8,128)(2,1)} %collective-permute-done.6), channel_id=1, source_target_pairs={{0,4},{2,6},{4,0},{6,2},{1,5},{3,7},{5,1},{7,3},{8,12},{10,14},{12... | collective-permute-start | bytes 3145736 | tf_op jit(solution)/shard_map/ppermute | solution.py:296
  147.8 25.3 %collective-permute-start.15 = (bf16[256,2048]{1,0:T(8,128)(2,1)}, bf16[256,2048]{1,0:T(8,128)(2,1)S(1)}, u32[]{:S(2)}, u32[]{:S(2)}) collective-permute-start(bf16[256,2048]{1,0:T(8,128)(2,1)} %collective-permute-done.10), channel_id=1, source_target_pairs={{0,4},{2,6},{4,0},{6,2},{1,5},{3,7},{5,1},{7,3},{8,12},{10,14},{12... | collective-permute-start | bytes 3145736 | tf_op jit(solution)/shard_map/ppermute | solution.py:296
  211.7 26.9 %collective-permute-start.16 = (f16[264,2048]{1,0:T(8,128)(2,1)S(1)}, f16[264,2048]{1,0:T(8,128)(2,1)S(1)}, u32[]{:S(2)}, u32[]{:S(2)}) collective-permute-start(f16[264,2048]{1,0:T(8,128)(2,1)S(1)} %pad_maximum_fusion.7), channel_id=1, source_target_pairs={{0,4},{2,6},{4,0},{6,2},{1,5},{3,7},{5,1},{7,3},{8,12},{10,14},{12... | collective-permute-start | bytes 3244040 | tf_op jit(solution)/shard_map/ppermute | solution.py:296
  240.4 26.8 %collective-permute-start.18 = (f16[264,2048]{1,0:T(8,128)(2,1)}, f16[264,2048]{1,0:T(8,128)(2,1)}, u32[]{:S(2)}, u32[]{:S(2)}) collective-permute-start(f16[264,2048]{1,0:T(8,128)(2,1)} %pad_maximum_fusion.6), channel_id=1, source_target_pairs={{0,4},{2,6},{4,0},{6,2},{1,5},{3,7},{5,1},{7,3},{8,12},{10,14},{12... | collective-permute-start | bytes 3244040 | tf_op jit(solution)/shard_map/ppermute | solution.py:296
  240.9 28.1 %collective-permute-start.19 = (f16[264,2048]{1,0:T(8,128)(2,1)}, f16[264,2048]{1,0:T(8,128)(2,1)}, u32[]{:S(2)}, u32[]{:S(2)}) collective-permute-start(f16[264,2048]{1,0:T(8,128)(2,1)} %pad_maximum_fusion.8), channel_id=1, source_target_pairs={{0,8},{8,16},{16,24},{24,0},{1,9},{9,17},{17,25},{25,1},{2,10},{10... | collective-permute-start | bytes 3244040 | tf_op jit(solution)/shard_map/ppermute | solution.py:287
  258.2 28.4 %collective-permute-start.21 = (f16[8,72,1024]{2,1,0:T(8,128)(2,1)}, f16[8,72,1024]{2,1,0:T(8,128)(2,1)}, u32[]{:S(2)}, u32[]{:S(2)}) collective-permute-start(f16[8,72,1024]{2,1,0:T(8,128)(2,1)} %divide_convert_fusion), channel_id=1, source_target_pairs={{0,1},{1,0},{2,3},{3,2},{4,5},{5,4},{6,7},{7,6},{8,9},{9,8},{10,11... | collective-permute-start | bytes 3538952 | tf_op jit(solution)/shard_map/ppermute | solution.py:303
  290.2 53.3 %collective-permute-start.28 = (f16[264,2048]{1,0:T(8,128)(2,1)S(1)}, f16[264,2048]{1,0:T(8,128)(2,1)S(1)}, u32[]{:S(2)}, u32[]{:S(2)}) collective-permute-start(f16[264,2048]{1,0:T(8,128)(2,1)S(1)} %pad_maximum_fusion.9), channel_id=1, source_target_pairs={{0,8},{8,16},{16,24},{24,0},{1,9},{9,17},{17,25},{25,1},{2,10},{10... | collective-permute-start | bytes 3244040 | tf_op jit(solution)/shard_map/ppermute | solution.py:287
  290.3 29.9 %collective-permute-start.20 = (f16[264,2048]{1,0:T(8,128)(2,1)S(1)}, f16[264,2048]{1,0:T(8,128)(2,1)S(1)}, u32[]{:S(2)}, u32[]{:S(2)}) collective-permute-start(f16[264,2048]{1,0:T(8,128)(2,1)S(1)} %copy-done.17), channel_id=1, source_target_pairs={{0,4},{2,6},{4,0},{6,2},{1,5},{3,7},{5,1},{7,3},{8,12},{10,14},{12... | collective-permute-start | bytes 3244040 | tf_op jit(solution)/shard_map/ppermute | solution.py:296
  291.5 28.2 %collective-permute-start.27 = (f32[9,1024]{1,0:T(8,128)S(1)}, f32[9,1024]{1,0:T(8,128)S(1)}, u32[]{:S(2)}, u32[]{:S(2)}) collective-permute-start(f32[9,1024]{1,0:T(8,128)S(1)} %fusion.23), channel_id=1, source_target_pairs={{0,8},{8,0},{16,24},{24,16},{1,9},{9,1},{17,25},{25,17},{2,10},{10... | collective-permute-start | bytes 110600 | tf_op jit(solution)/shard_map/ppermute | solution.py:290
  291.7 35.1 %collective-permute-start.23 = (bf16[2,72,1024]{2,1,0:T(8,128)(2,1)S(1)}, bf16[2,72,1024]{2,1,0:T(8,128)(2,1)S(1)}, u32[]{:S(2)}, u32[]{:S(2)}) collective-permute-start(bf16[2,72,1024]{2,1,0:T(8,128)(2,1)S(1)} %get-tuple-element.141), channel_id=1, source_target_pairs={{0,24},{8,0},{16,8},{24,16},{1,25},{9,1},{17,9},{25,17},{2,26},{10... | collective-permute-start | bytes 884744 | tf_op jit(solution)/shard_map/ppermute | solution.py:287
  294.9 48.7 %collective-permute-start.24 = (bf16[2,72,1024]{2,1,0:T(8,128)(2,1)S(1)}, bf16[2,72,1024]{2,1,0:T(8,128)(2,1)S(1)}, u32[]{:S(2)}, u32[]{:S(2)}) collective-permute-start(bf16[2,72,1024]{2,1,0:T(8,128)(2,1)S(1)} %get-tuple-element.140), channel_id=1, source_target_pairs={{0,16},{8,24},{16,0},{24,8},{1,17},{9,25},{17,1},{25,9},{2,18},{10... | collective-permute-start | bytes 884744 | tf_op jit(solution)/shard_map/ppermute | solution.py:287
  319.7 23.9 %collective-permute-start.25 = (bf16[2,72,1024]{2,1,0:T(8,128)(2,1)S(1)}, bf16[2,72,1024]{2,1,0:T(8,128)(2,1)S(1)}, u32[]{:S(2)}, u32[]{:S(2)}) collective-permute-start(bf16[2,72,1024]{2,1,0:T(8,128)(2,1)S(1)} %get-tuple-element.139), channel_id=1, source_target_pairs={{0,8},{8,16},{16,24},{24,0},{1,9},{9,17},{17,25},{25,1},{2,10},{10... | collective-permute-start | bytes 884744 | tf_op jit(solution)/shard_map/ppermute | solution.py:287
  346.7 30.1 %collective-permute-start.35 = (f16[264,2048]{1,0:T(8,128)(2,1)S(1)}, f16[264,2048]{1,0:T(8,128)(2,1)S(1)}, u32[]{:S(2)}, u32[]{:S(2)}) collective-permute-start(f16[264,2048]{1,0:T(8,128)(2,1)S(1)} %pad_maximum_fusion.4), channel_id=1, source_target_pairs={{0,4},{2,6},{4,0},{6,2},{1,5},{3,7},{5,1},{7,3},{8,12},{10,14},{12... | collective-permute-start | bytes 3244040 | tf_op jit(solution)/shard_map/ppermute | solution.py:296
  347.3 29.6 %collective-permute-start.29 = (f16[264,2048]{1,0:T(8,128)(2,1)S(1)}, f16[264,2048]{1,0:T(8,128)(2,1)S(1)}, u32[]{:S(2)}, u32[]{:S(2)}) collective-permute-start(f16[264,2048]{1,0:T(8,128)(2,1)S(1)} %pad_maximum_fusion.10), channel_id=1, source_target_pairs={{0,8},{8,16},{16,24},{24,0},{1,9},{9,17},{17,25},{25,1},{2,10},{10... | collective-permute-start | bytes 3244040 | tf_op jit(solution)/shard_map/ppermute | solution.py:287
  347.3 19.9 %collective-permute-start.32 = (bf16[2,72,1024]{2,1,0:T(8,128)(2,1)S(1)}, bf16[2,72,1024]{2,1,0:T(8,128)(2,1)S(1)}, u32[]{:S(2)}, u32[]{:S(2)}) collective-permute-start(bf16[2,72,1024]{2,1,0:T(8,128)(2,1)S(1)} %collective-permute-done.24), channel_id=1, source_target_pairs={{0,1},{1,0},{2,3},{3,2},{4,5},{5,4},{6,7},{7,6},{8,9},{9,8},{10,11... | collective-permute-start | bytes 884744 | tf_op jit(solution)/shard_map/ppermute | solution.py:303
  (38 other events, 425.0 us)

commit v10 on v8

--- a/solution.py
+++ b/solution.py
@@ -294,6 +294,10 @@
 
     def swap_y(value):
         return lax.ppermute(value, "space", [(i, i ^ 2) for i in range(spaces)])
+
+    def swap_xy(value):
+        pairs_xy = [(i, ((i // 2) ^ 2) * 2 + (i % 2 ^ 1)) for i in range(2 * spaces)]
+        return lax.ppermute(value, ("space", "tensor"), pairs_xy)
 
     def swap_x(value):
         return lax.ppermute(value, "tensor", [(0, 1), (1, 0)])
@@ -518,7 +522,10 @@
     arriving, grad_inputs, small = lax.optimization_barrier(
         (ring(payload, 1), grad_inputs, small)
     )
-    small = join_x(small + swap_y(small))
+    if tensors == 2:
+        small = join_x(small + swap_y(small), swap_x(small) + swap_xy(small))
+    else:
+        small = join_x(small + swap_y(small))
     total = chip_sum(depth - 1, arriving)[0] + unpack(arriving)[0]
     mine = lax.dynamic_slice_in_dim(total, core * shard_rows, shard_rows, 0)
     other = swap_core(lax.dynamic_slice_in_dim(total, (1 - core) * shard_rows, shard_rows, 0))

time: 380 us -> 380 us (level)
  transfers between devices with their start and end apart: 39 -> 40, of which waited for: 20 -> 21; matrix products, arithmetic and copies ran while one was open for 18% -> 18% of each run, Pallas kernels for 11% -> 11%
where the time goes in v10:
time: 380 us; the launch traced here: 379 us
  waiting for transfers between devices  161 us (42%)
  Pallas kernels  70.3 us (18%)
  other arithmetic  57.7 us (15%)
  local copies, waits for them, and re-layouts  44.2 us (12%)
  starting transfers between devices  41.5 us (11%)
    ppermute x12, waiting for transfers between devices, ring(): lax.ppermute(value, 'frame', [(i, (i + shift) % depth) for i in range(dep...  96.5 us
    ppermute x10, waiting for transfers between devices, swap_x(): return lax.ppermute(value, 'tensor', [(0, 1), (1, 0)])  35.8 us
    pallas_call x4, Pallas kernels, weight_product(): pl.pallas_call(weight_kernel, grid_spec=pltpu.PrefetchScalarGridSpec(num_...  33.1 us
    ppermute x12, starting transfers between devices, ring(): lax.ppermute(value, 'frame', [(i, (i + shift) % depth) for i in range(dep...  14.8 us
    dynamic_update_slice x7, local copies, waits for them, and re-layouts, settle(): return lax.dynamic_update_slice(weights, arrived, (start, 0))  13.8 us
    pallas_call x1, Pallas kernels, project(): pl.pallas_call(project_kernel, grid=(4, 2), in_specs=[pl.BlockSpec((rows,...  13.6 us
    ppermute x10, starting transfers between devices, swap_x(): return lax.ppermute(value, 'tensor', [(0, 1), (1, 0)])  13.1 us
    another operation x11, other arithmetic  12.7 us
  transfers between devices with their start and end apart: 40, of which 21 were waited for; matrix products, arithmetic and copies ran while one was open for 18% of the time, Pallas kernels for 11%

profile of v10, /device:TPU:0, one launch (start us, length us, event | category | flops | bytes accessed | tf_op | source)
XLA Modules:
  0.0 378.9 jit_solution(8207703203468302519)
XLA Ops:
  18.6 10.1 %collective-permute-done.3 = bf16[296,1024]{1,0:T(8,128)(2,1)} collective-permute-done((bf16[296,1024]{1,0:T(8,128)(2,1)S(1)}, bf16[296,1024]{1,0:T(8,128)(2,1)}, u32[]{:S(2)}, u32[]{:S(2)}) %collective-permute-start.3) | collective-permute-done | bytes 606240 | tf_op jit(solution)/shard_map/ppermute | solution.py:287
  32.4 4.4 %broadcast_in_dim.62 = bf16[2048,2048]{1,0:T(8,128)(2,1)} broadcast(bf16[]{:T(256)} %constant.276.clone.1), dimensions={} | broadcast | bytes 8388610 | tf_op jit(solution)/shard_map/broadcast_in_dim | solution.py:365
  37.9 38.7 %collective-permute-done.2 = bf16[296,1024]{1,0:T(8,128)(2,1)} collective-permute-done((bf16[296,1024]{1,0:T(8,128)(2,1)S(1)}, bf16[296,1024]{1,0:T(8,128)(2,1)}, u32[]{:S(2)}, u32[]{:S(2)}) %collective-permute-start.2) | collective-permute-done | bytes 606240 | tf_op jit(solution)/shard_map/ppermute | solution.py:287
  92.8 6.9 %collective-permute-done.9 = bf16[296,1024]{1,0:T(8,128)(2,1)S(1)} collective-permute-done((bf16[296,1024]{1,0:T(8,128)(2,1)}, bf16[296,1024]{1,0:T(8,128)(2,1)S(1)}, u32[]{:S(2)}, u32[]{:S(2)}) %collective-permute-start.9) | collective-permute-done | bytes 606240 | tf_op jit(solution)/shard_map/ppermute | solution.py:303
  101.0 15.8 %collective-permute-done.7 = bf16[296,1024]{1,0:T(8,128)(2,1)S(1)} collective-permute-done((bf16[296,1024]{1,0:T(8,128)(2,1)S(1)}, bf16[296,1024]{1,0:T(8,128)(2,1)S(1)}, u32[]{:S(2)}, u32[]{:S(2)}) %collective-permute-start.7) | collective-permute-done | bytes 606240 | tf_op jit(solution)/shard_map/ppermute | solution.py:287
  124.3 8.3 %collective-permute-done.11 = bf16[296,1024]{1,0:T(8,128)(2,1)S(1)} collective-permute-done((bf16[296,1024]{1,0:T(8,128)(2,1)S(1)}, bf16[296,1024]{1,0:T(8,128)(2,1)S(1)}, u32[]{:S(2)}, u32[]{:S(2)}) %collective-permute-start.11) | collective-permute-done | bytes 606240 | tf_op jit(solution)/shard_map/ppermute | solution.py:303
  137.5 7.9 %collective-permute-done.10 = bf16[256,2048]{1,0:T(8,128)(2,1)} collective-permute-done((bf16[256,2048]{1,0:T(8,128)(2,1)}, bf16[256,2048]{1,0:T(8,128)(2,1)}, u32[]{:S(2)}, u32[]{:S(2)}) %collective-permute-start.10) | collective-permute-done | bytes 1048608 | tf_op jit(solution)/shard_map/ppermute | solution.py:287
  174.2 13.6 %project.1 = (bf16[1152,1536]{1,0:T(8,128)(2,1)S(1)}, bf16[1152,512]{1,0:T(8,128)(2,1)S(1)}) custom-call(bf16[1152,2048]{1,0:T(8,128)(2,1)S(1)} %bitcast.106, bf16[1152,2048]{1,0:T(8,128)(2,1)S(1)} %bitcast.108, bf16[2048,2048]{1,0:T(8,128)(2,1)} %constant_dynamic-update-slice_fusion.weight_ref), custom_call_target="tpu_custom_call" | custom-call | flops 9663676416 | bytes 18874368 | tf_op jit(solution)/shard_map/project/pallas_call | solution.py:212
  187.8 7.8 %temporal_attention.1 = (bf16[8,144,512]{2,1,0:T(8,128)(2,1)S(1)}, bf16[8,144,1536]{2,1,0:T(8,128)(2,1)S(1)}, f32[2,8,128]{2,1,0:T(8,128)S(1)}) custom-call(f32[128,1]{1,0:T(8,128)S(1)} %broadcast_in_dim_reshape.9.late_ref, f32[1,128]{1,0:T(1,128)S(1)} %broadcast_in_dim_reshape.8.early_ref, bf16[8,144,1536]{2,1,0:T(8,128)(2,1)S(1)} %bitcast.113, ...), custom_call_target="tpu_custom_call" | custom-call | flops 1207959552 | bytes 9437184 | tf_op jit(solution)/shard_map/temporal_attention/pallas_call | solution.py:108
  201.2 8.3 %weight_product.4 = (f32[256,2048]{1,0:T(8,128)}, f32[256,2048]{1,0:T(8,128)}) custom-call(s32[2]{0:T(128)} %pad_add_fusion.1.place_ref, bf16[2048,1152]{1,0:T(8,128)(2,1)} %copy-done.2, bf16[2048,1152]{1,0:T(8,128)(2,1)} %copy-done.3, bf16[1152,1536]{1,0:T(8,128)(2,1)} %bitcast.100, bf16[1152,512]{1,0:T(8,128)(2,1)} %bitcast.109), custom_call_target="tpu_custom_call" | custom-call | flops 1 | bytes 1 | tf_op jit(solution)/shard_map/weight_product/pallas_call | solution.py:178
  213.3 11.0 %norm_product.1 = (f32[8,72,2048]{2,1,0:T(8,128)S(1)}, f32[8,72,2048]{2,1,0:T(8,128)}) custom-call(bf16[1152,1536]{1,0:T(8,128)(2,1)S(1)} %bitcast.104, bf16[2048,2048]{1,0:T(8,128)(2,1)} %constant_dynamic-update-slice_fusion.weight_ref), custom_call_target="tpu_custom_call" | custom-call | flops 1 | bytes 1 | tf_op jit(solution)/shard_map/norm_product/pallas_call | solution.py:253
  227.0 8.3 %weight_product.5 = (f32[256,2048]{1,0:T(8,128)}, f32[256,2048]{1,0:T(8,128)}) custom-call(s32[2]{0:T(128)} %pad_add_fusion.2.place_ref, bf16[2048,1152]{1,0:T(8,128)(2,1)} %copy-done.2, bf16[2048,1152]{1,0:T(8,128)(2,1)} %copy-done.3, bf16[1152,1536]{1,0:T(8,128)(2,1)} %bitcast.101, bf16[1152,512]{1,0:T(8,128)(2,1)} %bitcast.110), custom_call_target="tpu_custom_call" | custom-call | flops 1 | bytes 1 | tf_op jit(solution)/shard_map/weight_product/pallas_call | solution.py:178
  240.8 7.7 %collective-permute-done.17 = f32[8,72,2048]{2,1,0:T(8,128)} collective-permute-done((f32[8,72,2048]{2,1,0:T(8,128)}, f32[8,72,2048]{2,1,0:T(8,128)}, u32[]{:S(2)}, u32[]{:S(2)}) %collective-permute-start.17) | collective-permute-done | bytes 4718624 | tf_op jit(solution)/shard_map/ppermute | solution.py:293
  248.6 5.4 %multiply_reduce_fusion = (f32[8,72]{1,0:T(8,128)S(1)}, f32[8,72]{1,0:T(8,128)S(1)}, f32[8,72,2048]{2,1,0:T(8,128)S(1)}) fusion(bf16[8,72,2048]{2,1,0:T(8,128)(2,1)S(1)} %get-tuple-element.120, f32[2048]{0:T(1024)S(1)} %copy-done.16, f32[8,72]{1,0:T(8,128)S(1)} %add_rsqrt_fusion, f32[8,2048]{1,0:T(8,128)S(1)} %fusion.22, f32[8,72,2048]{2,1,0:T(8,128)} %copy-done.7, ...), kind=kLoop, calls=%fused_computation.2 | loop fusion | flops 10615680 | bytes 16595712 | tf_op jit(solution)/shard_map/reduce_sum | solution.py:469
  257.7 8.3 %weight_product.6 = (f32[256,2048]{1,0:T(8,128)}, f32[256,2048]{1,0:T(8,128)}) custom-call(s32[2]{0:T(128)} %pad_add_fusion.3.place_ref, bf16[2048,1152]{1,0:T(8,128)(2,1)} %copy-done.2, bf16[2048,1152]{1,0:T(8,128)(2,1)} %copy-done.3, bf16[1152,1536]{1,0:T(8,128)(2,1)} %bitcast.102, bf16[1152,512]{1,0:T(8,128)(2,1)} %bitcast.111), custom_call_target="tpu_custom_call" | custom-call | flops 1 | bytes 1 | tf_op jit(solution)/shard_map/weight_product/pallas_call | solution.py:178
  276.2 8.3 %weight_product.7 = (f32[256,2048]{1,0:T(8,128)}, f32[256,2048]{1,0:T(8,128)}) custom-call(s32[2]{0:T(128)} %pad_add_fusion.4.place_ref, bf16[2048,1152]{1,0:T(8,128)(2,1)} %copy-done.2, bf16[2048,1152]{1,0:T(8,128)(2,1)} %copy-done.3, bf16[1152,1536]{1,0:T(8,128)(2,1)} %bitcast.103, bf16[1152,512]{1,0:T(8,128)(2,1)} %bitcast.112), custom_call_target="tpu_custom_call" | custom-call | flops 1 | bytes 1 | tf_op jit(solution)/shard_map/weight_product/pallas_call | solution.py:178
  296.0 6.9 %collective-permute-done.27 = f32[9,1024]{1,0:T(8,128)S(1)} collective-permute-done((f32[9,1024]{1,0:T(8,128)S(1)}, f32[9,1024]{1,0:T(8,128)S(1)}, u32[]{:S(2)}, u32[]{:S(2)}) %collective-permute-start.27) | collective-permute-done | bytes 36896 | tf_op jit(solution)/shard_map/ppermute | solution.py:290
  302.9 7.6 %collective-permute-done.23 = bf16[2,72,1024]{2,1,0:T(8,128)(2,1)S(1)} collective-permute-done((bf16[2,72,1024]{2,1,0:T(8,128)(2,1)S(1)}, bf16[2,72,1024]{2,1,0:T(8,128)(2,1)S(1)}, u32[]{:S(2)}, u32[]{:S(2)}) %collective-permute-start.23) | collective-permute-done | bytes 294944 | tf_op jit(solution)/shard_map/ppermute | solution.py:287
  310.6 16.2 %collective-permute-done.24 = bf16[2,72,1024]{2,1,0:T(8,128)(2,1)S(1)} collective-permute-done((bf16[2,72,1024]{2,1,0:T(8,128)(2,1)S(1)}, bf16[2,72,1024]{2,1,0:T(8,128)(2,1)S(1)}, u32[]{:S(2)}, u32[]{:S(2)}) %collective-permute-start.24) | collective-permute-done | bytes 294944 | tf_op jit(solution)/shard_map/ppermute | solution.py:287
  336.2 4.9 %collective-permute-done.30 = bf16[2,72,1024]{2,1,0:T(8,128)(2,1)S(1)} collective-permute-done((bf16[2,72,1024]{2,1,0:T(8,128)(2,1)S(1)}, bf16[2,72,1024]{2,1,0:T(8,128)(2,1)S(1)}, u32[]{:S(2)}, u32[]{:S(2)}) %collective-permute-start.30) | collective-permute-done | bytes 294944 | tf_op jit(solution)/shard_map/ppermute | solution.py:303
  342.6 4.8 %collective-permute-done.31 = bf16[2,72,1024]{2,1,0:T(8,128)(2,1)S(1)} collective-permute-done((bf16[2,72,1024]{2,1,0:T(8,128)(2,1)S(1)}, bf16[2,72,1024]{2,1,0:T(8,128)(2,1)S(1)}, u32[]{:S(2)}, u32[]{:S(2)}) %collective-permute-start.31) | collective-permute-done | bytes 294944 | tf_op jit(solution)/shard_map/ppermute | solution.py:303
  349.1 4.6 %collective-permute-done.32 = bf16[2,72,1024]{2,1,0:T(8,128)(2,1)S(1)} collective-permute-done((bf16[2,72,1024]{2,1,0:T(8,128)(2,1)S(1)}, bf16[2,72,1024]{2,1,0:T(8,128)(2,1)S(1)}, u32[]{:S(2)}, u32[]{:S(2)}) %collective-permute-start.32) | collective-permute-done | bytes 294944 | tf_op jit(solution)/shard_map/ppermute | solution.py:303
  354.2 4.8 %collective-permute-done.33 = bf16[2,72,1024]{2,1,0:T(8,128)(2,1)S(1)} collective-permute-done((bf16[2,72,1024]{2,1,0:T(8,128)(2,1)S(1)}, bf16[2,72,1024]{2,1,0:T(8,128)(2,1)S(1)}, u32[]{:S(2)}, u32[]{:S(2)}) %collective-permute-start.33) | collective-permute-done | bytes 294944 | tf_op jit(solution)/shard_map/ppermute | solution.py:303
  359.2 5.3 %collective-permute-done.34 = f32[9,1024]{1,0:T(8,128)S(1)} collective-permute-done((f32[9,1024]{1,0:T(8,128)S(1)}, f32[9,1024]{1,0:T(8,128)S(1)}, u32[]{:S(2)}, u32[]{:S(2)}) %collective-permute-start.34) | collective-permute-done | bytes 36896 | tf_op jit(solution)/shard_map/ppermute | solution.py:290
  (229 shorter events, 149.6 us)
Async XLA Ops:
  9.0 19.7 %collective-permute-start.3 = (bf16[296,1024]{1,0:T(8,128)(2,1)S(1)}, bf16[296,1024]{1,0:T(8,128)(2,1)}, u32[]{:S(2)}, u32[]{:S(2)}) collective-permute-start(bf16[296,1024]{1,0:T(8,128)(2,1)S(1)} %pad_maximum_fusion.13), channel_id=1, source_target_pairs={{0,8},{8,16},{16,24},{24,0},{1,9},{9,17},{17,25},{25,1},{2,10},{10... | collective-permute-start | bytes 1818632 | tf_op jit(solution)/shard_map/ppermute | solution.py:287
  14.0 62.6 %collective-permute-start.1 = (bf16[256,2048]{1,0:T(8,128)(2,1)}, bf16[256,2048]{1,0:T(8,128)(2,1)}, u32[]{:S(2)}, u32[]{:S(2)}) collective-permute-start(bf16[256,2048]{1,0:T(8,128)(2,1)} %pad_maximum_fusion.11), channel_id=1, source_target_pairs={{0,8},{8,16},{16,24},{24,0},{1,9},{9,17},{17,25},{25,1},{2,10},{10... | collective-permute-start | bytes 3145736 | tf_op jit(solution)/shard_map/ppermute | solution.py:287
  15.6 61.1 %collective-permute-start.4 = (bf16[256,2048]{1,0:T(8,128)(2,1)}, bf16[256,2048]{1,0:T(8,128)(2,1)}, u32[]{:S(2)}, u32[]{:S(2)}) collective-permute-start(bf16[256,2048]{1,0:T(8,128)(2,1)} %pad_maximum_fusion.11), channel_id=1, source_target_pairs={{0,4},{2,6},{4,0},{6,2},{1,5},{3,7},{5,1},{7,3},{8,12},{10,14},{12... | collective-permute-start | bytes 3145736 | tf_op jit(solution)/shard_map/ppermute | solution.py:296
  17.3 59.3 %collective-permute-start.2 = (bf16[296,1024]{1,0:T(8,128)(2,1)S(1)}, bf16[296,1024]{1,0:T(8,128)(2,1)}, u32[]{:S(2)}, u32[]{:S(2)}) collective-permute-start(bf16[296,1024]{1,0:T(8,128)(2,1)S(1)} %pad_maximum_fusion.12), channel_id=1, source_target_pairs={{0,16},{8,24},{16,0},{24,8},{1,17},{9,25},{17,1},{25,9},{2,18},{10... | collective-permute-start | bytes 1818632 | tf_op jit(solution)/shard_map/ppermute | solution.py:287
  28.7 47.9 %collective-permute-start.5 = (bf16[296,1024]{1,0:T(8,128)(2,1)}, bf16[296,1024]{1,0:T(8,128)(2,1)S(1)}, u32[]{:S(2)}, u32[]{:S(2)}) collective-permute-start(bf16[296,1024]{1,0:T(8,128)(2,1)} %collective-permute-done.3), channel_id=1, source_target_pairs={{0,1},{1,0},{2,3},{3,2},{4,5},{5,4},{6,7},{7,6},{8,9},{9,8},{10,11... | collective-permute-start | bytes 1818632 | tf_op jit(solution)/shard_map/ppermute | solution.py:303
  76.6 40.2 %collective-permute-start.6 = (bf16[256,2048]{1,0:T(8,128)(2,1)}, bf16[256,2048]{1,0:T(8,128)(2,1)}, u32[]{:S(2)}, u32[]{:S(2)}) collective-permute-start(bf16[256,2048]{1,0:T(8,128)(2,1)} %collective-permute-done.1), channel_id=1, source_target_pairs={{0,8},{8,16},{16,24},{24,0},{1,9},{9,17},{17,25},{25,1},{2,10},{10... | collective-permute-start | bytes 3145736 | tf_op jit(solution)/shard_map/ppermute | solution.py:287
  79.0 37.8 %collective-permute-start.8 = (bf16[256,2048]{1,0:T(8,128)(2,1)}, bf16[256,2048]{1,0:T(8,128)(2,1)S(1)}, u32[]{:S(2)}, u32[]{:S(2)}) collective-permute-start(bf16[256,2048]{1,0:T(8,128)(2,1)} %collective-permute-done.1), channel_id=1, source_target_pairs={{0,4},{2,6},{4,0},{6,2},{1,5},{3,7},{5,1},{7,3},{8,12},{10,14},{12... | collective-permute-start | bytes 3145736 | tf_op jit(solution)/shard_map/ppermute | solution.py:296
  80.8 36.0 %collective-permute-start.7 = (bf16[296,1024]{1,0:T(8,128)(2,1)S(1)}, bf16[296,1024]{1,0:T(8,128)(2,1)S(1)}, u32[]{:S(2)}, u32[]{:S(2)}) collective-permute-start(bf16[296,1024]{1,0:T(8,128)(2,1)S(1)} %pad_maximum_fusion.14), channel_id=1, source_target_pairs={{0,24},{8,0},{16,8},{24,16},{1,25},{9,1},{17,9},{25,17},{2,26},{10... | collective-permute-start | bytes 1818632 | tf_op jit(solution)/shard_map/ppermute | solution.py:287
  118.5 26.9 %collective-permute-start.10 = (bf16[256,2048]{1,0:T(8,128)(2,1)}, bf16[256,2048]{1,0:T(8,128)(2,1)}, u32[]{:S(2)}, u32[]{:S(2)}) collective-permute-start(bf16[256,2048]{1,0:T(8,128)(2,1)} %collective-permute-done.6), channel_id=1, source_target_pairs={{0,8},{8,16},{16,24},{24,0},{1,9},{9,17},{17,25},{25,1},{2,10},{10... | collective-permute-start | bytes 3145736 | tf_op jit(solution)/shard_map/ppermute | solution.py:287
  119.0 26.4 %collective-permute-start.12 = (bf16[256,2048]{1,0:T(8,128)(2,1)}, bf16[256,2048]{1,0:T(8,128)(2,1)}, u32[]{:S(2)}, u32[]{:S(2)}) collective-permute-start(bf16[256,2048]{1,0:T(8,128)(2,1)} %collective-permute-done.6), channel_id=1, source_target_pairs={{0,4},{2,6},{4,0},{6,2},{1,5},{3,7},{5,1},{7,3},{8,12},{10,14},{12... | collective-permute-start | bytes 3145736 | tf_op jit(solution)/shard_map/ppermute | solution.py:296
  147.8 25.3 %collective-permute-start.15 = (bf16[256,2048]{1,0:T(8,128)(2,1)}, bf16[256,2048]{1,0:T(8,128)(2,1)S(1)}, u32[]{:S(2)}, u32[]{:S(2)}) collective-permute-start(bf16[256,2048]{1,0:T(8,128)(2,1)} %collective-permute-done.10), channel_id=1, source_target_pairs={{0,4},{2,6},{4,0},{6,2},{1,5},{3,7},{5,1},{7,3},{8,12},{10,14},{12... | collective-permute-start | bytes 3145736 | tf_op jit(solution)/shard_map/ppermute | solution.py:296
  211.7 26.8 %collective-permute-start.16 = (f16[264,2048]{1,0:T(8,128)(2,1)S(1)}, f16[264,2048]{1,0:T(8,128)(2,1)S(1)}, u32[]{:S(2)}, u32[]{:S(2)}) collective-permute-start(f16[264,2048]{1,0:T(8,128)(2,1)S(1)} %pad_maximum_fusion.7), channel_id=1, source_target_pairs={{0,4},{2,6},{4,0},{6,2},{1,5},{3,7},{5,1},{7,3},{8,12},{10,14},{12... | collective-permute-start | bytes 3244040 | tf_op jit(solution)/shard_map/ppermute | solution.py:296
  240.3 29.4 %collective-permute-start.21 = (f16[264,2048]{1,0:T(8,128)(2,1)}, f16[264,2048]{1,0:T(8,128)(2,1)}, u32[]{:S(2)}, u32[]{:S(2)}) collective-permute-start(f16[264,2048]{1,0:T(8,128)(2,1)} %pad_maximum_fusion.6), channel_id=1, source_target_pairs={{0,4},{2,6},{4,0},{6,2},{1,5},{3,7},{5,1},{7,3},{8,12},{10,14},{12... | collective-permute-start | bytes 3244040 | tf_op jit(solution)/shard_map/ppermute | solution.py:296
  240.8 28.9 %collective-permute-start.22 = (f16[264,2048]{1,0:T(8,128)(2,1)}, f16[264,2048]{1,0:T(8,128)(2,1)}, u32[]{:S(2)}, u32[]{:S(2)}) collective-permute-start(f16[264,2048]{1,0:T(8,128)(2,1)} %pad_maximum_fusion.8), channel_id=1, source_target_pairs={{0,8},{8,16},{16,24},{24,0},{1,9},{9,17},{17,25},{25,1},{2,10},{10... | collective-permute-start | bytes 3244040 | tf_op jit(solution)/shard_map/ppermute | solution.py:287
  257.2 29.5 %collective-permute-start.19 = (f16[8,72,1024]{2,1,0:T(8,128)(2,1)S(1)}, f16[8,72,1024]{2,1,0:T(8,128)(2,1)S(1)}, u32[]{:S(2)}, u32[]{:S(2)}) collective-permute-start(f16[8,72,1024]{2,1,0:T(8,128)(2,1)S(1)} %divide_convert_fusion), channel_id=1, source_target_pairs={{0,1},{1,0},{2,3},{3,2},{4,5},{5,4},{6,7},{7,6},{8,9},{9,8},{10,11... | collective-permute-start | bytes 3538952 | tf_op jit(solution)/shard_map/ppermute | solution.py:303
  269.2 33.7 %collective-permute-start.18 = (f16[264,2048]{1,0:T(8,128)(2,1)}, f16[264,2048]{1,0:T(8,128)(2,1)}, u32[]{:S(2)}, u32[]{:S(2)}) collective-permute-start(f16[264,2048]{1,0:T(8,128)(2,1)} %pad_maximum_fusion.5), channel_id=1, source_target_pairs={{0,4},{2,6},{4,0},{6,2},{1,5},{3,7},{5,1},{7,3},{8,12},{10,14},{12... | collective-permute-start | bytes 3244040 | tf_op jit(solution)/shard_map/ppermute | solution.py:296
  274.1 52.7 %collective-permute-start.28 = (f16[264,2048]{1,0:T(8,128)(2,1)}, f16[264,2048]{1,0:T(8,128)(2,1)}, u32[]{:S(2)}, u32[]{:S(2)}) collective-permute-start(f16[264,2048]{1,0:T(8,128)(2,1)} %pad_maximum_fusion.9), channel_id=1, source_target_pairs={{0,8},{8,16},{16,24},{24,0},{1,9},{9,17},{17,25},{25,1},{2,10},{10... | collective-permute-start | bytes 3244040 | tf_op jit(solution)/shard_map/ppermute | solution.py:287
  291.4 19.1 %collective-permute-start.23 = (bf16[2,72,1024]{2,1,0:T(8,128)(2,1)S(1)}, bf16[2,72,1024]{2,1,0:T(8,128)(2,1)S(1)}, u32[]{:S(2)}, u32[]{:S(2)}) collective-permute-start(bf16[2,72,1024]{2,1,0:T(8,128)(2,1)S(1)} %get-tuple-element.137), channel_id=1, source_target_pairs={{0,24},{8,0},{16,8},{24,16},{1,25},{9,1},{17,9},{25,17},{2,26},{10... | collective-permute-start | bytes 884744 | tf_op jit(solution)/shard_map/ppermute | solution.py:287
  295.3 31.5 %collective-permute-start.24 = (bf16[2,72,1024]{2,1,0:T(8,128)(2,1)S(1)}, bf16[2,72,1024]{2,1,0:T(8,128)(2,1)S(1)}, u32[]{:S(2)}, u32[]{:S(2)}) collective-permute-start(bf16[2,72,1024]{2,1,0:T(8,128)(2,1)S(1)} %get-tuple-element.136), channel_id=1, source_target_pairs={{0,16},{8,24},{16,0},{24,8},{1,17},{9,25},{17,1},{25,9},{2,18},{10... | collective-permute-start | bytes 884744 | tf_op jit(solution)/shard_map/ppermute | solution.py:287
  302.9 23.9 %collective-permute-start.25 = (bf16[2,72,1024]{2,1,0:T(8,128)(2,1)S(1)}, bf16[2,72,1024]{2,1,0:T(8,128)(2,1)S(1)}, u32[]{:S(2)}, u32[]{:S(2)}) collective-permute-start(bf16[2,72,1024]{2,1,0:T(8,128)(2,1)S(1)} %get-tuple-element.135), channel_id=1, source_target_pairs={{0,8},{8,16},{16,24},{24,0},{1,9},{9,17},{17,25},{25,1},{2,10},{10... | collective-permute-start | bytes 884744 | tf_op jit(solution)/shard_map/ppermute | solution.py:287
  333.2 32.0 %collective-permute-start.35 = (f16[264,2048]{1,0:T(8,128)(2,1)S(1)}, f16[264,2048]{1,0:T(8,128)(2,1)S(1)}, u32[]{:S(2)}, u32[]{:S(2)}) collective-permute-start(f16[264,2048]{1,0:T(8,128)(2,1)S(1)} %pad_maximum_fusion.4), channel_id=1, source_target_pairs={{0,4},{2,6},{4,0},{6,2},{1,5},{3,7},{5,1},{7,3},{8,12},{10,14},{12... | collective-permute-start | bytes 3244040 | tf_op jit(solution)/shard_map/ppermute | solution.py:296
  334.7 30.4 %collective-permute-start.29 = (f16[264,2048]{1,0:T(8,128)(2,1)}, f16[264,2048]{1,0:T(8,128)(2,1)S(1)}, u32[]{:S(2)}, u32[]{:S(2)}) collective-permute-start(f16[264,2048]{1,0:T(8,128)(2,1)} %pad_maximum_fusion.10), channel_id=1, source_target_pairs={{0,8},{8,16},{16,24},{24,0},{1,9},{9,17},{17,25},{25,1},{2,10},{10... | collective-permute-start | bytes 3244040 | tf_op jit(solution)/shard_map/ppermute | solution.py:287
  334.7 19.0 %collective-permute-start.32 = (bf16[2,72,1024]{2,1,0:T(8,128)(2,1)S(1)}, bf16[2,72,1024]{2,1,0:T(8,128)(2,1)S(1)}, u32[]{:S(2)}, u32[]{:S(2)}) collective-permute-start(bf16[2,72,1024]{2,1,0:T(8,128)(2,1)S(1)} %collective-permute-done.24), channel_id=1, source_target_pairs={{0,1},{1,0},{2,3},{3,2},{4,5},{5,4},{6,7},{7,6},{8,9},{9,8},{10,11... | collective-permute-start | bytes 884744 | tf_op jit(solution)/shard_map/ppermute | solution.py:303
  341.0 18.0 %collective-permute-start.33 = (bf16[2,72,1024]{2,1,0:T(8,128)(2,1)S(1)}, bf16[2,72,1024]{2,1,0:T(8,128)(2,1)S(1)}, u32[]{:S(2)}, u32[]{:S(2)}) collective-permute-start(bf16[2,72,1024]{2,1,0:T(8,128)(2,1)S(1)} %collective-permute-done.25), channel_id=1, source_target_pairs={{0,1},{1,0},{2,3},{3,2},{4,5},{5,4},{6,7},{7,6},{8,9},{9,8},{10,11... | collective-permute-start | bytes 884744 | tf_op jit(solution)/shard_map/ppermute | solution.py:303
  (36 other events, 383.1 us)

commit v11 on v8

--- a/solution.py
+++ b/solution.py
@@ -431,9 +431,9 @@
 
     def pack(value, bound):
         exponent = jnp.ceil(jnp.log2(bound / WIRE_TOP))
-        return jnp.concatenate(
-            [value * jnp.exp2(-exponent), jnp.broadcast_to(exponent, (8, width))], 0
-        ).astype(WIRE)
+        row = lax.broadcasted_iota(jnp.int32, (block_rows + 8, 1), 0)
+        padded = jnp.pad(value * jnp.exp2(-exponent), ((0, 8), (0, 0)))
+        return jnp.where(row < block_rows, padded, exponent).astype(WIRE)
 
     def unpack(sent):
         scale = jnp.exp2(sent[block_rows : block_rows + 1].astype(jnp.float32))

time: 380 us -> 380 us (level)
    another operation x11 -> x0, other arithmetic: 12.7 us -> none
    mul x0 -> x7, other arithmetic: none -> 12.2 us  [pack(): padded = jnp.pad(value * jnp.exp2(-exponent), ((0, 8), (0, 0)))]
    concatenate x7 -> x0, other arithmetic: 6.79 us -> none  [pack(): jnp.concatenate([value * jnp.exp2(-exponent), jnp.broadcast_to(exponent,...]
    convert_element_type x0 -> x7, other arithmetic: none -> 6.71 us  [pack(): return jnp.where(row < block_rows, padded, exponent).astype(WIRE)]
where the time goes in v11:
time: 380 us; the launch traced here: 379 us
  waiting for transfers between devices  164 us (43%)
  Pallas kernels  70.2 us (18%)
  other arithmetic  55.7 us (15%)
  local copies, waits for them, and re-layouts  45.4 us (12%)
  starting transfers between devices  40 us (11%)
    ppermute x12, waiting for transfers between devices, ring(): lax.ppermute(value, 'frame', [(i, (i + shift) % depth) for i in range(dep...  96.5 us
    ppermute x10, waiting for transfers between devices, swap_x(): return lax.ppermute(value, 'tensor', [(0, 1), (1, 0)])  37 us
    pallas_call x4, Pallas kernels, weight_product(): pl.pallas_call(weight_kernel, grid_spec=pltpu.PrefetchScalarGridSpec(num_...  33.1 us
    ppermute x12, starting transfers between devices, ring(): lax.ppermute(value, 'frame', [(i, (i + shift) % depth) for i in range(dep...  14.8 us
    dynamic_update_slice x7, local copies, waits for them, and re-layouts, settle(): return lax.dynamic_update_slice(weights, arrived, (start, 0))  13.9 us
    pallas_call x1, Pallas kernels, project(): pl.pallas_call(project_kernel, grid=(4, 2), in_specs=[pl.BlockSpec((rows,...  13.6 us
    ppermute x10, starting transfers between devices, swap_x(): return lax.ppermute(value, 'tensor', [(0, 1), (1, 0)])  13.2 us
    unnamed x39, local copies, waits for them, and re-layouts  13.1 us
  transfers between devices with their start and end apart: 39, of which 20 were waited for; matrix products, arithmetic and copies ran while one was open for 18% of the time, Pallas kernels for 11%

profile of v11, /device:TPU:0, one launch (start us, length us, event | category | flops | bytes accessed | tf_op | source)
XLA Modules:
  0.0 378.9 jit_solution(2903573094955377145)
XLA Ops:
  18.6 10.1 %collective-permute-done.3 = bf16[296,1024]{1,0:T(8,128)(2,1)} collective-permute-done((bf16[296,1024]{1,0:T(8,128)(2,1)S(1)}, bf16[296,1024]{1,0:T(8,128)(2,1)}, u32[]{:S(2)}, u32[]{:S(2)}) %collective-permute-start.3) | collective-permute-done | bytes 606240 | tf_op jit(solution)/shard_map/ppermute | solution.py:287
  32.4 4.4 %broadcast_in_dim.159 = bf16[2048,2048]{1,0:T(8,128)(2,1)} broadcast(bf16[]{:T(256)} %constant.279.clone.1), dimensions={} | broadcast | bytes 8388610 | tf_op jit(solution)/shard_map/broadcast_in_dim | solution.py:361
  37.9 38.7 %collective-permute-done.2 = bf16[296,1024]{1,0:T(8,128)(2,1)} collective-permute-done((bf16[296,1024]{1,0:T(8,128)(2,1)S(1)}, bf16[296,1024]{1,0:T(8,128)(2,1)}, u32[]{:S(2)}, u32[]{:S(2)}) %collective-permute-start.2) | collective-permute-done | bytes 606240 | tf_op jit(solution)/shard_map/ppermute | solution.py:287
  92.8 6.9 %collective-permute-done.9 = bf16[296,1024]{1,0:T(8,128)(2,1)S(1)} collective-permute-done((bf16[296,1024]{1,0:T(8,128)(2,1)}, bf16[296,1024]{1,0:T(8,128)(2,1)S(1)}, u32[]{:S(2)}, u32[]{:S(2)}) %collective-permute-start.9) | collective-permute-done | bytes 606240 | tf_op jit(solution)/shard_map/ppermute | solution.py:299
  101.0 15.8 %collective-permute-done.7 = bf16[296,1024]{1,0:T(8,128)(2,1)S(1)} collective-permute-done((bf16[296,1024]{1,0:T(8,128)(2,1)S(1)}, bf16[296,1024]{1,0:T(8,128)(2,1)S(1)}, u32[]{:S(2)}, u32[]{:S(2)}) %collective-permute-start.7) | collective-permute-done | bytes 606240 | tf_op jit(solution)/shard_map/ppermute | solution.py:287
  124.3 8.3 %collective-permute-done.11 = bf16[296,1024]{1,0:T(8,128)(2,1)S(1)} collective-permute-done((bf16[296,1024]{1,0:T(8,128)(2,1)S(1)}, bf16[296,1024]{1,0:T(8,128)(2,1)S(1)}, u32[]{:S(2)}, u32[]{:S(2)}) %collective-permute-start.11) | collective-permute-done | bytes 606240 | tf_op jit(solution)/shard_map/ppermute | solution.py:299
  137.5 7.8 %collective-permute-done.10 = bf16[256,2048]{1,0:T(8,128)(2,1)} collective-permute-done((bf16[256,2048]{1,0:T(8,128)(2,1)}, bf16[256,2048]{1,0:T(8,128)(2,1)}, u32[]{:S(2)}, u32[]{:S(2)}) %collective-permute-start.10) | collective-permute-done | bytes 1048608 | tf_op jit(solution)/shard_map/ppermute | solution.py:287
  174.2 13.6 %project.1 = (bf16[1152,1536]{1,0:T(8,128)(2,1)S(1)}, bf16[1152,512]{1,0:T(8,128)(2,1)S(1)}) custom-call(bf16[1152,2048]{1,0:T(8,128)(2,1)S(1)} %bitcast.109, bf16[1152,2048]{1,0:T(8,128)(2,1)S(1)} %bitcast.111, bf16[2048,2048]{1,0:T(8,128)(2,1)} %constant_dynamic-update-slice_fusion.weight_ref), custom_call_target="tpu_custom_call" | custom-call | flops 9663676416 | bytes 18874368 | tf_op jit(solution)/shard_map/project/pallas_call | solution.py:212
  187.8 7.8 %temporal_attention.1 = (bf16[8,144,512]{2,1,0:T(8,128)(2,1)S(1)}, bf16[8,144,1536]{2,1,0:T(8,128)(2,1)S(1)}, f32[2,8,128]{2,1,0:T(8,128)S(1)}) custom-call(f32[128,1]{1,0:T(8,128)S(1)} %broadcast_in_dim_reshape.9.late_ref, f32[1,128]{1,0:T(1,128)S(1)} %broadcast_in_dim_reshape.8.early_ref, bf16[8,144,1536]{2,1,0:T(8,128)(2,1)S(1)} %bitcast.116, ...), custom_call_target="tpu_custom_call" | custom-call | flops 1207959552 | bytes 9437184 | tf_op jit(solution)/shard_map/temporal_attention/pallas_call | solution.py:108
  201.1 8.3 %weight_product.4 = (f32[256,2048]{1,0:T(8,128)}, f32[256,2048]{1,0:T(8,128)}) custom-call(s32[2]{0:T(128)} %pad_add_fusion.1.place_ref, bf16[2048,1152]{1,0:T(8,128)(2,1)} %copy-done.2, bf16[2048,1152]{1,0:T(8,128)(2,1)} %copy-done.3, bf16[1152,1536]{1,0:T(8,128)(2,1)} %bitcast.103, bf16[1152,512]{1,0:T(8,128)(2,1)} %bitcast.112), custom_call_target="tpu_custom_call" | custom-call | flops 1 | bytes 1 | tf_op jit(solution)/shard_map/weight_product/pallas_call | solution.py:178
  213.3 11.0 %norm_product.1 = (f32[8,72,2048]{2,1,0:T(8,128)S(1)}, f32[8,72,2048]{2,1,0:T(8,128)}) custom-call(bf16[1152,1536]{1,0:T(8,128)(2,1)S(1)} %bitcast.107, bf16[2048,2048]{1,0:T(8,128)(2,1)} %constant_dynamic-update-slice_fusion.weight_ref), custom_call_target="tpu_custom_call" | custom-call | flops 1 | bytes 1 | tf_op jit(solution)/shard_map/norm_product/pallas_call | solution.py:253
  227.0 8.3 %weight_product.5 = (f32[256,2048]{1,0:T(8,128)}, f32[256,2048]{1,0:T(8,128)}) custom-call(s32[2]{0:T(128)} %pad_add_fusion.2.place_ref, bf16[2048,1152]{1,0:T(8,128)(2,1)} %copy-done.2, bf16[2048,1152]{1,0:T(8,128)(2,1)} %copy-done.3, bf16[1152,1536]{1,0:T(8,128)(2,1)} %bitcast.104, bf16[1152,512]{1,0:T(8,128)(2,1)} %bitcast.113), custom_call_target="tpu_custom_call" | custom-call | flops 1 | bytes 1 | tf_op jit(solution)/shard_map/weight_product/pallas_call | solution.py:178
  241.3 7.7 %collective-permute-done.17 = f32[8,72,2048]{2,1,0:T(8,128)} collective-permute-done((f32[8,72,2048]{2,1,0:T(8,128)}, f32[8,72,2048]{2,1,0:T(8,128)}, u32[]{:S(2)}, u32[]{:S(2)}) %collective-permute-start.17) | collective-permute-done | bytes 4718624 | tf_op jit(solution)/shard_map/ppermute | solution.py:293
  249.0 5.4 %multiply_reduce_fusion = (f32[8,72]{1,0:T(8,128)S(1)}, f32[8,72]{1,0:T(8,128)S(1)}, f32[8,72,2048]{2,1,0:T(8,128)S(1)}) fusion(bf16[8,72,2048]{2,1,0:T(8,128)(2,1)S(1)} %get-tuple-element.120, f32[2048]{0:T(1024)S(1)} %copy-done.16, f32[8,72]{1,0:T(8,128)S(1)} %add_rsqrt_fusion, f32[8,2048]{1,0:T(8,128)S(1)} %fusion.21, f32[8,72,2048]{2,1,0:T(8,128)} %copy-done.7, ...), kind=kLoop, calls=%fused_computation.2 | loop fusion | flops 10615680 | bytes 16595712 | tf_op jit(solution)/shard_map/reduce_sum | solution.py:465
  258.2 8.3 %weight_product.6 = (f32[256,2048]{1,0:T(8,128)}, f32[256,2048]{1,0:T(8,128)}) custom-call(s32[2]{0:T(128)} %pad_add_fusion.3.place_ref, bf16[2048,1152]{1,0:T(8,128)(2,1)} %copy-done.2, bf16[2048,1152]{1,0:T(8,128)(2,1)} %copy-done.3, bf16[1152,1536]{1,0:T(8,128)(2,1)} %bitcast.105, bf16[1152,512]{1,0:T(8,128)(2,1)} %bitcast.114), custom_call_target="tpu_custom_call" | custom-call | flops 1 | bytes 1 | tf_op jit(solution)/shard_map/weight_product/pallas_call | solution.py:178
  276.4 8.3 %weight_product.7 = (f32[256,2048]{1,0:T(8,128)}, f32[256,2048]{1,0:T(8,128)}) custom-call(s32[2]{0:T(128)} %pad_add_fusion.4.place_ref, bf16[2048,1152]{1,0:T(8,128)(2,1)} %copy-done.2, bf16[2048,1152]{1,0:T(8,128)(2,1)} %copy-done.3, bf16[1152,1536]{1,0:T(8,128)(2,1)} %bitcast.106, bf16[1152,512]{1,0:T(8,128)(2,1)} %bitcast.115), custom_call_target="tpu_custom_call" | custom-call | flops 1 | bytes 1 | tf_op jit(solution)/shard_map/weight_product/pallas_call | solution.py:178
  296.4 6.6 %collective-permute-done.27 = f32[9,1024]{1,0:T(8,128)S(1)} collective-permute-done((f32[9,1024]{1,0:T(8,128)S(1)}, f32[9,1024]{1,0:T(8,128)S(1)}, u32[]{:S(2)}, u32[]{:S(2)}) %collective-permute-start.27) | collective-permute-done | bytes 36896 | tf_op jit(solution)/shard_map/ppermute | solution.py:290
  303.1 7.6 %collective-permute-done.23 = bf16[2,72,1024]{2,1,0:T(8,128)(2,1)S(1)} collective-permute-done((bf16[2,72,1024]{2,1,0:T(8,128)(2,1)S(1)}, bf16[2,72,1024]{2,1,0:T(8,128)(2,1)S(1)}, u32[]{:S(2)}, u32[]{:S(2)}) %collective-permute-start.23) | collective-permute-done | bytes 294944 | tf_op jit(solution)/shard_map/ppermute | solution.py:287
  310.7 16.2 %collective-permute-done.24 = bf16[2,72,1024]{2,1,0:T(8,128)(2,1)S(1)} collective-permute-done((bf16[2,72,1024]{2,1,0:T(8,128)(2,1)S(1)}, bf16[2,72,1024]{2,1,0:T(8,128)(2,1)S(1)}, u32[]{:S(2)}, u32[]{:S(2)}) %collective-permute-start.24) | collective-permute-done | bytes 294944 | tf_op jit(solution)/shard_map/ppermute | solution.py:287
  336.3 4.8 %collective-permute-done.30 = bf16[2,72,1024]{2,1,0:T(8,128)(2,1)S(1)} collective-permute-done((bf16[2,72,1024]{2,1,0:T(8,128)(2,1)S(1)}, bf16[2,72,1024]{2,1,0:T(8,128)(2,1)S(1)}, u32[]{:S(2)}, u32[]{:S(2)}) %collective-permute-start.30) | collective-permute-done | bytes 294944 | tf_op jit(solution)/shard_map/ppermute | solution.py:299
  342.6 4.8 %collective-permute-done.31 = bf16[2,72,1024]{2,1,0:T(8,128)(2,1)S(1)} collective-permute-done((bf16[2,72,1024]{2,1,0:T(8,128)(2,1)S(1)}, bf16[2,72,1024]{2,1,0:T(8,128)(2,1)S(1)}, u32[]{:S(2)}, u32[]{:S(2)}) %collective-permute-start.31) | collective-permute-done | bytes 294944 | tf_op jit(solution)/shard_map/ppermute | solution.py:299
  349.2 4.6 %collective-permute-done.32 = bf16[2,72,1024]{2,1,0:T(8,128)(2,1)S(1)} collective-permute-done((bf16[2,72,1024]{2,1,0:T(8,128)(2,1)S(1)}, bf16[2,72,1024]{2,1,0:T(8,128)(2,1)S(1)}, u32[]{:S(2)}, u32[]{:S(2)}) %collective-permute-start.32) | collective-permute-done | bytes 294944 | tf_op jit(solution)/shard_map/ppermute | solution.py:299
  354.3 4.8 %collective-permute-done.33 = bf16[2,72,1024]{2,1,0:T(8,128)(2,1)S(1)} collective-permute-done((bf16[2,72,1024]{2,1,0:T(8,128)(2,1)S(1)}, bf16[2,72,1024]{2,1,0:T(8,128)(2,1)S(1)}, u32[]{:S(2)}, u32[]{:S(2)}) %collective-permute-start.33) | collective-permute-done | bytes 294944 | tf_op jit(solution)/shard_map/ppermute | solution.py:299
  359.3 5.3 %collective-permute-done.34 = f32[9,1024]{1,0:T(8,128)S(1)} collective-permute-done((f32[9,1024]{1,0:T(8,128)S(1)}, f32[9,1024]{1,0:T(8,128)S(1)}, u32[]{:S(2)}, u32[]{:S(2)}) %collective-permute-start.34) | collective-permute-done | bytes 36896 | tf_op jit(solution)/shard_map/ppermute | solution.py:290
  (222 shorter events, 150.0 us)
Async XLA Ops:
  9.0 19.7 %collective-permute-start.3 = (bf16[296,1024]{1,0:T(8,128)(2,1)S(1)}, bf16[296,1024]{1,0:T(8,128)(2,1)}, u32[]{:S(2)}, u32[]{:S(2)}) collective-permute-start(bf16[296,1024]{1,0:T(8,128)(2,1)S(1)} %pad_maximum_fusion.6), channel_id=1, source_target_pairs={{0,8},{8,16},{16,24},{24,0},{1,9},{9,17},{17,25},{25,1},{2,10},{10... | collective-permute-start | bytes 1818632 | tf_op jit(solution)/shard_map/ppermute | solution.py:287
  14.0 62.6 %collective-permute-start.1 = (bf16[256,2048]{1,0:T(8,128)(2,1)}, bf16[256,2048]{1,0:T(8,128)(2,1)}, u32[]{:S(2)}, u32[]{:S(2)}) collective-permute-start(bf16[256,2048]{1,0:T(8,128)(2,1)} %pad_maximum_fusion.4), channel_id=1, source_target_pairs={{0,8},{8,16},{16,24},{24,0},{1,9},{9,17},{17,25},{25,1},{2,10},{10... | collective-permute-start | bytes 3145736 | tf_op jit(solution)/shard_map/ppermute | solution.py:287
  15.6 61.1 %collective-permute-start.4 = (bf16[256,2048]{1,0:T(8,128)(2,1)}, bf16[256,2048]{1,0:T(8,128)(2,1)}, u32[]{:S(2)}, u32[]{:S(2)}) collective-permute-start(bf16[256,2048]{1,0:T(8,128)(2,1)} %pad_maximum_fusion.4), channel_id=1, source_target_pairs={{0,4},{2,6},{4,0},{6,2},{1,5},{3,7},{5,1},{7,3},{8,12},{10,14},{12... | collective-permute-start | bytes 3145736 | tf_op jit(solution)/shard_map/ppermute | solution.py:296
  17.3 59.3 %collective-permute-start.2 = (bf16[296,1024]{1,0:T(8,128)(2,1)S(1)}, bf16[296,1024]{1,0:T(8,128)(2,1)}, u32[]{:S(2)}, u32[]{:S(2)}) collective-permute-start(bf16[296,1024]{1,0:T(8,128)(2,1)S(1)} %pad_maximum_fusion.5), channel_id=1, source_target_pairs={{0,16},{8,24},{16,0},{24,8},{1,17},{9,25},{17,1},{25,9},{2,18},{10... | collective-permute-start | bytes 1818632 | tf_op jit(solution)/shard_map/ppermute | solution.py:287
  28.7 47.9 %collective-permute-start.5 = (bf16[296,1024]{1,0:T(8,128)(2,1)}, bf16[296,1024]{1,0:T(8,128)(2,1)S(1)}, u32[]{:S(2)}, u32[]{:S(2)}) collective-permute-start(bf16[296,1024]{1,0:T(8,128)(2,1)} %collective-permute-done.3), channel_id=1, source_target_pairs={{0,1},{1,0},{2,3},{3,2},{4,5},{5,4},{6,7},{7,6},{8,9},{9,8},{10,11... | collective-permute-start | bytes 1818632 | tf_op jit(solution)/shard_map/ppermute | solution.py:299
  76.6 40.2 %collective-permute-start.6 = (bf16[256,2048]{1,0:T(8,128)(2,1)}, bf16[256,2048]{1,0:T(8,128)(2,1)}, u32[]{:S(2)}, u32[]{:S(2)}) collective-permute-start(bf16[256,2048]{1,0:T(8,128)(2,1)} %collective-permute-done.1), channel_id=1, source_target_pairs={{0,8},{8,16},{16,24},{24,0},{1,9},{9,17},{17,25},{25,1},{2,10},{10... | collective-permute-start | bytes 3145736 | tf_op jit(solution)/shard_map/ppermute | solution.py:287
  79.0 37.8 %collective-permute-start.8 = (bf16[256,2048]{1,0:T(8,128)(2,1)}, bf16[256,2048]{1,0:T(8,128)(2,1)S(1)}, u32[]{:S(2)}, u32[]{:S(2)}) collective-permute-start(bf16[256,2048]{1,0:T(8,128)(2,1)} %collective-permute-done.1), channel_id=1, source_target_pairs={{0,4},{2,6},{4,0},{6,2},{1,5},{3,7},{5,1},{7,3},{8,12},{10,14},{12... | collective-permute-start | bytes 3145736 | tf_op jit(solution)/shard_map/ppermute | solution.py:296
  80.8 36.0 %collective-permute-start.7 = (bf16[296,1024]{1,0:T(8,128)(2,1)S(1)}, bf16[296,1024]{1,0:T(8,128)(2,1)S(1)}, u32[]{:S(2)}, u32[]{:S(2)}) collective-permute-start(bf16[296,1024]{1,0:T(8,128)(2,1)S(1)} %pad_maximum_fusion.7), channel_id=1, source_target_pairs={{0,24},{8,0},{16,8},{24,16},{1,25},{9,1},{17,9},{25,17},{2,26},{10... | collective-permute-start | bytes 1818632 | tf_op jit(solution)/shard_map/ppermute | solution.py:287
  118.5 26.9 %collective-permute-start.10 = (bf16[256,2048]{1,0:T(8,128)(2,1)}, bf16[256,2048]{1,0:T(8,128)(2,1)}, u32[]{:S(2)}, u32[]{:S(2)}) collective-permute-start(bf16[256,2048]{1,0:T(8,128)(2,1)} %collective-permute-done.6), channel_id=1, source_target_pairs={{0,8},{8,16},{16,24},{24,0},{1,9},{9,17},{17,25},{25,1},{2,10},{10... | collective-permute-start | bytes 3145736 | tf_op jit(solution)/shard_map/ppermute | solution.py:287
  119.0 26.4 %collective-permute-start.12 = (bf16[256,2048]{1,0:T(8,128)(2,1)}, bf16[256,2048]{1,0:T(8,128)(2,1)}, u32[]{:S(2)}, u32[]{:S(2)}) collective-permute-start(bf16[256,2048]{1,0:T(8,128)(2,1)} %collective-permute-done.6), channel_id=1, source_target_pairs={{0,4},{2,6},{4,0},{6,2},{1,5},{3,7},{5,1},{7,3},{8,12},{10,14},{12... | collective-permute-start | bytes 3145736 | tf_op jit(solution)/shard_map/ppermute | solution.py:296
  147.8 25.3 %collective-permute-start.15 = (bf16[256,2048]{1,0:T(8,128)(2,1)}, bf16[256,2048]{1,0:T(8,128)(2,1)S(1)}, u32[]{:S(2)}, u32[]{:S(2)}) collective-permute-start(bf16[256,2048]{1,0:T(8,128)(2,1)} %collective-permute-done.10), channel_id=1, source_target_pairs={{0,4},{2,6},{4,0},{6,2},{1,5},{3,7},{5,1},{7,3},{8,12},{10,14},{12... | collective-permute-start | bytes 3145736 | tf_op jit(solution)/shard_map/ppermute | solution.py:296
  211.7 26.6 %collective-permute-start.16 = (f16[264,2048]{1,0:T(8,128)(2,1)S(1)}, f16[264,2048]{1,0:T(8,128)(2,1)S(1)}, u32[]{:S(2)}, u32[]{:S(2)}) collective-permute-start(f16[264,2048]{1,0:T(8,128)(2,1)S(1)} %select_convert_fusion.6), channel_id=1, source_target_pairs={{0,4},{2,6},{4,0},{6,2},{1,5},{3,7},{5,1},{7,3},{8,12},{10,14},{12... | collective-permute-start | bytes 3244040 | tf_op jit(solution)/shard_map/ppermute | solution.py:296
  240.8 29.2 %collective-permute-start.21 = (f16[264,2048]{1,0:T(8,128)(2,1)}, f16[264,2048]{1,0:T(8,128)(2,1)}, u32[]{:S(2)}, u32[]{:S(2)}) collective-permute-start(f16[264,2048]{1,0:T(8,128)(2,1)} %select_convert_fusion.5), channel_id=1, source_target_pairs={{0,4},{2,6},{4,0},{6,2},{1,5},{3,7},{5,1},{7,3},{8,12},{10,14},{12... | collective-permute-start | bytes 3244040 | tf_op jit(solution)/shard_map/ppermute | solution.py:296
  241.3 28.8 %collective-permute-start.22 = (f16[264,2048]{1,0:T(8,128)(2,1)}, f16[264,2048]{1,0:T(8,128)(2,1)}, u32[]{:S(2)}, u32[]{:S(2)}) collective-permute-start(f16[264,2048]{1,0:T(8,128)(2,1)} %select_convert_fusion.4), channel_id=1, source_target_pairs={{0,8},{8,16},{16,24},{24,0},{1,9},{9,17},{17,25},{25,1},{2,10},{10... | collective-permute-start | bytes 3244040 | tf_op jit(solution)/shard_map/ppermute | solution.py:287
  257.6 29.1 %collective-permute-start.19 = (f16[8,72,1024]{2,1,0:T(8,128)(2,1)S(1)}, f16[8,72,1024]{2,1,0:T(8,128)(2,1)S(1)}, u32[]{:S(2)}, u32[]{:S(2)}) collective-permute-start(f16[8,72,1024]{2,1,0:T(8,128)(2,1)S(1)} %divide_convert_fusion), channel_id=1, source_target_pairs={{0,1},{1,0},{2,3},{3,2},{4,5},{5,4},{6,7},{7,6},{8,9},{9,8},{10,11... | collective-permute-start | bytes 3538952 | tf_op jit(solution)/shard_map/ppermute | solution.py:299
  269.5 33.6 %collective-permute-start.18 = (f16[264,2048]{1,0:T(8,128)(2,1)}, f16[264,2048]{1,0:T(8,128)(2,1)}, u32[]{:S(2)}, u32[]{:S(2)}) collective-permute-start(f16[264,2048]{1,0:T(8,128)(2,1)} %select_convert_fusion.3), channel_id=1, source_target_pairs={{0,4},{2,6},{4,0},{6,2},{1,5},{3,7},{5,1},{7,3},{8,12},{10,14},{12... | collective-permute-start | bytes 3244040 | tf_op jit(solution)/shard_map/ppermute | solution.py:296
  274.3 52.7 %collective-permute-start.28 = (f16[264,2048]{1,0:T(8,128)(2,1)}, f16[264,2048]{1,0:T(8,128)(2,1)}, u32[]{:S(2)}, u32[]{:S(2)}) collective-permute-start(f16[264,2048]{1,0:T(8,128)(2,1)} %select_convert_fusion.2), channel_id=1, source_target_pairs={{0,8},{8,16},{16,24},{24,0},{1,9},{9,17},{17,25},{25,1},{2,10},{10... | collective-permute-start | bytes 3244040 | tf_op jit(solution)/shard_map/ppermute | solution.py:287
  291.9 18.8 %collective-permute-start.23 = (bf16[2,72,1024]{2,1,0:T(8,128)(2,1)S(1)}, bf16[2,72,1024]{2,1,0:T(8,128)(2,1)S(1)}, u32[]{:S(2)}, u32[]{:S(2)}) collective-permute-start(bf16[2,72,1024]{2,1,0:T(8,128)(2,1)S(1)} %get-tuple-element.137), channel_id=1, source_target_pairs={{0,24},{8,0},{16,8},{24,16},{1,25},{9,1},{17,9},{25,17},{2,26},{10... | collective-permute-start | bytes 884744 | tf_op jit(solution)/shard_map/ppermute | solution.py:287
  295.8 31.2 %collective-permute-start.24 = (bf16[2,72,1024]{2,1,0:T(8,128)(2,1)S(1)}, bf16[2,72,1024]{2,1,0:T(8,128)(2,1)S(1)}, u32[]{:S(2)}, u32[]{:S(2)}) collective-permute-start(bf16[2,72,1024]{2,1,0:T(8,128)(2,1)S(1)} %get-tuple-element.136), channel_id=1, source_target_pairs={{0,16},{8,24},{16,0},{24,8},{1,17},{9,25},{17,1},{25,9},{2,18},{10... | collective-permute-start | bytes 884744 | tf_op jit(solution)/shard_map/ppermute | solution.py:287
  303.1 23.9 %collective-permute-start.25 = (bf16[2,72,1024]{2,1,0:T(8,128)(2,1)S(1)}, bf16[2,72,1024]{2,1,0:T(8,128)(2,1)S(1)}, u32[]{:S(2)}, u32[]{:S(2)}) collective-permute-start(bf16[2,72,1024]{2,1,0:T(8,128)(2,1)S(1)} %get-tuple-element.135), channel_id=1, source_target_pairs={{0,8},{8,16},{16,24},{24,0},{1,9},{9,17},{17,25},{25,1},{2,10},{10... | collective-permute-start | bytes 884744 | tf_op jit(solution)/shard_map/ppermute | solution.py:287
  333.3 31.4 %collective-permute-start.35 = (f16[264,2048]{1,0:T(8,128)(2,1)S(1)}, f16[264,2048]{1,0:T(8,128)(2,1)S(1)}, u32[]{:S(2)}, u32[]{:S(2)}) collective-permute-start(f16[264,2048]{1,0:T(8,128)(2,1)S(1)} %select_convert_fusion.1), channel_id=1, source_target_pairs={{0,4},{2,6},{4,0},{6,2},{1,5},{3,7},{5,1},{7,3},{8,12},{10,14},{12... | collective-permute-start | bytes 3244040 | tf_op jit(solution)/shard_map/ppermute | solution.py:296
  334.8 29.8 %collective-permute-start.29 = (f16[264,2048]{1,0:T(8,128)(2,1)}, f16[264,2048]{1,0:T(8,128)(2,1)S(1)}, u32[]{:S(2)}, u32[]{:S(2)}) collective-permute-start(f16[264,2048]{1,0:T(8,128)(2,1)} %select_convert_fusion), channel_id=1, source_target_pairs={{0,8},{8,16},{16,24},{24,0},{1,9},{9,17},{17,25},{25,1},{2,10},{10... | collective-permute-start | bytes 3244040 | tf_op jit(solution)/shard_map/ppermute | solution.py:287
  334.8 18.9 %collective-permute-start.32 = (bf16[2,72,1024]{2,1,0:T(8,128)(2,1)S(1)}, bf16[2,72,1024]{2,1,0:T(8,128)(2,1)S(1)}, u32[]{:S(2)}, u32[]{:S(2)}) collective-permute-start(bf16[2,72,1024]{2,1,0:T(8,128)(2,1)S(1)} %collective-permute-done.24), channel_id=1, source_target_pairs={{0,1},{1,0},{2,3},{3,2},{4,5},{5,4},{6,7},{7,6},{8,9},{9,8},{10,11... | collective-permute-start | bytes 884744 | tf_op jit(solution)/shard_map/ppermute | solution.py:299
  341.1 18.0 %collective-permute-start.33 = (bf16[2,72,1024]{2,1,0:T(8,128)(2,1)S(1)}, bf16[2,72,1024]{2,1,0:T(8,128)(2,1)S(1)}, u32[]{:S(2)}, u32[]{:S(2)}) collective-permute-start(bf16[2,72,1024]{2,1,0:T(8,128)(2,1)S(1)} %collective-permute-done.25), channel_id=1, source_target_pairs={{0,1},{1,0},{2,3},{3,2},{4,5},{5,4},{6,7},{7,6},{8,9},{9,8},{10,11... | collective-permute-start | bytes 884744 | tf_op jit(solution)/shard_map/ppermute | solution.py:299
  (35 other events, 369.9 us)
